TPU v7x, 256 devices: a whole 4x4x8 slice. The times are simulated.
256 devices in a mesh: gx: 8 (over x, core), gy: 32 (over y, z).
Axes of the slice: x: 4, y: 4, z: 8, core: 2. Of those that a mesh axis runs over, the one named last changes fastest.
Arguments:
- features: bfloat16 [2048, 64, 128], P(('gx', 'gy')), may hold values from -6 to 6
- weights: bfloat16 [27, 128, 128], replicated, may hold values from -0.109375 to 0.109375
- cotangent: bfloat16 [2048, 64, 128], P(('gx', 'gy')), may hold values from -6 to 6
- dst_index: int32 [27, 2048], P(None, ('gx', 'gy')), may hold values from 0 to 48, as said below
- recv_slot: int32 [10240], P(('gx', 'gy')), may hold values from 0 to 8, as said below
Outputs:
- outputs: bfloat16 [2048, 64, 128], P(('gx', 'gy'))
- input_grad: bfloat16 [2048, 64, 128], P(('gx', 'gy'))
- weight_grad: float32 [27, 128, 128], replicated
Inputs may be any that keep to these rules, and one draw needn't show every extreme that they name: `dst_index`: A value below 8 is an occupied slot of the same device; from 8 to 47 an occupied brick of the tile beside it; 48 means no occupied neighbour. Occupied slots of a device come first; an unoccupied slot has 48 for every offset. Some device has all 8 slots occupied. `recv_slot`: 8 marks a halo layer position with no occupied brick.
All inputs are finite; a program needn't handle non-finite values.
Results may differ from a plain program's by a relative error of at most 0.003.
Values may be sent and summed in bfloat16 or wider, within the bound.
No kernel may reach another device: no remote copies, remote signals or barrier semaphores. Data moves between devices by JAX's collectives and lax.ppermute only.
A program may use at most 64 MiB of HBM per device.

v0:
```python
import jax
import jax.numpy as jnp
from jax import lax
from jax.sharding import PartitionSpec as P

BRICK = 4
TILE = 4
BZ = 2
HALO = 40


DIRECTIONS = ((1, 0), (-1, 0), (0, 1), (0, -1), (1, 1), (1, -1), (-1, 1), (-1, -1))
OFFSETS = tuple(((a, b, c) for a in (-1, 0, 1) for b in (-1, 0, 1) for c in (-1, 0, 1)))


def passed_along(value, axis, steps):
    count = lax.axis_size(axis)
    initial, last = (max(0, -steps), min(count, count - steps))
    return lax.ppermute(value, axis, [(source, source + steps) for source in range(initial, last)])


def split_halo(buffers, axis_dim):
    portions = {}
    begin_at = 0
    for number, heading in enumerate(DIRECTIONS):
        length = TILE * BZ if number < 4 else BZ
        portions[heading] = lax.slice_in_dim(buffers, begin_at, begin_at + length, axis=axis_dim)
        begin_at += length
    return portions


def send_partials(outgoing):
    face_cells = TILE * BZ
    portions = split_halo(outgoing, 0)
    relayed = {}
    landed = {}
    for heading in (1, -1):
        packet = jnp.concatenate(
            (portions[heading, 0], portions[heading, 1], portions[heading, -1]), axis=0
        )
        arrived = passed_along(packet.astype(jnp.bfloat16), "gx", heading).astype(packet.dtype)
        landed[heading, 0] = arrived[:face_cells]
        relayed[heading, 1] = arrived[face_cells : face_cells + BZ]
        relayed[heading, -1] = arrived[face_cells + BZ :]
    for heading in (1, -1):
        packet = jnp.concatenate(
            (portions[0, heading], relayed[1, heading], relayed[-1, heading]), axis=0
        )
        arrived = passed_along(packet.astype(jnp.bfloat16), "gy", heading).astype(packet.dtype)
        landed[0, heading] = arrived[:face_cells]
        landed[1, heading] = arrived[face_cells : face_cells + BZ]
        landed[-1, heading] = arrived[face_cells + BZ :]
    return jnp.concatenate([landed[heading] for heading in DIRECTIONS], axis=0)


def fetch_bricks(buffers):
    face_cells = TILE * BZ
    portions = split_halo(buffers, 1)
    relayed = {}
    landed = {}
    for heading in (1, -1):
        packet = jnp.concatenate(
            (portions[0, -heading], portions[1, -heading], portions[-1, -heading]), axis=1
        )
        arrived = passed_along(packet, "gy", heading)
        landed[0, -heading] = arrived[:, :face_cells]
        relayed[1, -heading] = arrived[:, face_cells : face_cells + BZ]
        relayed[-1, -heading] = arrived[:, face_cells + BZ :]
    for heading in (1, -1):
        packet = jnp.concatenate(
            (portions[-heading, 0], relayed[-heading, 1], relayed[-heading, -1]), axis=1
        )
        arrived = passed_along(packet, "gx", heading)
        landed[-heading, 0] = arrived[:, :face_cells]
        landed[-heading, 1] = arrived[:, face_cells : face_cells + BZ]
        landed[-heading, -1] = arrived[:, face_cells + BZ :]
    return jnp.concatenate([landed[heading] for heading in DIRECTIONS], axis=1)


def brick_taps(gathered, orient):
    group_size = gathered.shape[0]
    channels = gathered.shape[-1]
    edge = BRICK
    volume = gathered.reshape(group_size, 3, 3, 3, edge, edge, edge, channels)
    volume = jnp.transpose(volume, (0, 1, 4, 2, 5, 3, 6, 7)).reshape(
        group_size, 3 * edge, 3 * edge, 3 * edge, channels
    )
    tap_list = []
    for shift_x, shift_y, shift_z in OFFSETS:
        begin_x = edge + orient * shift_x
        begin_y = edge + orient * shift_y
        begin_z = edge + orient * shift_z
        window = volume[
            :, begin_x : begin_x + edge, begin_y : begin_y + edge, begin_z : begin_z + edge
        ]
        tap_list.append(window.reshape(group_size, edge * edge * edge, channels))
    return jnp.concatenate(tap_list, axis=-1)


def region_pieces(spread):
    group_size = spread.shape[0]
    channels = spread.shape[-1] // 27
    edge = BRICK
    shaped = spread.reshape(group_size, edge, edge, edge, 27, channels)
    region = jnp.zeros((group_size, 3 * edge, 3 * edge, 3 * edge, channels), jnp.float32)
    for number, (shift_x, shift_y, shift_z) in enumerate(OFFSETS):
        region = region + jnp.pad(
            shaped[:, :, :, :, number],
            (
                (0, 0),
                (edge - shift_x, edge + shift_x),
                (edge - shift_y, edge + shift_y),
                (edge - shift_z, edge + shift_z),
                (0, 0),
            ),
        )
    pieces = region.reshape(group_size, 3, edge, 3, edge, 3, edge, channels)
    pieces = jnp.transpose(pieces, (0, 1, 3, 5, 2, 4, 6, 7))
    return pieces.reshape(group_size, 27, edge * edge * edge, channels)


def local(features, weights, cotangent, dst_index, recv_slot):
    bricks, voxels, channels = features.shape
    w_back = jnp.transpose(weights, (0, 2, 1)).reshape(27 * channels, channels)
    neighbour_ids = dst_index.T
    zero_rows = jnp.zeros((1, voxels, channels), jnp.bfloat16)
    w_spread = jnp.transpose(weights, (1, 0, 2)).reshape(channels, 27 * channels)
    totals = jnp.zeros((bricks + HALO + 1, voxels, channels), jnp.float32)
    spread = jnp.dot(features, w_spread, preferred_element_type=jnp.float32)
    totals = totals.at[neighbour_ids].add(region_pieces(spread))
    incoming = send_partials(totals[bricks : bricks + HALO])
    own_rows = jnp.concatenate(
        (totals[:bricks], jnp.zeros((1, voxels, channels), jnp.float32)), axis=0
    )
    outputs = own_rows.at[recv_slot].add(incoming)[:bricks].astype(jnp.bfloat16)
    values = cotangent[None]
    padding = jnp.zeros((values.shape[0], 1, voxels, channels), values.dtype)
    extended = jnp.concatenate((values, padding), axis=1)
    arrived = fetch_bricks(extended[:, recv_slot])
    grad_ext = jnp.concatenate((cotangent, arrived[0], zero_rows), axis=0)
    backward = brick_taps(grad_ext[neighbour_ids], -1)
    grad_list = jnp.dot(backward, w_back, preferred_element_type=jnp.float32).astype(jnp.bfloat16)
    grad_total = lax.dot_general(
        features.reshape(-1, channels),
        backward.reshape(-1, 27 * channels),
        (((0,), (0,)), ((), ())),
        preferred_element_type=jnp.float32,
    )
    grad_total = lax.psum(grad_total, ("gx", "gy"))
    weight_grad = jnp.transpose(grad_total.reshape(channels, 27, channels), (1, 0, 2)) / float(
        voxels * bricks
    )
    return (outputs, grad_list, weight_grad)


def solution(mesh):
    return jax.shard_map(
        local,
        mesh=mesh,
        in_specs=(
            P(("gx", "gy"), None, None),
            P(),
            P(("gx", "gy"), None, None),
            P(None, ("gx", "gy")),
            P(("gx", "gy")),
        ),
        out_specs=(P(("gx", "gy"), None, None), P(("gx", "gy"), None, None), P()),
        check_vma=False,
    )
```

profile of v0, /device:TPU:1, one launch (start us, length us, event | category | flops | bytes accessed | tf_op | source)
XLA Modules:
  0.0 376.0 jit_solution(17206433932038999144)
XLA Ops:
  7.2 0.8 compare_select_fusion
  8.0 0.1 reshape.166
  8.1 0.7 compare_select_fusion.1
  8.7 0.9 pad_bitcast_fusion
  9.7 0.7 gather_fusion
  10.4 0.7 fusion.7
  11.1 0.7 pad_maximum_fusion.4
  11.8 1.3 collective-permute-start.4
  13.1 0.7 pad_maximum_fusion.5
  13.8 5.7 %collective-permute-start.5 = (bf16[1,12,64,128]{3,2,1,0:T(8,128)(2,1)}, bf16[1,12,64,128]{3,2,1,0:T(8,128)(2,1)}, u32[]{:S(2)}, u32[]{:S(2)}) collective-permute-start(bf16[1,12,64,128]{3,2,1,0:T(8,128)(2,1)} %pad_maximum_fusion.5), channel_id=1, source_target_pairs={{0,1},{1,2},{2,3},{3,4},{4,5},{5,6},{6,7},{7,8},{8,9},{9,10},{10,1... | collective-permute-start | bytes 589832 | tf_op jit(solution)/shard_map/ppermute | solution.py:19
  19.5 1.3 copy.96
  20.8 1.1 fusion
  21.9 1.5 slice_bitcast_fusion.26
  23.4 1.3 slice_bitcast_fusion.25
  24.8 11.1 %pad_add_fusion = f32[8,12,12,12,128]{4,0,3,2,1:T(8,128)S(1)} fusion(f32[8,4,4,4,128]{4,0,3,2,1:T(8,128)} %get-tuple-element.28, f32[8,4,4,4,128]{4,0,3,2,1:T(8,128)} %get-tuple-element.29, f32[8,4,4,4,128]{4,0,3,2,1:T(8,128)S(1)} %get-tuple-element.4, f32[8,4,4,4,128]{4,0,3,2,1:T(8,128)S(1)} %get-tuple-element.5, ...), kind=kLoop, calls=%fused_computation.4 | loop fusion | flops 46006272 | bytes 14155776 | tf_op jit(solution)/shard_map/add | solution.py:107
  35.8 4.8 %copy.124 = f32[8,3,3,3,4,4,4,128]{7,6,5,4,3,2,1,0:T(4,128)} copy(f32[8,3,3,3,4,4,4,128]{7,0,6,3,5,2,4,1:T(8,128)S(1)} %bitcast.180) | data formatting | bytes 14155776 | tf_op jit(solution)/shard_map/transpose | solution.py:118
  40.6 0.2 broadcast_in_dim.19
  40.8 23.3 %scatter_fusion = f32[49,64,128]{2,1,0:T(8,128)S(1)} fusion(f32[49,64,128]{2,1,0:T(8,128)S(1)} %broadcast_in_dim.19, s32[216]{0:T(256)S(1)} %reshape.166, f32[216,64,128]{2,1,0:T(8,128)} %bitcast.181), kind=kCustom, calls=%fused_computation.2 | custom fusion | flops 1769472 | bytes 21234528 | tf_op jit(solution)/shard_map/scatter-add | solution.py:130
  64.1 0.1 convert.27
  64.4 4.7 %collective-permute-start.1 = (bf16[12,64,128]{2,1,0:T(8,128)(2,1)S(1)}, bf16[12,64,128]{2,1,0:T(8,128)(2,1)S(1)}, u32[]{:S(2)}, u32[]{:S(2)}) collective-permute-start(bf16[12,64,128]{2,1,0:T(8,128)(2,1)S(1)} %pad_maximum_fusion.1), channel_id=1, source_target_pairs={{32,0},{64,32},{96,64},{128,96},{160,128},{192,160},{224,192},{33,... | collective-permute-start | bytes 589832 | tf_op jit(solution)/shard_map/ppermute | solution.py:19
  69.1 1.9 collective-permute-start
  71.1 0.1 pad.139.clone
  71.1 0.1 slice_select_fusion
  71.2 0.8 fusion.9
  72.0 0.8 fusion.10
  72.8 2.4 collective-permute-start.6
  75.3 3.1 collective-permute-start.7
  78.6 1.3 collective-permute-start.3
  79.9 4.2 %collective-permute-start.2 = (bf16[12,64,128]{2,1,0:T(8,128)(2,1)S(1)}, bf16[12,64,128]{2,1,0:T(8,128)(2,1)S(1)}, u32[]{:S(2)}, u32[]{:S(2)}) collective-permute-start(bf16[12,64,128]{2,1,0:T(8,128)(2,1)S(1)} %pad_maximum_fusion.2), channel_id=1, source_target_pairs={{0,1},{1,2},{2,3},{3,4},{4,5},{5,6},{6,7},{7,8},{8,9},{9,10},{10,1... | collective-permute-start | bytes 589832 | tf_op jit(solution)/shard_map/ppermute | solution.py:19
  84.2 1.1 slice_dynamic-update-slice_fusion.3
  85.3 0.9 slice_dynamic-update-slice_fusion.2
  86.3 0.1 maximum_maximum_fusion
  86.4 2.8 gather_fusion.1
  89.2 6.1 %copy.125 = bf16[8,3,4,3,4,3,4,128]{7,0,6,5,4,3,2,1:T(8,128)(2,1)S(1)} copy(bf16[8,3,4,3,4,3,4,128]{7,6,4,2,5,3,1,0:T(4,128)(2,1)} %bitcast.184) | data formatting | bytes 7077888 | tf_op jit(solution)/shard_map/transpose | solution.py:85
  95.3 0.1 fusion.4
  95.5 0.5 fusion.3
  96.0 0.1 copy.126
  96.1 0.1 copy.127
  96.1 0.1 copy.128
  96.2 0.1 copy.129
  98.7 1.7 copy-done.8
  100.5 2.3 convolution_bitcast_fusion
  103.0 2.9 scatter_fusion.1
  106.0 0.7 slice.546
  106.7 3.7 convolution_convert_fusion
  110.4 255.2 %all-reduce.30.cloned.1.call-done = f32[128,3456]{0,1:T(8,128)} async-done(((f32[128,3456]{0,1:T(8,128)}), f32[128,3456]{0,1:T(8,128)}) %all-reduce.30.cloned.1.call-update) | async-done | bytes 1769488 | tf_op jit(solution)/shard_map/psum | solution.py:149
  365.6 1.6 broadcast_multiply_fusion
  367.2 1.9 copy.154
  (105 shorter events, 2.7 us)
Async XLA Ops:
  7.2 12.3 %copy-start.2 = (bf16[27,128,128]{2,1,0:T(8,128)(2,1)S(1)}, bf16[27,128,128]{2,1,0:T(8,128)(2,1)}, u32[]{:S(2)}) copy-start(bf16[27,128,128]{2,1,0:T(8,128)(2,1)} %param.6) | copy-start | bytes 2654212
  7.2 13.6 %copy-start.6 = (bf16[8,64,128]{2,1,0:T(8,128)(2,1)S(1)}, bf16[8,64,128]{2,1,0:T(8,128)(2,1)}, u32[]{:S(2)}) copy-start(bf16[8,64,128]{2,1,0:T(8,128)(2,1)} %param.5) | copy-start | bytes 393220
  7.2 358.5 %all-reduce.30.cloned.1.call-start = ((), (), s32[]{:S(2)}) async-start(), calls=%async_computation | async-start | bytes 3538944 | tf_op jit(solution)/shard_map/psum | solution.py:149
  11.8 59.4 %collective-permute-start.4 = (bf16[1,12,64,128]{3,2,1,0:T(8,128)(2,1)}, bf16[1,12,64,128]{3,2,1,0:T(8,128)(2,1)}, u32[]{:S(2)}, u32[]{:S(2)}) collective-permute-start(bf16[1,12,64,128]{3,2,1,0:T(8,128)(2,1)} %pad_maximum_fusion.4), channel_id=1, source_target_pairs={{1,0},{2,1},{3,2},{4,3},{5,4},{6,5},{7,6},{8,7},{9,8},{10,9},{11,1... | collective-permute-start | bytes 589832 | tf_op jit(solution)/shard_map/ppermute | solution.py:19
  13.8 58.2 %collective-permute-start.5 = (bf16[1,12,64,128]{3,2,1,0:T(8,128)(2,1)}, bf16[1,12,64,128]{3,2,1,0:T(8,128)(2,1)}, u32[]{:S(2)}, u32[]{:S(2)}) collective-permute-start(bf16[1,12,64,128]{3,2,1,0:T(8,128)(2,1)} %pad_maximum_fusion.5), channel_id=1, source_target_pairs={{0,1},{1,2},{2,3},{3,4},{4,5},{5,6},{6,7},{7,8},{8,9},{9,10},{10,1... | collective-permute-start | bytes 589832 | tf_op jit(solution)/shard_map/ppermute | solution.py:19
  64.1 7.0 %copy-start.9 = (pred[9]{0:T(512)(128)(4,1)S(1)}, pred[9]{0:T(512)(128)(4,1)}, u32[]{:S(2)}) copy-start(pred[9]{0:T(512)(128)(4,1)} %constant.7.clone.1) | copy-start | bytes 31
  64.1 8.7 %copy-start.5 = (bf16[1,8,64,128]{3,2,1,0:T(8,128)(2,1)S(1)}, bf16[1,8,64,128]{3,2,1,0:T(8,128)(2,1)}, u32[]{:S(2)}) copy-start(bf16[1,8,64,128]{3,2,1,0:T(8,128)(2,1)} %get-tuple-element.66) | copy-start | bytes 393220
  64.1 11.1 %copy-start.4 = (bf16[1,8,64,128]{3,2,1,0:T(8,128)(2,1)S(1)}, bf16[1,8,64,128]{3,2,1,0:T(8,128)(2,1)}, u32[]{:S(2)}) copy-start(bf16[1,8,64,128]{3,2,1,0:T(8,128)(2,1)} %get-tuple-element.63) | copy-start | bytes 393220
  64.3 22.0 %copy-start.3 = (bf16[8,64,128]{2,1,0:T(8,128)(2,1)S(1)}, bf16[8,64,128]{2,1,0:T(8,128)(2,1)}, u32[]{:S(2)}) copy-start(bf16[8,64,128]{2,1,0:T(8,128)(2,1)} %param.7) | copy-start | bytes 393220
  64.4 14.1 %collective-permute-start.1 = (bf16[12,64,128]{2,1,0:T(8,128)(2,1)S(1)}, bf16[12,64,128]{2,1,0:T(8,128)(2,1)S(1)}, u32[]{:S(2)}, u32[]{:S(2)}) collective-permute-start(bf16[12,64,128]{2,1,0:T(8,128)(2,1)S(1)} %pad_maximum_fusion.1), channel_id=1, source_target_pairs={{32,0},{64,32},{96,64},{128,96},{160,128},{192,160},{224,192},{33,... | collective-permute-start | bytes 589832 | tf_op jit(solution)/shard_map/ppermute | solution.py:19
  69.1 9.4 %collective-permute-start = (bf16[12,64,128]{2,1,0:T(8,128)(2,1)S(1)}, bf16[12,64,128]{2,1,0:T(8,128)(2,1)S(1)}, u32[]{:S(2)}, u32[]{:S(2)}) collective-permute-start(bf16[12,64,128]{2,1,0:T(8,128)(2,1)S(1)} %pad_maximum_fusion), channel_id=1, source_target_pairs={{0,32},{32,64},{64,96},{96,128},{128,160},{160,192},{192,224},{1,3... | collective-permute-start | bytes 589832 | tf_op jit(solution)/shard_map/ppermute | solution.py:19
  72.8 11.3 %collective-permute-start.6 = (bf16[1,12,64,128]{3,2,1,0:T(8,128)(2,1)S(1)}, bf16[1,12,64,128]{3,2,1,0:T(8,128)(2,1)S(1)}, u32[]{:S(2)}, u32[]{:S(2)}) collective-permute-start(bf16[1,12,64,128]{3,2,1,0:T(8,128)(2,1)S(1)} %pad_maximum_fusion.6), channel_id=1, source_target_pairs={{32,0},{64,32},{96,64},{128,96},{160,128},{192,160},{224,192},{33,... | collective-permute-start | bytes 589832 | tf_op jit(solution)/shard_map/ppermute | solution.py:19
  75.3 8.9 %collective-permute-start.7 = (bf16[1,12,64,128]{3,2,1,0:T(8,128)(2,1)S(1)}, bf16[1,12,64,128]{3,2,1,0:T(8,128)(2,1)S(1)}, u32[]{:S(2)}, u32[]{:S(2)}) collective-permute-start(bf16[1,12,64,128]{3,2,1,0:T(8,128)(2,1)S(1)} %pad_maximum_fusion.7), channel_id=1, source_target_pairs={{0,32},{32,64},{64,96},{96,128},{128,160},{160,192},{192,224},{1,3... | collective-permute-start | bytes 589832 | tf_op jit(solution)/shard_map/ppermute | solution.py:19
  78.6 24.4 %collective-permute-start.3 = (bf16[12,64,128]{2,1,0:T(8,128)(2,1)S(1)}, bf16[12,64,128]{2,1,0:T(8,128)(2,1)S(1)}, u32[]{:S(2)}, u32[]{:S(2)}) collective-permute-start(bf16[12,64,128]{2,1,0:T(8,128)(2,1)S(1)} %pad_maximum_fusion.3), channel_id=1, source_target_pairs={{1,0},{2,1},{3,2},{4,3},{5,4},{6,5},{7,6},{8,7},{9,8},{10,9},{11,1... | collective-permute-start | bytes 589832 | tf_op jit(solution)/shard_map/ppermute | solution.py:19
  79.9 22.9 %collective-permute-start.2 = (bf16[12,64,128]{2,1,0:T(8,128)(2,1)S(1)}, bf16[12,64,128]{2,1,0:T(8,128)(2,1)S(1)}, u32[]{:S(2)}, u32[]{:S(2)}) collective-permute-start(bf16[12,64,128]{2,1,0:T(8,128)(2,1)S(1)} %pad_maximum_fusion.2), channel_id=1, source_target_pairs={{0,1},{1,2},{2,3},{3,4},{4,5},{5,6},{6,7},{7,8},{8,9},{9,10},{10,1... | collective-permute-start | bytes 589832 | tf_op jit(solution)/shard_map/ppermute | solution.py:19
  84.1 2.1 copy-start
  97.6 2.9 copy-start.7
  98.7 1.8 copy-start.8
  100.5 2.4 copy-start.1
Sparse Core Ops, SparseCore 0:
  102.9 262.6 all-reduce.29
where the time goes:
time: 378 us; the launch traced here: 376 us
  waiting for transfers between devices  255 us (67%)
  other arithmetic  42.4 us (11%)
  local copies, waits for them, and re-layouts  31.6 us (8%)
  starting transfers between devices  24.6 us (7%)
  between operations  15 us (4%)
  matrix products  7.16 us (2%)
    psum x1, waiting for transfers between devices, local(): grad_total = lax.psum(grad_total, ('gx', 'gy'))  255 us
    ppermute x8, starting transfers between devices, passed_along(): lax.ppermute(value, axis, [(source, source + steps) for source in range(i...  24.6 us
    scatter-add x1, other arithmetic, local(): totals = totals.at[neighbour_ids].add(region_pieces(spread))  23.3 us
    add x1, other arithmetic, region_pieces(): region + jnp.pad(shaped[:, :, :, :, number], ((0, 0), (edge - shift_x, ed...  11.1 us
  transfers between devices with their start and end apart: 9, of which 1 were waited for; matrix products, arithmetic and copies ran while one was open for 19% of the time, Pallas kernels for 0%

commit v1 on v0

v1 whole, which is shorter than its diff:
```python
import functools

import jax
import jax.numpy as jnp
import numpy as np
from jax import lax
from jax.experimental import pallas as pl
from jax.experimental.pallas import tpu as pltpu
from jax.sharding import Mesh, PartitionSpec as P

BRICK = 4
TILE = 4
BZ = 2
HALO = 40
SLOTS = 8
VOXELS = 64
CHANNELS = 128
PLANE = BRICK * BRICK
PLANES = BRICK + 2
WIDE = 9 * CHANNELS
ROWS_M = 28

DIRECTIONS = ((1, 0), (-1, 0), (0, 1), (0, -1), (1, 1), (1, -1), (-1, 1), (-1, -1))
LENGTHS = (TILE * BZ,) * 4 + (BZ,) * 4
AXES = ("x", "c", "y", "z")
VMEM_LIMIT = 48 * 1024 * 1024


def shift_matrix():
    picked = np.zeros((9 * PLANE, 9 * PLANE), np.float32)
    for number in range(9):
        for voxel in range(PLANE):
            y = voxel // BRICK + number // 3 - 1 + BRICK
            z = voxel % BRICK + number % 3 - 1 + BRICK
            source = (y // BRICK * 3 + z // BRICK) * PLANE + y % BRICK * BRICK + z % BRICK
            picked[number * PLANE + voxel, source] = 1.0
    return picked


def pack_kernel(slot_ref, features_ref, cotangent_ref, *packets):
    begin_at = 0
    for packet in packets:
        for position in range(packet.shape[0]):
            slot = slot_ref[begin_at + position]
            row = jnp.clip(slot, 0, SLOTS - 1)

            @pl.when(slot < SLOTS)
            def _():
                packet[position, :, :CHANNELS] = features_ref[row]
                packet[position, :, CHANNELS:] = cotangent_ref[row]

            @pl.when(slot >= SLOTS)
            def _():
                packet[position] = jnp.zeros((VOXELS, 2 * CHANNELS), jnp.bfloat16)

        begin_at += packet.shape[0]


def pack(recv_slot, features, cotangent):
    vmem = pl.BlockSpec(memory_space=pltpu.VMEM)
    return pl.pallas_call(
        pack_kernel,
        in_specs=[pl.BlockSpec(memory_space=pltpu.SMEM), vmem, vmem],
        out_specs=[vmem] * 8,
        out_shape=[
            jax.ShapeDtypeStruct((length, VOXELS, 2 * CHANNELS), jnp.bfloat16) for length in LENGTHS
        ],
        compiler_params=pltpu.CompilerParams(vmem_limit_bytes=VMEM_LIMIT),
    )(recv_slot, features, cotangent)


def conv_kernel(
    core_ref, dst_ref, features_ref, cotangent_ref, *rest
):
    halos = rest[:8]
    (flipped_ref, shift_ref, weights_ref, w_back_ref, outputs_ref, grad_ref, send_ref, keep_ref,
     bricks, taps_f, taps_c) = rest[8:]
    bricks[:SLOTS, :, :CHANNELS] = features_ref[...]
    bricks[:SLOTS, :, CHANNELS:] = cotangent_ref[...]
    begin_at = SLOTS
    for halo in halos:
        bricks[begin_at : begin_at + halo.shape[0]] = halo[...]
        begin_at += halo.shape[0]
    bricks[begin_at] = jnp.zeros((VOXELS, 2 * CHANNELS), jnp.bfloat16)

    def one_slot(slot, carry):
        for plane in range(PLANES):
            side = 0 if plane == 0 else 2 if plane == PLANES - 1 else 1
            local = (plane - 1) % BRICK * PLANE
            around = [
                bricks[jnp.clip(dst_ref[side * 9 + number, slot], 0, SLOTS + HALO), local : local + PLANE]
                for number in range(9)
            ]
            moved = jnp.dot(
                shift_ref[...], jnp.concatenate(around, axis=0), preferred_element_type=jnp.float32
            ).astype(jnp.bfloat16)
            for number in range(9):
                rows = moved[number * PLANE : (number + 1) * PLANE]
                lanes = slice(number * CHANNELS, (number + 1) * CHANNELS)
                taps_f[slot, plane, :, lanes] = rows[:, :CHANNELS]
                taps_c[slot, plane, :, lanes] = rows[:, CHANNELS:]
        return carry

    lax.fori_loop(0, SLOTS, one_slot, 0)

    core = core_ref[0]
    flipped = jnp.concatenate((flipped_ref[1 - core], flipped_ref[core]), axis=0)
    half = CHANNELS // 2
    for side in range(3):
        tap = taps_c[:, side : side + BRICK].reshape(SLOTS * VOXELS, WIDE)
        part = jnp.dot(flipped, tap, preferred_element_type=jnp.float32)
        for number in range(9):
            block = part[:, number * CHANNELS : (number + 1) * CHANNELS]
            m = side * 9 + number
            for quarter in range(4):
                rows = slice(quarter * 16, quarter * 16 + 16)
                send_ref[quarter, m] = block[:half][rows].astype(jnp.bfloat16)
                keep_ref[quarter, m] = block[half:][rows]
    for quarter in range(4):
        send_ref[quarter, 27] = jnp.zeros((16, CHANNELS), jnp.bfloat16)
        keep_ref[quarter, 27] = jnp.zeros((16, CHANNELS), jnp.float32)

    for source, kernel, target in (
        (taps_f, weights_ref, outputs_ref), (taps_c, w_back_ref, grad_ref)
    ):
        total = None
        for side in range(3):
            tap = source[:, side : side + BRICK].reshape(SLOTS * VOXELS, WIDE)
            matrix = kernel[side * 9 : side * 9 + 9].reshape(WIDE, CHANNELS)
            part = jnp.dot(tap, matrix, preferred_element_type=jnp.float32)
            total = part if total is None else total + part
        target[...] = total.astype(jnp.bfloat16).reshape(SLOTS, VOXELS, CHANNELS)


def convolve(core, dst_index, features, cotangent, halos, flipped, shift, weights, w_back):
    vmem = pl.BlockSpec(memory_space=pltpu.VMEM)
    smem = pl.BlockSpec(memory_space=pltpu.SMEM)
    return pl.pallas_call(
        conv_kernel,
        in_specs=[smem, smem] + [vmem] * 14,
        out_specs=[vmem] * 4,
        out_shape=[
            jax.ShapeDtypeStruct((SLOTS, VOXELS, CHANNELS), jnp.bfloat16),
            jax.ShapeDtypeStruct((SLOTS, VOXELS, CHANNELS), jnp.bfloat16),
            jax.ShapeDtypeStruct((4, ROWS_M, 16, CHANNELS), jnp.bfloat16),
            jax.ShapeDtypeStruct((4, ROWS_M, 16, CHANNELS), jnp.float32),
        ],
        scratch_shapes=[
            pltpu.VMEM((SLOTS + HALO + 1, VOXELS, 2 * CHANNELS), jnp.bfloat16),
            pltpu.VMEM((SLOTS, PLANES, PLANE, WIDE), jnp.bfloat16),
            pltpu.VMEM((SLOTS, PLANES, PLANE, WIDE), jnp.bfloat16),
        ],
        compiler_params=pltpu.CompilerParams(vmem_limit_bytes=VMEM_LIMIT),
    )(core, dst_index, features, cotangent, *halos, flipped, shift, weights, w_back)


def pass_to(value, step_x, step_y):
    pairs = []
    for gx in range(8):
        for gy in range(32):
            if 0 <= gx + step_x < 8 and 0 <= gy + step_y < 32:
                pairs.append((gx * 32 + gy, (gx + step_x) * 32 + gy + step_y))
    return lax.ppermute(value, AXES, pairs)


def local(features, weights, cotangent, dst_index, recv_slot):
    packets = pack(recv_slot, features, cotangent)
    halos = [None] * 8
    for number in (2, 3, 0, 1, 4, 5, 6, 7):
        step_x, step_y = DIRECTIONS[number]
        halos[number] = pass_to(packets[number], -step_x, -step_y)
    core = lax.axis_index("c").astype(jnp.int32).reshape(1)
    flipped = jnp.transpose(features.reshape(SLOTS * VOXELS, CHANNELS)).reshape(2, CHANNELS // 2, SLOTS * VOXELS)
    w_back = jnp.transpose(weights[::-1], (0, 2, 1))
    shift = jnp.asarray(shift_matrix(), jnp.bfloat16)
    outputs, input_grad, send, keep = convolve(
        core, dst_index, features, cotangent, halos, flipped, shift, weights, w_back
    )
    arrived = lax.ppermute(send, "c", [(0, 1), (1, 0)])
    chip_sum = (keep + arrived.astype(jnp.float32)).astype(jnp.bfloat16)
    parts = chip_sum.reshape(16, 7, 16, CHANNELS)
    parts = lax.all_to_all(parts, ("x", "y"), 0, 0)
    share = jnp.sum(parts.astype(jnp.float32), axis=0)
    column = jnp.broadcast_to(share[None], (8,) + share.shape)
    column = lax.all_to_all(column, "z", 0, 0)
    share = (jnp.sum(column, axis=0) * (1.0 / (VOXELS * SLOTS))).astype(jnp.bfloat16)
    whole = jnp.broadcast_to(share[None], (16,) + share.shape)
    whole = lax.all_to_all(whole, ("x", "y"), 0, 0)
    whole = lax.all_gather(whole, "c")
    whole = whole.reshape(2, 4, ROWS_M, 16, CHANNELS)[:, :, :27]
    whole = jnp.transpose(whole, (2, 0, 1, 3, 4)).reshape(27, CHANNELS, CHANNELS)[::-1]
    return outputs, input_grad, whole.astype(jnp.float32)


def solution(mesh):
    fine = Mesh(mesh.devices.reshape(4, 2, 4, 8), AXES)
    bricks = P(AXES, None, None)
    return jax.shard_map(
        local,
        mesh=fine,
        in_specs=(bricks, P(), bricks, P(None, AXES), P(AXES)),
        out_specs=(bricks, bricks, P()),
        check_vma=False,
    )
```

time: 378 us -> 109 us (0.29)
  waiting for transfers between devices: 255 us -> 4.4 us
  blocking collectives: 0 us -> 61.6 us
  other arithmetic: 42.4 us -> 1.61 us
  local copies, waits for them, and re-layouts: 31.6 us -> 6.62 us
  between operations: 15 us -> 0.88 us
  Pallas kernels: 0 us -> 8.63 us
  matrix products: 7.16 us -> 0 us
    psum x1 -> x0, waiting for transfers between devices: 255 us -> none  [local(): grad_total = lax.psum(grad_total, ('gx', 'gy'))]
    all_to_all x0 -> x3, blocking collectives: none -> 55 us  [the longest x1 26.1 us: local(): parts = lax.all_to_all(parts, ('x', 'y'), 0, 0)]
    scatter-add x2 -> x0, other arithmetic: 26.3 us -> none  [the longest x1 23.3 us: local(): totals = totals.at[neighbour_ids].add(region_pieces(spread))]
    add x1 -> x0, other arithmetic: 11.1 us -> none  [region_pieces(): region + jnp.pad(shaped[:, :, :, :, number], ((0, 0), (edge - shift_x, ed...]
    transpose x2 -> x3, local copies, waits for them, and re-layouts: 10.9 us -> 1.63 us  [the longest x1 1.22 us: local(): w_back = jnp.transpose(weights[::-1], (0, 2, 1))]
    pallas_call x0 -> x2, Pallas kernels: none -> 8.63 us  [the longest x1 6.6 us: convolve(): pl.pallas_call(conv_kernel, in_specs=[smem, smem] + [vmem] * 14, out_spec...]
    dot_general x3 -> x0, matrix products: 7.16 us -> none  [the longest x1 3.74 us: local(): jnp.dot(backward, w_back, preferred_element_type=jnp.float32)]
    all_gather x0 -> x1, blocking collectives: none -> 6.57 us  [local(): whole = lax.all_gather(whole, 'c')]
  transfers between devices with their start and end apart: 9 -> 9, of which waited for: 1 -> 2; matrix products, arithmetic and copies ran while one was open for 19% -> 3% of each run, Pallas kernels for 0% -> 0%
where the time goes in v1:
time: 109 us
  blocking collectives  61.6 us (57%)
  starting transfers between devices  24.9 us (23%)
  Pallas kernels  8.63 us (8%)
  local copies, waits for them, and re-layouts  6.62 us (6%)
  waiting for transfers between devices  4.4 us (4%)
  other arithmetic  1.61 us (1%)
    all_to_all x1, blocking collectives, local(): parts = lax.all_to_all(parts, ('x', 'y'), 0, 0)  26.1 us
    ppermute x8, starting transfers between devices, pass_to(): return lax.ppermute(value, AXES, pairs)  24.9 us
    all_to_all x1, blocking collectives, local(): column = lax.all_to_all(column, 'z', 0, 0)  15.9 us
    all_to_all x1, blocking collectives, local(): whole = lax.all_to_all(whole, ('x', 'y'), 0, 0)  12.9 us
    pallas_call x1, Pallas kernels, convolve(): pl.pallas_call(conv_kernel, in_specs=[smem, smem] + [vmem] * 14, out_spec...  6.6 us
    all_gather x1, blocking collectives, local(): whole = lax.all_gather(whole, 'c')  6.57 us
    unnamed x18, local copies, waits for them, and re-layouts  4.79 us
    ppermute x8, waiting for transfers between devices, pass_to(): return lax.ppermute(value, AXES, pairs)  2.59 us
  transfers between devices with their start and end apart: 9, of which 2 were waited for; matrix products, arithmetic and copies ran while one was open for 3% of the time, Pallas kernels for 0%

profile of v1, /device:TPU:1, one launch (start us, length us, event | category | flops | bytes accessed | tf_op | source)
XLA Modules:
  0.0 108.6 jit_solution(8189373126846019640)
XLA Ops:
  0.6 0.0 copy-start.1
  0.6 0.9 copy-done.1
  1.5 0.9 copy-done.3
  2.4 0.7 copy-done.6
  3.1 2.0 %shard_map.85 = (bf16[8,64,256]{2,1,0:T(8,128)(2,1)}, bf16[8,64,256]{2,1,0:T(8,128)(2,1)}, bf16[8,64,256]{2,1,0:T(8,128)(2,1)}, bf16[8,64,256]{2,1,0:T(8,128)(2,...) custom-call(s32[40]{0:T(128)S(1)} %copy-done.6, ...), custom_call_target="tpu_custom_call" | custom-call | tf_op jit(solution)/shard_map/pallas_call | solution.py:61
  5.1 1.3 %collective-permute-start.4 = (bf16[2,64,256]{2,1,0:T(8,128)(2,1)S(1)}, bf16[2,64,256]{2,1,0:T(8,128)(2,1)S(1)}, u32[]{:S(2)}, u32[]{:S(2)}) collective-permute-start(bf16[2,64,256]{2,1,0:T(8,128)(2,1)S(1)} %get-tuple-element.19), channel_id=1, source_target_pairs={{33,0},{34,1},{35,2},{36,3},{37,4},{38,5},{39,6},{40,7},{41,8},{42... | collective-permute-start | bytes 196616 | tf_op jit(solution)/shard_map/ppermute | solution.py:163
  6.4 4.9 %collective-permute-start.5 = (bf16[2,64,256]{2,1,0:T(8,128)(2,1)S(1)}, bf16[2,64,256]{2,1,0:T(8,128)(2,1)S(1)}, u32[]{:S(2)}, u32[]{:S(2)}) collective-permute-start(bf16[2,64,256]{2,1,0:T(8,128)(2,1)S(1)} %get-tuple-element.20), channel_id=1, source_target_pairs={{32,1},{33,2},{34,3},{35,4},{36,5},{37,6},{38,7},{39,8},{40,9},{41... | collective-permute-start | bytes 196616 | tf_op jit(solution)/shard_map/ppermute | solution.py:163
  11.4 1.9 %collective-permute-start = (bf16[8,64,256]{2,1,0:T(8,128)(2,1)}, bf16[8,64,256]{2,1,0:T(8,128)(2,1)S(1)}, u32[]{:S(2)}, u32[]{:S(2)}) collective-permute-start(bf16[8,64,256]{2,1,0:T(8,128)(2,1)} %get-tuple-element.15), channel_id=1, source_target_pairs={{32,0},{33,1},{34,2},{35,3},{36,4},{37,5},{38,6},{39,7},{40,8},{41... | collective-permute-start | bytes 786440 | tf_op jit(solution)/shard_map/ppermute | solution.py:163
  13.3 5.5 %collective-permute-start.1 = (bf16[8,64,256]{2,1,0:T(8,128)(2,1)}, bf16[8,64,256]{2,1,0:T(8,128)(2,1)S(1)}, u32[]{:S(2)}, u32[]{:S(2)}) collective-permute-start(bf16[8,64,256]{2,1,0:T(8,128)(2,1)} %get-tuple-element.16), channel_id=1, source_target_pairs={{0,32},{1,33},{2,34},{3,35},{4,36},{5,37},{6,38},{7,39},{8,40},{9,... | collective-permute-start | bytes 786440 | tf_op jit(solution)/shard_map/ppermute | solution.py:163
  18.8 1.3 %collective-permute-start.2 = (bf16[8,64,256]{2,1,0:T(8,128)(2,1)}, bf16[8,64,256]{2,1,0:T(8,128)(2,1)S(1)}, u32[]{:S(2)}, u32[]{:S(2)}) collective-permute-start(bf16[8,64,256]{2,1,0:T(8,128)(2,1)} %get-tuple-element.17), channel_id=1, source_target_pairs={{1,0},{2,1},{3,2},{4,3},{5,4},{6,5},{7,6},{8,7},{9,8},{10,9},{11,1... | collective-permute-start | bytes 786440 | tf_op jit(solution)/shard_map/ppermute | solution.py:163
  20.1 0.0 collective-permute-done.4.rest_4_
  20.2 4.0 %collective-permute-start.3 = (bf16[8,64,256]{2,1,0:T(8,128)(2,1)}, bf16[8,64,256]{2,1,0:T(8,128)(2,1)S(1)}, u32[]{:S(2)}, u32[]{:S(2)}) collective-permute-start(bf16[8,64,256]{2,1,0:T(8,128)(2,1)} %get-tuple-element.18), channel_id=1, source_target_pairs={{0,1},{1,2},{2,3},{3,4},{4,5},{5,6},{6,7},{7,8},{8,9},{9,10},{10,1... | collective-permute-start | bytes 786440 | tf_op jit(solution)/shard_map/ppermute | solution.py:163
  24.2 0.0 collective-permute-done.5.rest_5_
  24.2 0.0 copy-start.7
  24.2 0.0 copy-start.2
  24.2 0.0 copy-start
  24.2 0.0 copy-start.4
  24.2 0.0 copy-start.5
  24.2 1.4 %collective-permute-start.6 = (bf16[2,64,256]{2,1,0:T(8,128)(2,1)S(1)}, bf16[2,64,256]{2,1,0:T(8,128)(2,1)S(1)}, u32[]{:S(2)}, u32[]{:S(2)}) collective-permute-start(bf16[2,64,256]{2,1,0:T(8,128)(2,1)S(1)} %get-tuple-element.21), channel_id=1, source_target_pairs={{1,32},{2,33},{3,34},{4,35},{5,36},{6,37},{7,38},{8,39},{9,40},{10... | collective-permute-start | bytes 196616 | tf_op jit(solution)/shard_map/ppermute | solution.py:163
  25.7 2.2 %copy.24 = bf16[27,128,128]{1,2,0:T(8,128)(2,1)} copy(bf16[27,128,128]{2,1,0:T(8,128)(2,1)} %rest_10_.1) | data formatting | bytes 1769472 | tf_op args[1]
  27.9 2.6 %collective-permute-done.6.rest_6_ = bf16[2,64,256]{2,1,0:T(8,128)(2,1)S(1)} collective-permute-done((bf16[2,64,256]{2,1,0:T(8,128)(2,1)S(1)}, bf16[2,64,256]{2,1,0:T(8,128)(2,1)S(1)}, u32[]{:S(2)}, u32[]{:S(2)}) %collective-permute-start.6) | collective-permute-done | bytes 65568 | tf_op jit(solution)/shard_map/ppermute | solution.py:163
  30.4 4.5 %collective-permute-start.7 = (bf16[2,64,256]{2,1,0:T(8,128)(2,1)}, bf16[2,64,256]{2,1,0:T(8,128)(2,1)}, u32[]{:S(2)}, u32[]{:S(2)}) collective-permute-start(bf16[2,64,256]{2,1,0:T(8,128)(2,1)} %get-tuple-element.22), channel_id=1, source_target_pairs={{0,33},{1,34},{2,35},{3,36},{4,37},{5,38},{6,39},{7,40},{8,41},{9,... | collective-permute-start | bytes 196616 | tf_op jit(solution)/shard_map/ppermute | solution.py:163
  34.9 1.2 %reverse_bitcast_fusion.rest_11_ = bf16[27,128,128]{2,1,0:T(8,128)(2,1)S(1)} fusion(bf16[27,128,128]{1,2,0:T(8,128)(2,1)} %copy.24), kind=kLoop, calls=%fused_computation.4 | loop fusion | bytes 1769472 | tf_op jit(solution)/shard_map/transpose | solution.py:174
  36.2 0.0 copy-done.7
  36.2 0.1 copy.25.dst_ref
  36.3 0.0 copy-done.2
  36.3 0.1 copy.23
  36.4 0.0 collective-permute-done.7.rest_7_
  36.4 0.0 collective-permute-done.rest_0_
  36.4 0.0 collective-permute-done.1.rest_1_
  36.4 0.0 collective-permute-done.2.rest_2_
  36.4 0.0 collective-permute-done.3.rest_3_
  36.4 0.0 copy-done
  36.4 0.0 copy-done.4
  36.5 0.0 copy-done.5
  36.5 6.6 %shard_map.86 = (bf16[8,64,128]{2,1,0:T(8,128)(2,1)}, bf16[8,64,128]{2,1,0:T(8,128)(2,1)}, bf16[4,28,16,128]{3,2,1,0:T(8,128)(2,1)S(1)}, f32[4,28,16,128]{3,2,1,0:T(8,128)S(1)}) custom-call(s32[1]{0:T(128)} %bitcast.core_ref, s32[27,8]{1,0:T(8,128)S(1)} %copy.25.dst_ref, bf16[8,64,128]{2,1,0:T(8,128)(2,1)S(1)} %copy-done.2, ...), custom_call_target="tpu_custom_call" | custom-call | tf_op jit(solution)/shard_map/pallas_call | solution.py:138
  43.1 0.0 collective-permute-start.8
  43.1 1.8 %collective-permute-done.8 = bf16[4,28,16,128]{3,2,1,0:T(8,128)(2,1)S(1)} collective-permute-done((bf16[4,28,16,128]{3,2,1,0:T(8,128)(2,1)S(1)}, bf16[4,28,16,128]{3,2,1,0:T(8,128)(2,1)S(1)}, u32[]{:S(2)}, u32[]{:S(2)}) %collective-permute-start.8) | collective-permute-done | bytes 458784 | tf_op jit(solution)/shard_map/ppermute | solution.py:179
  44.9 0.1 add_convert_fusion
  45.0 26.1 %all_to_all.15 = bf16[16,7,16,128]{3,2,1,0:T(8,128)(2,1)S(1)} all-to-all(bf16[16,7,16,128]{3,2,1,0:T(8,128)(2,1)S(1)} %bitcast.16), channel_id=1, replica_groups=mesh['x'=4,'c'=2,'y'=4,'z'=8] {'x','y'}, dimensions={0} | all-to-all | bytes 917504 | tf_op jit(solution)/shard_map/all_to_all | solution.py:182
  71.1 0.1 convert_reduce_fusion
  71.2 15.9 %all_to_all.16 = f32[8,7,16,128]{3,2,1,0:T(8,128)S(1)} all-to-all(f32[8,7,16,128]{3,2,1,0:T(8,128)S(1)} %broadcast_in_dim.4), channel_id=1, replica_groups=mesh['x'=4,'c'=2,'y'=4,'z'=8] {'z'}, dimensions={0} | all-to-all | bytes 917504 | tf_op jit(solution)/shard_map/all_to_all | solution.py:185
  87.2 0.1 broadcast_in_dim.5
  87.3 12.9 %all_to_all.17 = bf16[16,7,16,128]{3,2,1,0:T(8,128)(2,1)S(1)} all-to-all(bf16[16,7,16,128]{3,2,1,0:T(8,128)(2,1)S(1)} %broadcast_in_dim.5), channel_id=1, replica_groups=mesh['x'=4,'c'=2,'y'=4,'z'=8] {'x','y'}, dimensions={0} | all-to-all | bytes 917504 | tf_op jit(solution)/shard_map/all_to_all | solution.py:188
  100.2 6.6 %all-gather = bf16[32,7,16,128]{3,2,1,0:T(8,128)(2,1)S(1)} all-gather(bf16[16,7,16,128]{3,2,1,0:T(8,128)(2,1)S(1)} %all_to_all.17), channel_id=2, replica_groups=mesh['x'=4,'c'=2,'y'=4,'z'=8] {'c'}, dimensions={0}, use_global_device_ids=true | all-gather | bytes 1376256 | tf_op jit(solution)/shard_map/all_gather | solution.py:189
  106.8 0.2 slice_bitcast_fusion
  107.0 0.2 copy.26
  107.2 1.4 %reverse_convert_fusion = f32[27,128,128]{2,1,0:T(8,128)} fusion(bf16[27,128,128]{2,1,0:T(8,128)(2,1)S(1)} %bitcast.15), kind=kLoop, calls=%fused_computation.3 | loop fusion | flops 442368 | bytes 2654208 | tf_op jit(solution)/shard_map/convert_element_type | solution.py:192
  (5 shorter events, 0.1 us)
Async XLA Ops:
  0.6 0.9 copy-start.1
  1.5 0.9 copy-start.3
  2.4 0.7 copy-start.6
  5.1 15.0 %collective-permute-start.4 = (bf16[2,64,256]{2,1,0:T(8,128)(2,1)S(1)}, bf16[2,64,256]{2,1,0:T(8,128)(2,1)S(1)}, u32[]{:S(2)}, u32[]{:S(2)}) collective-permute-start(bf16[2,64,256]{2,1,0:T(8,128)(2,1)S(1)} %get-tuple-element.19), channel_id=1, source_target_pairs={{33,0},{34,1},{35,2},{36,3},{37,4},{38,5},{39,6},{40,7},{41,8},{42... | collective-permute-start | bytes 196616 | tf_op jit(solution)/shard_map/ppermute | solution.py:163
  6.4 17.7 %collective-permute-start.5 = (bf16[2,64,256]{2,1,0:T(8,128)(2,1)S(1)}, bf16[2,64,256]{2,1,0:T(8,128)(2,1)S(1)}, u32[]{:S(2)}, u32[]{:S(2)}) collective-permute-start(bf16[2,64,256]{2,1,0:T(8,128)(2,1)S(1)} %get-tuple-element.20), channel_id=1, source_target_pairs={{32,1},{33,2},{34,3},{35,4},{36,5},{37,6},{38,7},{39,8},{40,9},{41... | collective-permute-start | bytes 196616 | tf_op jit(solution)/shard_map/ppermute | solution.py:163
  11.4 25.0 %collective-permute-start = (bf16[8,64,256]{2,1,0:T(8,128)(2,1)}, bf16[8,64,256]{2,1,0:T(8,128)(2,1)S(1)}, u32[]{:S(2)}, u32[]{:S(2)}) collective-permute-start(bf16[8,64,256]{2,1,0:T(8,128)(2,1)} %get-tuple-element.15), channel_id=1, source_target_pairs={{32,0},{33,1},{34,2},{35,3},{36,4},{37,5},{38,6},{39,7},{40,8},{41... | collective-permute-start | bytes 786440 | tf_op jit(solution)/shard_map/ppermute | solution.py:163
  13.3 23.1 %collective-permute-start.1 = (bf16[8,64,256]{2,1,0:T(8,128)(2,1)}, bf16[8,64,256]{2,1,0:T(8,128)(2,1)S(1)}, u32[]{:S(2)}, u32[]{:S(2)}) collective-permute-start(bf16[8,64,256]{2,1,0:T(8,128)(2,1)} %get-tuple-element.16), channel_id=1, source_target_pairs={{0,32},{1,33},{2,34},{3,35},{4,36},{5,37},{6,38},{7,39},{8,40},{9,... | collective-permute-start | bytes 786440 | tf_op jit(solution)/shard_map/ppermute | solution.py:163
  18.8 17.6 %collective-permute-start.2 = (bf16[8,64,256]{2,1,0:T(8,128)(2,1)}, bf16[8,64,256]{2,1,0:T(8,128)(2,1)S(1)}, u32[]{:S(2)}, u32[]{:S(2)}) collective-permute-start(bf16[8,64,256]{2,1,0:T(8,128)(2,1)} %get-tuple-element.17), channel_id=1, source_target_pairs={{1,0},{2,1},{3,2},{4,3},{5,4},{6,5},{7,6},{8,7},{9,8},{10,9},{11,1... | collective-permute-start | bytes 786440 | tf_op jit(solution)/shard_map/ppermute | solution.py:163
  20.2 16.3 %collective-permute-start.3 = (bf16[8,64,256]{2,1,0:T(8,128)(2,1)}, bf16[8,64,256]{2,1,0:T(8,128)(2,1)S(1)}, u32[]{:S(2)}, u32[]{:S(2)}) collective-permute-start(bf16[8,64,256]{2,1,0:T(8,128)(2,1)} %get-tuple-element.18), channel_id=1, source_target_pairs={{0,1},{1,2},{2,3},{3,4},{4,5},{5,6},{6,7},{7,8},{8,9},{9,10},{10,1... | collective-permute-start | bytes 786440 | tf_op jit(solution)/shard_map/ppermute | solution.py:163
  24.2 12.0 %copy-start.7 = (s32[27,8]{0,1:T(8,128)S(1)}, s32[27,8]{0,1:T(8,128)}, u32[]{:S(2)}) copy-start(s32[27,8]{0,1:T(8,128)} %param.9) | copy-start | bytes 2596
  24.2 12.1 %copy-start.2 = (bf16[8,64,128]{2,1,0:T(8,128)(2,1)S(1)}, bf16[8,64,128]{2,1,0:T(8,128)(2,1)}, u32[]{:S(2)}) copy-start(bf16[8,64,128]{2,1,0:T(8,128)(2,1)} %features_ref.3) | copy-start | bytes 393220
  24.2 12.2 %copy-start = (bf16[27,128,128]{2,1,0:T(8,128)(2,1)S(1)}, bf16[27,128,128]{2,1,0:T(8,128)(2,1)}, u32[]{:S(2)}) copy-start(bf16[27,128,128]{2,1,0:T(8,128)(2,1)} %rest_10_.1) | copy-start | bytes 2654212
  24.2 12.2 %copy-start.4 = (bf16[8,64,128]{2,1,0:T(8,128)(2,1)S(1)}, bf16[8,64,128]{2,1,0:T(8,128)(2,1)}, u32[]{:S(2)}) copy-start(bf16[8,64,128]{2,1,0:T(8,128)(2,1)} %cotangent_ref.3) | copy-start | bytes 393220
  24.2 12.2 %copy-start.5 = (bf16[144,144]{1,0:T(8,128)(2,1)S(1)}, bf16[144,144]{1,0:T(8,128)(2,1)}, u32[]{:S(2)}) copy-start(bf16[144,144]{1,0:T(8,128)(2,1)} %constant.12.clone.rest_9_) | copy-start | bytes 124420
  24.2 6.2 %collective-permute-start.6 = (bf16[2,64,256]{2,1,0:T(8,128)(2,1)S(1)}, bf16[2,64,256]{2,1,0:T(8,128)(2,1)S(1)}, u32[]{:S(2)}, u32[]{:S(2)}) collective-permute-start(bf16[2,64,256]{2,1,0:T(8,128)(2,1)S(1)} %get-tuple-element.21), channel_id=1, source_target_pairs={{1,32},{2,33},{3,34},{4,35},{5,36},{6,37},{7,38},{8,39},{9,40},{10... | collective-permute-start | bytes 196616 | tf_op jit(solution)/shard_map/ppermute | solution.py:163
  30.4 5.9 %collective-permute-start.7 = (bf16[2,64,256]{2,1,0:T(8,128)(2,1)}, bf16[2,64,256]{2,1,0:T(8,128)(2,1)}, u32[]{:S(2)}, u32[]{:S(2)}) collective-permute-start(bf16[2,64,256]{2,1,0:T(8,128)(2,1)} %get-tuple-element.22), channel_id=1, source_target_pairs={{0,33},{1,34},{2,35},{3,36},{4,37},{5,38},{6,39},{7,40},{8,41},{9,... | collective-permute-start | bytes 196616 | tf_op jit(solution)/shard_map/ppermute | solution.py:163
  43.1 1.8 %collective-permute-start.8 = (bf16[4,28,16,128]{3,2,1,0:T(8,128)(2,1)S(1)}, bf16[4,28,16,128]{3,2,1,0:T(8,128)(2,1)S(1)}, u32[]{:S(2)}, u32[]{:S(2)}) collective-permute-start(bf16[4,28,16,128]{3,2,1,0:T(8,128)(2,1)S(1)} %get-tuple-element.26), channel_id=1, source_target_pairs={{0,32},{32,0},{1,33},{33,1},{2,34},{34,2},{3,35},{35,3},{4,36},{36... | collective-permute-start | bytes 1376264 | tf_op jit(solution)/shard_map/ppermute | solution.py:179

commit v2 on v1

--- a/solution.py
+++ b/solution.py
@@ -22,6 +22,7 @@
 
 DIRECTIONS = ((1, 0), (-1, 0), (0, 1), (0, -1), (1, 1), (1, -1), (-1, 1), (-1, -1))
 LENGTHS = (TILE * BZ,) * 4 + (BZ,) * 4
+STARTS = tuple(int(start) for start in np.cumsum((0,) + LENGTHS[:-1]))
 AXES = ("x", "c", "y", "z")
 VMEM_LIMIT = 48 * 1024 * 1024
 
@@ -37,7 +38,109 @@
     return picked
 
 
-def pack_kernel(slot_ref, features_ref, cotangent_ref, *packets):
+def layer_matrix():
+    picked = np.zeros((2 * PLANE, VOXELS), np.float32)
+    for side, vy in enumerate((0, BRICK - 1)):
+        for vx in range(BRICK):
+            for vz in range(BRICK):
+                picked[side * PLANE + vx * BRICK + vz, vx * PLANE + vy * BRICK + vz] = 1.0
+    return picked
+
+
+def pack_layers_kernel(slot_ref, layer_ref, features_ref, cotangent_ref, to_y_down, to_y_up, to_x_down, to_x_up,
+                       bricks, sides, sems):
+    copies = [
+        pltpu.make_async_copy(ref, bricks.at[number], sems.at[number])
+        for number, ref in enumerate((features_ref, cotangent_ref))
+    ]
+    for copy in copies:
+        copy.start()
+    for copy in copies:
+        copy.wait()
+    layer = layer_ref[...]
+    for kind in range(2):
+        for slot in range(SLOTS):
+            sides[kind, slot] = jnp.dot(
+                layer, bricks[kind, slot], preferred_element_type=jnp.float32
+            ).astype(jnp.bfloat16)
+    zero = jnp.zeros((PLANE, 2 * CHANNELS), jnp.bfloat16)
+
+    def put(packet, position, halo, from_sides, begin):
+        slot = slot_ref[halo]
+        row = jnp.clip(slot, 0, SLOTS - 1)
+        source = sides if from_sides else bricks
+
+        @pl.when(slot < SLOTS)
+        def _():
+            packet[position, :, :CHANNELS] = source[0, row, begin : begin + PLANE]
+            packet[position, :, CHANNELS:] = source[1, row, begin : begin + PLANE]
+
+        @pl.when(slot >= SLOTS)
+        def _():
+            packet[position] = zero
+
+    for packet, numbers, begin in (
+        (to_y_down, (2, 4, 6), 0),
+        (to_y_up, (3, 5, 7), PLANE),
+    ):
+        position = 0
+        for number in numbers:
+            for halo in range(STARTS[number], STARTS[number] + LENGTHS[number]):
+                put(packet, position, halo, True, begin)
+                position += 1
+    for packet, number, begin in ((to_x_down, 0, 0), (to_x_up, 1, VOXELS - PLANE)):
+        for position in range(LENGTHS[number]):
+            put(packet, position, STARTS[number] + position, False, begin)
+
+
+def pack_layers(recv_slot, layer, features, cotangent):
+    vmem = pl.BlockSpec(memory_space=pltpu.VMEM)
+    smem = pl.BlockSpec(memory_space=pltpu.SMEM)
+    hbm = pl.BlockSpec(memory_space=pl.ANY)
+    return pl.pallas_call(
+        pack_layers_kernel,
+        in_specs=[smem, vmem, hbm, hbm],
+        out_specs=[vmem] * 4,
+        out_shape=[
+            jax.ShapeDtypeStruct((length, PLANE, 2 * CHANNELS), jnp.bfloat16) for length in (12, 12, 8, 8)
+        ],
+        scratch_shapes=[
+            pltpu.VMEM((2, SLOTS, VOXELS, CHANNELS), jnp.bfloat16),
+            pltpu.VMEM((2, SLOTS, 2 * PLANE, CHANNELS), jnp.bfloat16),
+            pltpu.SemaphoreType.DMA((2,)),
+        ],
+        compiler_params=pltpu.CompilerParams(vmem_limit_bytes=VMEM_LIMIT),
+    )(recv_slot, layer, features, cotangent)
+
+
+def fill_bricks(halos, bricks):
+    begin_at = SLOTS
+    for halo in halos:
+        bricks[begin_at : begin_at + halo.shape[0]] = halo[...]
+        begin_at += halo.shape[0]
+
+
+def fill_layers(halos, bricks):
+    expand_ref, y_above, y_below, x_above, x_below = halos
+    for position in range(SLOTS):
+        bricks[SLOTS + STARTS[0] + position, :PLANE] = x_above[position]
+        bricks[SLOTS + STARTS[1] + position, VOXELS - PLANE :] = x_below[position]
+    for side, faces, number in ((0, y_above, 2), (1, y_below, 3)):
+        corner = SLOTS + 2 * side
+        tiles = [faces[position] for position in range(SLOTS)]
+        tiles += [x_above[corner + position] for position in range(BZ)]
+        tiles += [x_below[corner + position] for position in range(BZ)]
+        targets = list(range(STARTS[number], STARTS[number] + SLOTS))
+        targets += list(range(STARTS[4 + side], STARTS[4 + side] + BZ))
+        targets += list(range(STARTS[6 + side], STARTS[6 + side] + BZ))
+        whole = jnp.dot(
+            expand_ref[side], jnp.concatenate(tiles, axis=1), preferred_element_type=jnp.float32
+        ).astype(jnp.bfloat16)
+        for position, target in enumerate(targets):
+            bricks[SLOTS + target] = whole[:, position * 2 * CHANNELS : (position + 1) * 2 * CHANNELS]
+
+
+def pack_bricks_kernel(slot_ref, features_ref, cotangent_ref, *packets):
     begin_at = 0
     for packet in packets:
         for position in range(packet.shape[0]):
@@ -56,10 +159,10 @@
         begin_at += packet.shape[0]
 
 
-def pack(recv_slot, features, cotangent):
+def pack_bricks(recv_slot, features, cotangent):
     vmem = pl.BlockSpec(memory_space=pltpu.VMEM)
     return pl.pallas_call(
-        pack_kernel,
+        pack_bricks_kernel,
         in_specs=[pl.BlockSpec(memory_space=pltpu.SMEM), vmem, vmem],
         out_specs=[vmem] * 8,
         out_shape=[
@@ -69,19 +172,14 @@
     )(recv_slot, features, cotangent)
 
 
-def conv_kernel(
-    core_ref, dst_ref, features_ref, cotangent_ref, *rest
-):
-    halos = rest[:8]
+def conv_kernel(fill, count, core_ref, flag_ref, dst_ref, features_ref, cotangent_ref, *rest):
+    halos = rest[:count]
     (flipped_ref, shift_ref, weights_ref, w_back_ref, outputs_ref, grad_ref, send_ref, keep_ref,
-     bricks, taps_f, taps_c) = rest[8:]
+     bricks, taps_f, taps_c) = rest[count:]
     bricks[:SLOTS, :, :CHANNELS] = features_ref[...]
     bricks[:SLOTS, :, CHANNELS:] = cotangent_ref[...]
-    begin_at = SLOTS
-    for halo in halos:
-        bricks[begin_at : begin_at + halo.shape[0]] = halo[...]
-        begin_at += halo.shape[0]
-    bricks[begin_at] = jnp.zeros((VOXELS, 2 * CHANNELS), jnp.bfloat16)
+    fill(halos, bricks)
+    bricks[SLOTS + HALO] = jnp.zeros((VOXELS, 2 * CHANNELS), jnp.bfloat16)
 
     def one_slot(slot, carry):
         for plane in range(PLANES):
@@ -117,8 +215,9 @@
                 send_ref[quarter, m] = block[:half][rows].astype(jnp.bfloat16)
                 keep_ref[quarter, m] = block[half:][rows]
     for quarter in range(4):
-        send_ref[quarter, 27] = jnp.zeros((16, CHANNELS), jnp.bfloat16)
-        keep_ref[quarter, 27] = jnp.zeros((16, CHANNELS), jnp.float32)
+        spread = jnp.full((16, CHANNELS), flag_ref[0], jnp.float32)
+        send_ref[quarter, 27] = spread.astype(jnp.bfloat16)
+        keep_ref[quarter, 27] = spread
 
     for source, kernel, target in (
         (taps_f, weights_ref, outputs_ref), (taps_c, w_back_ref, grad_ref)
@@ -132,12 +231,12 @@
         target[...] = total.astype(jnp.bfloat16).reshape(SLOTS, VOXELS, CHANNELS)
 
 
-def convolve(core, dst_index, features, cotangent, halos, flipped, shift, weights, w_back):
+def convolve(fill, core, flag, dst_index, features, cotangent, halos, flipped, shift, weights, w_back):
     vmem = pl.BlockSpec(memory_space=pltpu.VMEM)
     smem = pl.BlockSpec(memory_space=pltpu.SMEM)
     return pl.pallas_call(
-        conv_kernel,
-        in_specs=[smem, smem] + [vmem] * 14,
+        functools.partial(conv_kernel, fill, len(halos)),
+        in_specs=[smem] * 3 + [vmem] * (6 + len(halos)),
         out_specs=[vmem] * 4,
         out_shape=[
             jax.ShapeDtypeStruct((SLOTS, VOXELS, CHANNELS), jnp.bfloat16),
@@ -151,7 +250,7 @@
             pltpu.VMEM((SLOTS, PLANES, PLANE, WIDE), jnp.bfloat16),
         ],
         compiler_params=pltpu.CompilerParams(vmem_limit_bytes=VMEM_LIMIT),
-    )(core, dst_index, features, cotangent, *halos, flipped, shift, weights, w_back)
+    )(core, flag, dst_index, features, cotangent, *halos, flipped, shift, weights, w_back)
 
 
 def pass_to(value, step_x, step_y):
@@ -163,19 +262,21 @@
     return lax.ppermute(value, AXES, pairs)
 
 
-def local(features, weights, cotangent, dst_index, recv_slot):
-    packets = pack(recv_slot, features, cotangent)
-    halos = [None] * 8
-    for number in (2, 3, 0, 1, 4, 5, 6, 7):
-        step_x, step_y = DIRECTIONS[number]
-        halos[number] = pass_to(packets[number], -step_x, -step_y)
-    core = lax.axis_index("c").astype(jnp.int32).reshape(1)
-    flipped = jnp.transpose(features.reshape(SLOTS * VOXELS, CHANNELS)).reshape(2, CHANNELS // 2, SLOTS * VOXELS)
-    w_back = jnp.transpose(weights[::-1], (0, 2, 1))
-    shift = jnp.asarray(shift_matrix(), jnp.bfloat16)
-    outputs, input_grad, send, keep = convolve(
-        core, dst_index, features, cotangent, halos, flipped, shift, weights, w_back
-    )
+def out_of_place(dst_index):
+    offsets = np.array([(a, b, c) for a in (-1, 0, 1) for b in (-1, 0, 1) for c in (-1, 0, 1)], np.int32)
+    allowed = np.zeros((27, 8), bool)
+    for k in range(27):
+        for number, heading in enumerate(DIRECTIONS):
+            allowed[k, number] = all(heading[d] in (0, offsets[k, d]) for d in range(2))
+    wrong = jnp.zeros(dst_index.shape, bool)
+    for number in range(8):
+        start = SLOTS + STARTS[number]
+        inside = (dst_index >= start) & (dst_index < start + LENGTHS[number])
+        wrong = wrong | (inside & jnp.asarray(~allowed[:, number : number + 1]))
+    return jnp.max(wrong.astype(jnp.float32)).reshape(1)
+
+
+def sum_everywhere(send, keep):
     arrived = lax.ppermute(send, "c", [(0, 1), (1, 0)])
     chip_sum = (keep + arrived.astype(jnp.float32)).astype(jnp.bfloat16)
     parts = chip_sum.reshape(16, 7, 16, CHANNELS)
@@ -185,11 +286,65 @@
     column = lax.all_to_all(column, "z", 0, 0)
     share = (jnp.sum(column, axis=0) * (1.0 / (VOXELS * SLOTS))).astype(jnp.bfloat16)
     whole = jnp.broadcast_to(share[None], (16,) + share.shape)
-    whole = lax.all_to_all(whole, ("x", "y"), 0, 0)
-    whole = lax.all_gather(whole, "c")
-    whole = whole.reshape(2, 4, ROWS_M, 16, CHANNELS)[:, :, :27]
-    whole = jnp.transpose(whole, (2, 0, 1, 3, 4)).reshape(27, CHANNELS, CHANNELS)[::-1]
-    return outputs, input_grad, whole.astype(jnp.float32)
+    own = lax.all_to_all(whole, ("x", "y"), 0, 0).reshape(4, ROWS_M, 16, CHANNELS)
+    return own, lax.ppermute(own, "c", [(0, 1), (1, 0)])
+
+
+def spread_kernel(core_ref, own_ref, other_ref, out_ref):
+    half = CHANNELS // 2
+    core = core_ref[0]
+    for number in range(out_ref.shape[0]):
+        for quarter in range(4):
+            target = out_ref.shape[0] - 1 - number
+            for ref, side in ((own_ref, core), (other_ref, 1 - core)):
+                begin = pl.multiple_of(side * half + quarter * 16, 16)
+                out_ref[target, pl.ds(begin, 16)] = ref[quarter, number].astype(jnp.float32)
+
+
+def spread_out(core, own, other):
+    block = pl.BlockSpec((4, 3, 16, CHANNELS), lambda step: (0, step, 0, 0))
+    return pl.pallas_call(
+        spread_kernel,
+        grid=(9,),
+        in_specs=[pl.BlockSpec(memory_space=pltpu.SMEM), block, block],
+        out_specs=pl.BlockSpec((3, CHANNELS, CHANNELS), lambda step: (8 - step, 0, 0)),
+        out_shape=jax.ShapeDtypeStruct((27, CHANNELS, CHANNELS), jnp.float32),
+    )(core, own, other)
+
+
+def local(features, weights, cotangent, dst_index, recv_slot):
+    core = lax.axis_index("c").astype(jnp.int32).reshape(1)
+    flag = out_of_place(dst_index)
+    layer = layer_matrix()
+    expand = jnp.asarray(np.stack((layer[:PLANE].T, layer[PLANE:].T)), jnp.bfloat16)
+    layer = jnp.asarray(layer, jnp.bfloat16)
+    shift = jnp.asarray(shift_matrix(), jnp.bfloat16)
+    flipped = jnp.transpose(features.reshape(SLOTS * VOXELS, CHANNELS)).reshape(2, CHANNELS // 2, SLOTS * VOXELS)
+    w_back = jnp.transpose(weights[::-1], (0, 2, 1))
+
+    to_y_down, to_y_up, to_x_down, to_x_up = pack_layers(recv_slot, layer, features, cotangent)
+    y_above = pass_to(to_y_down, 0, -1)
+    y_below = pass_to(to_y_up, 0, 1)
+    x_above = pass_to(jnp.concatenate((to_x_down, y_above[8:10], y_below[8:10]), axis=0), -1, 0)
+    x_below = pass_to(jnp.concatenate((to_x_up, y_above[10:], y_below[10:]), axis=0), 1, 0)
+    outputs, input_grad, send, keep = convolve(
+        fill_layers, core, flag, dst_index, features, cotangent,
+        (expand, y_above, y_below, x_above, x_below), flipped, shift, weights, w_back,
+    )
+    own, other = sum_everywhere(send, keep)
+
+    def with_whole_bricks(results):
+        packets = pack_bricks(recv_slot, features, cotangent)
+        halos = [pass_to(packet, -heading[0], -heading[1]) for packet, heading in zip(packets, DIRECTIONS)]
+        outputs, input_grad, send, keep = convolve(
+            fill_bricks, core, flag, dst_index, features, cotangent, halos, flipped, shift, weights, w_back
+        )
+        return outputs, input_grad, *sum_everywhere(send, keep)
+
+    outputs, input_grad, own, other = lax.cond(
+        own[0, 27, 0, 0] > 0, with_whole_bricks, lambda results: results, (outputs, input_grad, own, other)
+    )
+    return outputs, input_grad, spread_out(core, own, other)
 
 
 def solution(mesh):

time: 109 us -> 96.2 us (0.88)
  blocking collectives: 61.6 us -> 51.7 us
  starting transfers between devices: 24.9 us -> 17.3 us
  Pallas kernels: 8.63 us -> 15.2 us
  waiting for transfers between devices: 4.4 us -> 2.75 us
    ppermute x8 -> x4, starting transfers between devices: 24.9 us -> 12.9 us  [pass_to(): return lax.ppermute(value, AXES, pairs)]
    pallas_call x2 -> x3, Pallas kernels: 8.63 us -> 15.2 us  [the longest x1 7.41 us: convolve(): pl.pallas_call(functools.partial(conv_kernel, fill, len(halos)), in_specs...]
    all_gather x1 -> x0, blocking collectives: 6.57 us -> none  [local(): whole = lax.all_gather(whole, 'c')]
    ppermute x1 -> x2, starting transfers between devices: 0.01 us -> 4.37 us  [the longest x1 4.36 us: sum_everywhere(): return (own, lax.ppermute(own, 'c', [(0, 1), (1, 0)]))]
    all_to_all x3, blocking collectives: 55 us -> 51.7 us  [the longest x1 23.1 us: sum_everywhere(): parts = lax.all_to_all(parts, ('x', 'y'), 0, 0)]
    ppermute x8 -> x4, waiting for transfers between devices: 2.59 us -> 0.86 us  [pass_to(): return lax.ppermute(value, AXES, pairs)]
    convert_element_type x3 -> x2, other arithmetic: 1.51 us -> 0.1 us  [the longest x1 0.1 us: sum_everywhere(): chip_sum = (keep + arrived.astype(jnp.float32)).astype(jnp.bfloat16)]
    unnamed x18 -> x36, local copies, waits for them, and re-layouts: 4.79 us -> 3.56 us
  transfers between devices with their start and end apart: 9 -> 6, of which waited for: 2 -> 3; matrix products, arithmetic and copies ran while one was open for 3% -> 6% of each run, Pallas kernels for 0% -> 0%
where the time goes in v2:
time: 96.2 us; the launch traced here: 95.3 us
  blocking collectives  51.7 us (54%)
  starting transfers between devices  17.3 us (18%)
  Pallas kernels  15.2 us (16%)
  local copies, waits for them, and re-layouts  5.89 us (6%)
  waiting for transfers between devices  2.75 us (3%)
  between operations  1.57 us (2%)
    all_to_all x1, blocking collectives, sum_everywhere(): parts = lax.all_to_all(parts, ('x', 'y'), 0, 0)  23.1 us
    all_to_all x1, blocking collectives, sum_everywhere(): column = lax.all_to_all(column, 'z', 0, 0)  15.4 us
    all_to_all x1, blocking collectives, sum_everywhere(): lax.all_to_all(whole, ('x', 'y'), 0, 0).reshape(4, ROWS_M, 16, CHANNELS)  13.1 us
    ppermute x4, starting transfers between devices, pass_to(): return lax.ppermute(value, AXES, pairs)  12.9 us
    pallas_call x1, Pallas kernels, convolve(): pl.pallas_call(functools.partial(conv_kernel, fill, len(halos)), in_specs...  7.41 us
    pallas_call x1, Pallas kernels, spread_out(): pl.pallas_call(spread_kernel, grid=(9,), in_specs=[pl.BlockSpec(memory_sp...  5.55 us
    ppermute x1, starting transfers between devices, sum_everywhere(): return (own, lax.ppermute(own, 'c', [(0, 1), (1, 0)]))  4.36 us
    unnamed x36, local copies, waits for them, and re-layouts  3.56 us
  transfers between devices with their start and end apart: 6, of which 3 were waited for; matrix products, arithmetic and copies ran while one was open for 6% of the time, Pallas kernels for 0%

profile of v2, /device:TPU:1, one launch (start us, length us, event | category | flops | bytes accessed | tf_op | source)
XLA Modules:
  0.0 95.3 jit_solution(13978725705573053933)
XLA Ops:
  0.6 0.0 copy-start.1
  0.6 0.7 copy-done.1
  1.3 2.3 %shard_map.175 = (bf16[12,16,256]{2,1,0:T(8,128)(2,1)S(1)}, bf16[12,16,256]{2,1,0:T(8,128)(2,1)S(1)}, bf16[8,16,256]{2,1,0:T(8,128)(2,1)S(1)}, bf16[8,16,256]{2,1,0:T(8,128)(2,1)S(1)}) custom-call(s32[40]{0:T(128)} %slot_ref.1, bf16[32,64]{1,0:T(8,128)(2,1)S(1)} %copy-done.1, bf16[8,64,128]{2,1,0:T(8,128)(2,1)} %features_ref.3, bf16[8,64,128]{2,1,0:T(8,128)(2,1)} %cotangent_ref.3), custom_call_target="tpu_custom_call" | custom-call | tf_op jit(solution)/shard_map/pallas_call | solution.py:100
  3.6 1.3 %collective-permute-start.10 = (bf16[12,16,256]{2,1,0:T(8,128)(2,1)S(1)}, bf16[12,16,256]{2,1,0:T(8,128)(2,1)S(1)}, u32[]{:S(2)}, u32[]{:S(2)}) collective-permute-start(bf16[12,16,256]{2,1,0:T(8,128)(2,1)S(1)} %get-tuple-element.65), channel_id=1, source_target_pairs={{1,0},{2,1},{3,2},{4,3},{5,4},{6,5},{7,6},{8,7},{9,8},{10,9},{11,1... | collective-permute-start | bytes 294920 | tf_op jit(solution)/shard_map/ppermute | solution.py:262
  4.9 5.0 %collective-permute-start.11 = (bf16[12,16,256]{2,1,0:T(8,128)(2,1)S(1)}, bf16[12,16,256]{2,1,0:T(8,128)(2,1)S(1)}, u32[]{:S(2)}, u32[]{:S(2)}) collective-permute-start(bf16[12,16,256]{2,1,0:T(8,128)(2,1)S(1)} %get-tuple-element.66), channel_id=1, source_target_pairs={{0,1},{1,2},{2,3},{3,4},{4,5},{5,6},{6,7},{7,8},{8,9},{9,10},{10,1... | collective-permute-start | bytes 294920 | tf_op jit(solution)/shard_map/ppermute | solution.py:262
  9.9 0.8 copy.25.dst_ref
  10.7 1.0 %copy.23 = bf16[512,128]{0,1:T(8,128)(2,1)S(1)} copy(bf16[512,128]{1,0:T(8,128)(2,1)} %bitcast.13) | data formatting | bytes 262144 | tf_op jit(solution)/shard_map/reshape | solution.py:322
  11.7 0.0 copy-start.9
  11.7 0.0 copy-start.11
  11.7 0.0 copy-start.12
  11.7 0.0 copy-start.13
  11.8 0.0 copy-start.14
  11.8 0.0 copy-start.15
  11.8 0.0 copy-start.16
  11.8 0.0 copy-start.17
  11.8 0.0 copy-start.18
  11.8 0.0 copy-start
  11.8 0.0 copy-start.2
  11.8 0.0 copy-start.4
  11.9 0.0 copy-start.5
  11.9 0.0 copy-start.8
  11.9 2.0 %copy.24 = bf16[27,128,128]{1,2,0:T(8,128)(2,1)S(1)} copy(bf16[27,128,128]{2,1,0:T(8,128)(2,1)} %rest_7_.1) | data formatting | bytes 1769472 | tf_op args[1]
  13.9 0.1 reverse_bitcast_fusion.rest_8_
  14.0 0.0 copy-start.3
  14.0 0.0 collective-permute-done.10.rest_1_
  14.0 0.0 collective-permute-done.11.rest_2_
  14.0 4.7 %collective-permute-start.12 = (bf16[12,16,256]{2,1,0:T(8,128)(2,1)S(1)}, bf16[12,16,256]{2,1,0:T(8,128)(2,1)S(1)}, u32[]{:S(2)}, u32[]{:S(2)}) collective-permute-start(bf16[12,16,256]{2,1,0:T(8,128)(2,1)S(1)} %pad_maximum_fusion), channel_id=1, source_target_pairs={{32,0},{33,1},{34,2},{35,3},{36,4},{37,5},{38,6},{39,7},{40,8},{41... | collective-permute-start | bytes 294920 | tf_op jit(solution)/shard_map/ppermute | solution.py:262
  18.8 1.9 %collective-permute-start.13 = (bf16[12,16,256]{2,1,0:T(8,128)(2,1)S(1)}, bf16[12,16,256]{2,1,0:T(8,128)(2,1)S(1)}, u32[]{:S(2)}, u32[]{:S(2)}) collective-permute-start(bf16[12,16,256]{2,1,0:T(8,128)(2,1)S(1)} %pad_maximum_fusion.1), channel_id=1, source_target_pairs={{0,32},{1,33},{2,34},{3,35},{4,36},{5,37},{6,38},{7,39},{8,40},{9,... | collective-permute-start | bytes 294920 | tf_op jit(solution)/shard_map/ppermute | solution.py:262
  20.7 0.0 copy-done.9
  20.8 0.7 convert_reduce_fusion.2
  21.5 0.0 collective-permute-done.12.rest_3_
  21.5 0.8 collective-permute-done.13.rest_4_
  22.3 0.0 copy-done.2
  22.3 0.0 copy-done.5
  22.3 7.4 %shard_map.176 = (bf16[8,64,128]{2,1,0:T(8,128)(2,1)}, bf16[8,64,128]{2,1,0:T(8,128)(2,1)}, bf16[4,28,16,128]{3,2,1,0:T(8,128)(2,1)S(1)}, f32[4,28,16,128]{3,2,1,0:T(8,128)S(1)}) custom-call(s32[1]{0:T(128)} %bitcast.2.core_ref, f32[1]{0:T(128)} %bitcast.3.flag_ref, s32[27,8]{1,0:T(8,128)S(1)} %copy.25.dst_ref, bf16[8,64,128]{2,1,0:T(8,128)(2,1)S(1)} %copy-done.4, ...), custom_call_target="tpu_custom_call" | custom-call | tf_op jit(solution)/shard_map/pallas_call | solution.py:237
  29.7 0.0 collective-permute-start.14
  29.7 1.8 %collective-permute-done.14 = bf16[4,28,16,128]{3,2,1,0:T(8,128)(2,1)S(1)} collective-permute-done((bf16[4,28,16,128]{3,2,1,0:T(8,128)(2,1)S(1)}, bf16[4,28,16,128]{3,2,1,0:T(8,128)(2,1)S(1)}, u32[]{:S(2)}, u32[]{:S(2)}) %collective-permute-start.14) | collective-permute-done | bytes 458784 | tf_op jit(solution)/shard_map/ppermute | solution.py:280
  31.6 0.1 add_convert_fusion.1
  31.7 23.1 %all_to_all.30 = bf16[16,7,16,128]{3,2,1,0:T(8,128)(2,1)S(1)} all-to-all(bf16[16,7,16,128]{3,2,1,0:T(8,128)(2,1)S(1)} %bitcast.14), channel_id=1, replica_groups=mesh['x'=4,'c'=2,'y'=4,'z'=8] {'x','y'}, dimensions={0} | all-to-all | bytes 917504 | tf_op jit(solution)/shard_map/all_to_all | solution.py:283
  54.8 0.1 convert_reduce_fusion.1
  54.9 0.0 copy-start.10
  54.9 15.4 %all_to_all.31 = f32[8,7,16,128]{3,2,1,0:T(8,128)S(1)} all-to-all(f32[8,7,16,128]{3,2,1,0:T(8,128)S(1)} %broadcast_in_dim.8), channel_id=1, replica_groups=mesh['x'=4,'c'=2,'y'=4,'z'=8] {'z'}, dimensions={0} | all-to-all | bytes 917504 | tf_op jit(solution)/shard_map/all_to_all | solution.py:286
  70.4 0.1 broadcast_in_dim.9
  70.4 13.1 %all_to_all.32 = bf16[16,7,16,128]{3,2,1,0:T(8,128)(2,1)} all-to-all(bf16[16,7,16,128]{3,2,1,0:T(8,128)(2,1)S(1)} %broadcast_in_dim.9), channel_id=1, replica_groups=mesh['x'=4,'c'=2,'y'=4,'z'=8] {'x','y'}, dimensions={0} | all-to-all | bytes 917504 | tf_op jit(solution)/shard_map/all_to_all | solution.py:289
  83.6 4.4 %collective-permute-start.15 = (bf16[4,28,16,128]{3,2,1,0:T(8,128)(2,1)}, bf16[4,28,16,128]{3,2,1,0:T(8,128)(2,1)}, u32[]{:S(2)}, u32[]{:S(2)}) collective-permute-start(bf16[4,28,16,128]{3,2,1,0:T(8,128)(2,1)} %bitcast.9), channel_id=1, source_target_pairs={{0,32},{32,0},{1,33},{33,1},{2,34},{34,2},{3,35},{35,3},{4,36},{36... | collective-permute-start | bytes 1376264 | tf_op jit(solution)/shard_map/ppermute | solution.py:290
  87.9 1.1 %slice.24 = bf16[1,1,1,1]{3,2,1,0:T(2,128)(2,1)} slice(bf16[4,28,16,128]{3,2,1,0:T(8,128)(2,1)} %bitcast.9), slice={[0:1], [27:28], [0:1], [0:1]} | slice | bytes 4 | tf_op jit(solution)/shard_map/slice | solution.py:345
  89.6 0.1 collective-permute-done.15
  89.7 5.5 %shard_map.177 = f32[27,128,128]{2,1,0:T(8,128)} custom-call(s32[1]{0:T(128)} %bitcast.2.core_ref, bf16[4,28,16,128]{3,2,1,0:T(8,128)(2,1)} %get-tuple-element.75.own_ref, bf16[4,28,16,128]{3,2,1,0:T(8,128)(2,1)} %get-tuple-element.76.other_ref), custom_call_target="tpu_custom_call" | custom-call | tf_op jit(solution)/shard_map/pallas_call | solution.py:306
  (21 shorter events, 0.1 us)
Async XLA Ops:
  0.6 0.7 copy-start.1
  3.6 10.4 %collective-permute-start.10 = (bf16[12,16,256]{2,1,0:T(8,128)(2,1)S(1)}, bf16[12,16,256]{2,1,0:T(8,128)(2,1)S(1)}, u32[]{:S(2)}, u32[]{:S(2)}) collective-permute-start(bf16[12,16,256]{2,1,0:T(8,128)(2,1)S(1)} %get-tuple-element.65), channel_id=1, source_target_pairs={{1,0},{2,1},{3,2},{4,3},{5,4},{6,5},{7,6},{8,7},{9,8},{10,9},{11,1... | collective-permute-start | bytes 294920 | tf_op jit(solution)/shard_map/ppermute | solution.py:262
  4.9 9.1 %collective-permute-start.11 = (bf16[12,16,256]{2,1,0:T(8,128)(2,1)S(1)}, bf16[12,16,256]{2,1,0:T(8,128)(2,1)S(1)}, u32[]{:S(2)}, u32[]{:S(2)}) collective-permute-start(bf16[12,16,256]{2,1,0:T(8,128)(2,1)S(1)} %get-tuple-element.66), channel_id=1, source_target_pairs={{0,1},{1,2},{2,3},{3,4},{4,5},{5,6},{6,7},{7,8},{8,9},{9,10},{10,1... | collective-permute-start | bytes 294920 | tf_op jit(solution)/shard_map/ppermute | solution.py:262
  11.7 9.0 %copy-start.9 = (s32[27,8]{0,1:T(8,128)S(1)}, s32[27,8]{0,1:T(8,128)}, u32[]{:S(2)}) copy-start(s32[27,8]{0,1:T(8,128)} %param.21) | copy-start | bytes 2596
  11.7 9.0 %copy-start.11 = (pred[27]{0:T(512)(128)(4,1)S(1)}, pred[27]{0:T(512)(128)(4,1)}, u32[]{:S(2)}) copy-start(pred[27]{0:T(512)(128)(4,1)} %constant.81) | copy-start | bytes 85
  11.7 9.0 %copy-start.12 = (pred[27]{0:T(512)(128)(4,1)S(1)}, pred[27]{0:T(512)(128)(4,1)}, u32[]{:S(2)}) copy-start(pred[27]{0:T(512)(128)(4,1)} %constant.80) | copy-start | bytes 85
  11.7 9.0 %copy-start.13 = (pred[27]{0:T(512)(128)(4,1)S(1)}, pred[27]{0:T(512)(128)(4,1)}, u32[]{:S(2)}) copy-start(pred[27]{0:T(512)(128)(4,1)} %constant.79) | copy-start | bytes 85
  11.8 9.0 %copy-start.14 = (pred[27]{0:T(512)(128)(4,1)S(1)}, pred[27]{0:T(512)(128)(4,1)}, u32[]{:S(2)}) copy-start(pred[27]{0:T(512)(128)(4,1)} %constant.78) | copy-start | bytes 85
  11.8 9.0 %copy-start.15 = (pred[27]{0:T(512)(128)(4,1)S(1)}, pred[27]{0:T(512)(128)(4,1)}, u32[]{:S(2)}) copy-start(pred[27]{0:T(512)(128)(4,1)} %constant.77) | copy-start | bytes 85
  11.8 9.0 %copy-start.16 = (pred[27]{0:T(512)(128)(4,1)S(1)}, pred[27]{0:T(512)(128)(4,1)}, u32[]{:S(2)}) copy-start(pred[27]{0:T(512)(128)(4,1)} %constant.76) | copy-start | bytes 85
  11.8 9.0 %copy-start.17 = (pred[27]{0:T(512)(128)(4,1)S(1)}, pred[27]{0:T(512)(128)(4,1)}, u32[]{:S(2)}) copy-start(pred[27]{0:T(512)(128)(4,1)} %constant.75) | copy-start | bytes 85
  11.8 9.0 %copy-start.18 = (pred[27]{0:T(512)(128)(4,1)S(1)}, pred[27]{0:T(512)(128)(4,1)}, u32[]{:S(2)}) copy-start(pred[27]{0:T(512)(128)(4,1)} %constant.74) | copy-start | bytes 85
  11.8 10.5 %copy-start = (bf16[2,64,16]{2,1,0:T(8,128)(2,1)S(1)}, bf16[2,64,16]{2,1,0:T(8,128)(2,1)}, u32[]{:S(2)}) copy-start(bf16[2,64,16]{2,1,0:T(8,128)(2,1)} %constant.67.clone.rest_0_) | copy-start | bytes 12292
  11.8 10.5 %copy-start.2 = (bf16[27,128,128]{2,1,0:T(8,128)(2,1)S(1)}, bf16[27,128,128]{2,1,0:T(8,128)(2,1)}, u32[]{:S(2)}) copy-start(bf16[27,128,128]{2,1,0:T(8,128)(2,1)} %rest_7_.1) | copy-start | bytes 2654212
  11.8 10.5 %copy-start.4 = (bf16[8,64,128]{2,1,0:T(8,128)(2,1)S(1)}, bf16[8,64,128]{2,1,0:T(8,128)(2,1)}, u32[]{:S(2)}) copy-start(bf16[8,64,128]{2,1,0:T(8,128)(2,1)} %features_ref.3) | copy-start | bytes 393220
  11.9 10.5 %copy-start.5 = (bf16[8,64,128]{2,1,0:T(8,128)(2,1)S(1)}, bf16[8,64,128]{2,1,0:T(8,128)(2,1)}, u32[]{:S(2)}) copy-start(bf16[8,64,128]{2,1,0:T(8,128)(2,1)} %cotangent_ref.3) | copy-start | bytes 393220
  11.9 10.4 %copy-start.8 = (bf16[144,144]{1,0:T(8,128)(2,1)S(1)}, bf16[144,144]{1,0:T(8,128)(2,1)}, u32[]{:S(2)}) copy-start(bf16[144,144]{1,0:T(8,128)(2,1)} %constant.69.clone.rest_6_) | copy-start | bytes 124420
  14.0 17.7 %copy-start.3 = (bf16[27,128,128]{2,1,0:T(8,128)(2,1)}, bf16[27,128,128]{2,1,0:T(8,128)(2,1)S(1)}, u32[]{:S(2)}) copy-start(bf16[27,128,128]{2,1,0:T(8,128)(2,1)S(1)} %reverse_bitcast_fusion.rest_8_) | copy-start | bytes 2654212
  14.0 7.4 %collective-permute-start.12 = (bf16[12,16,256]{2,1,0:T(8,128)(2,1)S(1)}, bf16[12,16,256]{2,1,0:T(8,128)(2,1)S(1)}, u32[]{:S(2)}, u32[]{:S(2)}) collective-permute-start(bf16[12,16,256]{2,1,0:T(8,128)(2,1)S(1)} %pad_maximum_fusion), channel_id=1, source_target_pairs={{32,0},{33,1},{34,2},{35,3},{36,4},{37,5},{38,6},{39,7},{40,8},{41... | collective-permute-start | bytes 294920 | tf_op jit(solution)/shard_map/ppermute | solution.py:262
  18.8 3.5 %collective-permute-start.13 = (bf16[12,16,256]{2,1,0:T(8,128)(2,1)S(1)}, bf16[12,16,256]{2,1,0:T(8,128)(2,1)S(1)}, u32[]{:S(2)}, u32[]{:S(2)}) collective-permute-start(bf16[12,16,256]{2,1,0:T(8,128)(2,1)S(1)} %pad_maximum_fusion.1), channel_id=1, source_target_pairs={{0,32},{1,33},{2,34},{3,35},{4,36},{5,37},{6,38},{7,39},{8,40},{9,... | collective-permute-start | bytes 294920 | tf_op jit(solution)/shard_map/ppermute | solution.py:262
  29.7 1.8 %collective-permute-start.14 = (bf16[4,28,16,128]{3,2,1,0:T(8,128)(2,1)S(1)}, bf16[4,28,16,128]{3,2,1,0:T(8,128)(2,1)S(1)}, u32[]{:S(2)}, u32[]{:S(2)}) collective-permute-start(bf16[4,28,16,128]{3,2,1,0:T(8,128)(2,1)S(1)} %get-tuple-element.70), channel_id=1, source_target_pairs={{0,32},{32,0},{1,33},{33,1},{2,34},{34,2},{3,35},{35,3},{4,36},{36... | collective-permute-start | bytes 1376264 | tf_op jit(solution)/shard_map/ppermute | solution.py:280
  54.9 34.9 %copy-start.10 = (s32[40]{0:T(128)S(1)}, s32[40]{0:T(128)}, u32[]{:S(2)}) copy-start(s32[40]{0:T(128)} %slot_ref.1) | copy-start | bytes 484
  83.6 6.2 %collective-permute-start.15 = (bf16[4,28,16,128]{3,2,1,0:T(8,128)(2,1)}, bf16[4,28,16,128]{3,2,1,0:T(8,128)(2,1)}, u32[]{:S(2)}, u32[]{:S(2)}) collective-permute-start(bf16[4,28,16,128]{3,2,1,0:T(8,128)(2,1)} %bitcast.9), channel_id=1, source_target_pairs={{0,32},{32,0},{1,33},{33,1},{2,34},{34,2},{3,35},{35,3},{4,36},{36... | collective-permute-start | bytes 1376264 | tf_op jit(solution)/shard_map/ppermute | solution.py:290

commit v3 on v2

v3 whole, which is shorter than its diff:
```python
import functools

import jax
import jax.numpy as jnp
import numpy as np
from jax import lax
from jax.experimental import pallas as pl
from jax.experimental.pallas import tpu as pltpu
from jax.sharding import Mesh, PartitionSpec as P

BRICK = 4
TILE = 4
BZ = 2
HALO = 40
SLOTS = 8
VOXELS = 64
CHANNELS = 128
PLANE = BRICK * BRICK
PLANES = BRICK + 2
WIDE = 9 * CHANNELS
ROWS_M = 28

DIRECTIONS = ((1, 0), (-1, 0), (0, 1), (0, -1), (1, 1), (1, -1), (-1, 1), (-1, -1))
LENGTHS = (TILE * BZ,) * 4 + (BZ,) * 4
STARTS = tuple(int(start) for start in np.cumsum((0,) + LENGTHS[:-1]))
AXES = ("x", "c", "y", "z")
VMEM_LIMIT = 48 * 1024 * 1024


def shift_matrix():
    picked = np.zeros((9 * PLANE, 9 * PLANE), np.float32)
    for number in range(9):
        for voxel in range(PLANE):
            y = voxel // BRICK + number // 3 - 1 + BRICK
            z = voxel % BRICK + number % 3 - 1 + BRICK
            source = (y // BRICK * 3 + z // BRICK) * PLANE + y % BRICK * BRICK + z % BRICK
            picked[number * PLANE + voxel, source] = 1.0
    return picked


def layer_matrix():
    picked = np.zeros((2 * PLANE, VOXELS), np.float32)
    for side, vy in enumerate((0, BRICK - 1)):
        for vx in range(BRICK):
            for vz in range(BRICK):
                picked[side * PLANE + vx * BRICK + vz, vx * PLANE + vy * BRICK + vz] = 1.0
    return picked


def pack_layers_kernel(slot_ref, layer_ref, features_ref, cotangent_ref, to_y_down, to_y_up, to_x_down, to_x_up,
                       bricks, sides, sems):
    copies = [
        pltpu.make_async_copy(ref, bricks.at[number, pl.ds(0, SLOTS)], sems.at[number])
        for number, ref in enumerate((features_ref, cotangent_ref))
    ]
    for copy in copies:
        copy.start()
    bricks[:, SLOTS] = jnp.zeros((2, VOXELS, CHANNELS), jnp.bfloat16)
    sides[:, SLOTS] = jnp.zeros((2, 2 * PLANE, CHANNELS), jnp.bfloat16)
    for copy in copies:
        copy.wait()
    layer = layer_ref[...]
    for kind in range(2):
        beside = jnp.concatenate([bricks[kind, slot] for slot in range(SLOTS)], axis=1)
        picked = jnp.dot(layer, beside, preferred_element_type=jnp.float32).astype(jnp.bfloat16)
        for slot in range(SLOTS):
            sides[kind, slot] = picked[:, slot * CHANNELS : (slot + 1) * CHANNELS]

    def put(packet, position, halo, source, begin):
        slot = jnp.clip(slot_ref[halo], 0, SLOTS)
        packet[position, :, :CHANNELS] = source[0, slot, begin : begin + PLANE]
        packet[position, :, CHANNELS:] = source[1, slot, begin : begin + PLANE]

    for packet, numbers, begin in (
        (to_y_down, (2, 4, 6), 0),
        (to_y_up, (3, 5, 7), PLANE),
    ):
        position = 0
        for number in numbers:
            for halo in range(STARTS[number], STARTS[number] + LENGTHS[number]):
                put(packet, position, halo, sides, begin)
                position += 1
    for packet, number, begin in ((to_x_down, 0, 0), (to_x_up, 1, VOXELS - PLANE)):
        for position in range(LENGTHS[number]):
            put(packet, position, STARTS[number] + position, bricks, begin)


def pack_layers(recv_slot, layer, features, cotangent):
    vmem = pl.BlockSpec(memory_space=pltpu.VMEM)
    smem = pl.BlockSpec(memory_space=pltpu.SMEM)
    hbm = pl.BlockSpec(memory_space=pltpu.HBM)
    return pl.pallas_call(
        pack_layers_kernel,
        in_specs=[smem, vmem, hbm, hbm],
        out_specs=[vmem] * 4,
        out_shape=[
            jax.ShapeDtypeStruct((length, PLANE, 2 * CHANNELS), jnp.bfloat16) for length in (12, 12, 8, 8)
        ],
        scratch_shapes=[
            pltpu.VMEM((2, SLOTS + 1, VOXELS, CHANNELS), jnp.bfloat16),
            pltpu.VMEM((2, SLOTS + 1, 2 * PLANE, CHANNELS), jnp.bfloat16),
            pltpu.SemaphoreType.DMA((2,)),
        ],
        compiler_params=pltpu.CompilerParams(vmem_limit_bytes=VMEM_LIMIT),
    )(recv_slot, layer, features, cotangent)


def fill_bricks(halos, lanes, bricks):
    begin_at = SLOTS
    for halo in halos:
        bricks[begin_at : begin_at + halo.shape[0]] = halo[:, :, lanes]
        begin_at += halo.shape[0]


def fill_layers(halos, lanes, bricks):
    expand_ref, y_above, y_below, x_above, x_below = halos
    for position in range(SLOTS):
        bricks[SLOTS + STARTS[0] + position, :PLANE] = x_above[position, :, lanes]
        bricks[SLOTS + STARTS[1] + position, VOXELS - PLANE :] = x_below[position, :, lanes]
    for side, faces, number in ((0, y_above, 2), (1, y_below, 3)):
        corner = SLOTS + 2 * side
        tiles = [faces[position, :, lanes] for position in range(SLOTS)]
        tiles += [x_above[corner + position, :, lanes] for position in range(BZ)]
        tiles += [x_below[corner + position, :, lanes] for position in range(BZ)]
        targets = list(range(STARTS[number], STARTS[number] + SLOTS))
        targets += list(range(STARTS[4 + side], STARTS[4 + side] + BZ))
        targets += list(range(STARTS[6 + side], STARTS[6 + side] + BZ))
        whole = jnp.dot(
            expand_ref[side], jnp.concatenate(tiles, axis=1), preferred_element_type=jnp.float32
        ).astype(jnp.bfloat16)
        for position, target in enumerate(targets):
            bricks[SLOTS + target] = whole[:, position * CHANNELS : (position + 1) * CHANNELS]


def build_taps(fill, halos, lanes, own_ref, dst_ref, shift_ref, bricks, taps):
    bricks[:SLOTS] = own_ref[...]
    fill(halos, lanes, bricks)
    bricks[SLOTS + HALO] = jnp.zeros((VOXELS, CHANNELS), jnp.bfloat16)

    def around(slot, plane):
        side = 0 if plane == 0 else 2 if plane == PLANES - 1 else 1
        local = (plane - 1) % BRICK * PLANE
        return jnp.concatenate(
            [
                bricks[jnp.clip(dst_ref[slot, side * 9 + number], 0, SLOTS + HALO), local : local + PLANE]
                for number in range(9)
            ],
            axis=0,
        )

    def one_slot(slot, carry):
        for plane in range(0, PLANES, 2):
            pair = jnp.concatenate((around(slot, plane), around(slot, plane + 1)), axis=1)
            moved = jnp.dot(shift_ref[...], pair, preferred_element_type=jnp.float32).astype(jnp.bfloat16)
            for number in range(9):
                rows = moved[number * PLANE : (number + 1) * PLANE]
                target = slice(number * CHANNELS, (number + 1) * CHANNELS)
                taps[slot, plane, :, target] = rows[:, :CHANNELS]
                taps[slot, plane + 1, :, target] = rows[:, CHANNELS:]
        return carry

    lax.fori_loop(0, SLOTS, one_slot, 0)


def weight_kernel(fill, count, core_ref, flag_ref, dst_ref, cotangent_ref, *rest):
    halos = rest[:count]
    flipped_ref, shift_ref, send_ref, keep_ref, taps, bricks = rest[count:]
    build_taps(fill, halos, slice(CHANNELS, 2 * CHANNELS), cotangent_ref, dst_ref, shift_ref, bricks, taps)
    core = core_ref[0]
    flipped = jnp.concatenate((flipped_ref[1 - core], flipped_ref[core]), axis=0)
    half = CHANNELS // 2
    for side in range(3):
        tap = taps[:, side : side + BRICK].reshape(SLOTS * VOXELS, WIDE)
        part = jnp.dot(flipped, tap, preferred_element_type=jnp.float32)
        for number in range(9):
            block = part[:, number * CHANNELS : (number + 1) * CHANNELS]
            m = side * 9 + number
            for quarter in range(4):
                rows = slice(quarter * 16, quarter * 16 + 16)
                send_ref[quarter, m] = block[:half][rows].astype(jnp.bfloat16)
                keep_ref[quarter, m] = block[half:][rows]
    for quarter in range(4):
        spread = jnp.full((16, CHANNELS), flag_ref[0], jnp.float32)
        send_ref[quarter, 27] = spread.astype(jnp.bfloat16)
        keep_ref[quarter, 27] = spread


def output_kernel(fill, count, dst_ref, features_ref, *rest):
    halos = rest[:count]
    shift_ref, weights_ref, taps_c, outputs_ref, grad_ref, bricks, taps_f = rest[count:]
    build_taps(fill, halos, slice(0, CHANNELS), features_ref, dst_ref, shift_ref, bricks, taps_f)
    outputs = None
    grad = None
    for side in range(3):
        tap = taps_f[:, side : side + BRICK].reshape(SLOTS * VOXELS, WIDE)
        matrix = weights_ref[side * 9 : side * 9 + 9].reshape(WIDE, CHANNELS)
        part = jnp.dot(tap, matrix, preferred_element_type=jnp.float32)
        outputs = part if outputs is None else outputs + part
    outputs_ref[...] = outputs.astype(jnp.bfloat16).reshape(SLOTS, VOXELS, CHANNELS)
    for side in range(3):
        tap = taps_c[:, side : side + BRICK].reshape(SLOTS * VOXELS, WIDE)
        matrix = jnp.concatenate([weights_ref[26 - side * 9 - number] for number in range(9)], axis=1)
        part = lax.dot_general(tap, matrix, (((1,), (1,)), ((), ())), preferred_element_type=jnp.float32)
        grad = part if grad is None else grad + part
    grad_ref[...] = grad.astype(jnp.bfloat16).reshape(SLOTS, VOXELS, CHANNELS)


def weight_sums(fill, core, flag, dst, cotangent, halos, flipped, shift):
    vmem = pl.BlockSpec(memory_space=pltpu.VMEM)
    smem = pl.BlockSpec(memory_space=pltpu.SMEM)
    return pl.pallas_call(
        functools.partial(weight_kernel, fill, len(halos)),
        in_specs=[smem] * 3 + [vmem] * (3 + len(halos)),
        out_specs=[vmem] * 3,
        out_shape=[
            jax.ShapeDtypeStruct((4, ROWS_M, 16, CHANNELS), jnp.bfloat16),
            jax.ShapeDtypeStruct((4, ROWS_M, 16, CHANNELS), jnp.float32),
            jax.ShapeDtypeStruct((SLOTS, PLANES, PLANE, WIDE), jnp.bfloat16),
        ],
        scratch_shapes=[pltpu.VMEM((SLOTS + HALO + 1, VOXELS, CHANNELS), jnp.bfloat16)],
        compiler_params=pltpu.CompilerParams(vmem_limit_bytes=VMEM_LIMIT),
        cost_estimate=pl.CostEstimate(flops=2 * 512 * 3456 * 128 * 2, bytes_accessed=4_000_000, transcendentals=0),
    )(core, flag, dst, cotangent, *halos, flipped, shift)


def both_outputs(fill, dst, features, halos, shift, weights, taps):
    vmem = pl.BlockSpec(memory_space=pltpu.VMEM)
    smem = pl.BlockSpec(memory_space=pltpu.SMEM)
    return pl.pallas_call(
        functools.partial(output_kernel, fill, len(halos)),
        in_specs=[smem] + [vmem] * (4 + len(halos)),
        out_specs=[vmem] * 2,
        out_shape=[jax.ShapeDtypeStruct((SLOTS, VOXELS, CHANNELS), jnp.bfloat16)] * 2,
        scratch_shapes=[
            pltpu.VMEM((SLOTS + HALO + 1, VOXELS, CHANNELS), jnp.bfloat16),
            pltpu.VMEM((SLOTS, PLANES, PLANE, WIDE), jnp.bfloat16),
        ],
        compiler_params=pltpu.CompilerParams(vmem_limit_bytes=VMEM_LIMIT),
        cost_estimate=pl.CostEstimate(flops=2 * 512 * 3456 * 128 * 3, bytes_accessed=4_000_000, transcendentals=0),
    )(dst, features, *halos, shift, weights, taps)


def pack_bricks_kernel(slot_ref, features_ref, cotangent_ref, *packets):
    begin_at = 0
    for packet in packets:
        for position in range(packet.shape[0]):
            slot = slot_ref[begin_at + position]
            row = jnp.clip(slot, 0, SLOTS - 1)

            @pl.when(slot < SLOTS)
            def _():
                packet[position, :, :CHANNELS] = features_ref[row]
                packet[position, :, CHANNELS:] = cotangent_ref[row]

            @pl.when(slot >= SLOTS)
            def _():
                packet[position] = jnp.zeros((VOXELS, 2 * CHANNELS), jnp.bfloat16)

        begin_at += packet.shape[0]


def pack_bricks(recv_slot, features, cotangent):
    vmem = pl.BlockSpec(memory_space=pltpu.VMEM)
    return pl.pallas_call(
        pack_bricks_kernel,
        in_specs=[pl.BlockSpec(memory_space=pltpu.SMEM), vmem, vmem],
        out_specs=[vmem] * 8,
        out_shape=[
            jax.ShapeDtypeStruct((length, VOXELS, 2 * CHANNELS), jnp.bfloat16) for length in LENGTHS
        ],
        compiler_params=pltpu.CompilerParams(vmem_limit_bytes=VMEM_LIMIT),
    )(recv_slot, features, cotangent)


def pass_to(value, step_x, step_y):
    pairs = []
    for gx in range(8):
        for gy in range(32):
            if 0 <= gx + step_x < 8 and 0 <= gy + step_y < 32:
                pairs.append((gx * 32 + gy, (gx + step_x) * 32 + gy + step_y))
    return lax.ppermute(value, AXES, pairs)


def out_of_place(dst_index):
    offsets = np.array([(a, b, c) for a in (-1, 0, 1) for b in (-1, 0, 1) for c in (-1, 0, 1)], np.int32)
    allowed = np.zeros((27, 8), bool)
    for k in range(27):
        for number, heading in enumerate(DIRECTIONS):
            allowed[k, number] = all(heading[d] in (0, offsets[k, d]) for d in range(2))
    wrong = jnp.zeros(dst_index.shape, bool)
    for number in range(8):
        start = SLOTS + STARTS[number]
        inside = (dst_index >= start) & (dst_index < start + LENGTHS[number])
        wrong = wrong | (inside & jnp.asarray(~allowed[:, number][None]))
    return jnp.max(wrong.astype(jnp.float32)).reshape(1)


def sum_everywhere(send, keep):
    arrived = lax.ppermute(send, "c", [(0, 1), (1, 0)])
    chip_sum = (keep + arrived.astype(jnp.float32)).astype(jnp.bfloat16)
    parts = chip_sum.reshape(16, 7, 16, CHANNELS)
    parts = lax.all_to_all(parts, ("x", "y"), 0, 0)
    share = jnp.sum(parts.astype(jnp.float32), axis=0)
    column = jnp.broadcast_to(share[None], (8,) + share.shape)
    column = lax.all_to_all(column, "z", 0, 0)
    share = (jnp.sum(column, axis=0) * (1.0 / (VOXELS * SLOTS))).astype(jnp.bfloat16)
    whole = jnp.broadcast_to(share[None], (16,) + share.shape)
    own = lax.all_to_all(whole, ("x", "y"), 0, 0).reshape(4, ROWS_M, 16, CHANNELS)
    return own, lax.ppermute(own, "c", [(0, 1), (1, 0)])


def spread_kernel(core_ref, own_ref, other_ref, out_ref, whole, sems):
    half = CHANNELS // 2
    core = core_ref[0]
    copies = []
    for chunk in range(9):
        for m in range(3 * chunk, 3 * chunk + 3):
            for quarter in range(4):
                for ref, side in ((own_ref, core), (other_ref, 1 - core)):
                    begin = pl.multiple_of(side * half + quarter * 16, 16)
                    whole[26 - m, pl.ds(begin, 16)] = ref[quarter, m].astype(jnp.float32)
        rows = pl.ds(24 - 3 * chunk, 3)
        copies.append(pltpu.make_async_copy(whole.at[rows], out_ref.at[rows], sems.at[chunk]))
        copies[-1].start()
    for copy in copies:
        copy.wait()


def spread_out(core, own, other):
    vmem = pl.BlockSpec(memory_space=pltpu.VMEM)
    return pl.pallas_call(
        spread_kernel,
        in_specs=[pl.BlockSpec(memory_space=pltpu.SMEM), vmem, vmem],
        out_specs=pl.BlockSpec(memory_space=pltpu.HBM),
        out_shape=jax.ShapeDtypeStruct((27, CHANNELS, CHANNELS), jnp.float32),
        scratch_shapes=[
            pltpu.VMEM((27, CHANNELS, CHANNELS), jnp.float32),
            pltpu.SemaphoreType.DMA((9,)),
        ],
        compiler_params=pltpu.CompilerParams(vmem_limit_bytes=VMEM_LIMIT),
    )(core, own, other)


def local(features, weights, cotangent, dst_index, recv_slot):
    core = lax.axis_index("c").astype(jnp.int32).reshape(1)
    dst = dst_index.T
    flag = out_of_place(dst)
    layer = layer_matrix()
    expand = jnp.asarray(np.stack((layer[:PLANE].T, layer[PLANE:].T)), jnp.bfloat16)
    layer = jnp.asarray(layer, jnp.bfloat16)
    shift = jnp.asarray(shift_matrix(), jnp.bfloat16)
    flipped = jnp.transpose(features.reshape(SLOTS * VOXELS, CHANNELS)).reshape(2, CHANNELS // 2, SLOTS * VOXELS)

    to_y_down, to_y_up, to_x_down, to_x_up = pack_layers(recv_slot, layer, features, cotangent)
    y_above = pass_to(to_y_down, 0, -1)
    y_below = pass_to(to_y_up, 0, 1)
    x_above = pass_to(jnp.concatenate((to_x_down, y_above[8:10], y_below[8:10]), axis=0), -1, 0)
    x_below = pass_to(jnp.concatenate((to_x_up, y_above[10:], y_below[10:]), axis=0), 1, 0)
    halos = (expand, y_above, y_below, x_above, x_below)
    send, keep, taps = weight_sums(fill_layers, core, flag, dst, cotangent, halos, flipped, shift)
    outputs, input_grad = both_outputs(fill_layers, dst, features, halos, shift, weights, taps)
    own, other = sum_everywhere(send, keep)

    def with_whole_bricks(results):
        packets = pack_bricks(recv_slot, features, cotangent)
        halos = [pass_to(packet, -heading[0], -heading[1]) for packet, heading in zip(packets, DIRECTIONS)]
        send, keep, taps = weight_sums(fill_bricks, core, flag, dst, cotangent, halos, flipped, shift)
        outputs, input_grad = both_outputs(fill_bricks, dst, features, halos, shift, weights, taps)
        return outputs, input_grad, *sum_everywhere(send, keep)

    outputs, input_grad, own, other = lax.cond(
        own[0, 27, 0, 0] > 0, with_whole_bricks, lambda results: results, (outputs, input_grad, own, other)
    )
    return outputs, input_grad, spread_out(core, own, other)


def solution(mesh):
    fine = Mesh(mesh.devices.reshape(4, 2, 4, 8), AXES)
    bricks = P(AXES, None, None)
    return jax.shard_map(
        local,
        mesh=fine,
        in_specs=(bricks, P(), bricks, P(None, AXES), P(AXES)),
        out_specs=(bricks, bricks, P()),
        check_vma=False,
    )
```

time: 96.2 us -> 96.8 us (level)
  local copies, waits for them, and re-layouts: 5.89 us -> 3.76 us
  blocking collectives: 51.7 us -> 53.8 us
    unnamed x36 -> x14, local copies, waits for them, and re-layouts: 3.56 us -> 1.48 us
    all_to_all x1, blocking collectives: 23.1 us -> 25 us  [sum_everywhere(): parts = lax.all_to_all(parts, ('x', 'y'), 0, 0)]
    pallas_call x2 -> x3, Pallas kernels: 13 us -> 13.2 us  [the longest x1 6.16 us: both_outputs(): pl.pallas_call(functools.partial(output_kernel, fill, len(halos)), in_spe...]
  transfers between devices with their start and end apart: 6 -> 6, of which waited for: 3 -> 3; matrix products, arithmetic and copies ran while one was open for 6% -> 4% of each run, Pallas kernels for 0% -> 6%
where the time goes in v3:
time: 96.8 us; the launch traced here: 96.2 us
  blocking collectives  53.8 us (56%)
  starting transfers between devices  18.2 us (19%)
  Pallas kernels  15.1 us (16%)
  local copies, waits for them, and re-layouts  3.76 us (4%)
  waiting for transfers between devices  2.22 us (2%)
  other arithmetic  1.69 us (2%)
  between operations  1.49 us (2%)
    all_to_all x1, blocking collectives, sum_everywhere(): parts = lax.all_to_all(parts, ('x', 'y'), 0, 0)  25 us
    all_to_all x1, blocking collectives, sum_everywhere(): column = lax.all_to_all(column, 'z', 0, 0)  16.1 us
    ppermute x4, starting transfers between devices, pass_to(): return lax.ppermute(value, AXES, pairs)  13.5 us
    all_to_all x1, blocking collectives, sum_everywhere(): lax.all_to_all(whole, ('x', 'y'), 0, 0).reshape(4, ROWS_M, 16, CHANNELS)  12.7 us
    pallas_call x1, Pallas kernels, both_outputs(): pl.pallas_call(functools.partial(output_kernel, fill, len(halos)), in_spe...  6.16 us
    pallas_call x1, Pallas kernels, weight_sums(): pl.pallas_call(functools.partial(weight_kernel, fill, len(halos)), in_spe...  4.62 us
    ppermute x1, starting transfers between devices, sum_everywhere(): return (own, lax.ppermute(own, 'c', [(0, 1), (1, 0)]))  4.25 us
    pallas_call x1, Pallas kernels, spread_out(): pl.pallas_call(spread_kernel, in_specs=[pl.BlockSpec(memory_space=pltpu.S...  2.44 us
  transfers between devices with their start and end apart: 6, of which 3 were waited for; matrix products, arithmetic and copies ran while one was open for 4% of the time, Pallas kernels for 6%

profile of v3, /device:TPU:1, one launch (start us, length us, event | category | flops | bytes accessed | tf_op | source)
XLA Modules:
  0.0 96.2 jit_solution(6249711502297098747)
XLA Ops:
  0.6 0.0 copy-start
  0.6 0.7 copy-done
  1.3 1.9 %shard_map.175 = (bf16[12,16,256]{2,1,0:T(8,128)(2,1)S(1)}, bf16[12,16,256]{2,1,0:T(8,128)(2,1)S(1)}, bf16[8,16,256]{2,1,0:T(8,128)(2,1)S(1)}, bf16[8,16,256]{2,1,0:T(8,128)(2,1)S(1)}) custom-call(s32[40]{0:T(128)} %slot_ref.1, bf16[32,64]{1,0:T(8,128)(2,1)S(1)} %copy-done, bf16[8,64,128]{2,1,0:T(8,128)(2,1)} %features_ref.3, bf16[8,64,128]{2,1,0:T(8,128)(2,1)} %cotangent_ref.3), custom_call_target="tpu_custom_call" | custom-call | tf_op jit(solution)/shard_map/pallas_call | solution.py:92
  3.2 1.3 %collective-permute-start.10 = (bf16[12,16,256]{2,1,0:T(8,128)(2,1)S(1)}, bf16[12,16,256]{2,1,0:T(8,128)(2,1)S(1)}, u32[]{:S(2)}, u32[]{:S(2)}) collective-permute-start(bf16[12,16,256]{2,1,0:T(8,128)(2,1)S(1)} %get-tuple-element.64), channel_id=1, source_target_pairs={{1,0},{2,1},{3,2},{4,3},{5,4},{6,5},{7,6},{8,7},{9,8},{10,9},{11,1... | collective-permute-start | bytes 294920 | tf_op jit(solution)/shard_map/ppermute | solution.py:281
  4.5 5.0 %collective-permute-start.11 = (bf16[12,16,256]{2,1,0:T(8,128)(2,1)S(1)}, bf16[12,16,256]{2,1,0:T(8,128)(2,1)S(1)}, u32[]{:S(2)}, u32[]{:S(2)}) collective-permute-start(bf16[12,16,256]{2,1,0:T(8,128)(2,1)S(1)} %get-tuple-element.65), channel_id=1, source_target_pairs={{0,1},{1,2},{2,3},{3,4},{4,5},{5,6},{6,7},{7,8},{8,9},{9,10},{10,1... | collective-permute-start | bytes 294920 | tf_op jit(solution)/shard_map/ppermute | solution.py:281
  9.5 1.0 %copy.20 = bf16[512,128]{0,1:T(8,128)(2,1)S(1)} copy(bf16[512,128]{1,0:T(8,128)(2,1)} %bitcast.15) | data formatting | bytes 262144 | tf_op jit(solution)/shard_map/reshape | solution.py:352
  10.5 0.0 collective-permute-done.10.rest_1_
  10.5 0.6 collective-permute-done.11.rest_2_
  11.1 5.3 %collective-permute-start.12 = (bf16[12,16,256]{2,1,0:T(8,128)(2,1)S(1)}, bf16[12,16,256]{2,1,0:T(8,128)(2,1)S(1)}, u32[]{:S(2)}, u32[]{:S(2)}) collective-permute-start(bf16[12,16,256]{2,1,0:T(8,128)(2,1)S(1)} %pad_maximum_fusion), channel_id=1, source_target_pairs={{32,0},{33,1},{34,2},{35,3},{36,4},{37,5},{38,6},{39,7},{40,8},{41... | collective-permute-start | bytes 294920 | tf_op jit(solution)/shard_map/ppermute | solution.py:281
  16.4 1.9 %collective-permute-start.13 = (bf16[12,16,256]{2,1,0:T(8,128)(2,1)S(1)}, bf16[12,16,256]{2,1,0:T(8,128)(2,1)S(1)}, u32[]{:S(2)}, u32[]{:S(2)}) collective-permute-start(bf16[12,16,256]{2,1,0:T(8,128)(2,1)S(1)} %pad_maximum_fusion.1), channel_id=1, source_target_pairs={{0,32},{1,33},{2,34},{3,35},{4,36},{5,37},{6,38},{7,39},{8,40},{9,... | collective-permute-start | bytes 294920 | tf_op jit(solution)/shard_map/ppermute | solution.py:281
  18.4 1.5 %convert_reduce_fusion.2 = f32[]{:T(128)} fusion(pred[27]{0:T(512)(128)(4,1)} %constant.81, pred[27]{0:T(512)(128)(4,1)} %constant.80, pred[27]{0:T(512)(128)(4,1)} %constant.79, pred[27]{0:T(512)(128)(4,1)} %constant.78, pred[27]{0:T(512)(128)(4,1)} %constant.77, pred[27]{0:T(512)(128)(4,1)} %constant.76, pred[27]{0:T(512)(128)(4,1)} %constant.75, ...), kind=kLoop, calls=%fused_computation.8 | loop fusion | flops 8855 | bytes 1084 | tf_op jit(solution)/shard_map/reduce_max | solution.py:295
  19.8 0.0 collective-permute-done.12.rest_3_
  19.8 0.2 collective-permute-done.13.rest_4_
  20.0 0.0 copy-start.1
  20.0 0.8 copy-done.1
  20.7 4.6 %shard_map.176 = (bf16[4,28,16,128]{3,2,1,0:T(8,128)(2,1)S(1)}, f32[4,28,16,128]{3,2,1,0:T(8,128)S(1)}, bf16[8,6,16,1152]{3,2,1,0:T(8,128)(2,1)S(1)}) custom-call(s32[1]{0:T(128)} %bitcast.2.core_ref, f32[1]{0:T(128)} %bitcast.4.flag_ref, s32[8,27]{1,0:T(8,128)} %bitcast.18, bf16[8,64,128]{2,1,0:T(8,128)(2,1)} %cotangent_ref.3, ...), custom_call_target="tpu_custom_call" | custom-call | flops 905969664 | bytes 4000000 | tf_op jit(solution)/shard_map/pallas_call | solution.py:211
  25.4 0.4 collective-permute-start.14
  25.8 1.5 %collective-permute-done.14 = bf16[4,28,16,128]{3,2,1,0:T(8,128)(2,1)S(1)} collective-permute-done((bf16[4,28,16,128]{3,2,1,0:T(8,128)(2,1)S(1)}, bf16[4,28,16,128]{3,2,1,0:T(8,128)(2,1)S(1)}, u32[]{:S(2)}, u32[]{:S(2)}) %collective-permute-start.14) | collective-permute-done | bytes 458784 | tf_op jit(solution)/shard_map/ppermute | solution.py:299
  27.3 0.1 add_convert_fusion.1
  27.4 25.0 %all_to_all.30 = bf16[16,7,16,128]{3,2,1,0:T(8,128)(2,1)S(1)} all-to-all(bf16[16,7,16,128]{3,2,1,0:T(8,128)(2,1)S(1)} %bitcast.13), channel_id=1, replica_groups=mesh['x'=4,'c'=2,'y'=4,'z'=8] {'x','y'}, dimensions={0} | all-to-all | bytes 917504 | tf_op jit(solution)/shard_map/all_to_all | solution.py:302
  52.4 0.1 convert_reduce_fusion.1
  52.5 0.0 copy-start.2
  52.5 0.0 copy-start.5
  52.5 0.0 copy-start.7
  52.5 16.1 %all_to_all.31 = f32[8,7,16,128]{3,2,1,0:T(8,128)S(1)} all-to-all(f32[8,7,16,128]{3,2,1,0:T(8,128)S(1)} %broadcast_in_dim.8), channel_id=1, replica_groups=mesh['x'=4,'c'=2,'y'=4,'z'=8] {'z'}, dimensions={0} | all-to-all | bytes 917504 | tf_op jit(solution)/shard_map/all_to_all | solution.py:305
  68.7 0.1 broadcast_in_dim.9
  68.8 12.7 %all_to_all.32 = bf16[16,7,16,128]{3,2,1,0:T(8,128)(2,1)} all-to-all(bf16[16,7,16,128]{3,2,1,0:T(8,128)(2,1)S(1)} %broadcast_in_dim.9), channel_id=1, replica_groups=mesh['x'=4,'c'=2,'y'=4,'z'=8] {'x','y'}, dimensions={0} | all-to-all | bytes 917504 | tf_op jit(solution)/shard_map/all_to_all | solution.py:308
  81.5 4.2 %collective-permute-start.15 = (bf16[4,28,16,128]{3,2,1,0:T(8,128)(2,1)}, bf16[4,28,16,128]{3,2,1,0:T(8,128)(2,1)}, u32[]{:S(2)}, u32[]{:S(2)}) collective-permute-start(bf16[4,28,16,128]{3,2,1,0:T(8,128)(2,1)} %bitcast.9), channel_id=1, source_target_pairs={{0,32},{32,0},{1,33},{33,1},{2,34},{34,2},{3,35},{35,3},{4,36},{36... | collective-permute-start | bytes 1376264 | tf_op jit(solution)/shard_map/ppermute | solution.py:309
  85.7 0.0 copy-done.2
  85.7 0.0 copy-done.5
  85.7 0.0 copy-done.7
  85.7 0.0 copy-start.4
  85.7 0.0 copy-start.6
  85.7 6.2 %shard_map.177 = (bf16[8,64,128]{2,1,0:T(8,128)(2,1)}, bf16[8,64,128]{2,1,0:T(8,128)(2,1)}) custom-call(s32[8,27]{1,0:T(8,128)S(1)} %bitcast.19, bf16[8,64,128]{2,1,0:T(8,128)(2,1)S(1)} %copy-done.2, bf16[2,64,16]{2,1,0:T(8,128)(2,1)S(1)} %copy-done.1, bf16[12,16,256]{2,1,0:T(8,128)(2,1)S(1)} %collective-permute-done.10.rest_1_, ...), custom_call_target="tpu_custom_call" | custom-call | flops 1358954496 | bytes 4000000 | tf_op jit(solution)/shard_map/pallas_call | solution.py:229
  91.9 1.2 %slice.24 = bf16[1,1,1,1]{3,2,1,0:T(2,128)(2,1)} slice(bf16[4,28,16,128]{3,2,1,0:T(8,128)(2,1)} %bitcast.9), slice={[0:1], [27:28], [0:1], [0:1]} | slice | bytes 4 | tf_op jit(solution)/shard_map/slice | solution.py:372
  93.7 0.0 collective-permute-done.15
  93.7 0.0 copy-done.4
  93.8 0.0 copy-done.6
  93.8 2.4 %shard_map.178 = f32[27,128,128]{2,1,0:T(8,128)} custom-call(s32[1]{0:T(128)} %bitcast.2.core_ref, bf16[4,28,16,128]{3,2,1,0:T(8,128)(2,1)} %get-tuple-element.75.own_ref, bf16[4,28,16,128]{3,2,1,0:T(8,128)(2,1)} %get-tuple-element.76.other_ref), custom_call_target="tpu_custom_call" | custom-call | tf_op jit(solution)/shard_map/pallas_call | solution.py:331
  (8 shorter events, 0.1 us)
Async XLA Ops:
  0.6 0.7 copy-start
  3.2 7.3 %collective-permute-start.10 = (bf16[12,16,256]{2,1,0:T(8,128)(2,1)S(1)}, bf16[12,16,256]{2,1,0:T(8,128)(2,1)S(1)}, u32[]{:S(2)}, u32[]{:S(2)}) collective-permute-start(bf16[12,16,256]{2,1,0:T(8,128)(2,1)S(1)} %get-tuple-element.64), channel_id=1, source_target_pairs={{1,0},{2,1},{3,2},{4,3},{5,4},{6,5},{7,6},{8,7},{9,8},{10,9},{11,1... | collective-permute-start | bytes 294920 | tf_op jit(solution)/shard_map/ppermute | solution.py:281
  4.5 6.6 %collective-permute-start.11 = (bf16[12,16,256]{2,1,0:T(8,128)(2,1)S(1)}, bf16[12,16,256]{2,1,0:T(8,128)(2,1)S(1)}, u32[]{:S(2)}, u32[]{:S(2)}) collective-permute-start(bf16[12,16,256]{2,1,0:T(8,128)(2,1)S(1)} %get-tuple-element.65), channel_id=1, source_target_pairs={{0,1},{1,2},{2,3},{3,4},{4,5},{5,6},{6,7},{7,8},{8,9},{9,10},{10,1... | collective-permute-start | bytes 294920 | tf_op jit(solution)/shard_map/ppermute | solution.py:281
  11.1 8.7 %collective-permute-start.12 = (bf16[12,16,256]{2,1,0:T(8,128)(2,1)S(1)}, bf16[12,16,256]{2,1,0:T(8,128)(2,1)S(1)}, u32[]{:S(2)}, u32[]{:S(2)}) collective-permute-start(bf16[12,16,256]{2,1,0:T(8,128)(2,1)S(1)} %pad_maximum_fusion), channel_id=1, source_target_pairs={{32,0},{33,1},{34,2},{35,3},{36,4},{37,5},{38,6},{39,7},{40,8},{41... | collective-permute-start | bytes 294920 | tf_op jit(solution)/shard_map/ppermute | solution.py:281
  16.4 3.5 %collective-permute-start.13 = (bf16[12,16,256]{2,1,0:T(8,128)(2,1)S(1)}, bf16[12,16,256]{2,1,0:T(8,128)(2,1)S(1)}, u32[]{:S(2)}, u32[]{:S(2)}) collective-permute-start(bf16[12,16,256]{2,1,0:T(8,128)(2,1)S(1)} %pad_maximum_fusion.1), channel_id=1, source_target_pairs={{0,32},{1,33},{2,34},{3,35},{4,36},{5,37},{6,38},{7,39},{8,40},{9,... | collective-permute-start | bytes 294920 | tf_op jit(solution)/shard_map/ppermute | solution.py:281
  20.0 0.8 copy-start.1
  25.4 1.9 %collective-permute-start.14 = (bf16[4,28,16,128]{3,2,1,0:T(8,128)(2,1)S(1)}, bf16[4,28,16,128]{3,2,1,0:T(8,128)(2,1)S(1)}, u32[]{:S(2)}, u32[]{:S(2)}) collective-permute-start(bf16[4,28,16,128]{3,2,1,0:T(8,128)(2,1)S(1)} %get-tuple-element.69), channel_id=1, source_target_pairs={{0,32},{32,0},{1,33},{33,1},{2,34},{34,2},{3,35},{35,3},{4,36},{36... | collective-permute-start | bytes 1376264 | tf_op jit(solution)/shard_map/ppermute | solution.py:299
  52.5 33.2 %copy-start.2 = (bf16[8,64,128]{2,1,0:T(8,128)(2,1)S(1)}, bf16[8,64,128]{2,1,0:T(8,128)(2,1)}, u32[]{:S(2)}) copy-start(bf16[8,64,128]{2,1,0:T(8,128)(2,1)} %features_ref.3) | copy-start | bytes 393220
  52.5 33.2 %copy-start.5 = (s32[27,8]{0,1:T(8,128)S(1)}, s32[27,8]{0,1:T(8,128)}, u32[]{:S(2)}) copy-start(s32[27,8]{0,1:T(8,128)} %param.21) | copy-start | bytes 2596
  52.5 33.2 %copy-start.7 = (bf16[144,144]{1,0:T(8,128)(2,1)S(1)}, bf16[144,144]{1,0:T(8,128)(2,1)}, u32[]{:S(2)}) copy-start(bf16[144,144]{1,0:T(8,128)(2,1)} %constant.69.clone.rest_6_.rest_5_) | copy-start | bytes 124420
  81.5 12.3 %collective-permute-start.15 = (bf16[4,28,16,128]{3,2,1,0:T(8,128)(2,1)}, bf16[4,28,16,128]{3,2,1,0:T(8,128)(2,1)}, u32[]{:S(2)}, u32[]{:S(2)}) collective-permute-start(bf16[4,28,16,128]{3,2,1,0:T(8,128)(2,1)} %bitcast.9), channel_id=1, source_target_pairs={{0,32},{32,0},{1,33},{33,1},{2,34},{34,2},{3,35},{35,3},{4,36},{36... | collective-permute-start | bytes 1376264 | tf_op jit(solution)/shard_map/ppermute | solution.py:309
  85.7 8.0 %copy-start.4 = (bf16[8,64,128]{2,1,0:T(8,128)(2,1)S(1)}, bf16[8,64,128]{2,1,0:T(8,128)(2,1)}, u32[]{:S(2)}) copy-start(bf16[8,64,128]{2,1,0:T(8,128)(2,1)} %cotangent_ref.3) | copy-start | bytes 393220
  85.7 8.0 %copy-start.6 = (s32[40]{0:T(128)S(1)}, s32[40]{0:T(128)}, u32[]{:S(2)}) copy-start(s32[40]{0:T(128)} %slot_ref.1) | copy-start | bytes 484

commit v4 on v3

v4 whole, which is shorter than its diff:
```python
import functools

import jax
import jax.numpy as jnp
import numpy as np
from jax import lax
from jax.experimental import pallas as pl
from jax.experimental.pallas import tpu as pltpu
from jax.sharding import Mesh, PartitionSpec as P

BRICK = 4
TILE = 4
BZ = 2
HALO = 40
SLOTS = 8
VOXELS = 64
CHANNELS = 128
PLANE = BRICK * BRICK
PLANES = BRICK + 2
WIDE = 9 * CHANNELS
ROWS_M = 28

DIRECTIONS = ((1, 0), (-1, 0), (0, 1), (0, -1), (1, 1), (1, -1), (-1, 1), (-1, -1))
LENGTHS = (TILE * BZ,) * 4 + (BZ,) * 4
STARTS = tuple(int(start) for start in np.cumsum((0,) + LENGTHS[:-1]))
AXES = ("x", "c", "y", "z")
VMEM_LIMIT = 48 * 1024 * 1024


def where_equal(left, right):
    return jnp.where(left == right, 1.0, 0.0).astype(jnp.bfloat16)


def shift_matrix():
    row = lax.broadcasted_iota(jnp.int32, (9 * PLANE, 9 * PLANE), 0)
    column = lax.broadcasted_iota(jnp.int32, (9 * PLANE, 9 * PLANE), 1)
    number = row >> 4
    third = (number * 11) >> 5
    y = ((row >> 2) & 3) + third + 3
    z = (row & 3) + number - 3 * third + 3
    return where_equal(column, ((y >> 2) * 3 + (z >> 2)) * PLANE + (y & 3) * BRICK + (z & 3))


def layer_matrix():
    row = lax.broadcasted_iota(jnp.int32, (2 * PLANE, VOXELS), 0)
    column = lax.broadcasted_iota(jnp.int32, (2 * PLANE, VOXELS), 1)
    return where_equal(column, ((row >> 2) & 3) * PLANE + (row >> 4) * 12 + (row & 3))


def expand_matrix(side):
    row = lax.broadcasted_iota(jnp.int32, (VOXELS, PLANE), 0)
    column = lax.broadcasted_iota(jnp.int32, (VOXELS, PLANE), 1)
    return where_equal(row, (column >> 2) * PLANE + side * 12 + (column & 3))


def pack_layers_kernel(place_ref, slot_ref, features_ref, cotangent_ref, to_first, to_second, to_sibling, to_outer,
                       bricks, sides, sems):
    copies = [
        pltpu.make_async_copy(ref, bricks.at[number, pl.ds(0, SLOTS)], sems.at[number])
        for number, ref in enumerate((features_ref, cotangent_ref))
    ]
    for copy in copies:
        copy.start()
    bricks[:, SLOTS] = jnp.zeros((2, VOXELS, CHANNELS), jnp.bfloat16)
    sides[:, SLOTS] = jnp.zeros((2, 2 * PLANE, CHANNELS), jnp.bfloat16)
    core = place_ref[0]
    odd = place_ref[1]
    layer = layer_matrix()
    for copy in copies:
        copy.wait()
    for kind in range(2):
        beside = jnp.concatenate([bricks[kind, slot] for slot in range(SLOTS)], axis=1)
        picked = jnp.dot(layer, beside, preferred_element_type=jnp.float32).astype(jnp.bfloat16)
        for slot in range(SLOTS):
            sides[kind, slot] = picked[:, slot * CHANNELS : (slot + 1) * CHANNELS]

    def put(packet, position, halo, source, begin):
        slot = jnp.clip(slot_ref[halo], 0, SLOTS)
        rows = pl.ds(begin, PLANE)
        packet[position, :, :CHANNELS] = source[0, slot, rows]
        packet[position, :, CHANNELS:] = source[1, slot, rows]

    for packet, up in ((to_first, 1 - odd), (to_second, odd)):
        begin = pl.multiple_of(up * PLANE, PLANE)
        position = 0
        for number in (2, 4, 6):
            for halo in range(LENGTHS[number]):
                put(packet, position, STARTS[number] + up * LENGTHS[number] + halo, sides, begin)
                position += 1
    for packet, up in ((to_sibling, 1 - core), (to_outer, core)):
        begin = pl.multiple_of(up * (VOXELS - PLANE), PLANE)
        for position in range(LENGTHS[0]):
            put(packet, position, up * LENGTHS[0] + position, bricks, begin)


def pack_layers(place, recv_slot, features, cotangent):
    vmem = pl.BlockSpec(memory_space=pltpu.VMEM)
    smem = pl.BlockSpec(memory_space=pltpu.SMEM)
    hbm = pl.BlockSpec(memory_space=pltpu.HBM)
    return pl.pallas_call(
        pack_layers_kernel,
        in_specs=[smem, smem, hbm, hbm],
        out_specs=[vmem] * 4,
        out_shape=[
            jax.ShapeDtypeStruct((length, PLANE, 2 * CHANNELS), jnp.bfloat16) for length in (12, 12, 8, 8)
        ],
        scratch_shapes=[
            pltpu.VMEM((2, SLOTS + 1, VOXELS, CHANNELS), jnp.bfloat16),
            pltpu.VMEM((2, SLOTS + 1, 2 * PLANE, CHANNELS), jnp.bfloat16),
            pltpu.SemaphoreType.DMA((2,)),
        ],
        compiler_params=pltpu.CompilerParams(vmem_limit_bytes=VMEM_LIMIT),
    )(place, recv_slot, features, cotangent)


def fill_bricks(core, odd, halos, bricks):
    begin_at = SLOTS
    for halo in halos:
        bricks[begin_at : begin_at + halo.shape[0]] = halo[...]
        begin_at += halo.shape[0]


def fill_layers(core, odd, halos, bricks):
    y_first, y_second, x_sibling, x_outer = halos
    both = ((x_sibling, core), (x_outer, 1 - core))
    for packet, below in both:
        for position in range(SLOTS):
            tile = packet[position]
            target = SLOTS + below * LENGTHS[0] + position
            bricks[target, :PLANE] = tile
            bricks[target, VOXELS - PLANE :] = tile
    for order, (faces, side) in enumerate(((y_first, odd), (y_second, 1 - odd))):
        tiles = [faces[position] for position in range(SLOTS)]
        targets = [STARTS[2] + side * LENGTHS[2] + position for position in range(SLOTS)]
        for packet, below in both:
            for position in range(BZ):
                tiles.append(packet[SLOTS + BZ * order + position])
                targets.append(STARTS[4] + side * BZ + below * 2 * BZ + position)
        whole = jnp.dot(
            expand_matrix(side), jnp.concatenate(tiles, axis=1), preferred_element_type=jnp.float32
        ).astype(jnp.bfloat16)
        for position, target in enumerate(targets):
            bricks[SLOTS + target] = whole[:, position * 2 * CHANNELS : (position + 1) * 2 * CHANNELS]


def out_of_place(dst):
    k = lax.broadcasted_iota(jnp.int32, dst.shape, 1)
    ninth = jnp.where(k >= 18, 2, jnp.where(k >= 9, 1, 0))
    rest = k - 9 * ninth
    offset = (ninth - 1, jnp.where(rest >= 6, 2, jnp.where(rest >= 3, 1, 0)) - 1)
    wrong = jnp.zeros(dst.shape, jnp.float32)
    for number, heading in enumerate(DIRECTIONS):
        start = SLOTS + STARTS[number]
        here = (dst >= start) & (dst < start + LENGTHS[number])
        for axis in range(2):
            if heading[axis]:
                wrong = jnp.where(here & (offset[axis] != heading[axis]), 1.0, wrong)
    return jnp.max(jnp.max(wrong, axis=1, keepdims=True), axis=0, keepdims=True)


def conv_kernel(fill, unroll, count, place_ref, dst_ref, table_ref, features_ref, cotangent_ref, *rest):
    halos = rest[:count]
    (flipped_ref, weights_ref, outputs_ref, grad_ref, send_ref, keep_ref, bricks, taps_f, taps_c) = rest[count:]
    core = place_ref[0]
    bricks[:SLOTS, :, :CHANNELS] = features_ref[...]
    bricks[:SLOTS, :, CHANNELS:] = cotangent_ref[...]
    fill(core, place_ref[1], halos, bricks)
    bricks[SLOTS + HALO] = jnp.zeros((VOXELS, 2 * CHANNELS), jnp.bfloat16)
    shift = shift_matrix()

    def one_slot(slot, carry):
        for plane in range(PLANES):
            side = 0 if plane == 0 else 2 if plane == PLANES - 1 else 1
            local = (plane - 1) % BRICK * PLANE
            around = [
                bricks[jnp.clip(dst_ref[slot, side * 9 + number], 0, SLOTS + HALO), local : local + PLANE]
                for number in range(9)
            ]
            moved = jnp.dot(
                shift, jnp.concatenate(around, axis=0), preferred_element_type=jnp.float32
            ).astype(jnp.bfloat16)
            for number in range(9):
                rows = moved[number * PLANE : (number + 1) * PLANE]
                lanes = slice(number * CHANNELS, (number + 1) * CHANNELS)
                taps_f[slot, plane, :, lanes] = rows[:, :CHANNELS]
                taps_c[slot, plane, :, lanes] = rows[:, CHANNELS:]
        return carry

    lax.fori_loop(0, SLOTS, one_slot, 0, unroll=unroll)

    flipped = jnp.concatenate((flipped_ref[1 - core], flipped_ref[core]), axis=0)
    half = CHANNELS // 2
    for side in range(3):
        tap = taps_c[:, side : side + BRICK].reshape(SLOTS * VOXELS, WIDE)
        part = jnp.dot(flipped, tap, preferred_element_type=jnp.float32)
        for number in range(9):
            block = part[:, number * CHANNELS : (number + 1) * CHANNELS]
            m = side * 9 + number
            for quarter in range(4):
                rows = slice(quarter * 16, quarter * 16 + 16)
                send_ref[quarter, m] = block[:half][rows].astype(jnp.bfloat16)
                keep_ref[quarter, m] = block[half:][rows]
    flag = jnp.broadcast_to(out_of_place(table_ref[...]), (16, CHANNELS))
    for quarter in range(4):
        send_ref[quarter, 27] = flag.astype(jnp.bfloat16)
        keep_ref[quarter, 27] = flag

    outputs = None
    grad = None
    for side in range(3):
        tap = taps_f[:, side : side + BRICK].reshape(SLOTS * VOXELS, WIDE)
        matrix = weights_ref[side * 9 : side * 9 + 9].reshape(WIDE, CHANNELS)
        part = jnp.dot(tap, matrix, preferred_element_type=jnp.float32)
        outputs = part if outputs is None else outputs + part
    outputs_ref[...] = outputs.astype(jnp.bfloat16).reshape(SLOTS, VOXELS, CHANNELS)
    for side in range(3):
        tap = taps_c[:, side : side + BRICK].reshape(SLOTS * VOXELS, WIDE)
        matrix = jnp.concatenate([weights_ref[26 - side * 9 - number] for number in range(9)], axis=1)
        part = lax.dot_general(tap, matrix, (((1,), (1,)), ((), ())), preferred_element_type=jnp.float32)
        grad = part if grad is None else grad + part
    grad_ref[...] = grad.astype(jnp.bfloat16).reshape(SLOTS, VOXELS, CHANNELS)


def convolve(fill, unroll, place, dst, features, cotangent, halos, flipped, weights):
    vmem = pl.BlockSpec(memory_space=pltpu.VMEM)
    smem = pl.BlockSpec(memory_space=pltpu.SMEM)
    return pl.pallas_call(
        functools.partial(conv_kernel, fill, unroll, len(halos)),
        in_specs=[smem, smem] + [vmem] * (5 + len(halos)),
        out_specs=[vmem] * 4,
        out_shape=[
            jax.ShapeDtypeStruct((SLOTS, VOXELS, CHANNELS), jnp.bfloat16),
            jax.ShapeDtypeStruct((SLOTS, VOXELS, CHANNELS), jnp.bfloat16),
            jax.ShapeDtypeStruct((4, ROWS_M, 16, CHANNELS), jnp.bfloat16),
            jax.ShapeDtypeStruct((4, ROWS_M, 16, CHANNELS), jnp.float32),
        ],
        scratch_shapes=[
            pltpu.VMEM((SLOTS + HALO + 1, VOXELS, 2 * CHANNELS), jnp.bfloat16),
            pltpu.VMEM((SLOTS, PLANES, PLANE, WIDE), jnp.bfloat16),
            pltpu.VMEM((SLOTS, PLANES, PLANE, WIDE), jnp.bfloat16),
        ],
        compiler_params=pltpu.CompilerParams(vmem_limit_bytes=VMEM_LIMIT),
    )(place, dst, dst, features, cotangent, *halos, flipped, weights)


def pack_bricks_kernel(slot_ref, features_ref, cotangent_ref, *packets):
    begin_at = 0
    for packet in packets:
        for position in range(packet.shape[0]):
            slot = slot_ref[begin_at + position]
            row = jnp.clip(slot, 0, SLOTS - 1)

            @pl.when(slot < SLOTS)
            def _():
                packet[position, :, :CHANNELS] = features_ref[row]
                packet[position, :, CHANNELS:] = cotangent_ref[row]

            @pl.when(slot >= SLOTS)
            def _():
                packet[position] = jnp.zeros((VOXELS, 2 * CHANNELS), jnp.bfloat16)

        begin_at += packet.shape[0]


def pack_bricks(recv_slot, features, cotangent):
    vmem = pl.BlockSpec(memory_space=pltpu.VMEM)
    return pl.pallas_call(
        pack_bricks_kernel,
        in_specs=[pl.BlockSpec(memory_space=pltpu.SMEM), vmem, vmem],
        out_specs=[vmem] * 8,
        out_shape=[
            jax.ShapeDtypeStruct((length, VOXELS, 2 * CHANNELS), jnp.bfloat16) for length in LENGTHS
        ],
        compiler_params=pltpu.CompilerParams(vmem_limit_bytes=VMEM_LIMIT),
    )(recv_slot, features, cotangent)


def pass_to(value, step_x, step_y):
    pairs = []
    for gx in range(8):
        for gy in range(32):
            if 0 <= gx + step_x < 8 and 0 <= gy + step_y < 32:
                pairs.append((gx * 32 + gy, (gx + step_x) * 32 + gy + step_y))
    return lax.ppermute(value, AXES, pairs)


def sum_everywhere(send, keep):
    arrived = lax.ppermute(send, "c", [(0, 1), (1, 0)])
    chip_sum = (keep + arrived.astype(jnp.float32)).astype(jnp.bfloat16)
    parts = chip_sum.reshape(16, 7, 16, CHANNELS)
    parts = lax.all_to_all(parts, ("x", "y"), 0, 0)
    share = jnp.sum(parts.astype(jnp.float32), axis=0)
    column = jnp.broadcast_to(share[None], (8,) + share.shape)
    column = lax.all_to_all(column, "z", 0, 0)
    share = (jnp.sum(column, axis=0) * (1.0 / (VOXELS * SLOTS))).astype(jnp.bfloat16)
    whole = jnp.broadcast_to(share[None], (16,) + share.shape)
    own = lax.all_to_all(whole, ("x", "y"), 0, 0).reshape(4, ROWS_M, 16, CHANNELS)
    return own, lax.ppermute(own, "c", [(0, 1), (1, 0)])


def spread_kernel(core_ref, own_ref, other_ref, out_ref, whole, sems):
    half = CHANNELS // 2
    core = core_ref[0]
    copies = []
    for chunk in range(9):
        for m in range(3 * chunk, 3 * chunk + 3):
            for quarter in range(4):
                for ref, side in ((own_ref, core), (other_ref, 1 - core)):
                    begin = pl.multiple_of(side * half + quarter * 16, 16)
                    whole[26 - m, pl.ds(begin, 16)] = ref[quarter, m].astype(jnp.float32)
        rows = pl.ds(24 - 3 * chunk, 3)
        copies.append(pltpu.make_async_copy(whole.at[rows], out_ref.at[rows], sems.at[chunk]))
        copies[-1].start()
    for copy in copies:
        copy.wait()


def spread_out(core, own, other):
    vmem = pl.BlockSpec(memory_space=pltpu.VMEM)
    return pl.pallas_call(
        spread_kernel,
        in_specs=[pl.BlockSpec(memory_space=pltpu.SMEM), vmem, vmem],
        out_specs=pl.BlockSpec(memory_space=pltpu.HBM),
        out_shape=jax.ShapeDtypeStruct((27, CHANNELS, CHANNELS), jnp.float32),
        scratch_shapes=[
            pltpu.VMEM((27, CHANNELS, CHANNELS), jnp.float32),
            pltpu.SemaphoreType.DMA((9,)),
        ],
        compiler_params=pltpu.CompilerParams(vmem_limit_bytes=VMEM_LIMIT),
    )(core, own, other)


def local(features, weights, cotangent, dst_index, recv_slot):
    core = lax.axis_index("c").astype(jnp.int32)
    first = core.reshape(1)
    place = jnp.stack((core, (lax.axis_index("z") % 2).astype(jnp.int32)))
    dst = dst_index.T
    flipped = jnp.transpose(features.reshape(SLOTS * VOXELS, CHANNELS)).reshape(2, CHANNELS // 2, SLOTS * VOXELS)

    to_first, to_second, to_sibling, to_outer = pack_layers(place, recv_slot, features, cotangent)
    y_first = lax.ppermute(to_first, ("y", "z"), [(gy, gy ^ 1) for gy in range(32)])
    y_second = lax.ppermute(to_second, ("y", "z"), [(gy, ((gy + 1) ^ 1) - 1) for gy in range(1, 31)])

    def relayed(packet, up):
        corners = [lax.dynamic_slice_in_dim(value, SLOTS + BZ * up, BZ, axis=0) for value in (y_first, y_second)]
        return jnp.concatenate((packet, *corners), axis=0)

    x_outer = lax.ppermute(relayed(to_outer, core), ("x", "c"), [(2 * x + 1, 2 * x + 2) for x in range(3)]
                           + [(2 * x + 2, 2 * x + 1) for x in range(3)])
    x_sibling = lax.ppermute(relayed(to_sibling, 1 - core), "c", [(0, 1), (1, 0)])
    halos = (y_first, y_second, x_sibling, x_outer)
    outputs, input_grad, send, keep = convolve(
        fill_layers, SLOTS, place, dst, features, cotangent, halos, flipped, weights
    )
    own, other = sum_everywhere(send, keep)

    def with_whole_bricks(results):
        packets = pack_bricks(recv_slot, features, cotangent)
        halos = [pass_to(packet, -heading[0], -heading[1]) for packet, heading in zip(packets, DIRECTIONS)]
        outputs, input_grad, send, keep = convolve(
            fill_bricks, 1, place, dst, features, cotangent, halos, flipped, weights
        )
        return outputs, input_grad, spread_out(first, *sum_everywhere(send, keep))

    def as_they_are(results):
        outputs, input_grad, own, other = results
        return outputs, input_grad, spread_out(first, own, other)

    return lax.cond(
        own[0, 27, 0, 0] > 0, with_whole_bricks, as_they_are, (outputs, input_grad, own, other)
    )


def solution(mesh):
    fine = Mesh(mesh.devices.reshape(4, 2, 4, 8), AXES)
    bricks = P(AXES, None, None)
    return jax.shard_map(
        local,
        mesh=fine,
        in_specs=(bricks, P(), bricks, P(None, AXES), P(AXES)),
        out_specs=(bricks, bricks, P()),
        check_vma=False,
    )
```

time: 96.8 us -> 85.3 us (0.88)
  Pallas kernels: 15.1 us -> 9 us
  starting transfers between devices: 18.2 us -> 12.8 us
  waiting for transfers between devices: 2.22 us -> 6.41 us
  local copies, waits for them, and re-layouts: 3.76 us -> 1.65 us
  other arithmetic: 1.69 us -> 0.31 us
    pallas_call x3 -> x2, Pallas kernels: 12.6 us -> 7.71 us  [the longest x1 5.85 us: convolve(): pl.pallas_call(functools.partial(conv_kernel, fill, unroll, len(halos)),...]
    ppermute x4, starting transfers between devices: 13.5 us -> 8.6 us  [the longest x1 3.47 us: local(): lax.ppermute(relayed(to_sibling, 1 - core), 'c', [(0, 1), (1, 0)])]
    all_to_all x1, blocking collectives: 25 us -> 21.3 us  [sum_everywhere(): parts = lax.all_to_all(parts, ('x', 'y'), 0, 0)]
    ppermute x4, waiting for transfers between devices: 0.74 us -> 4.33 us  [the longest x1 2.98 us: local(): lax.ppermute(relayed(to_outer, core), ('x', 'c'), [(2 * x + 1, 2 * x + 2)...]
    all_to_all x1, blocking collectives: 16.1 us -> 18.3 us  [sum_everywhere(): column = lax.all_to_all(column, 'z', 0, 0)]
    reduce_max x1 -> x0, other arithmetic: 1.46 us -> none  [out_of_place(): return jnp.max(wrong.astype(jnp.float32)).reshape(1)]
    unnamed x14 -> x10, local copies, waits for them, and re-layouts: 1.48 us -> 0.03 us
    pallas_call x1, Pallas kernels: 2.44 us -> 1.29 us  [spread_out(): pl.pallas_call(spread_kernel, in_specs=[pl.BlockSpec(memory_space=pltpu.S...]
  transfers between devices with their start and end apart: 6 -> 6, of which waited for: 3 -> 4; matrix products, arithmetic and copies ran while one was open for 4% -> 2% of each run, Pallas kernels for 6% -> 0%
where the time goes in v4:
time: 85.3 us; the launch traced here: 85 us
  blocking collectives  53.3 us (62%)
  starting transfers between devices  12.8 us (15%)
  Pallas kernels  9 us (11%)
  waiting for transfers between devices  6.41 us (8%)
  local copies, waits for them, and re-layouts  1.65 us (2%)
  between operations  1.45 us (2%)
    all_to_all x1, blocking collectives, sum_everywhere(): parts = lax.all_to_all(parts, ('x', 'y'), 0, 0)  21.3 us
    all_to_all x1, blocking collectives, sum_everywhere(): column = lax.all_to_all(column, 'z', 0, 0)  18.3 us
    all_to_all x1, blocking collectives, sum_everywhere(): lax.all_to_all(whole, ('x', 'y'), 0, 0).reshape(4, ROWS_M, 16, CHANNELS)  13.8 us
    pallas_call x1, Pallas kernels, convolve(): pl.pallas_call(functools.partial(conv_kernel, fill, unroll, len(halos)),...  5.85 us
    ppermute x1, starting transfers between devices, sum_everywhere(): return (own, lax.ppermute(own, 'c', [(0, 1), (1, 0)]))  4.24 us
    ppermute x1, starting transfers between devices, local(): lax.ppermute(relayed(to_sibling, 1 - core), 'c', [(0, 1), (1, 0)])  3.47 us
    ppermute x1, waiting for transfers between devices, local(): lax.ppermute(relayed(to_outer, core), ('x', 'c'), [(2 * x + 1, 2 * x + 2)...  2.98 us
    ppermute x1, starting transfers between devices, local(): lax.ppermute(to_first, ('y', 'z'), [(gy, gy ^ 1) for gy in range(32)])  2.55 us
  transfers between devices with their start and end apart: 6, of which 4 were waited for; matrix products, arithmetic and copies ran while one was open for 2% of the time, Pallas kernels for 0%

profile of v4, /device:TPU:1, one launch (start us, length us, event | category | flops | bytes accessed | tf_op | source)
XLA Modules:
  0.0 85.0 jit_solution(16538794414552897951)
XLA Ops:
  0.6 0.1 pad_add_fusion.place_ref
  0.7 1.9 %shard_map.78 = (bf16[12,16,256]{2,1,0:T(8,128)(2,1)S(1)}, bf16[12,16,256]{2,1,0:T(8,128)(2,1)S(1)}, bf16[8,16,256]{2,1,0:T(8,128)(2,1)S(1)}, bf16[8,16,256]{2,1,0:T(8,128)(2,1)S(1)}) custom-call(s32[2]{0:T(128)S(1)} %pad_add_fusion.place_ref, s32[40]{0:T(128)} %slot_ref.1, bf16[8,64,128]{2,1,0:T(8,128)(2,1)} %features_ref.3, bf16[8,64,128]{2,1,0:T(8,128)(2,1)} %cotangent_ref.3), custom_call_target="tpu_custom_call" | custom-call | tf_op jit(solution)/shard_map/pallas_call | solution.py:100
  2.6 2.6 %collective-permute-start.10 = (bf16[12,16,256]{2,1,0:T(8,128)(2,1)S(1)}, bf16[12,16,256]{2,1,0:T(8,128)(2,1)S(1)}, u32[]{:S(2)}, u32[]{:S(2)}) collective-permute-start(bf16[12,16,256]{2,1,0:T(8,128)(2,1)S(1)} %get-tuple-element.62), channel_id=1, source_target_pairs={{0,1},{1,0},{2,3},{3,2},{4,5},{5,4},{6,7},{7,6},{8,9},{9,8},{10,11... | collective-permute-start | bytes 294920 | tf_op jit(solution)/shard_map/ppermute | solution.py:341
  5.1 0.7 collective-permute-start.11
  5.8 1.3 %collective-permute-done.10.rest_0_ = bf16[12,16,256]{2,1,0:T(8,128)(2,1)S(1)} collective-permute-done((bf16[12,16,256]{2,1,0:T(8,128)(2,1)S(1)}, bf16[12,16,256]{2,1,0:T(8,128)(2,1)S(1)}, u32[]{:S(2)}, u32[]{:S(2)}) %collective-permute-start.10) | collective-permute-done | bytes 98336 | tf_op jit(solution)/shard_map/ppermute | solution.py:341
  7.2 0.0 collective-permute-done.11.rest_1_
  7.2 3.5 %collective-permute-start.12 = (bf16[12,16,256]{2,1,0:T(8,128)(2,1)S(1)}, bf16[12,16,256]{2,1,0:T(8,128)(2,1)S(1)}, u32[]{:S(2)}, u32[]{:S(2)}) collective-permute-start(bf16[12,16,256]{2,1,0:T(8,128)(2,1)S(1)} %pad_maximum_fusion), channel_id=1, source_target_pairs={{0,32},{32,0},{1,33},{33,1},{2,34},{34,2},{3,35},{35,3},{4,36},{36... | collective-permute-start | bytes 294920 | tf_op jit(solution)/shard_map/ppermute | solution.py:350
  10.7 1.9 %collective-permute-start.13 = (bf16[12,16,256]{2,1,0:T(8,128)(2,1)S(1)}, bf16[12,16,256]{2,1,0:T(8,128)(2,1)S(1)}, u32[]{:S(2)}, u32[]{:S(2)}) collective-permute-start(bf16[12,16,256]{2,1,0:T(8,128)(2,1)S(1)} %pad_maximum_fusion.1), channel_id=1, source_target_pairs={{32,64},{96,128},{160,192},{64,32},{128,96},{192,160},{33,65},{97,... | collective-permute-start | bytes 294920 | tf_op jit(solution)/shard_map/ppermute | solution.py:348
  12.6 1.0 %copy.11 = bf16[512,128]{0,1:T(8,128)(2,1)S(1)} copy(bf16[512,128]{1,0:T(8,128)(2,1)} %bitcast.14) | data formatting | bytes 262144 | tf_op jit(solution)/shard_map/reshape | solution.py:338
  13.6 0.0 collective-permute-done.12.rest_2_
  13.6 3.0 %collective-permute-done.13.rest_3_ = bf16[12,16,256]{2,1,0:T(8,128)(2,1)S(1)} collective-permute-done((bf16[12,16,256]{2,1,0:T(8,128)(2,1)S(1)}, bf16[12,16,256]{2,1,0:T(8,128)(2,1)S(1)}, u32[]{:S(2)}, u32[]{:S(2)}) %collective-permute-start.13) | collective-permute-done | bytes 98336 | tf_op jit(solution)/shard_map/ppermute | solution.py:348
  16.6 5.8 %shard_map.79 = (bf16[8,64,128]{2,1,0:T(8,128)(2,1)}, bf16[8,64,128]{2,1,0:T(8,128)(2,1)}, bf16[4,28,16,128]{3,2,1,0:T(8,128)(2,1)S(1)}, f32[4,28,16,128]{3,2,1,0:T(8,128)S(1)}) custom-call(s32[2]{0:T(128)S(1)} %pad_add_fusion.place_ref, s32[8,27]{1,0:T(8,128)} %bitcast.22, s32[8,27]{1,0:T(8,128)} %bitcast.23, bf16[8,64,128]{2,1,0:T(8,128)(2,1)} %features_ref.3, ...), custom_call_target="tpu_custom_call" | custom-call | tf_op jit(solution)/shard_map/pallas_call | solution.py:227
  22.5 0.0 collective-permute-start.14
  22.5 1.8 %collective-permute-done.14 = bf16[4,28,16,128]{3,2,1,0:T(8,128)(2,1)S(1)} collective-permute-done((bf16[4,28,16,128]{3,2,1,0:T(8,128)(2,1)S(1)}, bf16[4,28,16,128]{3,2,1,0:T(8,128)(2,1)S(1)}, u32[]{:S(2)}, u32[]{:S(2)}) %collective-permute-start.14) | collective-permute-done | bytes 458784 | tf_op jit(solution)/shard_map/ppermute | solution.py:288
  24.3 0.1 add_convert_fusion.1
  24.4 21.3 %all_to_all.30 = bf16[16,7,16,128]{3,2,1,0:T(8,128)(2,1)S(1)} all-to-all(bf16[16,7,16,128]{3,2,1,0:T(8,128)(2,1)S(1)} %bitcast.15), channel_id=1, replica_groups=mesh['x'=4,'c'=2,'y'=4,'z'=8] {'x','y'}, dimensions={0} | all-to-all | bytes 917504 | tf_op jit(solution)/shard_map/all_to_all | solution.py:291
  45.6 0.1 convert_reduce_fusion.1
  45.7 0.0 copy-start
  45.7 0.0 copy-start.1
  45.7 0.0 copy-start.2
  45.7 0.0 copy-start.3
  45.8 0.0 copy-start.4
  45.8 18.3 %all_to_all.31 = f32[8,7,16,128]{3,2,1,0:T(8,128)S(1)} all-to-all(f32[8,7,16,128]{3,2,1,0:T(8,128)S(1)} %broadcast_in_dim.8), channel_id=1, replica_groups=mesh['x'=4,'c'=2,'y'=4,'z'=8] {'z'}, dimensions={0} | all-to-all | bytes 917504 | tf_op jit(solution)/shard_map/all_to_all | solution.py:294
  64.1 0.1 broadcast_in_dim.9
  64.2 13.8 %all_to_all.32 = bf16[16,7,16,128]{3,2,1,0:T(8,128)(2,1)S(1)} all-to-all(bf16[16,7,16,128]{3,2,1,0:T(8,128)(2,1)S(1)} %broadcast_in_dim.9), channel_id=1, replica_groups=mesh['x'=4,'c'=2,'y'=4,'z'=8] {'x','y'}, dimensions={0} | all-to-all | bytes 917504 | tf_op jit(solution)/shard_map/all_to_all | solution.py:297
  78.0 4.2 %collective-permute-start.15 = (bf16[4,28,16,128]{3,2,1,0:T(8,128)(2,1)S(1)}, bf16[4,28,16,128]{3,2,1,0:T(8,128)(2,1)S(1)}, u32[]{:S(2)}, u32[]{:S(2)}) collective-permute-start(bf16[4,28,16,128]{3,2,1,0:T(8,128)(2,1)S(1)} %bitcast.17), channel_id=1, source_target_pairs={{0,32},{32,0},{1,33},{33,1},{2,34},{34,2},{3,35},{35,3},{4,36},{36... | collective-permute-start | bytes 1376264 | tf_op jit(solution)/shard_map/ppermute | solution.py:298
  82.2 0.5 slice.4
  83.4 0.3 collective-permute-done.15
  83.6 0.0 copy-done
  83.6 0.0 copy-done.1
  83.7 0.0 copy-done.2
  83.7 0.0 copy-done.3
  83.7 0.0 copy-done.4
  83.7 1.3 %conditional.1 = (bf16[8,64,128]{2,1,0:T(8,128)(2,1)}, bf16[8,64,128]{2,1,0:T(8,128)(2,1)}, f32[27,128,128]{2,1,0:T(8,128)}) conditional(s32[]{:T(128)} %bitcast.10, (s32[1]{0:T(128)}, bf16[4,28,16,128]{3,2,1,0:T(8,128)(2,1)S(1)}, bf16[4,28,16,128]{3,2,1,0:T(8,128)(2,1)S(1)}, bf16[8,64,128]{2,1,0:T(8,128)(2,1)}, ...), branch_computations={%region_2.3_spmd, %region_3.6_spmd} | conditional | flops 1261568 | bytes 15622572 | solution.py:369
  83.7 1.3 %branch_0_fun.1 = f32[27,128,128]{2,1,0:T(8,128)} custom-call(s32[1]{0:T(128)} %get-tuple-element.28.core_ref, bf16[4,28,16,128]{3,2,1,0:T(8,128)(2,1)S(1)} %get-tuple-element.29.own_ref, bf16[4,28,16,128]{3,2,1,0:T(8,128)(2,1)S(1)} %get-tuple-element.30.other_ref), custom_call_target="tpu_custom_call" | custom-call | tf_op jit(solution)/shard_map/cond/branch_0_fun/pallas_call | solution.py:320
  (7 shorter events, 0.1 us)
Async XLA Ops:
  2.6 4.6 %collective-permute-start.10 = (bf16[12,16,256]{2,1,0:T(8,128)(2,1)S(1)}, bf16[12,16,256]{2,1,0:T(8,128)(2,1)S(1)}, u32[]{:S(2)}, u32[]{:S(2)}) collective-permute-start(bf16[12,16,256]{2,1,0:T(8,128)(2,1)S(1)} %get-tuple-element.62), channel_id=1, source_target_pairs={{0,1},{1,0},{2,3},{3,2},{4,5},{5,4},{6,7},{7,6},{8,9},{9,8},{10,11... | collective-permute-start | bytes 294920 | tf_op jit(solution)/shard_map/ppermute | solution.py:341
  5.1 2.0 %collective-permute-start.11 = (bf16[12,16,256]{2,1,0:T(8,128)(2,1)S(1)}, bf16[12,16,256]{2,1,0:T(8,128)(2,1)S(1)}, u32[]{:S(2)}, u32[]{:S(2)}) collective-permute-start(bf16[12,16,256]{2,1,0:T(8,128)(2,1)S(1)} %get-tuple-element.63), channel_id=1, source_target_pairs={{1,2},{2,1},{3,4},{4,3},{5,6},{6,5},{7,8},{8,7},{9,10},{10,9},{11,... | collective-permute-start | bytes 294920 | tf_op jit(solution)/shard_map/ppermute | solution.py:342
  7.2 6.4 %collective-permute-start.12 = (bf16[12,16,256]{2,1,0:T(8,128)(2,1)S(1)}, bf16[12,16,256]{2,1,0:T(8,128)(2,1)S(1)}, u32[]{:S(2)}, u32[]{:S(2)}) collective-permute-start(bf16[12,16,256]{2,1,0:T(8,128)(2,1)S(1)} %pad_maximum_fusion), channel_id=1, source_target_pairs={{0,32},{32,0},{1,33},{33,1},{2,34},{34,2},{3,35},{35,3},{4,36},{36... | collective-permute-start | bytes 294920 | tf_op jit(solution)/shard_map/ppermute | solution.py:350
  10.7 5.9 %collective-permute-start.13 = (bf16[12,16,256]{2,1,0:T(8,128)(2,1)S(1)}, bf16[12,16,256]{2,1,0:T(8,128)(2,1)S(1)}, u32[]{:S(2)}, u32[]{:S(2)}) collective-permute-start(bf16[12,16,256]{2,1,0:T(8,128)(2,1)S(1)} %pad_maximum_fusion.1), channel_id=1, source_target_pairs={{32,64},{96,128},{160,192},{64,32},{128,96},{192,160},{33,65},{97,... | collective-permute-start | bytes 294920 | tf_op jit(solution)/shard_map/ppermute | solution.py:348
  22.5 1.8 %collective-permute-start.14 = (bf16[4,28,16,128]{3,2,1,0:T(8,128)(2,1)S(1)}, bf16[4,28,16,128]{3,2,1,0:T(8,128)(2,1)S(1)}, u32[]{:S(2)}, u32[]{:S(2)}) collective-permute-start(bf16[4,28,16,128]{3,2,1,0:T(8,128)(2,1)S(1)} %get-tuple-element.67), channel_id=1, source_target_pairs={{0,32},{32,0},{1,33},{33,1},{2,34},{34,2},{3,35},{35,3},{4,36},{36... | collective-permute-start | bytes 1376264 | tf_op jit(solution)/shard_map/ppermute | solution.py:288
  45.7 37.9 %copy-start = (bf16[27,128,128]{2,1,0:T(8,128)(2,1)S(1)}, bf16[27,128,128]{2,1,0:T(8,128)(2,1)}, u32[]{:S(2)}) copy-start(bf16[27,128,128]{2,1,0:T(8,128)(2,1)} %rest_5_.1) | copy-start | bytes 2654212
  45.7 37.9 %copy-start.1 = (bf16[8,64,128]{2,1,0:T(8,128)(2,1)S(1)}, bf16[8,64,128]{2,1,0:T(8,128)(2,1)}, u32[]{:S(2)}) copy-start(bf16[8,64,128]{2,1,0:T(8,128)(2,1)} %features_ref.3) | copy-start | bytes 393220
  45.7 37.9 %copy-start.2 = (bf16[8,64,128]{2,1,0:T(8,128)(2,1)S(1)}, bf16[8,64,128]{2,1,0:T(8,128)(2,1)}, u32[]{:S(2)}) copy-start(bf16[8,64,128]{2,1,0:T(8,128)(2,1)} %cotangent_ref.3) | copy-start | bytes 393220
  45.7 37.9 %copy-start.3 = (s32[27,8]{0,1:T(8,128)S(1)}, s32[27,8]{0,1:T(8,128)}, u32[]{:S(2)}) copy-start(s32[27,8]{0,1:T(8,128)} %param.10) | copy-start | bytes 2596
  45.8 37.9 %copy-start.4 = (s32[40]{0:T(128)S(1)}, s32[40]{0:T(128)}, u32[]{:S(2)}) copy-start(s32[40]{0:T(128)} %slot_ref.1) | copy-start | bytes 484
  78.0 5.7 %collective-permute-start.15 = (bf16[4,28,16,128]{3,2,1,0:T(8,128)(2,1)S(1)}, bf16[4,28,16,128]{3,2,1,0:T(8,128)(2,1)S(1)}, u32[]{:S(2)}, u32[]{:S(2)}) collective-permute-start(bf16[4,28,16,128]{3,2,1,0:T(8,128)(2,1)S(1)} %bitcast.17), channel_id=1, source_target_pairs={{0,32},{32,0},{1,33},{33,1},{2,34},{34,2},{3,35},{35,3},{4,36},{36... | collective-permute-start | bytes 1376264 | tf_op jit(solution)/shard_map/ppermute | solution.py:298

commit v5 on v4

--- a/solution.py
+++ b/solution.py
@@ -127,8 +127,8 @@
         for position in range(SLOTS):
             tile = packet[position]
             target = SLOTS + below * LENGTHS[0] + position
-            bricks[target, :PLANE] = tile
-            bricks[target, VOXELS - PLANE :] = tile
+            for begin in range(0, VOXELS, PLANE):
+                bricks[target, begin : begin + PLANE] = tile
     for order, (faces, side) in enumerate(((y_first, odd), (y_second, 1 - odd))):
         tiles = [faces[position] for position in range(SLOTS)]
         targets = [STARTS[2] + side * LENGTHS[2] + position for position in range(SLOTS)]
@@ -284,16 +284,47 @@
     return lax.ppermute(value, AXES, pairs)
 
 
+def share_kernel(parts_ref, scaled_ref):
+    count = parts_ref.shape[1]
+    total = parts_ref[0].astype(jnp.float32)
+    for number in range(1, parts_ref.shape[0]):
+        total = total + parts_ref[number].astype(jnp.float32)
+    largest = jnp.max(jnp.abs(total), axis=0)
+    largest = jnp.max(jnp.max(largest, axis=1, keepdims=True), axis=0, keepdims=True)
+    power = jnp.clip(jnp.ceil(jnp.log2(jnp.maximum(largest, 1e-37))), -100.0, 100.0)
+    power = jnp.broadcast_to(power, (16, CHANNELS))
+    scale = jnp.exp2(14.0 - power)
+    for number in range(count):
+        scaled_ref[number] = total[number] * scale
+    scaled_ref[count] = power
+
+
+def column_kernel(column_ref, whole_ref):
+    count = whole_ref.shape[1]
+    scales = [jnp.exp2(column_ref[z, count] - 14.0) for z in range(column_ref.shape[0])]
+    for number in range(count):
+        total = column_ref[0, number] * scales[0]
+        for z in range(1, column_ref.shape[0]):
+            total = total + column_ref[z, number] * scales[z]
+        total = (total * (1.0 / (VOXELS * SLOTS))).astype(jnp.bfloat16)
+        for target in range(whole_ref.shape[0]):
+            whole_ref[target, number] = total
+
+
 def sum_everywhere(send, keep):
+    vmem = pl.BlockSpec(memory_space=pltpu.VMEM)
     arrived = lax.ppermute(send, "c", [(0, 1), (1, 0)])
     chip_sum = (keep + arrived.astype(jnp.float32)).astype(jnp.bfloat16)
     parts = chip_sum.reshape(16, 7, 16, CHANNELS)
     parts = lax.all_to_all(parts, ("x", "y"), 0, 0)
-    share = jnp.sum(parts.astype(jnp.float32), axis=0)
-    column = jnp.broadcast_to(share[None], (8,) + share.shape)
-    column = lax.all_to_all(column, "z", 0, 0)
-    share = (jnp.sum(column, axis=0) * (1.0 / (VOXELS * SLOTS))).astype(jnp.bfloat16)
-    whole = jnp.broadcast_to(share[None], (16,) + share.shape)
+    share = pl.pallas_call(
+        share_kernel, in_specs=[vmem], out_specs=vmem, out_shape=jax.ShapeDtypeStruct((8, 16, CHANNELS), jnp.float32)
+    )(parts)
+    column = jnp.broadcast_to(share.astype(jnp.float16)[None], (8,) + share.shape)
+    column = lax.all_to_all(column, "z", 0, 0).astype(jnp.float32)
+    whole = pl.pallas_call(
+        column_kernel, in_specs=[vmem], out_specs=vmem, out_shape=jax.ShapeDtypeStruct((16, 7, 16, CHANNELS), jnp.bfloat16)
+    )(column)
     own = lax.all_to_all(whole, ("x", "y"), 0, 0).reshape(4, ROWS_M, 16, CHANNELS)
     return own, lax.ppermute(own, "c", [(0, 1), (1, 0)])
 
@@ -367,7 +398,7 @@
         return outputs, input_grad, spread_out(first, own, other)
 
     return lax.cond(
-        own[0, 27, 0, 0] > 0, with_whole_bricks, as_they_are, (outputs, input_grad, own, other)
+        own[0, 27, 0, 0] != 0, with_whole_bricks, as_they_are, (outputs, input_grad, own, other)
     )
 
 

time: 85.3 us -> 86.8 us (1.018)
  blocking collectives: 53.3 us -> 49.3 us
  Pallas kernels: 9 us -> 12.7 us
  other arithmetic: 0.31 us -> 1.89 us
    pallas_call x0 -> x2, Pallas kernels: none -> 3.71 us  [the longest x1 1.88 us: sum_everywhere(): pl.pallas_call(column_kernel, in_specs=[vmem], out_specs=vmem, out_shape=...]
    all_to_all x1, blocking collectives: 18.3 us -> 15 us  [sum_everywhere(): column = lax.all_to_all(column, 'z', 0, 0).astype(jnp.float32)]
    convert_element_type x1 -> x2, other arithmetic: 0.01 us -> 1.69 us  [the longest x1 0.85 us: sum_everywhere(): share.astype(jnp.float16)[None]]
where the time goes in v5:
time: 86.8 us; the launch traced here: 86.3 us
  blocking collectives  49.3 us (57%)
  starting transfers between devices  12.9 us (15%)
  Pallas kernels  12.7 us (15%)
  waiting for transfers between devices  6.41 us (7%)
  other arithmetic  1.89 us (2%)
  local copies, waits for them, and re-layouts  1.59 us (2%)
  between operations  1.43 us (2%)
    all_to_all x1, blocking collectives, sum_everywhere(): parts = lax.all_to_all(parts, ('x', 'y'), 0, 0)  21.4 us
    all_to_all x1, blocking collectives, sum_everywhere(): column = lax.all_to_all(column, 'z', 0, 0).astype(jnp.float32)  15 us
    all_to_all x1, blocking collectives, sum_everywhere(): lax.all_to_all(whole, ('x', 'y'), 0, 0).reshape(4, ROWS_M, 16, CHANNELS)  13 us
    pallas_call x1, Pallas kernels, convolve(): pl.pallas_call(functools.partial(conv_kernel, fill, unroll, len(halos)),...  5.86 us
    ppermute x1, starting transfers between devices, sum_everywhere(): return (own, lax.ppermute(own, 'c', [(0, 1), (1, 0)]))  4.32 us
    ppermute x1, starting transfers between devices, local(): lax.ppermute(relayed(to_sibling, 1 - core), 'c', [(0, 1), (1, 0)])  3.47 us
    ppermute x1, waiting for transfers between devices, local(): lax.ppermute(relayed(to_outer, core), ('x', 'c'), [(2 * x + 1, 2 * x + 2)...  2.98 us
    ppermute x1, starting transfers between devices, local(): lax.ppermute(to_first, ('y', 'z'), [(gy, gy ^ 1) for gy in range(32)])  2.55 us
  transfers between devices with their start and end apart: 6, of which 4 were waited for; matrix products, arithmetic and copies ran while one was open for 2% of the time, Pallas kernels for 0%

profile of v5, /device:TPU:1, one launch (start us, length us, event | category | flops | bytes accessed | tf_op | source)
XLA Modules:
  0.0 86.3 jit_solution(8468028374813398376)
XLA Ops:
  0.6 0.1 pad_add_fusion.place_ref
  0.7 1.9 %shard_map.78 = (bf16[12,16,256]{2,1,0:T(8,128)(2,1)S(1)}, bf16[12,16,256]{2,1,0:T(8,128)(2,1)S(1)}, bf16[8,16,256]{2,1,0:T(8,128)(2,1)S(1)}, bf16[8,16,256]{2,1,0:T(8,128)(2,1)S(1)}) custom-call(s32[2]{0:T(128)S(1)} %pad_add_fusion.place_ref, s32[40]{0:T(128)} %slot_ref.1, bf16[8,64,128]{2,1,0:T(8,128)(2,1)} %features_ref.3, bf16[8,64,128]{2,1,0:T(8,128)(2,1)} %cotangent_ref.3), custom_call_target="tpu_custom_call" | custom-call | tf_op jit(solution)/shard_map/pallas_call | solution.py:100
  2.6 2.6 %collective-permute-start.10 = (bf16[12,16,256]{2,1,0:T(8,128)(2,1)S(1)}, bf16[12,16,256]{2,1,0:T(8,128)(2,1)S(1)}, u32[]{:S(2)}, u32[]{:S(2)}) collective-permute-start(bf16[12,16,256]{2,1,0:T(8,128)(2,1)S(1)} %get-tuple-element.62), channel_id=1, source_target_pairs={{0,1},{1,0},{2,3},{3,2},{4,5},{5,4},{6,7},{7,6},{8,9},{9,8},{10,11... | collective-permute-start | bytes 294920 | tf_op jit(solution)/shard_map/ppermute | solution.py:372
  5.1 0.7 collective-permute-start.11
  5.8 1.3 %collective-permute-done.10.rest_0_ = bf16[12,16,256]{2,1,0:T(8,128)(2,1)S(1)} collective-permute-done((bf16[12,16,256]{2,1,0:T(8,128)(2,1)S(1)}, bf16[12,16,256]{2,1,0:T(8,128)(2,1)S(1)}, u32[]{:S(2)}, u32[]{:S(2)}) %collective-permute-start.10) | collective-permute-done | bytes 98336 | tf_op jit(solution)/shard_map/ppermute | solution.py:372
  7.2 0.0 collective-permute-done.11.rest_1_
  7.2 3.5 %collective-permute-start.12 = (bf16[12,16,256]{2,1,0:T(8,128)(2,1)S(1)}, bf16[12,16,256]{2,1,0:T(8,128)(2,1)S(1)}, u32[]{:S(2)}, u32[]{:S(2)}) collective-permute-start(bf16[12,16,256]{2,1,0:T(8,128)(2,1)S(1)} %pad_maximum_fusion), channel_id=1, source_target_pairs={{0,32},{32,0},{1,33},{33,1},{2,34},{34,2},{3,35},{35,3},{4,36},{36... | collective-permute-start | bytes 294920 | tf_op jit(solution)/shard_map/ppermute | solution.py:381
  10.7 1.9 %collective-permute-start.13 = (bf16[12,16,256]{2,1,0:T(8,128)(2,1)S(1)}, bf16[12,16,256]{2,1,0:T(8,128)(2,1)S(1)}, u32[]{:S(2)}, u32[]{:S(2)}) collective-permute-start(bf16[12,16,256]{2,1,0:T(8,128)(2,1)S(1)} %pad_maximum_fusion.1), channel_id=1, source_target_pairs={{32,64},{96,128},{160,192},{64,32},{128,96},{192,160},{33,65},{97,... | collective-permute-start | bytes 294920 | tf_op jit(solution)/shard_map/ppermute | solution.py:379
  12.6 1.0 %copy.10 = bf16[512,128]{0,1:T(8,128)(2,1)S(1)} copy(bf16[512,128]{1,0:T(8,128)(2,1)} %bitcast.14) | data formatting | bytes 262144 | tf_op jit(solution)/shard_map/reshape | solution.py:369
  13.6 0.0 collective-permute-done.12.rest_2_
  13.6 3.0 %collective-permute-done.13.rest_3_ = bf16[12,16,256]{2,1,0:T(8,128)(2,1)S(1)} collective-permute-done((bf16[12,16,256]{2,1,0:T(8,128)(2,1)S(1)}, bf16[12,16,256]{2,1,0:T(8,128)(2,1)S(1)}, u32[]{:S(2)}, u32[]{:S(2)}) %collective-permute-start.13) | collective-permute-done | bytes 98336 | tf_op jit(solution)/shard_map/ppermute | solution.py:379
  16.6 5.9 %shard_map.79 = (bf16[8,64,128]{2,1,0:T(8,128)(2,1)}, bf16[8,64,128]{2,1,0:T(8,128)(2,1)}, bf16[4,28,16,128]{3,2,1,0:T(8,128)(2,1)S(1)}, f32[4,28,16,128]{3,2,1,0:T(8,128)S(1)}) custom-call(s32[2]{0:T(128)S(1)} %pad_add_fusion.place_ref, s32[8,27]{1,0:T(8,128)} %bitcast.22, s32[8,27]{1,0:T(8,128)} %bitcast.23, bf16[8,64,128]{2,1,0:T(8,128)(2,1)} %features_ref.3, ...), custom_call_target="tpu_custom_call" | custom-call | tf_op jit(solution)/shard_map/pallas_call | solution.py:227
  22.5 0.0 collective-permute-start.14
  22.5 1.8 %collective-permute-done.14 = bf16[4,28,16,128]{3,2,1,0:T(8,128)(2,1)S(1)} collective-permute-done((bf16[4,28,16,128]{3,2,1,0:T(8,128)(2,1)S(1)}, bf16[4,28,16,128]{3,2,1,0:T(8,128)(2,1)S(1)}, u32[]{:S(2)}, u32[]{:S(2)}) %collective-permute-start.14) | collective-permute-done | bytes 458784 | tf_op jit(solution)/shard_map/ppermute | solution.py:316
  24.3 0.1 add_convert_fusion.1
  24.4 21.4 %all_to_all.30.parts_ref = bf16[16,7,16,128]{3,2,1,0:T(8,128)(2,1)} all-to-all(bf16[16,7,16,128]{3,2,1,0:T(8,128)(2,1)S(1)} %bitcast.15), channel_id=1, replica_groups=mesh['x'=4,'c'=2,'y'=4,'z'=8] {'x','y'}, dimensions={0} | all-to-all | bytes 917504 | tf_op jit(solution)/shard_map/all_to_all | solution.py:319
  45.8 1.8 %shard_map.80 = f32[8,16,128]{2,1,0:T(8,128)} custom-call(bf16[16,7,16,128]{3,2,1,0:T(8,128)(2,1)} %all_to_all.30.parts_ref), custom_call_target="tpu_custom_call" | custom-call | tf_op jit(solution)/shard_map/pallas_call | solution.py:320
  47.6 0.8 convert_element_type.32
  48.4 0.0 copy-start
  48.4 0.0 copy-start.1
  48.4 0.0 copy-start.2
  48.4 0.0 copy-start.3
  48.5 0.0 copy-start.4
  48.5 15.0 %all_to_all.31 = f16[8,8,16,128]{3,2,1,0:T(8,128)(2,1)S(1)} all-to-all(f16[8,8,16,128]{3,2,1,0:T(8,128)(2,1)S(1)} %broadcast_in_dim.4), channel_id=1, replica_groups=mesh['x'=4,'c'=2,'y'=4,'z'=8] {'z'}, dimensions={0} | all-to-all | bytes 524288 | tf_op jit(solution)/shard_map/all_to_all | solution.py:324
  63.5 0.8 convert_element_type.33.column_ref
  64.3 1.9 %shard_map.81 = bf16[16,7,16,128]{3,2,1,0:T(8,128)(2,1)} custom-call(f32[8,8,16,128]{3,2,1,0:T(8,128)} %convert_element_type.33.column_ref), custom_call_target="tpu_custom_call" | custom-call | tf_op jit(solution)/shard_map/pallas_call | solution.py:325
  66.2 13.0 %all_to_all.32 = bf16[16,7,16,128]{3,2,1,0:T(8,128)(2,1)S(1)} all-to-all(bf16[16,7,16,128]{3,2,1,0:T(8,128)(2,1)} %shard_map.81), channel_id=1, replica_groups=mesh['x'=4,'c'=2,'y'=4,'z'=8] {'x','y'}, dimensions={0} | all-to-all | bytes 917504 | tf_op jit(solution)/shard_map/all_to_all | solution.py:328
  79.2 4.3 %collective-permute-start.15 = (bf16[4,28,16,128]{3,2,1,0:T(8,128)(2,1)S(1)}, bf16[4,28,16,128]{3,2,1,0:T(8,128)(2,1)S(1)}, u32[]{:S(2)}, u32[]{:S(2)}) collective-permute-start(bf16[4,28,16,128]{3,2,1,0:T(8,128)(2,1)S(1)} %bitcast.17), channel_id=1, source_target_pairs={{0,32},{32,0},{1,33},{33,1},{2,34},{34,2},{3,35},{35,3},{4,36},{36... | collective-permute-start | bytes 1376264 | tf_op jit(solution)/shard_map/ppermute | solution.py:329
  83.5 0.5 slice.4
  84.7 0.3 collective-permute-done.15
  85.0 0.0 copy-done
  85.0 0.0 copy-done.1
  85.0 0.0 copy-done.2
  85.0 0.0 copy-done.3
  85.0 0.0 copy-done.4
  85.0 1.3 %conditional.1 = (bf16[8,64,128]{2,1,0:T(8,128)(2,1)}, bf16[8,64,128]{2,1,0:T(8,128)(2,1)}, f32[27,128,128]{2,1,0:T(8,128)}) conditional(s32[]{:T(128)} %bitcast.10, (s32[1]{0:T(128)}, bf16[4,28,16,128]{3,2,1,0:T(8,128)(2,1)S(1)}, bf16[4,28,16,128]{3,2,1,0:T(8,128)(2,1)S(1)}, bf16[8,64,128]{2,1,0:T(8,128)(2,1)}, ...), branch_computations={%region_0.1_spmd, %region_1.2_spmd} | conditional | flops 835584 | bytes 14287272 | solution.py:400
  85.0 1.3 %branch_0_fun.1 = f32[27,128,128]{2,1,0:T(8,128)} custom-call(s32[1]{0:T(128)} %get-tuple-element.28.core_ref, bf16[4,28,16,128]{3,2,1,0:T(8,128)(2,1)S(1)} %get-tuple-element.29.own_ref, bf16[4,28,16,128]{3,2,1,0:T(8,128)(2,1)S(1)} %get-tuple-element.30.other_ref), custom_call_target="tpu_custom_call" | custom-call | tf_op jit(solution)/shard_map/cond/branch_0_fun/pallas_call | solution.py:351
  (5 shorter events, 0.1 us)
Async XLA Ops:
  2.6 4.6 %collective-permute-start.10 = (bf16[12,16,256]{2,1,0:T(8,128)(2,1)S(1)}, bf16[12,16,256]{2,1,0:T(8,128)(2,1)S(1)}, u32[]{:S(2)}, u32[]{:S(2)}) collective-permute-start(bf16[12,16,256]{2,1,0:T(8,128)(2,1)S(1)} %get-tuple-element.62), channel_id=1, source_target_pairs={{0,1},{1,0},{2,3},{3,2},{4,5},{5,4},{6,7},{7,6},{8,9},{9,8},{10,11... | collective-permute-start | bytes 294920 | tf_op jit(solution)/shard_map/ppermute | solution.py:372
  5.1 2.0 %collective-permute-start.11 = (bf16[12,16,256]{2,1,0:T(8,128)(2,1)S(1)}, bf16[12,16,256]{2,1,0:T(8,128)(2,1)S(1)}, u32[]{:S(2)}, u32[]{:S(2)}) collective-permute-start(bf16[12,16,256]{2,1,0:T(8,128)(2,1)S(1)} %get-tuple-element.63), channel_id=1, source_target_pairs={{1,2},{2,1},{3,4},{4,3},{5,6},{6,5},{7,8},{8,7},{9,10},{10,9},{11,... | collective-permute-start | bytes 294920 | tf_op jit(solution)/shard_map/ppermute | solution.py:373
  7.2 6.4 %collective-permute-start.12 = (bf16[12,16,256]{2,1,0:T(8,128)(2,1)S(1)}, bf16[12,16,256]{2,1,0:T(8,128)(2,1)S(1)}, u32[]{:S(2)}, u32[]{:S(2)}) collective-permute-start(bf16[12,16,256]{2,1,0:T(8,128)(2,1)S(1)} %pad_maximum_fusion), channel_id=1, source_target_pairs={{0,32},{32,0},{1,33},{33,1},{2,34},{34,2},{3,35},{35,3},{4,36},{36... | collective-permute-start | bytes 294920 | tf_op jit(solution)/shard_map/ppermute | solution.py:381
  10.7 5.9 %collective-permute-start.13 = (bf16[12,16,256]{2,1,0:T(8,128)(2,1)S(1)}, bf16[12,16,256]{2,1,0:T(8,128)(2,1)S(1)}, u32[]{:S(2)}, u32[]{:S(2)}) collective-permute-start(bf16[12,16,256]{2,1,0:T(8,128)(2,1)S(1)} %pad_maximum_fusion.1), channel_id=1, source_target_pairs={{32,64},{96,128},{160,192},{64,32},{128,96},{192,160},{33,65},{97,... | collective-permute-start | bytes 294920 | tf_op jit(solution)/shard_map/ppermute | solution.py:379
  22.5 1.8 %collective-permute-start.14 = (bf16[4,28,16,128]{3,2,1,0:T(8,128)(2,1)S(1)}, bf16[4,28,16,128]{3,2,1,0:T(8,128)(2,1)S(1)}, u32[]{:S(2)}, u32[]{:S(2)}) collective-permute-start(bf16[4,28,16,128]{3,2,1,0:T(8,128)(2,1)S(1)} %get-tuple-element.67), channel_id=1, source_target_pairs={{0,32},{32,0},{1,33},{33,1},{2,34},{34,2},{3,35},{35,3},{4,36},{36... | collective-permute-start | bytes 1376264 | tf_op jit(solution)/shard_map/ppermute | solution.py:316
  48.4 36.5 %copy-start = (bf16[27,128,128]{2,1,0:T(8,128)(2,1)S(1)}, bf16[27,128,128]{2,1,0:T(8,128)(2,1)}, u32[]{:S(2)}) copy-start(bf16[27,128,128]{2,1,0:T(8,128)(2,1)} %rest_5_.1) | copy-start | bytes 2654212
  48.4 36.5 %copy-start.1 = (bf16[8,64,128]{2,1,0:T(8,128)(2,1)S(1)}, bf16[8,64,128]{2,1,0:T(8,128)(2,1)}, u32[]{:S(2)}) copy-start(bf16[8,64,128]{2,1,0:T(8,128)(2,1)} %features_ref.3) | copy-start | bytes 393220
  48.4 36.5 %copy-start.2 = (bf16[8,64,128]{2,1,0:T(8,128)(2,1)S(1)}, bf16[8,64,128]{2,1,0:T(8,128)(2,1)}, u32[]{:S(2)}) copy-start(bf16[8,64,128]{2,1,0:T(8,128)(2,1)} %cotangent_ref.3) | copy-start | bytes 393220
  48.4 36.5 %copy-start.3 = (s32[27,8]{0,1:T(8,128)S(1)}, s32[27,8]{0,1:T(8,128)}, u32[]{:S(2)}) copy-start(s32[27,8]{0,1:T(8,128)} %param.10) | copy-start | bytes 2596
  48.5 36.5 %copy-start.4 = (s32[40]{0:T(128)S(1)}, s32[40]{0:T(128)}, u32[]{:S(2)}) copy-start(s32[40]{0:T(128)} %slot_ref.1) | copy-start | bytes 484
  79.2 5.8 %collective-permute-start.15 = (bf16[4,28,16,128]{3,2,1,0:T(8,128)(2,1)S(1)}, bf16[4,28,16,128]{3,2,1,0:T(8,128)(2,1)S(1)}, u32[]{:S(2)}, u32[]{:S(2)}) collective-permute-start(bf16[4,28,16,128]{3,2,1,0:T(8,128)(2,1)S(1)} %bitcast.17), channel_id=1, source_target_pairs={{0,32},{32,0},{1,33},{33,1},{2,34},{34,2},{3,35},{35,3},{4,36},{36... | collective-permute-start | bytes 1376264 | tf_op jit(solution)/shard_map/ppermute | solution.py:329

commit v6 on v4

--- a/solution.py
+++ b/solution.py
@@ -127,8 +127,8 @@
         for position in range(SLOTS):
             tile = packet[position]
             target = SLOTS + below * LENGTHS[0] + position
-            bricks[target, :PLANE] = tile
-            bricks[target, VOXELS - PLANE :] = tile
+            for begin in range(0, VOXELS, PLANE):
+                bricks[target, begin : begin + PLANE] = tile
     for order, (faces, side) in enumerate(((y_first, odd), (y_second, 1 - odd))):
         tiles = [faces[position] for position in range(SLOTS)]
         targets = [STARTS[2] + side * LENGTHS[2] + position for position in range(SLOTS)]
@@ -289,10 +289,14 @@
     chip_sum = (keep + arrived.astype(jnp.float32)).astype(jnp.bfloat16)
     parts = chip_sum.reshape(16, 7, 16, CHANNELS)
     parts = lax.all_to_all(parts, ("x", "y"), 0, 0)
-    share = jnp.sum(parts.astype(jnp.float32), axis=0)
-    column = jnp.broadcast_to(share[None], (8,) + share.shape)
-    column = lax.all_to_all(column, "z", 0, 0)
-    share = (jnp.sum(column, axis=0) * (1.0 / (VOXELS * SLOTS))).astype(jnp.bfloat16)
+    total = jnp.sum(parts.astype(jnp.float32), axis=0)
+    largest = jnp.max(jnp.abs(total), axis=(0, 1))
+    power = jnp.clip(jnp.ceil(jnp.log2(jnp.maximum(largest, 1e-37))), -100.0, 100.0)
+    power = jnp.broadcast_to(power, (1, 16, CHANNELS))
+    share = jnp.concatenate((total * jnp.exp2(14.0 - power), power), axis=0).astype(jnp.float16)
+    column = lax.all_to_all(jnp.broadcast_to(share[None], (8,) + share.shape), "z", 0, 0).astype(jnp.float32)
+    total = jnp.sum(column[:, :7] * jnp.exp2(column[:, 7:] - 14.0), axis=0)
+    share = (total * (1.0 / (VOXELS * SLOTS))).astype(jnp.bfloat16)
     whole = jnp.broadcast_to(share[None], (16,) + share.shape)
     own = lax.all_to_all(whole, ("x", "y"), 0, 0).reshape(4, ROWS_M, 16, CHANNELS)
     return own, lax.ppermute(own, "c", [(0, 1), (1, 0)])
@@ -367,7 +371,7 @@
         return outputs, input_grad, spread_out(first, own, other)
 
     return lax.cond(
-        own[0, 27, 0, 0] > 0, with_whole_bricks, as_they_are, (outputs, input_grad, own, other)
+        own[0, 27, 0, 0] != 0, with_whole_bricks, as_they_are, (outputs, input_grad, own, other)
     )
 
 

time: 85.3 us -> 81.3 us (0.953)
  blocking collectives: 53.3 us -> 49 us
    all_to_all x1, blocking collectives: 18.3 us -> 15 us  [sum_everywhere(): lax.all_to_all(jnp.broadcast_to(share[None], (8,) + share.shape), 'z', 0, 0)]
    all_to_all x1, blocking collectives: 13.8 us -> 12.8 us  [sum_everywhere(): lax.all_to_all(whole, ('x', 'y'), 0, 0).reshape(4, ROWS_M, 16, CHANNELS)]
where the time goes in v6:
time: 81.3 us; the launch traced here: 81 us
  blocking collectives  49 us (60%)
  starting transfers between devices  12.9 us (16%)
  Pallas kernels  9.01 us (11%)
  waiting for transfers between devices  6.41 us (8%)
  local copies, waits for them, and re-layouts  1.66 us (2%)
  between operations  1.49 us (2%)
    all_to_all x1, blocking collectives, sum_everywhere(): parts = lax.all_to_all(parts, ('x', 'y'), 0, 0)  21.3 us
    all_to_all x1, blocking collectives, sum_everywhere(): lax.all_to_all(jnp.broadcast_to(share[None], (8,) + share.shape), 'z', 0, 0)  15 us
    all_to_all x1, blocking collectives, sum_everywhere(): lax.all_to_all(whole, ('x', 'y'), 0, 0).reshape(4, ROWS_M, 16, CHANNELS)  12.8 us
    pallas_call x1, Pallas kernels, convolve(): pl.pallas_call(functools.partial(conv_kernel, fill, unroll, len(halos)),...  5.86 us
    ppermute x1, starting transfers between devices, sum_everywhere(): return (own, lax.ppermute(own, 'c', [(0, 1), (1, 0)]))  4.32 us
    ppermute x1, starting transfers between devices, local(): lax.ppermute(relayed(to_sibling, 1 - core), 'c', [(0, 1), (1, 0)])  3.47 us
    ppermute x1, waiting for transfers between devices, local(): lax.ppermute(relayed(to_outer, core), ('x', 'c'), [(2 * x + 1, 2 * x + 2)...  2.98 us
    ppermute x1, starting transfers between devices, local(): lax.ppermute(to_first, ('y', 'z'), [(gy, gy ^ 1) for gy in range(32)])  2.55 us
  transfers between devices with their start and end apart: 6, of which 4 were waited for; matrix products, arithmetic and copies ran while one was open for 2% of the time, Pallas kernels for 0%

profile of v6, /device:TPU:1, one launch (start us, length us, event | category | flops | bytes accessed | tf_op | source)
XLA Modules:
  0.0 81.0 jit_solution(9296756641296182095)
XLA Ops:
  0.6 0.1 pad_add_fusion.place_ref
  0.7 1.9 %shard_map.78 = (bf16[12,16,256]{2,1,0:T(8,128)(2,1)S(1)}, bf16[12,16,256]{2,1,0:T(8,128)(2,1)S(1)}, bf16[8,16,256]{2,1,0:T(8,128)(2,1)S(1)}, bf16[8,16,256]{2,1,0:T(8,128)(2,1)S(1)}) custom-call(s32[2]{0:T(128)S(1)} %pad_add_fusion.place_ref, s32[40]{0:T(128)} %slot_ref.1, bf16[8,64,128]{2,1,0:T(8,128)(2,1)} %features_ref.3, bf16[8,64,128]{2,1,0:T(8,128)(2,1)} %cotangent_ref.3), custom_call_target="tpu_custom_call" | custom-call | tf_op jit(solution)/shard_map/pallas_call | solution.py:100
  2.6 2.6 %collective-permute-start.10 = (bf16[12,16,256]{2,1,0:T(8,128)(2,1)S(1)}, bf16[12,16,256]{2,1,0:T(8,128)(2,1)S(1)}, u32[]{:S(2)}, u32[]{:S(2)}) collective-permute-start(bf16[12,16,256]{2,1,0:T(8,128)(2,1)S(1)} %get-tuple-element.62), channel_id=1, source_target_pairs={{0,1},{1,0},{2,3},{3,2},{4,5},{5,4},{6,7},{7,6},{8,9},{9,8},{10,11... | collective-permute-start | bytes 294920 | tf_op jit(solution)/shard_map/ppermute | solution.py:345
  5.1 0.7 collective-permute-start.11
  5.8 1.3 %collective-permute-done.10.rest_0_ = bf16[12,16,256]{2,1,0:T(8,128)(2,1)S(1)} collective-permute-done((bf16[12,16,256]{2,1,0:T(8,128)(2,1)S(1)}, bf16[12,16,256]{2,1,0:T(8,128)(2,1)S(1)}, u32[]{:S(2)}, u32[]{:S(2)}) %collective-permute-start.10) | collective-permute-done | bytes 98336 | tf_op jit(solution)/shard_map/ppermute | solution.py:345
  7.2 0.0 collective-permute-done.11.rest_1_
  7.2 3.5 %collective-permute-start.12 = (bf16[12,16,256]{2,1,0:T(8,128)(2,1)S(1)}, bf16[12,16,256]{2,1,0:T(8,128)(2,1)S(1)}, u32[]{:S(2)}, u32[]{:S(2)}) collective-permute-start(bf16[12,16,256]{2,1,0:T(8,128)(2,1)S(1)} %pad_maximum_fusion.1), channel_id=1, source_target_pairs={{0,32},{32,0},{1,33},{33,1},{2,34},{34,2},{3,35},{35,3},{4,36},{36... | collective-permute-start | bytes 294920 | tf_op jit(solution)/shard_map/ppermute | solution.py:354
  10.7 1.9 %collective-permute-start.13 = (bf16[12,16,256]{2,1,0:T(8,128)(2,1)S(1)}, bf16[12,16,256]{2,1,0:T(8,128)(2,1)S(1)}, u32[]{:S(2)}, u32[]{:S(2)}) collective-permute-start(bf16[12,16,256]{2,1,0:T(8,128)(2,1)S(1)} %pad_maximum_fusion.2), channel_id=1, source_target_pairs={{32,64},{96,128},{160,192},{64,32},{128,96},{192,160},{33,65},{97,... | collective-permute-start | bytes 294920 | tf_op jit(solution)/shard_map/ppermute | solution.py:352
  12.6 1.0 %copy.11 = bf16[512,128]{0,1:T(8,128)(2,1)S(1)} copy(bf16[512,128]{1,0:T(8,128)(2,1)} %bitcast.18) | data formatting | bytes 262144 | tf_op jit(solution)/shard_map/reshape | solution.py:342
  13.6 0.0 collective-permute-done.12.rest_2_
  13.6 3.0 %collective-permute-done.13.rest_3_ = bf16[12,16,256]{2,1,0:T(8,128)(2,1)S(1)} collective-permute-done((bf16[12,16,256]{2,1,0:T(8,128)(2,1)S(1)}, bf16[12,16,256]{2,1,0:T(8,128)(2,1)S(1)}, u32[]{:S(2)}, u32[]{:S(2)}) %collective-permute-start.13) | collective-permute-done | bytes 98336 | tf_op jit(solution)/shard_map/ppermute | solution.py:352
  16.6 5.9 %shard_map.79 = (bf16[8,64,128]{2,1,0:T(8,128)(2,1)}, bf16[8,64,128]{2,1,0:T(8,128)(2,1)}, bf16[4,28,16,128]{3,2,1,0:T(8,128)(2,1)S(1)}, f32[4,28,16,128]{3,2,1,0:T(8,128)S(1)}) custom-call(s32[2]{0:T(128)S(1)} %pad_add_fusion.place_ref, s32[8,27]{1,0:T(8,128)} %bitcast.26, s32[8,27]{1,0:T(8,128)} %bitcast.27, bf16[8,64,128]{2,1,0:T(8,128)(2,1)} %features_ref.3, ...), custom_call_target="tpu_custom_call" | custom-call | tf_op jit(solution)/shard_map/pallas_call | solution.py:227
  22.5 0.0 collective-permute-start.14
  22.5 1.8 %collective-permute-done.14 = bf16[4,28,16,128]{3,2,1,0:T(8,128)(2,1)S(1)} collective-permute-done((bf16[4,28,16,128]{3,2,1,0:T(8,128)(2,1)S(1)}, bf16[4,28,16,128]{3,2,1,0:T(8,128)(2,1)S(1)}, u32[]{:S(2)}, u32[]{:S(2)}) %collective-permute-start.14) | collective-permute-done | bytes 458784 | tf_op jit(solution)/shard_map/ppermute | solution.py:288
  24.3 0.1 add_convert_fusion.1
  24.4 21.3 %all_to_all.30 = bf16[16,7,16,128]{3,2,1,0:T(8,128)(2,1)S(1)} all-to-all(bf16[16,7,16,128]{3,2,1,0:T(8,128)(2,1)S(1)} %bitcast.19), channel_id=1, replica_groups=mesh['x'=4,'c'=2,'y'=4,'z'=8] {'x','y'}, dimensions={0} | all-to-all | bytes 917504 | tf_op jit(solution)/shard_map/all_to_all | solution.py:291
  45.6 0.1 convert_reduce_fusion.1
  45.9 0.0 copy-start
  45.9 0.0 copy-start.1
  45.9 0.0 copy-start.2
  45.9 0.0 copy-start.3
  45.9 0.0 copy-start.4
  45.9 15.0 %all_to_all.31 = f16[8,8,16,128]{3,2,1,0:T(8,128)(2,1)S(1)} all-to-all(f16[8,8,16,128]{3,2,1,0:T(8,128)(2,1)S(1)} %broadcast_in_dim.13), channel_id=1, replica_groups=mesh['x'=4,'c'=2,'y'=4,'z'=8] {'z'}, dimensions={0} | all-to-all | bytes 524288 | tf_op jit(solution)/shard_map/all_to_all | solution.py:297
  61.0 0.1 broadcast_in_dim.14
  61.1 12.8 %all_to_all.32 = bf16[16,7,16,128]{3,2,1,0:T(8,128)(2,1)S(1)} all-to-all(bf16[16,7,16,128]{3,2,1,0:T(8,128)(2,1)S(1)} %broadcast_in_dim.14), channel_id=1, replica_groups=mesh['x'=4,'c'=2,'y'=4,'z'=8] {'x','y'}, dimensions={0} | all-to-all | bytes 917504 | tf_op jit(solution)/shard_map/all_to_all | solution.py:301
  73.9 4.3 %collective-permute-start.15 = (bf16[4,28,16,128]{3,2,1,0:T(8,128)(2,1)S(1)}, bf16[4,28,16,128]{3,2,1,0:T(8,128)(2,1)S(1)}, u32[]{:S(2)}, u32[]{:S(2)}) collective-permute-start(bf16[4,28,16,128]{3,2,1,0:T(8,128)(2,1)S(1)} %bitcast.21), channel_id=1, source_target_pairs={{0,32},{32,0},{1,33},{33,1},{2,34},{34,2},{3,35},{35,3},{4,36},{36... | collective-permute-start | bytes 1376264 | tf_op jit(solution)/shard_map/ppermute | solution.py:302
  78.2 0.5 slice.22
  79.4 0.3 collective-permute-done.15
  79.6 0.0 copy-done
  79.6 0.0 copy-done.1
  79.6 0.0 copy-done.2
  79.6 0.0 copy-done.3
  79.6 0.0 copy-done.4
  79.7 1.3 %conditional.1 = (bf16[8,64,128]{2,1,0:T(8,128)(2,1)}, bf16[8,64,128]{2,1,0:T(8,128)(2,1)}, f32[27,128,128]{2,1,0:T(8,128)}) conditional(s32[]{:T(128)} %bitcast.12, (s32[1]{0:T(128)}, bf16[4,28,16,128]{3,2,1,0:T(8,128)(2,1)S(1)}, bf16[4,28,16,128]{3,2,1,0:T(8,128)(2,1)S(1)}, bf16[8,64,128]{2,1,0:T(8,128)(2,1)}, ...), branch_computations={%region_3.4_spmd, %region_4.8_spmd} | conditional | flops 1614592 | bytes 16206760 | solution.py:373
  79.7 1.3 %branch_0_fun.1 = f32[27,128,128]{2,1,0:T(8,128)} custom-call(s32[1]{0:T(128)} %get-tuple-element.28.core_ref, bf16[4,28,16,128]{3,2,1,0:T(8,128)(2,1)S(1)} %get-tuple-element.29.own_ref, bf16[4,28,16,128]{3,2,1,0:T(8,128)(2,1)S(1)} %get-tuple-element.30.other_ref), custom_call_target="tpu_custom_call" | custom-call | tf_op jit(solution)/shard_map/cond/branch_0_fun/pallas_call | solution.py:324
  (14 shorter events, 0.3 us)
Async XLA Ops:
  2.6 4.6 %collective-permute-start.10 = (bf16[12,16,256]{2,1,0:T(8,128)(2,1)S(1)}, bf16[12,16,256]{2,1,0:T(8,128)(2,1)S(1)}, u32[]{:S(2)}, u32[]{:S(2)}) collective-permute-start(bf16[12,16,256]{2,1,0:T(8,128)(2,1)S(1)} %get-tuple-element.62), channel_id=1, source_target_pairs={{0,1},{1,0},{2,3},{3,2},{4,5},{5,4},{6,7},{7,6},{8,9},{9,8},{10,11... | collective-permute-start | bytes 294920 | tf_op jit(solution)/shard_map/ppermute | solution.py:345
  5.1 2.0 %collective-permute-start.11 = (bf16[12,16,256]{2,1,0:T(8,128)(2,1)S(1)}, bf16[12,16,256]{2,1,0:T(8,128)(2,1)S(1)}, u32[]{:S(2)}, u32[]{:S(2)}) collective-permute-start(bf16[12,16,256]{2,1,0:T(8,128)(2,1)S(1)} %get-tuple-element.63), channel_id=1, source_target_pairs={{1,2},{2,1},{3,4},{4,3},{5,6},{6,5},{7,8},{8,7},{9,10},{10,9},{11,... | collective-permute-start | bytes 294920 | tf_op jit(solution)/shard_map/ppermute | solution.py:346
  7.2 6.4 %collective-permute-start.12 = (bf16[12,16,256]{2,1,0:T(8,128)(2,1)S(1)}, bf16[12,16,256]{2,1,0:T(8,128)(2,1)S(1)}, u32[]{:S(2)}, u32[]{:S(2)}) collective-permute-start(bf16[12,16,256]{2,1,0:T(8,128)(2,1)S(1)} %pad_maximum_fusion.1), channel_id=1, source_target_pairs={{0,32},{32,0},{1,33},{33,1},{2,34},{34,2},{3,35},{35,3},{4,36},{36... | collective-permute-start | bytes 294920 | tf_op jit(solution)/shard_map/ppermute | solution.py:354
  10.7 5.9 %collective-permute-start.13 = (bf16[12,16,256]{2,1,0:T(8,128)(2,1)S(1)}, bf16[12,16,256]{2,1,0:T(8,128)(2,1)S(1)}, u32[]{:S(2)}, u32[]{:S(2)}) collective-permute-start(bf16[12,16,256]{2,1,0:T(8,128)(2,1)S(1)} %pad_maximum_fusion.2), channel_id=1, source_target_pairs={{32,64},{96,128},{160,192},{64,32},{128,96},{192,160},{33,65},{97,... | collective-permute-start | bytes 294920 | tf_op jit(solution)/shard_map/ppermute | solution.py:352
  22.5 1.8 %collective-permute-start.14 = (bf16[4,28,16,128]{3,2,1,0:T(8,128)(2,1)S(1)}, bf16[4,28,16,128]{3,2,1,0:T(8,128)(2,1)S(1)}, u32[]{:S(2)}, u32[]{:S(2)}) collective-permute-start(bf16[4,28,16,128]{3,2,1,0:T(8,128)(2,1)S(1)} %get-tuple-element.67), channel_id=1, source_target_pairs={{0,32},{32,0},{1,33},{33,1},{2,34},{34,2},{3,35},{35,3},{4,36},{36... | collective-permute-start | bytes 1376264 | tf_op jit(solution)/shard_map/ppermute | solution.py:288
  45.9 33.8 %copy-start = (bf16[27,128,128]{2,1,0:T(8,128)(2,1)S(1)}, bf16[27,128,128]{2,1,0:T(8,128)(2,1)}, u32[]{:S(2)}) copy-start(bf16[27,128,128]{2,1,0:T(8,128)(2,1)} %rest_5_.1) | copy-start | bytes 2654212
  45.9 33.8 %copy-start.1 = (bf16[8,64,128]{2,1,0:T(8,128)(2,1)S(1)}, bf16[8,64,128]{2,1,0:T(8,128)(2,1)}, u32[]{:S(2)}) copy-start(bf16[8,64,128]{2,1,0:T(8,128)(2,1)} %features_ref.3) | copy-start | bytes 393220
  45.9 33.8 %copy-start.2 = (bf16[8,64,128]{2,1,0:T(8,128)(2,1)S(1)}, bf16[8,64,128]{2,1,0:T(8,128)(2,1)}, u32[]{:S(2)}) copy-start(bf16[8,64,128]{2,1,0:T(8,128)(2,1)} %cotangent_ref.3) | copy-start | bytes 393220
  45.9 33.8 %copy-start.3 = (s32[27,8]{0,1:T(8,128)S(1)}, s32[27,8]{0,1:T(8,128)}, u32[]{:S(2)}) copy-start(s32[27,8]{0,1:T(8,128)} %param.10) | copy-start | bytes 2596
  45.9 33.7 %copy-start.4 = (s32[40]{0:T(128)S(1)}, s32[40]{0:T(128)}, u32[]{:S(2)}) copy-start(s32[40]{0:T(128)} %slot_ref.1) | copy-start | bytes 484
  73.9 5.8 %collective-permute-start.15 = (bf16[4,28,16,128]{3,2,1,0:T(8,128)(2,1)S(1)}, bf16[4,28,16,128]{3,2,1,0:T(8,128)(2,1)S(1)}, u32[]{:S(2)}, u32[]{:S(2)}) collective-permute-start(bf16[4,28,16,128]{3,2,1,0:T(8,128)(2,1)S(1)} %bitcast.21), channel_id=1, source_target_pairs={{0,32},{32,0},{1,33},{33,1},{2,34},{34,2},{3,35},{35,3},{4,36},{36... | collective-permute-start | bytes 1376264 | tf_op jit(solution)/shard_map/ppermute | solution.py:302

commit v7 on v6

--- a/solution.py
+++ b/solution.py
@@ -24,7 +24,7 @@
 LENGTHS = (TILE * BZ,) * 4 + (BZ,) * 4
 STARTS = tuple(int(start) for start in np.cumsum((0,) + LENGTHS[:-1]))
 AXES = ("x", "c", "y", "z")
-VMEM_LIMIT = 48 * 1024 * 1024
+VMEM_LIMIT = 24 * 1024 * 1024
 
 
 def where_equal(left, right):
@@ -53,15 +53,21 @@
     return where_equal(row, (column >> 2) * PLANE + side * 12 + (column & 3))
 
 
-def pack_layers_kernel(place_ref, slot_ref, features_ref, cotangent_ref, to_first, to_second, to_sibling, to_outer,
-                       bricks, sides, sems):
+def pack_layers_kernel(place_ref, recv_slot_ref, features_ref, cotangent_ref, to_first, to_second, to_sibling, to_outer,
+                       own_f, own_c, sides, slot_ref, sems):
+    bricks = (own_f, own_c)
     copies = [
-        pltpu.make_async_copy(ref, bricks.at[number, pl.ds(0, SLOTS)], sems.at[number])
-        for number, ref in enumerate((features_ref, cotangent_ref))
+        pltpu.make_async_copy(ref, target, sems.at[number])
+        for number, (ref, target) in enumerate((
+            (features_ref, own_f.at[pl.ds(0, SLOTS)]),
+            (cotangent_ref, own_c.at[pl.ds(0, SLOTS)]),
+            (recv_slot_ref, slot_ref),
+        ))
     ]
     for copy in copies:
         copy.start()
-    bricks[:, SLOTS] = jnp.zeros((2, VOXELS, CHANNELS), jnp.bfloat16)
+    for own in bricks:
+        own[SLOTS] = jnp.zeros((VOXELS, CHANNELS), jnp.bfloat16)
     sides[:, SLOTS] = jnp.zeros((2, 2 * PLANE, CHANNELS), jnp.bfloat16)
     core = place_ref[0]
     odd = place_ref[1]
@@ -69,7 +75,7 @@
     for copy in copies:
         copy.wait()
     for kind in range(2):
-        beside = jnp.concatenate([bricks[kind, slot] for slot in range(SLOTS)], axis=1)
+        beside = jnp.concatenate([bricks[kind][slot] for slot in range(SLOTS)], axis=1)
         picked = jnp.dot(layer, beside, preferred_element_type=jnp.float32).astype(jnp.bfloat16)
         for slot in range(SLOTS):
             sides[kind, slot] = picked[:, slot * CHANNELS : (slot + 1) * CHANNELS]
@@ -77,15 +83,15 @@
     def put(packet, position, halo, source, begin):
         slot = jnp.clip(slot_ref[halo], 0, SLOTS)
         rows = pl.ds(begin, PLANE)
-        packet[position, :, :CHANNELS] = source[0, slot, rows]
-        packet[position, :, CHANNELS:] = source[1, slot, rows]
+        packet[position, :, :CHANNELS] = source[0][slot, rows]
+        packet[position, :, CHANNELS:] = source[1][slot, rows]
 
     for packet, up in ((to_first, 1 - odd), (to_second, odd)):
         begin = pl.multiple_of(up * PLANE, PLANE)
         position = 0
         for number in (2, 4, 6):
             for halo in range(LENGTHS[number]):
-                put(packet, position, STARTS[number] + up * LENGTHS[number] + halo, sides, begin)
+                put(packet, position, STARTS[number] + up * LENGTHS[number] + halo, (sides.at[0], sides.at[1]), begin)
                 position += 1
     for packet, up in ((to_sibling, 1 - core), (to_outer, core)):
         begin = pl.multiple_of(up * (VOXELS - PLANE), PLANE)
@@ -99,48 +105,48 @@
     hbm = pl.BlockSpec(memory_space=pltpu.HBM)
     return pl.pallas_call(
         pack_layers_kernel,
-        in_specs=[smem, smem, hbm, hbm],
-        out_specs=[vmem] * 4,
+        in_specs=[smem, hbm, hbm, hbm],
+        out_specs=[vmem] * 6,
         out_shape=[
             jax.ShapeDtypeStruct((length, PLANE, 2 * CHANNELS), jnp.bfloat16) for length in (12, 12, 8, 8)
-        ],
+        ] + [jax.ShapeDtypeStruct((SLOTS + 1, VOXELS, CHANNELS), jnp.bfloat16)] * 2,
         scratch_shapes=[
-            pltpu.VMEM((2, SLOTS + 1, VOXELS, CHANNELS), jnp.bfloat16),
             pltpu.VMEM((2, SLOTS + 1, 2 * PLANE, CHANNELS), jnp.bfloat16),
-            pltpu.SemaphoreType.DMA((2,)),
+            pltpu.SMEM((HALO,), jnp.int32),
+            pltpu.SemaphoreType.DMA((3,)),
         ],
         compiler_params=pltpu.CompilerParams(vmem_limit_bytes=VMEM_LIMIT),
     )(place, recv_slot, features, cotangent)
 
 
-def fill_bricks(core, odd, halos, bricks):
+def fill_bricks(core, odd, halos, lanes, bricks):
     begin_at = SLOTS
     for halo in halos:
-        bricks[begin_at : begin_at + halo.shape[0]] = halo[...]
+        bricks[begin_at : begin_at + halo.shape[0]] = halo[:, :, lanes]
         begin_at += halo.shape[0]
 
 
-def fill_layers(core, odd, halos, bricks):
+def fill_layers(core, odd, halos, lanes, bricks):
     y_first, y_second, x_sibling, x_outer = halos
     both = ((x_sibling, core), (x_outer, 1 - core))
     for packet, below in both:
         for position in range(SLOTS):
-            tile = packet[position]
+            tile = packet[position, :, lanes]
             target = SLOTS + below * LENGTHS[0] + position
             for begin in range(0, VOXELS, PLANE):
                 bricks[target, begin : begin + PLANE] = tile
     for order, (faces, side) in enumerate(((y_first, odd), (y_second, 1 - odd))):
-        tiles = [faces[position] for position in range(SLOTS)]
+        tiles = [faces[position, :, lanes] for position in range(SLOTS)]
         targets = [STARTS[2] + side * LENGTHS[2] + position for position in range(SLOTS)]
         for packet, below in both:
             for position in range(BZ):
-                tiles.append(packet[SLOTS + BZ * order + position])
+                tiles.append(packet[SLOTS + BZ * order + position, :, lanes])
                 targets.append(STARTS[4] + side * BZ + below * 2 * BZ + position)
         whole = jnp.dot(
             expand_matrix(side), jnp.concatenate(tiles, axis=1), preferred_element_type=jnp.float32
         ).astype(jnp.bfloat16)
         for position, target in enumerate(targets):
-            bricks[SLOTS + target] = whole[:, position * 2 * CHANNELS : (position + 1) * 2 * CHANNELS]
+            bricks[SLOTS + target] = whole[:, position * CHANNELS : (position + 1) * CHANNELS]
 
 
 def out_of_place(dst):
@@ -158,40 +164,42 @@
     return jnp.max(jnp.max(wrong, axis=1, keepdims=True), axis=0, keepdims=True)
 
 
-def conv_kernel(fill, unroll, count, place_ref, dst_ref, table_ref, features_ref, cotangent_ref, *rest):
-    halos = rest[:count]
-    (flipped_ref, weights_ref, outputs_ref, grad_ref, send_ref, keep_ref, bricks, taps_f, taps_c) = rest[count:]
-    core = place_ref[0]
-    bricks[:SLOTS, :, :CHANNELS] = features_ref[...]
-    bricks[:SLOTS, :, CHANNELS:] = cotangent_ref[...]
-    fill(core, place_ref[1], halos, bricks)
-    bricks[SLOTS + HALO] = jnp.zeros((VOXELS, 2 * CHANNELS), jnp.bfloat16)
+def build_taps(fill, unroll, place_ref, dst_ref, own_ref, halos, lanes, bricks, taps):
+    bricks[:SLOTS] = own_ref[:SLOTS]
+    fill(place_ref[0], place_ref[1], halos, lanes, bricks)
+    bricks[SLOTS + HALO] = jnp.zeros((VOXELS, CHANNELS), jnp.bfloat16)
     shift = shift_matrix()
 
+    def around(slot, plane):
+        side = 0 if plane == 0 else 2 if plane == PLANES - 1 else 1
+        local = (plane - 1) % BRICK * PLANE
+        return jnp.concatenate(
+            [bricks[dst_ref[slot, side * 9 + number], local : local + PLANE] for number in range(9)], axis=0
+        )
+
     def one_slot(slot, carry):
-        for plane in range(PLANES):
-            side = 0 if plane == 0 else 2 if plane == PLANES - 1 else 1
-            local = (plane - 1) % BRICK * PLANE
-            around = [
-                bricks[jnp.clip(dst_ref[slot, side * 9 + number], 0, SLOTS + HALO), local : local + PLANE]
-                for number in range(9)
-            ]
-            moved = jnp.dot(
-                shift, jnp.concatenate(around, axis=0), preferred_element_type=jnp.float32
-            ).astype(jnp.bfloat16)
+        for plane in range(0, PLANES, 2):
+            pair = jnp.concatenate((around(slot, plane), around(slot, plane + 1)), axis=1)
+            moved = jnp.dot(shift, pair, preferred_element_type=jnp.float32).astype(jnp.bfloat16)
             for number in range(9):
                 rows = moved[number * PLANE : (number + 1) * PLANE]
-                lanes = slice(number * CHANNELS, (number + 1) * CHANNELS)
-                taps_f[slot, plane, :, lanes] = rows[:, :CHANNELS]
-                taps_c[slot, plane, :, lanes] = rows[:, CHANNELS:]
+                target = slice(number * CHANNELS, (number + 1) * CHANNELS)
+                taps[slot, plane, :, target] = rows[:, :CHANNELS]
+                taps[slot, plane + 1, :, target] = rows[:, CHANNELS:]
         return carry
 
     lax.fori_loop(0, SLOTS, one_slot, 0, unroll=unroll)
 
+
+def weight_kernel(fill, unroll, count, place_ref, dst_ref, table_ref, cotangent_ref, *rest):
+    halos = rest[:count]
+    flipped_ref, send_ref, keep_ref, taps, bricks = rest[count:]
+    build_taps(fill, unroll, place_ref, dst_ref, cotangent_ref, halos, slice(CHANNELS, 2 * CHANNELS), bricks, taps)
+    core = place_ref[0]
     flipped = jnp.concatenate((flipped_ref[1 - core], flipped_ref[core]), axis=0)
     half = CHANNELS // 2
     for side in range(3):
-        tap = taps_c[:, side : side + BRICK].reshape(SLOTS * VOXELS, WIDE)
+        tap = taps[:, side : side + BRICK].reshape(SLOTS * VOXELS, WIDE)
         part = jnp.dot(flipped, tap, preferred_element_type=jnp.float32)
         for number in range(9):
             block = part[:, number * CHANNELS : (number + 1) * CHANNELS]
@@ -205,42 +213,70 @@
         send_ref[quarter, 27] = flag.astype(jnp.bfloat16)
         keep_ref[quarter, 27] = flag
 
-    outputs = None
+
+def grad_kernel(taps, weights_ref, grad_ref):
     grad = None
     for side in range(3):
-        tap = taps_f[:, side : side + BRICK].reshape(SLOTS * VOXELS, WIDE)
+        tap = taps[:, side : side + BRICK].reshape(SLOTS * VOXELS, WIDE)
+        matrix = jnp.concatenate([weights_ref[26 - side * 9 - number] for number in range(9)], axis=1)
+        part = lax.dot_general(tap, matrix, (((1,), (1,)), ((), ())), preferred_element_type=jnp.float32)
+        grad = part if grad is None else grad + part
+    grad_ref[...] = grad.astype(jnp.bfloat16).reshape(SLOTS, VOXELS, CHANNELS)
+
+
+def output_kernel(fill, unroll, count, place_ref, dst_ref, features_ref, *rest):
+    halos = rest[:count]
+    weights_ref, outputs_ref, bricks, taps = rest[count:]
+    build_taps(fill, unroll, place_ref, dst_ref, features_ref, halos, slice(0, CHANNELS), bricks, taps)
+    outputs = None
+    for side in range(3):
+        tap = taps[:, side : side + BRICK].reshape(SLOTS * VOXELS, WIDE)
         matrix = weights_ref[side * 9 : side * 9 + 9].reshape(WIDE, CHANNELS)
         part = jnp.dot(tap, matrix, preferred_element_type=jnp.float32)
         outputs = part if outputs is None else outputs + part
     outputs_ref[...] = outputs.astype(jnp.bfloat16).reshape(SLOTS, VOXELS, CHANNELS)
-    for side in range(3):
-        tap = taps_c[:, side : side + BRICK].reshape(SLOTS * VOXELS, WIDE)
-        matrix = jnp.concatenate([weights_ref[26 - side * 9 - number] for number in range(9)], axis=1)
-        part = lax.dot_general(tap, matrix, (((1,), (1,)), ((), ())), preferred_element_type=jnp.float32)
-        grad = part if grad is None else grad + part
-    grad_ref[...] = grad.astype(jnp.bfloat16).reshape(SLOTS, VOXELS, CHANNELS)
-
-
-def convolve(fill, unroll, place, dst, features, cotangent, halos, flipped, weights):
+
+
+def convolve(fill, unroll, place, dst, own_f, own_c, halos, flipped, weights):
     vmem = pl.BlockSpec(memory_space=pltpu.VMEM)
     smem = pl.BlockSpec(memory_space=pltpu.SMEM)
-    return pl.pallas_call(
-        functools.partial(conv_kernel, fill, unroll, len(halos)),
-        in_specs=[smem, smem] + [vmem] * (5 + len(halos)),
-        out_specs=[vmem] * 4,
+    brick = jax.ShapeDtypeStruct((SLOTS, VOXELS, CHANNELS), jnp.bfloat16)
+    taps = (SLOTS, PLANES, PLANE, WIDE)
+    bricks = pltpu.VMEM((SLOTS + HALO + 1, VOXELS, CHANNELS), jnp.bfloat16)
+    params = pltpu.CompilerParams(vmem_limit_bytes=VMEM_LIMIT)
+    flops = 2 * SLOTS * VOXELS * 27 * CHANNELS * CHANNELS
+    cost = pl.CostEstimate(flops=2 * flops, bytes_accessed=4_000_000, transcendentals=0)
+    send, keep, taps_c = pl.pallas_call(
+        functools.partial(weight_kernel, fill, unroll, len(halos)),
+        in_specs=[smem, smem] + [vmem] * (3 + len(halos)),
+        out_specs=[vmem] * 3,
         out_shape=[
-            jax.ShapeDtypeStruct((SLOTS, VOXELS, CHANNELS), jnp.bfloat16),
-            jax.ShapeDtypeStruct((SLOTS, VOXELS, CHANNELS), jnp.bfloat16),
             jax.ShapeDtypeStruct((4, ROWS_M, 16, CHANNELS), jnp.bfloat16),
             jax.ShapeDtypeStruct((4, ROWS_M, 16, CHANNELS), jnp.float32),
+            jax.ShapeDtypeStruct(taps, jnp.bfloat16),
         ],
-        scratch_shapes=[
-            pltpu.VMEM((SLOTS + HALO + 1, VOXELS, 2 * CHANNELS), jnp.bfloat16),
-            pltpu.VMEM((SLOTS, PLANES, PLANE, WIDE), jnp.bfloat16),
-            pltpu.VMEM((SLOTS, PLANES, PLANE, WIDE), jnp.bfloat16),
-        ],
-        compiler_params=pltpu.CompilerParams(vmem_limit_bytes=VMEM_LIMIT),
-    )(place, dst, dst, features, cotangent, *halos, flipped, weights)
+        scratch_shapes=[bricks],
+        compiler_params=params,
+        cost_estimate=cost,
+    )(place, dst, dst, own_c, *halos, flipped)
+    grad = pl.pallas_call(
+        grad_kernel,
+        in_specs=[vmem, vmem],
+        out_specs=vmem,
+        out_shape=brick,
+        compiler_params=params,
+        cost_estimate=cost,
+    )(taps_c, weights)
+    outputs = pl.pallas_call(
+        functools.partial(output_kernel, fill, unroll, len(halos)),
+        in_specs=[smem, smem] + [vmem] * (2 + len(halos)),
+        out_specs=vmem,
+        out_shape=brick,
+        scratch_shapes=[bricks, pltpu.VMEM(taps, jnp.bfloat16)],
+        compiler_params=params,
+        cost_estimate=cost,
+    )(place, dst, own_f, *halos, weights)
+    return outputs, grad, send, keep
 
 
 def pack_bricks_kernel(slot_ref, features_ref, cotangent_ref, *packets):
@@ -284,8 +320,9 @@
     return lax.ppermute(value, AXES, pairs)
 
 
-def sum_everywhere(send, keep):
+def sum_everywhere(send, keep, grad):
     arrived = lax.ppermute(send, "c", [(0, 1), (1, 0)])
+    arrived, grad = lax.optimization_barrier((arrived, grad))
     chip_sum = (keep + arrived.astype(jnp.float32)).astype(jnp.bfloat16)
     parts = chip_sum.reshape(16, 7, 16, CHANNELS)
     parts = lax.all_to_all(parts, ("x", "y"), 0, 0)
@@ -299,7 +336,7 @@
     share = (total * (1.0 / (VOXELS * SLOTS))).astype(jnp.bfloat16)
     whole = jnp.broadcast_to(share[None], (16,) + share.shape)
     own = lax.all_to_all(whole, ("x", "y"), 0, 0).reshape(4, ROWS_M, 16, CHANNELS)
-    return own, lax.ppermute(own, "c", [(0, 1), (1, 0)])
+    return own, lax.ppermute(own, "c", [(0, 1), (1, 0)]), grad
 
 
 def spread_kernel(core_ref, own_ref, other_ref, out_ref, whole, sems):
@@ -338,10 +375,10 @@
     core = lax.axis_index("c").astype(jnp.int32)
     first = core.reshape(1)
     place = jnp.stack((core, (lax.axis_index("z") % 2).astype(jnp.int32)))
-    dst = dst_index.T
-    flipped = jnp.transpose(features.reshape(SLOTS * VOXELS, CHANNELS)).reshape(2, CHANNELS // 2, SLOTS * VOXELS)
-
-    to_first, to_second, to_sibling, to_outer = pack_layers(place, recv_slot, features, cotangent)
+    dst = jnp.clip(dst_index.T, 0, SLOTS + HALO)
+    to_first, to_second, to_sibling, to_outer, own_f, own_c = pack_layers(place, recv_slot, features, cotangent)
+    flipped = jnp.transpose(own_f[:SLOTS].reshape(SLOTS * VOXELS, CHANNELS))
+    flipped = flipped.reshape(2, CHANNELS // 2, SLOTS * VOXELS)
     y_first = lax.ppermute(to_first, ("y", "z"), [(gy, gy ^ 1) for gy in range(32)])
     y_second = lax.ppermute(to_second, ("y", "z"), [(gy, ((gy + 1) ^ 1) - 1) for gy in range(1, 31)])
 
@@ -354,17 +391,18 @@
     x_sibling = lax.ppermute(relayed(to_sibling, 1 - core), "c", [(0, 1), (1, 0)])
     halos = (y_first, y_second, x_sibling, x_outer)
     outputs, input_grad, send, keep = convolve(
-        fill_layers, SLOTS, place, dst, features, cotangent, halos, flipped, weights
+        fill_layers, SLOTS, place, dst, own_f, own_c, halos, flipped, weights
     )
-    own, other = sum_everywhere(send, keep)
+    own, other, input_grad = sum_everywhere(send, keep, input_grad)
 
     def with_whole_bricks(results):
         packets = pack_bricks(recv_slot, features, cotangent)
         halos = [pass_to(packet, -heading[0], -heading[1]) for packet, heading in zip(packets, DIRECTIONS)]
         outputs, input_grad, send, keep = convolve(
-            fill_bricks, 1, place, dst, features, cotangent, halos, flipped, weights
+            fill_bricks, 1, place, dst, own_f, own_c, halos, flipped, weights
         )
-        return outputs, input_grad, spread_out(first, *sum_everywhere(send, keep))
+        own, other, input_grad = sum_everywhere(send, keep, input_grad)
+        return outputs, input_grad, spread_out(first, own, other)
 
     def as_they_are(results):
         outputs, input_grad, own, other = results

time: 81.3 us -> 80.3 us (0.988)
  waiting for transfers between devices: 6.41 us -> 4.55 us
  blocking collectives: 49 us -> 47.9 us
  Pallas kernels: 9.01 us -> 10 us
  local copies, waits for them, and re-layouts: 1.66 us -> 0.77 us
    ppermute x1, waiting for transfers between devices: 1.81 us -> 0.04 us  [sum_everywhere(): arrived = lax.ppermute(send, 'c', [(0, 1), (1, 0)])]
    all_to_all x1, blocking collectives: 12.8 us -> 11.7 us  [sum_everywhere(): lax.all_to_all(whole, ('x', 'y'), 0, 0).reshape(4, ROWS_M, 16, CHANNELS)]
    pallas_call x2 -> x4, Pallas kernels: 7.72 us -> 8.73 us  [the longest x1 3.06 us: convolve(): pl.pallas_call(functools.partial(output_kernel, fill, unroll, len(halos))...]
    reshape x1, local copies, waits for them, and re-layouts: 1.01 us -> 0.11 us  [local(): flipped = jnp.transpose(own_f[:SLOTS].reshape(SLOTS * VOXELS, CHANNELS))]
  transfers between devices with their start and end apart: 6 -> 6, of which waited for: 4 -> 2; matrix products, arithmetic and copies ran while one was open for 2% -> 2% of each run, Pallas kernels for 0% -> 6%
where the time goes in v7:
time: 80.3 us; the launch traced here: 80 us
  blocking collectives  47.9 us (60%)
  starting transfers between devices  13.7 us (17%)
  Pallas kernels  10 us (12%)
  waiting for transfers between devices  4.55 us (6%)
  between operations  1.69 us (2%)
  other arithmetic  1.13 us (1%)
    all_to_all x1, blocking collectives, sum_everywhere(): parts = lax.all_to_all(parts, ('x', 'y'), 0, 0)  21.3 us
    all_to_all x1, blocking collectives, sum_everywhere(): lax.all_to_all(jnp.broadcast_to(share[None], (8,) + share.shape), 'z', 0, 0)  14.9 us
    all_to_all x1, blocking collectives, sum_everywhere(): lax.all_to_all(whole, ('x', 'y'), 0, 0).reshape(4, ROWS_M, 16, CHANNELS)  11.7 us
    ppermute x1, starting transfers between devices, sum_everywhere(): return (own, lax.ppermute(own, 'c', [(0, 1), (1, 0)]), grad)  5 us
    ppermute x1, starting transfers between devices, local(): lax.ppermute(relayed(to_sibling, 1 - core), 'c', [(0, 1), (1, 0)])  3.47 us
    ppermute x1, waiting for transfers between devices, local(): lax.ppermute(relayed(to_outer, core), ('x', 'c'), [(2 * x + 1, 2 * x + 2)...  3.16 us
    pallas_call x1, Pallas kernels, convolve(): pl.pallas_call(functools.partial(output_kernel, fill, unroll, len(halos))...  3.06 us
    ppermute x1, starting transfers between devices, local(): lax.ppermute(to_first, ('y', 'z'), [(gy, gy ^ 1) for gy in range(32)])  2.55 us
  transfers between devices with their start and end apart: 6, of which 2 were waited for; matrix products, arithmetic and copies ran while one was open for 2% of the time, Pallas kernels for 6%

profile of v7, /device:TPU:1, one launch (start us, length us, event | category | flops | bytes accessed | tf_op | source)
XLA Modules:
  0.0 80.0 jit_solution(10348080380152303609)
XLA Ops:
  0.6 0.1 pad_add_fusion.place_ref
  0.7 1.8 %shard_map.78 = (bf16[12,16,256]{2,1,0:T(8,128)(2,1)S(1)}, bf16[12,16,256]{2,1,0:T(8,128)(2,1)S(1)}, bf16[8,16,256]{2,1,0:T(8,128)(2,1)S(1)}, bf16[8,16,256]{2,1...) custom-call(s32[2]{0:T(128)S(1)} %pad_add_fusion.place_ref, s32[40]{0:T(128)} %recv_slot_ref.1, ...), custom_call_target="tpu_custom_call" | custom-call | tf_op jit(solution)/shard_map/pallas_call | solution.py:106
  2.5 2.5 %collective-permute-start.10 = (bf16[12,16,256]{2,1,0:T(8,128)(2,1)S(1)}, bf16[12,16,256]{2,1,0:T(8,128)(2,1)S(1)}, u32[]{:S(2)}, u32[]{:S(2)}) collective-permute-start(bf16[12,16,256]{2,1,0:T(8,128)(2,1)S(1)} %get-tuple-element.73), channel_id=1, source_target_pairs={{0,1},{1,0},{2,3},{3,2},{4,5},{5,4},{6,7},{7,6},{8,9},{9,8},{10,11... | collective-permute-start | bytes 294920 | tf_op jit(solution)/shard_map/ppermute | solution.py:382
  5.1 0.7 collective-permute-start.11
  5.8 1.3 %collective-permute-done.10.rest_0_ = bf16[12,16,256]{2,1,0:T(8,128)(2,1)S(1)} collective-permute-done((bf16[12,16,256]{2,1,0:T(8,128)(2,1)S(1)}, bf16[12,16,256]{2,1,0:T(8,128)(2,1)S(1)}, u32[]{:S(2)}, u32[]{:S(2)}) %collective-permute-start.10) | collective-permute-done | bytes 98336 | tf_op jit(solution)/shard_map/ppermute | solution.py:382
  7.1 0.0 collective-permute-done.11.rest_1_
  7.1 3.5 %collective-permute-start.12 = (bf16[12,16,256]{2,1,0:T(8,128)(2,1)S(1)}, bf16[12,16,256]{2,1,0:T(8,128)(2,1)S(1)}, u32[]{:S(2)}, u32[]{:S(2)}) collective-permute-start(bf16[12,16,256]{2,1,0:T(8,128)(2,1)S(1)} %pad_maximum_fusion.1), channel_id=1, source_target_pairs={{0,32},{32,0},{1,33},{33,1},{2,34},{34,2},{3,35},{35,3},{4,36},{36... | collective-permute-start | bytes 294920 | tf_op jit(solution)/shard_map/ppermute | solution.py:391
  10.6 1.9 %collective-permute-start.13 = (bf16[12,16,256]{2,1,0:T(8,128)(2,1)S(1)}, bf16[12,16,256]{2,1,0:T(8,128)(2,1)S(1)}, u32[]{:S(2)}, u32[]{:S(2)}) collective-permute-start(bf16[12,16,256]{2,1,0:T(8,128)(2,1)S(1)} %pad_maximum_fusion.2), channel_id=1, source_target_pairs={{32,64},{96,128},{160,192},{64,32},{128,96},{192,160},{33,65},{97,... | collective-permute-start | bytes 294920 | tf_op jit(solution)/shard_map/ppermute | solution.py:389
  12.5 0.7 clamp_bitcast_fusion.dst_ref.table_ref
  13.3 0.0 copy-start.3
  13.3 0.1 copy.11
  13.4 0.0 collective-permute-done.12.rest_2_
  13.4 3.2 %collective-permute-done.13.rest_3_ = bf16[12,16,256]{2,1,0:T(8,128)(2,1)S(1)} collective-permute-done((bf16[12,16,256]{2,1,0:T(8,128)(2,1)S(1)}, bf16[12,16,256]{2,1,0:T(8,128)(2,1)S(1)}, u32[]{:S(2)}, u32[]{:S(2)}) %collective-permute-start.13) | collective-permute-done | bytes 98336 | tf_op jit(solution)/shard_map/ppermute | solution.py:389
  16.6 2.1 %shard_map.79 = (bf16[4,28,16,128]{3,2,1,0:T(8,128)(2,1)S(1)}, f32[4,28,16,128]{3,2,1,0:T(8,128)S(1)}, bf16[8,6,16,1152]{3,2,1,0:T(8,128)(2,1)S(1)}) custom-call(s32[2]{0:T(128)S(1)} %pad_add_fusion.place_ref, s32[8,27]{1,0:T(8,128)S(1)} %clamp_bitcast_fusion.dst_ref.table_ref, s32[8,27]{1,0:T(8,128)S(1)} %clamp_bitcast_fusion.dst_ref.table_ref, ...), custom_call_target="tpu_custom_call" | custom-call | flops 905969664 | bytes 4000000 | tf_op jit(solution)/shard_map/pallas_call | solution.py:249
  18.7 0.1 collective-permute-start.14
  18.8 0.0 copy-done.3
  18.8 1.8 %shard_map.80 = bf16[8,64,128]{2,1,0:T(8,128)(2,1)} custom-call(bf16[8,6,16,1152]{3,2,1,0:T(8,128)(2,1)S(1)} %get-tuple-element.80.taps, bf16[27,128,128]{2,1,0:T(8,128)(2,1)S(1)} %copy-done.3), custom_call_target="tpu_custom_call" | custom-call | flops 905969664 | bytes 4000000 | tf_op jit(solution)/shard_map/pallas_call | solution.py:262
  20.5 0.0 collective-permute-done.14
  20.6 0.1 add_convert_fusion.1
  20.7 21.3 %all_to_all.30 = bf16[16,7,16,128]{3,2,1,0:T(8,128)(2,1)S(1)} all-to-all(bf16[16,7,16,128]{3,2,1,0:T(8,128)(2,1)S(1)} %bitcast.19), channel_id=1, replica_groups=mesh['x'=4,'c'=2,'y'=4,'z'=8] {'x','y'}, dimensions={0} | all-to-all | bytes 917504 | tf_op jit(solution)/shard_map/all_to_all | solution.py:328
  42.0 0.1 convert_reduce_fusion.1
  42.2 14.9 %all_to_all.31 = f16[8,8,16,128]{3,2,1,0:T(8,128)(2,1)S(1)} all-to-all(f16[8,8,16,128]{3,2,1,0:T(8,128)(2,1)S(1)} %broadcast_in_dim.13), channel_id=1, replica_groups=mesh['x'=4,'c'=2,'y'=4,'z'=8] {'z'}, dimensions={0} | all-to-all | bytes 524288 | tf_op jit(solution)/shard_map/all_to_all | solution.py:334
  57.2 0.1 broadcast_in_dim.14
  57.3 11.7 %all_to_all.32 = bf16[16,7,16,128]{3,2,1,0:T(8,128)(2,1)S(1)} all-to-all(bf16[16,7,16,128]{3,2,1,0:T(8,128)(2,1)S(1)} %broadcast_in_dim.14), channel_id=1, replica_groups=mesh['x'=4,'c'=2,'y'=4,'z'=8] {'x','y'}, dimensions={0} | all-to-all | bytes 917504 | tf_op jit(solution)/shard_map/all_to_all | solution.py:338
  69.0 0.0 copy-start
  69.0 0.0 copy-start.1
  69.0 0.0 copy-start.2
  69.0 5.0 %collective-permute-start.15 = (bf16[4,28,16,128]{3,2,1,0:T(8,128)(2,1)S(1)}, bf16[4,28,16,128]{3,2,1,0:T(8,128)(2,1)S(1)}, u32[]{:S(2)}, u32[]{:S(2)}) collective-permute-start(bf16[4,28,16,128]{3,2,1,0:T(8,128)(2,1)S(1)} %bitcast.21), channel_id=1, source_target_pairs={{0,32},{32,0},{1,33},{33,1},{2,34},{34,2},{3,35},{35,3},{4,36},{36... | collective-permute-start | bytes 1376264 | tf_op jit(solution)/shard_map/ppermute | solution.py:339
  74.0 3.1 %shard_map.81 = bf16[8,64,128]{2,1,0:T(8,128)(2,1)} custom-call(s32[2]{0:T(128)S(1)} %pad_add_fusion.place_ref, s32[8,27]{1,0:T(8,128)S(1)} %clamp_bitcast_fusion.dst_ref.table_ref, bf16[9,64,128]{2,1,0:T(8,128)(2,1)S(1)} %get-tuple-element.77.features_ref, bf16[12,16,256]{2,1,0:T(8,128)(2,1)S(1)} %collective-permute-done.10.rest_0_, ...), custom_call_target="tpu_custom_call" | custom-call | flops 905969664 | bytes 4000000 | tf_op jit(solution)/shard_map/pallas_call | solution.py:270
  77.1 0.5 slice.26
  78.2 0.0 collective-permute-done.15
  78.2 0.0 copy-done
  78.3 0.0 copy-done.1
  78.3 0.0 copy-done.2
  78.3 1.5 %conditional.1 = (bf16[8,64,128]{2,1,0:T(8,128)(2,1)}, bf16[8,64,128]{2,1,0:T(8,128)(2,1)}, f32[27,128,128]{2,1,0:T(8,128)}) conditional(s32[]{:T(128)} %bitcast.12, (s32[1]{0:T(128)}, bf16[4,28,16,128]{3,2,1,0:T(8,128)(2,1)S(1)}, bf16[4,28,16,128]{3,2,1,0:T(8,128)(2,1)S(1)}, bf16[8,64,128]{2,1,0:T(8,128)(2,1)}, ...), branch_computations={%region_3.4_spmd, %region_4.8_spmd} | conditional | flops 2719523840 | bytes 28206760 | solution.py:411
  78.3 1.3 %branch_0_fun.1 = f32[27,128,128]{2,1,0:T(8,128)} custom-call(s32[1]{0:T(128)} %get-tuple-element.32.core_ref, bf16[4,28,16,128]{3,2,1,0:T(8,128)(2,1)S(1)} %get-tuple-element.33.own_ref, bf16[4,28,16,128]{3,2,1,0:T(8,128)(2,1)S(1)} %get-tuple-element.34.other_ref), custom_call_target="tpu_custom_call" | custom-call | tf_op jit(solution)/shard_map/cond/branch_0_fun/pallas_call | solution.py:361
  (15 shorter events, 0.3 us)
Async XLA Ops:
  2.5 4.6 %collective-permute-start.10 = (bf16[12,16,256]{2,1,0:T(8,128)(2,1)S(1)}, bf16[12,16,256]{2,1,0:T(8,128)(2,1)S(1)}, u32[]{:S(2)}, u32[]{:S(2)}) collective-permute-start(bf16[12,16,256]{2,1,0:T(8,128)(2,1)S(1)} %get-tuple-element.73), channel_id=1, source_target_pairs={{0,1},{1,0},{2,3},{3,2},{4,5},{5,4},{6,7},{7,6},{8,9},{9,8},{10,11... | collective-permute-start | bytes 294920 | tf_op jit(solution)/shard_map/ppermute | solution.py:382
  5.1 2.0 %collective-permute-start.11 = (bf16[12,16,256]{2,1,0:T(8,128)(2,1)S(1)}, bf16[12,16,256]{2,1,0:T(8,128)(2,1)S(1)}, u32[]{:S(2)}, u32[]{:S(2)}) collective-permute-start(bf16[12,16,256]{2,1,0:T(8,128)(2,1)S(1)} %get-tuple-element.74), channel_id=1, source_target_pairs={{1,2},{2,1},{3,4},{4,3},{5,6},{6,5},{7,8},{8,7},{9,10},{10,9},{11,... | collective-permute-start | bytes 294920 | tf_op jit(solution)/shard_map/ppermute | solution.py:383
  7.1 6.3 %collective-permute-start.12 = (bf16[12,16,256]{2,1,0:T(8,128)(2,1)S(1)}, bf16[12,16,256]{2,1,0:T(8,128)(2,1)S(1)}, u32[]{:S(2)}, u32[]{:S(2)}) collective-permute-start(bf16[12,16,256]{2,1,0:T(8,128)(2,1)S(1)} %pad_maximum_fusion.1), channel_id=1, source_target_pairs={{0,32},{32,0},{1,33},{33,1},{2,34},{34,2},{3,35},{35,3},{4,36},{36... | collective-permute-start | bytes 294920 | tf_op jit(solution)/shard_map/ppermute | solution.py:391
  10.6 5.9 %collective-permute-start.13 = (bf16[12,16,256]{2,1,0:T(8,128)(2,1)S(1)}, bf16[12,16,256]{2,1,0:T(8,128)(2,1)S(1)}, u32[]{:S(2)}, u32[]{:S(2)}) collective-permute-start(bf16[12,16,256]{2,1,0:T(8,128)(2,1)S(1)} %pad_maximum_fusion.2), channel_id=1, source_target_pairs={{32,64},{96,128},{160,192},{64,32},{128,96},{192,160},{33,65},{97,... | collective-permute-start | bytes 294920 | tf_op jit(solution)/shard_map/ppermute | solution.py:389
  13.3 5.5 %copy-start.3 = (bf16[27,128,128]{2,1,0:T(8,128)(2,1)S(1)}, bf16[27,128,128]{2,1,0:T(8,128)(2,1)}, u32[]{:S(2)}) copy-start(bf16[27,128,128]{2,1,0:T(8,128)(2,1)} %rest_4_.1) | copy-start | bytes 2654212
  18.7 1.9 %collective-permute-start.14 = (bf16[4,28,16,128]{3,2,1,0:T(8,128)(2,1)S(1)}, bf16[4,28,16,128]{3,2,1,0:T(8,128)(2,1)S(1)}, u32[]{:S(2)}, u32[]{:S(2)}) collective-permute-start(bf16[4,28,16,128]{3,2,1,0:T(8,128)(2,1)S(1)} %get-tuple-element.79), channel_id=1, source_target_pairs={{0,32},{32,0},{1,33},{33,1},{2,34},{34,2},{3,35},{35,3},{4,36},{36... | collective-permute-start | bytes 1376264 | tf_op jit(solution)/shard_map/ppermute | solution.py:324
  69.0 9.3 %copy-start = (bf16[8,64,128]{2,1,0:T(8,128)(2,1)S(1)}, bf16[8,64,128]{2,1,0:T(8,128)(2,1)}, u32[]{:S(2)}) copy-start(bf16[8,64,128]{2,1,0:T(8,128)(2,1)} %features_ref.1) | copy-start | bytes 393220
  69.0 9.3 %copy-start.1 = (bf16[8,64,128]{2,1,0:T(8,128)(2,1)S(1)}, bf16[8,64,128]{2,1,0:T(8,128)(2,1)}, u32[]{:S(2)}) copy-start(bf16[8,64,128]{2,1,0:T(8,128)(2,1)} %cotangent_ref.1) | copy-start | bytes 393220
  69.0 9.3 %copy-start.2 = (s32[40]{0:T(128)S(1)}, s32[40]{0:T(128)}, u32[]{:S(2)}) copy-start(s32[40]{0:T(128)} %recv_slot_ref.1) | copy-start | bytes 484
  69.0 9.2 %collective-permute-start.15 = (bf16[4,28,16,128]{3,2,1,0:T(8,128)(2,1)S(1)}, bf16[4,28,16,128]{3,2,1,0:T(8,128)(2,1)S(1)}, u32[]{:S(2)}, u32[]{:S(2)}) collective-permute-start(bf16[4,28,16,128]{3,2,1,0:T(8,128)(2,1)S(1)} %bitcast.21), channel_id=1, source_target_pairs={{0,32},{32,0},{1,33},{33,1},{2,34},{34,2},{3,35},{35,3},{4,36},{36... | collective-permute-start | bytes 1376264 | tf_op jit(solution)/shard_map/ppermute | solution.py:339

commit v8 on v7

--- a/solution.py
+++ b/solution.py
@@ -53,7 +53,7 @@
     return where_equal(row, (column >> 2) * PLANE + side * 12 + (column & 3))
 
 
-def pack_layers_kernel(place_ref, recv_slot_ref, features_ref, cotangent_ref, to_first, to_second, to_sibling, to_outer,
+def pack_layers_kernel(recv_slot_ref, features_ref, cotangent_ref, to_first, to_second, to_sibling, to_outer,
                        own_f, own_c, sides, slot_ref, sems):
     bricks = (own_f, own_c)
     copies = [
@@ -69,8 +69,8 @@
     for own in bricks:
         own[SLOTS] = jnp.zeros((VOXELS, CHANNELS), jnp.bfloat16)
     sides[:, SLOTS] = jnp.zeros((2, 2 * PLANE, CHANNELS), jnp.bfloat16)
-    core = place_ref[0]
-    odd = place_ref[1]
+    core = lax.axis_index("c")
+    odd = lax.axis_index("z") & 1
     layer = layer_matrix()
     for copy in copies:
         copy.wait()
@@ -99,13 +99,12 @@
             put(packet, position, up * LENGTHS[0] + position, bricks, begin)
 
 
-def pack_layers(place, recv_slot, features, cotangent):
+def pack_layers(recv_slot, features, cotangent):
     vmem = pl.BlockSpec(memory_space=pltpu.VMEM)
-    smem = pl.BlockSpec(memory_space=pltpu.SMEM)
     hbm = pl.BlockSpec(memory_space=pltpu.HBM)
     return pl.pallas_call(
         pack_layers_kernel,
-        in_specs=[smem, hbm, hbm, hbm],
+        in_specs=[hbm, hbm, hbm],
         out_specs=[vmem] * 6,
         out_shape=[
             jax.ShapeDtypeStruct((length, PLANE, 2 * CHANNELS), jnp.bfloat16) for length in (12, 12, 8, 8)
@@ -116,7 +115,7 @@
             pltpu.SemaphoreType.DMA((3,)),
         ],
         compiler_params=pltpu.CompilerParams(vmem_limit_bytes=VMEM_LIMIT),
-    )(place, recv_slot, features, cotangent)
+    )(recv_slot, features, cotangent)
 
 
 def fill_bricks(core, odd, halos, lanes, bricks):
@@ -164,9 +163,9 @@
     return jnp.max(jnp.max(wrong, axis=1, keepdims=True), axis=0, keepdims=True)
 
 
-def build_taps(fill, unroll, place_ref, dst_ref, own_ref, halos, lanes, bricks, taps):
+def build_taps(fill, unroll, dst_ref, own_ref, halos, lanes, bricks, taps):
     bricks[:SLOTS] = own_ref[:SLOTS]
-    fill(place_ref[0], place_ref[1], halos, lanes, bricks)
+    fill(lax.axis_index("c"), lax.axis_index("z") & 1, halos, lanes, bricks)
     bricks[SLOTS + HALO] = jnp.zeros((VOXELS, CHANNELS), jnp.bfloat16)
     shift = shift_matrix()
 
@@ -191,11 +190,11 @@
     lax.fori_loop(0, SLOTS, one_slot, 0, unroll=unroll)
 
 
-def weight_kernel(fill, unroll, count, place_ref, dst_ref, table_ref, cotangent_ref, *rest):
+def weight_kernel(fill, unroll, count, dst_ref, table_ref, cotangent_ref, *rest):
     halos = rest[:count]
     flipped_ref, send_ref, keep_ref, taps, bricks = rest[count:]
-    build_taps(fill, unroll, place_ref, dst_ref, cotangent_ref, halos, slice(CHANNELS, 2 * CHANNELS), bricks, taps)
-    core = place_ref[0]
+    build_taps(fill, unroll, dst_ref, cotangent_ref, halos, slice(CHANNELS, 2 * CHANNELS), bricks, taps)
+    core = lax.axis_index("c")
     flipped = jnp.concatenate((flipped_ref[1 - core], flipped_ref[core]), axis=0)
     half = CHANNELS // 2
     for side in range(3):
@@ -224,10 +223,12 @@
     grad_ref[...] = grad.astype(jnp.bfloat16).reshape(SLOTS, VOXELS, CHANNELS)
 
 
-def output_kernel(fill, unroll, count, place_ref, dst_ref, features_ref, *rest):
-    halos = rest[:count]
-    weights_ref, outputs_ref, bricks, taps = rest[count:]
-    build_taps(fill, unroll, place_ref, dst_ref, features_ref, halos, slice(0, CHANNELS), bricks, taps)
+def taps_kernel(fill, unroll, count, dst_ref, features_ref, *rest):
+    taps, bricks = rest[count:]
+    build_taps(fill, unroll, dst_ref, features_ref, rest[:count], slice(0, CHANNELS), bricks, taps)
+
+
+def output_kernel(taps, weights_ref, outputs_ref):
     outputs = None
     for side in range(3):
         tap = taps[:, side : side + BRICK].reshape(SLOTS * VOXELS, WIDE)
@@ -237,46 +238,64 @@
     outputs_ref[...] = outputs.astype(jnp.bfloat16).reshape(SLOTS, VOXELS, CHANNELS)
 
 
-def convolve(fill, unroll, place, dst, own_f, own_c, halos, flipped, weights):
-    vmem = pl.BlockSpec(memory_space=pltpu.VMEM)
-    smem = pl.BlockSpec(memory_space=pltpu.SMEM)
-    brick = jax.ShapeDtypeStruct((SLOTS, VOXELS, CHANNELS), jnp.bfloat16)
-    taps = (SLOTS, PLANES, PLANE, WIDE)
-    bricks = pltpu.VMEM((SLOTS + HALO + 1, VOXELS, CHANNELS), jnp.bfloat16)
-    params = pltpu.CompilerParams(vmem_limit_bytes=VMEM_LIMIT)
-    flops = 2 * SLOTS * VOXELS * 27 * CHANNELS * CHANNELS
-    cost = pl.CostEstimate(flops=2 * flops, bytes_accessed=4_000_000, transcendentals=0)
-    send, keep, taps_c = pl.pallas_call(
+VMEM_SPEC = pl.BlockSpec(memory_space=pltpu.VMEM)
+SMEM_SPEC = pl.BlockSpec(memory_space=pltpu.SMEM)
+BRICK_SHAPE = jax.ShapeDtypeStruct((SLOTS, VOXELS, CHANNELS), jnp.bfloat16)
+TAPS_SHAPE = jax.ShapeDtypeStruct((SLOTS, PLANES, PLANE, WIDE), jnp.bfloat16)
+ALL_BRICKS = pltpu.VMEM((SLOTS + HALO + 1, VOXELS, CHANNELS), jnp.bfloat16)
+PARAMS = pltpu.CompilerParams(vmem_limit_bytes=VMEM_LIMIT)
+COST = pl.CostEstimate(flops=4 * SLOTS * VOXELS * 27 * CHANNELS * CHANNELS, bytes_accessed=4_000_000, transcendentals=0)
+
+
+def weight_sums(fill, unroll, dst, own_c, halos, flipped):
+    return pl.pallas_call(
         functools.partial(weight_kernel, fill, unroll, len(halos)),
-        in_specs=[smem, smem] + [vmem] * (3 + len(halos)),
-        out_specs=[vmem] * 3,
+        in_specs=[SMEM_SPEC] + [VMEM_SPEC] * (3 + len(halos)),
+        out_specs=[VMEM_SPEC] * 3,
         out_shape=[
             jax.ShapeDtypeStruct((4, ROWS_M, 16, CHANNELS), jnp.bfloat16),
             jax.ShapeDtypeStruct((4, ROWS_M, 16, CHANNELS), jnp.float32),
-            jax.ShapeDtypeStruct(taps, jnp.bfloat16),
+            TAPS_SHAPE,
         ],
-        scratch_shapes=[bricks],
-        compiler_params=params,
-        cost_estimate=cost,
-    )(place, dst, dst, own_c, *halos, flipped)
-    grad = pl.pallas_call(
-        grad_kernel,
-        in_specs=[vmem, vmem],
-        out_specs=vmem,
-        out_shape=brick,
-        compiler_params=params,
-        cost_estimate=cost,
-    )(taps_c, weights)
-    outputs = pl.pallas_call(
-        functools.partial(output_kernel, fill, unroll, len(halos)),
-        in_specs=[smem, smem] + [vmem] * (2 + len(halos)),
-        out_specs=vmem,
-        out_shape=brick,
-        scratch_shapes=[bricks, pltpu.VMEM(taps, jnp.bfloat16)],
-        compiler_params=params,
-        cost_estimate=cost,
-    )(place, dst, own_f, *halos, weights)
-    return outputs, grad, send, keep
+        scratch_shapes=[ALL_BRICKS],
+        compiler_params=PARAMS,
+        cost_estimate=COST,
+    )(dst, dst, own_c, *halos, flipped)
+
+
+def feature_taps(fill, unroll, dst, own_f, halos):
+    return pl.pallas_call(
+        functools.partial(taps_kernel, fill, unroll, len(halos)),
+        in_specs=[SMEM_SPEC] + [VMEM_SPEC] * (1 + len(halos)),
+        out_specs=VMEM_SPEC,
+        out_shape=TAPS_SHAPE,
+        scratch_shapes=[ALL_BRICKS],
+        compiler_params=PARAMS,
+        cost_estimate=COST,
+    )(dst, own_f, *halos)
+
+
+def product(kernel, taps, weights):
+    return pl.pallas_call(
+        kernel,
+        in_specs=[VMEM_SPEC] * 2,
+        out_specs=VMEM_SPEC,
+        out_shape=BRICK_SHAPE,
+        compiler_params=PARAMS,
+        cost_estimate=COST,
+    )(taps, weights)
+
+
+def convolve(fill, unroll, dst, own_f, own_c, halos, flipped, weights):
+    send, keep, taps_c = weight_sums(fill, unroll, dst, own_c, halos, flipped)
+    arrived = lax.ppermute(send, "c", [(0, 1), (1, 0)])
+    input_grad = product(grad_kernel, taps_c, weights)
+    taps_f = feature_taps(fill, unroll, dst, own_f, halos)
+    arrived, input_grad, taps_f = lax.optimization_barrier((arrived, input_grad, taps_f))
+    own = sum_everywhere(arrived, keep)
+    other = lax.ppermute(own, "c", [(0, 1), (1, 0)])
+    outputs = product(output_kernel, taps_f, weights)
+    return outputs, input_grad, own, other
 
 
 def pack_bricks_kernel(slot_ref, features_ref, cotangent_ref, *packets):
@@ -320,9 +339,7 @@
     return lax.ppermute(value, AXES, pairs)
 
 
-def sum_everywhere(send, keep, grad):
-    arrived = lax.ppermute(send, "c", [(0, 1), (1, 0)])
-    arrived, grad = lax.optimization_barrier((arrived, grad))
+def sum_everywhere(arrived, keep):
     chip_sum = (keep + arrived.astype(jnp.float32)).astype(jnp.bfloat16)
     parts = chip_sum.reshape(16, 7, 16, CHANNELS)
     parts = lax.all_to_all(parts, ("x", "y"), 0, 0)
@@ -335,14 +352,18 @@
     total = jnp.sum(column[:, :7] * jnp.exp2(column[:, 7:] - 14.0), axis=0)
     share = (total * (1.0 / (VOXELS * SLOTS))).astype(jnp.bfloat16)
     whole = jnp.broadcast_to(share[None], (16,) + share.shape)
-    own = lax.all_to_all(whole, ("x", "y"), 0, 0).reshape(4, ROWS_M, 16, CHANNELS)
-    return own, lax.ppermute(own, "c", [(0, 1), (1, 0)]), grad
-
-
-def spread_kernel(core_ref, own_ref, other_ref, out_ref, whole, sems):
+    return lax.all_to_all(whole, ("x", "y"), 0, 0).reshape(4, ROWS_M, 16, CHANNELS)
+
+
+def spread_kernel(own_ref, other_ref, outputs_ref, grad_ref, outputs_out, grad_out, out_ref, whole, sems):
     half = CHANNELS // 2
-    core = core_ref[0]
-    copies = []
+    core = lax.axis_index("c")
+    copies = [
+        pltpu.make_async_copy(outputs_ref, outputs_out, sems.at[9]),
+        pltpu.make_async_copy(grad_ref, grad_out, sems.at[10]),
+    ]
+    for copy in copies:
+        copy.start()
     for chunk in range(9):
         for m in range(3 * chunk, 3 * chunk + 3):
             for quarter in range(4):
@@ -356,27 +377,25 @@
         copy.wait()
 
 
-def spread_out(core, own, other):
-    vmem = pl.BlockSpec(memory_space=pltpu.VMEM)
+def spread_out(outputs, input_grad, own, other):
     return pl.pallas_call(
         spread_kernel,
-        in_specs=[pl.BlockSpec(memory_space=pltpu.SMEM), vmem, vmem],
-        out_specs=pl.BlockSpec(memory_space=pltpu.HBM),
-        out_shape=jax.ShapeDtypeStruct((27, CHANNELS, CHANNELS), jnp.float32),
+        in_specs=[VMEM_SPEC] * 4,
+        out_specs=[pl.BlockSpec(memory_space=pltpu.HBM)] * 3,
+        out_shape=[BRICK_SHAPE, BRICK_SHAPE, jax.ShapeDtypeStruct((27, CHANNELS, CHANNELS), jnp.float32)],
         scratch_shapes=[
             pltpu.VMEM((27, CHANNELS, CHANNELS), jnp.float32),
-            pltpu.SemaphoreType.DMA((9,)),
+            pltpu.SemaphoreType.DMA((11,)),
         ],
-        compiler_params=pltpu.CompilerParams(vmem_limit_bytes=VMEM_LIMIT),
-    )(core, own, other)
+        compiler_params=PARAMS,
+    )(own, other, outputs, input_grad)
 
 
 def local(features, weights, cotangent, dst_index, recv_slot):
-    core = lax.axis_index("c").astype(jnp.int32)
-    first = core.reshape(1)
-    place = jnp.stack((core, (lax.axis_index("z") % 2).astype(jnp.int32)))
+    core = lax.axis_index("c")
     dst = jnp.clip(dst_index.T, 0, SLOTS + HALO)
-    to_first, to_second, to_sibling, to_outer, own_f, own_c = pack_layers(place, recv_slot, features, cotangent)
+
+    to_first, to_second, to_sibling, to_outer, own_f, own_c = pack_layers(recv_slot, features, cotangent)
     flipped = jnp.transpose(own_f[:SLOTS].reshape(SLOTS * VOXELS, CHANNELS))
     flipped = flipped.reshape(2, CHANNELS // 2, SLOTS * VOXELS)
     y_first = lax.ppermute(to_first, ("y", "z"), [(gy, gy ^ 1) for gy in range(32)])
@@ -390,27 +409,18 @@
                            + [(2 * x + 2, 2 * x + 1) for x in range(3)])
     x_sibling = lax.ppermute(relayed(to_sibling, 1 - core), "c", [(0, 1), (1, 0)])
     halos = (y_first, y_second, x_sibling, x_outer)
-    outputs, input_grad, send, keep = convolve(
-        fill_layers, SLOTS, place, dst, own_f, own_c, halos, flipped, weights
-    )
-    own, other, input_grad = sum_everywhere(send, keep, input_grad)
+    results = convolve(fill_layers, SLOTS, dst, own_f, own_c, halos, flipped, weights)
 
     def with_whole_bricks(results):
         packets = pack_bricks(recv_slot, features, cotangent)
         halos = [pass_to(packet, -heading[0], -heading[1]) for packet, heading in zip(packets, DIRECTIONS)]
-        outputs, input_grad, send, keep = convolve(
-            fill_bricks, 1, place, dst, own_f, own_c, halos, flipped, weights
-        )
-        own, other, input_grad = sum_everywhere(send, keep, input_grad)
-        return outputs, input_grad, spread_out(first, own, other)
+        return spread_out(*convolve(fill_bricks, 1, dst, own_f, own_c, halos, flipped, weights))
 
     def as_they_are(results):
-        outputs, input_grad, own, other = results
-        return outputs, input_grad, spread_out(first, own, other)
-
-    return lax.cond(
-        own[0, 27, 0, 0] != 0, with_whole_bricks, as_they_are, (outputs, input_grad, own, other)
-    )
+        return spread_out(*results)
+
+    own = results[2]
+    return tuple(lax.cond(own[0, 27, 0, 0] != 0, with_whole_bricks, as_they_are, results))
 
 
 def solution(mesh):

time: 80.3 us -> 78.8 us (0.981)
  blocking collectives: 47.9 us -> 51.5 us
  waiting for transfers between devices: 4.55 us -> 2.67 us
  Pallas kernels: 10 us -> 8.36 us
  starting transfers between devices: 13.7 us -> 12.3 us
    ppermute x1, starting transfers between devices: 3.47 us -> 0.09 us  [local(): lax.ppermute(relayed(to_sibling, 1 - core), 'c', [(0, 1), (1, 0)])]
    ppermute x1, starting transfers between devices: 1.92 us -> 4.75 us  [local(): lax.ppermute(relayed(to_outer, core), ('x', 'c'), [(2 * x + 1, 2 * x + 2)...]
    all_to_all x1, blocking collectives: 21.3 us -> 23.4 us  [sum_everywhere(): parts = lax.all_to_all(parts, ('x', 'y'), 0, 0)]
    ppermute x1, waiting for transfers between devices: 3.16 us -> 1.32 us  [local(): lax.ppermute(relayed(to_outer, core), ('x', 'c'), [(2 * x + 1, 2 * x + 2)...]
    pallas_call x5 -> x6, Pallas kernels: 10 us -> 8.36 us  [the longest x2 2.17 us: product(): pl.pallas_call(kernel, in_specs=[VMEM_SPEC] * 2, out_specs=VMEM_SPEC, out...]
    all_to_all x1, blocking collectives: 11.7 us -> 13.3 us  [sum_everywhere(): lax.all_to_all(whole, ('x', 'y'), 0, 0).reshape(4, ROWS_M, 16, CHANNELS)]
    ppermute x2, starting transfers between devices: 5.09 us -> 4.24 us  [the longest x1 4.15 us: convolve(): other = lax.ppermute(own, 'c', [(0, 1), (1, 0)])]
  transfers between devices with their start and end apart: 6 -> 6, of which waited for: 2 -> 2; matrix products, arithmetic and copies ran while one was open for 2% -> 2% of each run, Pallas kernels for 6% -> 5%
where the time goes in v8:
time: 78.8 us; the launch traced here: 78.5 us
  blocking collectives  51.5 us (65%)
  starting transfers between devices  12.3 us (16%)
  Pallas kernels  8.36 us (11%)
  waiting for transfers between devices  2.67 us (3%)
  between operations  1.71 us (2%)
  other arithmetic  1.06 us (1%)
    all_to_all x1, blocking collectives, sum_everywhere(): parts = lax.all_to_all(parts, ('x', 'y'), 0, 0)  23.4 us
    all_to_all x1, blocking collectives, sum_everywhere(): lax.all_to_all(jnp.broadcast_to(share[None], (8,) + share.shape), 'z', 0, 0)  14.8 us
    all_to_all x1, blocking collectives, sum_everywhere(): lax.all_to_all(whole, ('x', 'y'), 0, 0).reshape(4, ROWS_M, 16, CHANNELS)  13.3 us
    ppermute x1, starting transfers between devices, local(): lax.ppermute(relayed(to_outer, core), ('x', 'c'), [(2 * x + 1, 2 * x + 2)...  4.75 us
    ppermute x1, starting transfers between devices, convolve(): other = lax.ppermute(own, 'c', [(0, 1), (1, 0)])  4.15 us
    ppermute x1, starting transfers between devices, local(): lax.ppermute(to_first, ('y', 'z'), [(gy, gy ^ 1) for gy in range(32)])  2.55 us
    pallas_call x2, Pallas kernels, product(): pl.pallas_call(kernel, in_specs=[VMEM_SPEC] * 2, out_specs=VMEM_SPEC, out...  2.17 us
    pallas_call x1, Pallas kernels, weight_sums(): pl.pallas_call(functools.partial(weight_kernel, fill, unroll, len(halos))...  2.08 us
  transfers between devices with their start and end apart: 6, of which 2 were waited for; matrix products, arithmetic and copies ran while one was open for 2% of the time, Pallas kernels for 5%

profile of v8, /device:TPU:1, one launch (start us, length us, event | category | flops | bytes accessed | tf_op | source)
XLA Modules:
  0.0 78.5 jit_solution(16909709280993648542)
XLA Ops:
  0.6 1.3 %shard_map.82 = (bf16[12,16,256]{2,1,0:T(8,128)(2,1)S(1)}, bf16[12,16,256]{2,1,0:T(8,128)(2,1)S(1)}, bf16[8,16,256]{2,1,0:T(8,128)(2,1)S(1)}, bf16[8,16,256]{2,1...) custom-call(s32[40]{0:T(128)} %recv_slot_ref.1, bf16[8,64,128]{2,1,0:T(8,128)(2,1)} %features_ref.1, ...), custom_call_target="tpu_custom_call" | custom-call | tf_op jit(solution)/shard_map/pallas_call | solution.py:105
  1.9 2.6 %collective-permute-start.10 = (bf16[12,16,256]{2,1,0:T(8,128)(2,1)S(1)}, bf16[12,16,256]{2,1,0:T(8,128)(2,1)S(1)}, u32[]{:S(2)}, u32[]{:S(2)}) collective-permute-start(bf16[12,16,256]{2,1,0:T(8,128)(2,1)S(1)} %get-tuple-element.66), channel_id=1, source_target_pairs={{0,1},{1,0},{2,3},{3,2},{4,5},{5,4},{6,7},{7,6},{8,9},{9,8},{10,11... | collective-permute-start | bytes 294920 | tf_op jit(solution)/shard_map/ppermute | solution.py:401
  4.5 0.7 collective-permute-start.11
  5.1 1.3 %collective-permute-done.10.rest_0_ = bf16[12,16,256]{2,1,0:T(8,128)(2,1)S(1)} collective-permute-done((bf16[12,16,256]{2,1,0:T(8,128)(2,1)S(1)}, bf16[12,16,256]{2,1,0:T(8,128)(2,1)S(1)}, u32[]{:S(2)}, u32[]{:S(2)}) %collective-permute-start.10) | collective-permute-done | bytes 98336 | tf_op jit(solution)/shard_map/ppermute | solution.py:401
  6.5 0.0 collective-permute-done.11.rest_1_
  6.5 4.7 %collective-permute-start.13 = (bf16[12,16,256]{2,1,0:T(8,128)(2,1)S(1)}, bf16[12,16,256]{2,1,0:T(8,128)(2,1)S(1)}, u32[]{:S(2)}, u32[]{:S(2)}) collective-permute-start(bf16[12,16,256]{2,1,0:T(8,128)(2,1)S(1)} %pad_maximum_fusion.2), channel_id=1, source_target_pairs={{32,64},{96,128},{160,192},{64,32},{128,96},{192,160},{33,65},{97,... | collective-permute-start | bytes 294920 | tf_op jit(solution)/shard_map/ppermute | solution.py:408
  11.3 0.1 collective-permute-start.12
  11.4 0.7 clamp_bitcast_fusion.dst_ref.table_ref
  12.1 0.0 copy-start.3
  12.1 0.1 copy.15
  12.2 1.3 %collective-permute-done.13.rest_3_ = bf16[12,16,256]{2,1,0:T(8,128)(2,1)S(1)} collective-permute-done((bf16[12,16,256]{2,1,0:T(8,128)(2,1)S(1)}, bf16[12,16,256]{2,1,0:T(8,128)(2,1)S(1)}, u32[]{:S(2)}, u32[]{:S(2)}) %collective-permute-start.13) | collective-permute-done | bytes 98336 | tf_op jit(solution)/shard_map/ppermute | solution.py:408
  13.6 0.0 collective-permute-done.12.rest_2_
  13.6 2.1 %shard_map.83 = (bf16[4,28,16,128]{3,2,1,0:T(8,128)(2,1)S(1)}, f32[4,28,16,128]{3,2,1,0:T(8,128)S(1)}, bf16[8,6,16,1152]{3,2,1,0:T(8,128)(2,1)S(1)}) custom-call(s32[8,27]{1,0:T(8,128)S(1)} %clamp_bitcast_fusion.dst_ref.table_ref, s32[8,27]{1,0:T(8,128)S(1)} %clamp_bitcast_fusion.dst_ref.table_ref, bf16[9,64,128]{2,1,0:T(8,128)(2,1)S(1)} %get-tuple-element.65.cotangent_ref, ...), custom_call_target="tpu_custom_call" | custom-call | flops 905969664 | bytes 4000000 | tf_op jit(solution)/shard_map/pallas_call | solution.py:251
  15.6 0.1 collective-permute-start.14
  15.7 0.0 copy-done.3
  15.7 1.1 %shard_map.84 = bf16[8,64,128]{2,1,0:T(8,128)(2,1)S(1)} custom-call(bf16[8,6,16,1152]{3,2,1,0:T(8,128)(2,1)S(1)} %get-tuple-element.73.taps, bf16[27,128,128]{2,1,0:T(8,128)(2,1)S(1)} %copy-done.3), custom_call_target="tpu_custom_call" | custom-call | flops 905969664 | bytes 4000000 | tf_op jit(solution)/shard_map/pallas_call | solution.py:279
  16.8 1.5 %shard_map.85.taps = bf16[8,6,16,1152]{3,2,1,0:T(8,128)(2,1)S(1)} custom-call(s32[8,27]{1,0:T(8,128)S(1)} %clamp_bitcast_fusion.dst_ref.table_ref, bf16[9,64,128]{2,1,0:T(8,128)(2,1)S(1)} %get-tuple-element.70.features_ref, bf16[12,16,256]{2,1,0:T(8,128)(2,1)S(1)} %collective-permute-done.10.rest_0_, ...), custom_call_target="tpu_custom_call" | custom-call | flops 905969664 | bytes 4000000 | tf_op jit(solution)/shard_map/pallas_call | solution.py:267
  18.3 0.0 collective-permute-done.14
  18.3 0.1 add_convert_fusion.1
  18.4 23.4 %all_to_all.30 = bf16[16,7,16,128]{3,2,1,0:T(8,128)(2,1)S(1)} all-to-all(bf16[16,7,16,128]{3,2,1,0:T(8,128)(2,1)S(1)} %bitcast.17), channel_id=1, replica_groups=mesh['x'=4,'c'=2,'y'=4,'z'=8] {'x','y'}, dimensions={0} | all-to-all | bytes 917504 | tf_op jit(solution)/shard_map/all_to_all | solution.py:345
  41.8 0.1 convert_reduce_fusion.1
  42.0 14.8 %all_to_all.31 = f16[8,8,16,128]{3,2,1,0:T(8,128)(2,1)S(1)} all-to-all(f16[8,8,16,128]{3,2,1,0:T(8,128)(2,1)S(1)} %broadcast_in_dim.13), channel_id=1, replica_groups=mesh['x'=4,'c'=2,'y'=4,'z'=8] {'z'}, dimensions={0} | all-to-all | bytes 524288 | tf_op jit(solution)/shard_map/all_to_all | solution.py:351
  57.0 0.1 broadcast_in_dim.14
  57.0 13.3 %all_to_all.32 = bf16[16,7,16,128]{3,2,1,0:T(8,128)(2,1)S(1)} all-to-all(bf16[16,7,16,128]{3,2,1,0:T(8,128)(2,1)S(1)} %broadcast_in_dim.14), channel_id=1, replica_groups=mesh['x'=4,'c'=2,'y'=4,'z'=8] {'x','y'}, dimensions={0} | all-to-all | bytes 917504 | tf_op jit(solution)/shard_map/all_to_all | solution.py:355
  70.3 0.0 copy-start
  70.3 0.0 copy-start.1
  70.3 0.0 copy-start.2
  70.3 4.1 %collective-permute-start.15 = (bf16[4,28,16,128]{3,2,1,0:T(8,128)(2,1)S(1)}, bf16[4,28,16,128]{3,2,1,0:T(8,128)(2,1)S(1)}, u32[]{:S(2)}, u32[]{:S(2)}) collective-permute-start(bf16[4,28,16,128]{3,2,1,0:T(8,128)(2,1)S(1)} %bitcast.19), channel_id=1, source_target_pairs={{0,32},{32,0},{1,33},{33,1},{2,34},{34,2},{3,35},{35,3},{4,36},{36... | collective-permute-start | bytes 1376264 | tf_op jit(solution)/shard_map/ppermute | solution.py:296
  74.4 1.1 %shard_map.86 = bf16[8,64,128]{2,1,0:T(8,128)(2,1)S(1)} custom-call(bf16[8,6,16,1152]{3,2,1,0:T(8,128)(2,1)S(1)} %shard_map.85.taps, bf16[27,128,128]{2,1,0:T(8,128)(2,1)S(1)} %copy-done.3), custom_call_target="tpu_custom_call" | custom-call | flops 905969664 | bytes 4000000 | tf_op jit(solution)/shard_map/pallas_call | solution.py:279
  75.5 0.5 slice.26
  76.7 0.0 collective-permute-done.15
  76.7 0.0 copy-done
  76.7 0.0 copy-done.1
  76.7 0.0 copy-done.2
  76.7 1.6 %conditional.1 = ((bf16[8,64,128]{2,1,0:T(8,128)(2,1)}, bf16[8,64,128]{2,1,0:T(8,128)(2,1)}, f32[27,128,128]{2,1,0:T(8,128)})) conditional(s32[]{:T(128)} %bitcast.10, (bf16[4,28,16,128]{3,2,1,0:T(8,128)(2,1)S(1)}, bf16[4,28,16,128]{3,2,1,0:T(8,128)(2,1)S(1)}, bf16[8,64,128]{2,1,0:T(8,128)(2,1)S(1)}, bf16[8,64,128]{2,1,0:T(8,128)(2,1)S(1)}) %tuple.32, ...), branch_computations={%region_3.4_spmd, %region_4.8_spmd} | conditional | flops 3625493248 | bytes 32206744 | solution.py:423
  76.8 1.4 %branch_0_fun.1 = (bf16[8,64,128]{2,1,0:T(8,128)(2,1)}, bf16[8,64,128]{2,1,0:T(8,128)(2,1)}, f32[27,128,128]{2,1,0:T(8,128)}) custom-call(bf16[4,28,16,128]{3,2,1,0:T(8,128)(2,1)S(1)} %get-tuple-element.24.own_ref, bf16[4,28,16,128]{3,2,1,0:T(8,128)(2,1)S(1)} %get-tuple-element.25.other_ref, bf16[8,64,128]{2,1,0:T(8,128)(2,1)S(1)} %get-tuple-element.26.outputs_ref, ...), custom_call_target="tpu_custom_call" | custom-call | tf_op jit(solution)/shard_map/cond/branch_0_fun/pallas_call | solution.py:381
  (15 shorter events, 0.3 us)
Async XLA Ops:
  1.9 4.6 %collective-permute-start.10 = (bf16[12,16,256]{2,1,0:T(8,128)(2,1)S(1)}, bf16[12,16,256]{2,1,0:T(8,128)(2,1)S(1)}, u32[]{:S(2)}, u32[]{:S(2)}) collective-permute-start(bf16[12,16,256]{2,1,0:T(8,128)(2,1)S(1)} %get-tuple-element.66), channel_id=1, source_target_pairs={{0,1},{1,0},{2,3},{3,2},{4,5},{5,4},{6,7},{7,6},{8,9},{9,8},{10,11... | collective-permute-start | bytes 294920 | tf_op jit(solution)/shard_map/ppermute | solution.py:401
  4.5 2.0 %collective-permute-start.11 = (bf16[12,16,256]{2,1,0:T(8,128)(2,1)S(1)}, bf16[12,16,256]{2,1,0:T(8,128)(2,1)S(1)}, u32[]{:S(2)}, u32[]{:S(2)}) collective-permute-start(bf16[12,16,256]{2,1,0:T(8,128)(2,1)S(1)} %get-tuple-element.67), channel_id=1, source_target_pairs={{1,2},{2,1},{3,4},{4,3},{5,6},{6,5},{7,8},{8,7},{9,10},{10,9},{11,... | collective-permute-start | bytes 294920 | tf_op jit(solution)/shard_map/ppermute | solution.py:402
  6.5 7.0 %collective-permute-start.13 = (bf16[12,16,256]{2,1,0:T(8,128)(2,1)S(1)}, bf16[12,16,256]{2,1,0:T(8,128)(2,1)S(1)}, u32[]{:S(2)}, u32[]{:S(2)}) collective-permute-start(bf16[12,16,256]{2,1,0:T(8,128)(2,1)S(1)} %pad_maximum_fusion.2), channel_id=1, source_target_pairs={{32,64},{96,128},{160,192},{64,32},{128,96},{192,160},{33,65},{97,... | collective-permute-start | bytes 294920 | tf_op jit(solution)/shard_map/ppermute | solution.py:408
  11.3 2.3 %collective-permute-start.12 = (bf16[12,16,256]{2,1,0:T(8,128)(2,1)S(1)}, bf16[12,16,256]{2,1,0:T(8,128)(2,1)S(1)}, u32[]{:S(2)}, u32[]{:S(2)}) collective-permute-start(bf16[12,16,256]{2,1,0:T(8,128)(2,1)S(1)} %pad_maximum_fusion.1), channel_id=1, source_target_pairs={{0,32},{32,0},{1,33},{33,1},{2,34},{34,2},{3,35},{35,3},{4,36},{36... | collective-permute-start | bytes 294920 | tf_op jit(solution)/shard_map/ppermute | solution.py:410
  12.1 3.6 %copy-start.3 = (bf16[27,128,128]{2,1,0:T(8,128)(2,1)S(1)}, bf16[27,128,128]{2,1,0:T(8,128)(2,1)}, u32[]{:S(2)}) copy-start(bf16[27,128,128]{2,1,0:T(8,128)(2,1)} %weights_ref.3) | copy-start | bytes 2654212
  15.6 2.7 %collective-permute-start.14 = (bf16[4,28,16,128]{3,2,1,0:T(8,128)(2,1)S(1)}, bf16[4,28,16,128]{3,2,1,0:T(8,128)(2,1)S(1)}, u32[]{:S(2)}, u32[]{:S(2)}) collective-permute-start(bf16[4,28,16,128]{3,2,1,0:T(8,128)(2,1)S(1)} %get-tuple-element.72), channel_id=1, source_target_pairs={{0,32},{32,0},{1,33},{33,1},{2,34},{34,2},{3,35},{35,3},{4,36},{36... | collective-permute-start | bytes 1376264 | tf_op jit(solution)/shard_map/ppermute | solution.py:291
  70.3 6.4 %copy-start = (bf16[8,64,128]{2,1,0:T(8,128)(2,1)S(1)}, bf16[8,64,128]{2,1,0:T(8,128)(2,1)}, u32[]{:S(2)}) copy-start(bf16[8,64,128]{2,1,0:T(8,128)(2,1)} %features_ref.1) | copy-start | bytes 393220
  70.3 6.4 %copy-start.1 = (bf16[8,64,128]{2,1,0:T(8,128)(2,1)S(1)}, bf16[8,64,128]{2,1,0:T(8,128)(2,1)}, u32[]{:S(2)}) copy-start(bf16[8,64,128]{2,1,0:T(8,128)(2,1)} %cotangent_ref.1) | copy-start | bytes 393220
  70.3 6.4 %copy-start.2 = (s32[40]{0:T(128)S(1)}, s32[40]{0:T(128)}, u32[]{:S(2)}) copy-start(s32[40]{0:T(128)} %recv_slot_ref.1) | copy-start | bytes 484
  70.3 6.4 %collective-permute-start.15 = (bf16[4,28,16,128]{3,2,1,0:T(8,128)(2,1)S(1)}, bf16[4,28,16,128]{3,2,1,0:T(8,128)(2,1)S(1)}, u32[]{:S(2)}, u32[]{:S(2)}) collective-permute-start(bf16[4,28,16,128]{3,2,1,0:T(8,128)(2,1)S(1)} %bitcast.19), channel_id=1, source_target_pairs={{0,32},{32,0},{1,33},{33,1},{2,34},{34,2},{3,35},{35,3},{4,36},{36... | collective-permute-start | bytes 1376264 | tf_op jit(solution)/shard_map/ppermute | solution.py:296

commit v9 on v8

--- a/solution.py
+++ b/solution.py
@@ -118,34 +118,50 @@
     )(recv_slot, features, cotangent)
 
 
-def fill_bricks(core, odd, halos, lanes, bricks):
+def fill_bricks(halos, lanes, bricks):
     begin_at = SLOTS
     for halo in halos:
         bricks[begin_at : begin_at + halo.shape[0]] = halo[:, :, lanes]
         begin_at += halo.shape[0]
 
 
-def fill_layers(core, odd, halos, lanes, bricks):
-    y_first, y_second, x_sibling, x_outer = halos
-    both = ((x_sibling, core), (x_outer, 1 - core))
+def expand_tiles(side, tiles, targets, bricks):
+    whole = jnp.dot(
+        expand_matrix(side), jnp.concatenate(tiles, axis=1), preferred_element_type=jnp.float32
+    ).astype(jnp.bfloat16)
+    for position, target in enumerate(targets):
+        bricks[SLOTS + target] = whole[:, position * CHANNELS : (position + 1) * CHANNELS]
+
+
+def fill_along_y(halos, lanes, bricks):
+    odd = lax.axis_index("z") & 1
+    for faces, side in ((halos[0], odd), (halos[1], 1 - odd)):
+        tiles = [faces[position, :, lanes] for position in range(SLOTS)]
+        targets = [STARTS[2] + side * LENGTHS[2] + position for position in range(SLOTS)]
+        expand_tiles(side, tiles, targets, bricks)
+
+
+def fill_along_x(halos, lanes, bricks):
+    core, odd = lax.axis_index("c"), lax.axis_index("z") & 1
+    both = ((halos[0], core), (halos[1], 1 - core))
     for packet, below in both:
         for position in range(SLOTS):
             tile = packet[position, :, lanes]
             target = SLOTS + below * LENGTHS[0] + position
             for begin in range(0, VOXELS, PLANE):
                 bricks[target, begin : begin + PLANE] = tile
-    for order, (faces, side) in enumerate(((y_first, odd), (y_second, 1 - odd))):
-        tiles = [faces[position, :, lanes] for position in range(SLOTS)]
-        targets = [STARTS[2] + side * LENGTHS[2] + position for position in range(SLOTS)]
+    for order, side in ((0, odd), (1, 1 - odd)):
+        tiles = []
+        targets = []
         for packet, below in both:
             for position in range(BZ):
                 tiles.append(packet[SLOTS + BZ * order + position, :, lanes])
                 targets.append(STARTS[4] + side * BZ + below * 2 * BZ + position)
-        whole = jnp.dot(
-            expand_matrix(side), jnp.concatenate(tiles, axis=1), preferred_element_type=jnp.float32
-        ).astype(jnp.bfloat16)
-        for position, target in enumerate(targets):
-            bricks[SLOTS + target] = whole[:, position * CHANNELS : (position + 1) * CHANNELS]
+        expand_tiles(side, tiles, targets, bricks)
+
+
+def fill_nothing(halos, lanes, bricks):
+    pass
 
 
 def out_of_place(dst):
@@ -163,10 +179,7 @@
     return jnp.max(jnp.max(wrong, axis=1, keepdims=True), axis=0, keepdims=True)
 
 
-def build_taps(fill, unroll, dst_ref, own_ref, halos, lanes, bricks, taps):
-    bricks[:SLOTS] = own_ref[:SLOTS]
-    fill(lax.axis_index("c"), lax.axis_index("z") & 1, halos, lanes, bricks)
-    bricks[SLOTS + HALO] = jnp.zeros((VOXELS, CHANNELS), jnp.bfloat16)
+def build_taps(unroll, dst_ref, bricks, planes, taps):
     shift = shift_matrix()
 
     def around(slot, plane):
@@ -177,29 +190,50 @@
         )
 
     def one_slot(slot, carry):
-        for plane in range(0, PLANES, 2):
-            pair = jnp.concatenate((around(slot, plane), around(slot, plane + 1)), axis=1)
+        for index in range(0, len(planes), 2):
+            pair = jnp.concatenate((around(slot, planes[index]), around(slot, planes[index + 1])), axis=1)
             moved = jnp.dot(shift, pair, preferred_element_type=jnp.float32).astype(jnp.bfloat16)
             for number in range(9):
                 rows = moved[number * PLANE : (number + 1) * PLANE]
                 target = slice(number * CHANNELS, (number + 1) * CHANNELS)
-                taps[slot, plane, :, target] = rows[:, :CHANNELS]
-                taps[slot, plane + 1, :, target] = rows[:, CHANNELS:]
+                taps[slot, index, :, target] = rows[:, :CHANNELS]
+                taps[slot, index + 1, :, target] = rows[:, CHANNELS:]
         return carry
 
     lax.fori_loop(0, SLOTS, one_slot, 0, unroll=unroll)
 
 
-def weight_kernel(fill, unroll, count, dst_ref, table_ref, cotangent_ref, *rest):
+def taps_of(mid, edge, side):
+    if side == 0:
+        planes = jnp.concatenate((edge[:, :1], mid[:, :3]), axis=1)
+    elif side == 1:
+        planes = mid[...]
+    else:
+        planes = jnp.concatenate((mid[:, 1:], edge[:, 1:]), axis=1)
+    return planes.reshape(SLOTS * VOXELS, WIDE)
+
+
+def mid_kernel(fill, unroll, count, dst_ref, features_ref, cotangent_ref, *rest):
     halos = rest[:count]
-    flipped_ref, send_ref, keep_ref, taps, bricks = rest[count:]
-    build_taps(fill, unroll, dst_ref, cotangent_ref, halos, slice(CHANNELS, 2 * CHANNELS), bricks, taps)
+    mid_f, mid_c, bricks_f, bricks_c = rest[count:]
+    for kind, (own, bricks, mid) in enumerate(((features_ref, bricks_f, mid_f), (cotangent_ref, bricks_c, mid_c))):
+        bricks[:SLOTS] = own[:SLOTS]
+        for begin, end in ((SLOTS, SLOTS + STARTS[2]), (SLOTS + STARTS[4], SLOTS + HALO + 1)):
+            bricks[begin:end] = jnp.zeros((end - begin, VOXELS, CHANNELS), jnp.bfloat16)
+        fill(halos, slice(kind * CHANNELS, (kind + 1) * CHANNELS), bricks)
+        build_taps(unroll, dst_ref, bricks, (1, 2, 3, 4), mid)
+
+
+def weight_kernel(fill, unroll, count, dst_ref, table_ref, mid, _, *rest):
+    halos = rest[:count]
+    flipped_ref, send_ref, keep_ref, edge, bricks = rest[count:]
+    fill(halos, slice(CHANNELS, 2 * CHANNELS), bricks)
+    build_taps(unroll, dst_ref, bricks, (0, PLANES - 1), edge)
     core = lax.axis_index("c")
     flipped = jnp.concatenate((flipped_ref[1 - core], flipped_ref[core]), axis=0)
     half = CHANNELS // 2
-    for side in range(3):
-        tap = taps[:, side : side + BRICK].reshape(SLOTS * VOXELS, WIDE)
-        part = jnp.dot(flipped, tap, preferred_element_type=jnp.float32)
+    for side in (1, 0, 2):
+        part = jnp.dot(flipped, taps_of(mid, edge, side), preferred_element_type=jnp.float32)
         for number in range(9):
             block = part[:, number * CHANNELS : (number + 1) * CHANNELS]
             m = side * 9 + number
@@ -213,27 +247,28 @@
         keep_ref[quarter, 27] = flag
 
 
-def grad_kernel(taps, weights_ref, grad_ref):
+def grad_kernel(mid, edge, weights_ref, grad_ref):
     grad = None
     for side in range(3):
-        tap = taps[:, side : side + BRICK].reshape(SLOTS * VOXELS, WIDE)
         matrix = jnp.concatenate([weights_ref[26 - side * 9 - number] for number in range(9)], axis=1)
-        part = lax.dot_general(tap, matrix, (((1,), (1,)), ((), ())), preferred_element_type=jnp.float32)
+        part = lax.dot_general(
+            taps_of(mid, edge, side), matrix, (((1,), (1,)), ((), ())), preferred_element_type=jnp.float32
+        )
         grad = part if grad is None else grad + part
     grad_ref[...] = grad.astype(jnp.bfloat16).reshape(SLOTS, VOXELS, CHANNELS)
 
 
-def taps_kernel(fill, unroll, count, dst_ref, features_ref, *rest):
-    taps, bricks = rest[count:]
-    build_taps(fill, unroll, dst_ref, features_ref, rest[:count], slice(0, CHANNELS), bricks, taps)
-
-
-def output_kernel(taps, weights_ref, outputs_ref):
+def edge_kernel(fill, unroll, count, dst_ref, _, *rest):
+    edge, bricks = rest[count:]
+    fill(rest[:count], slice(0, CHANNELS), bricks)
+    build_taps(unroll, dst_ref, bricks, (0, PLANES - 1), edge)
+
+
+def output_kernel(mid, edge, weights_ref, outputs_ref):
     outputs = None
     for side in range(3):
-        tap = taps[:, side : side + BRICK].reshape(SLOTS * VOXELS, WIDE)
         matrix = weights_ref[side * 9 : side * 9 + 9].reshape(WIDE, CHANNELS)
-        part = jnp.dot(tap, matrix, preferred_element_type=jnp.float32)
+        part = jnp.dot(taps_of(mid, edge, side), matrix, preferred_element_type=jnp.float32)
         outputs = part if outputs is None else outputs + part
     outputs_ref[...] = outputs.astype(jnp.bfloat16).reshape(SLOTS, VOXELS, CHANNELS)
 
@@ -241,60 +276,74 @@
 VMEM_SPEC = pl.BlockSpec(memory_space=pltpu.VMEM)
 SMEM_SPEC = pl.BlockSpec(memory_space=pltpu.SMEM)
 BRICK_SHAPE = jax.ShapeDtypeStruct((SLOTS, VOXELS, CHANNELS), jnp.bfloat16)
-TAPS_SHAPE = jax.ShapeDtypeStruct((SLOTS, PLANES, PLANE, WIDE), jnp.bfloat16)
-ALL_BRICKS = pltpu.VMEM((SLOTS + HALO + 1, VOXELS, CHANNELS), jnp.bfloat16)
+MID_SHAPE = jax.ShapeDtypeStruct((SLOTS, BRICK, PLANE, WIDE), jnp.bfloat16)
+EDGE_SHAPE = jax.ShapeDtypeStruct((SLOTS, 2, PLANE, WIDE), jnp.bfloat16)
+ALL_BRICKS = jax.ShapeDtypeStruct((SLOTS + HALO + 1, VOXELS, CHANNELS), jnp.bfloat16)
 PARAMS = pltpu.CompilerParams(vmem_limit_bytes=VMEM_LIMIT)
 COST = pl.CostEstimate(flops=4 * SLOTS * VOXELS * 27 * CHANNELS * CHANNELS, bytes_accessed=4_000_000, transcendentals=0)
 
 
-def weight_sums(fill, unroll, dst, own_c, halos, flipped):
+def mid_taps(fill, unroll, dst, own_f, own_c, halos):
+    return pl.pallas_call(
+        functools.partial(mid_kernel, fill, unroll, len(halos)),
+        in_specs=[SMEM_SPEC] + [VMEM_SPEC] * (2 + len(halos)),
+        out_specs=[VMEM_SPEC] * 4,
+        out_shape=[MID_SHAPE, MID_SHAPE, ALL_BRICKS, ALL_BRICKS],
+        compiler_params=PARAMS,
+        cost_estimate=COST,
+    )(dst, own_f, own_c, *halos)
+
+
+def weight_sums(fill, unroll, dst, mid, bricks, halos, flipped):
     return pl.pallas_call(
         functools.partial(weight_kernel, fill, unroll, len(halos)),
-        in_specs=[SMEM_SPEC] + [VMEM_SPEC] * (3 + len(halos)),
-        out_specs=[VMEM_SPEC] * 3,
+        in_specs=[SMEM_SPEC] + [VMEM_SPEC] * (4 + len(halos)),
+        out_specs=[VMEM_SPEC] * 4,
         out_shape=[
             jax.ShapeDtypeStruct((4, ROWS_M, 16, CHANNELS), jnp.bfloat16),
             jax.ShapeDtypeStruct((4, ROWS_M, 16, CHANNELS), jnp.float32),
-            TAPS_SHAPE,
+            EDGE_SHAPE,
+            ALL_BRICKS,
         ],
-        scratch_shapes=[ALL_BRICKS],
+        input_output_aliases={3: 3},
         compiler_params=PARAMS,
         cost_estimate=COST,
-    )(dst, dst, own_c, *halos, flipped)
-
-
-def feature_taps(fill, unroll, dst, own_f, halos):
-    return pl.pallas_call(
-        functools.partial(taps_kernel, fill, unroll, len(halos)),
+    )(dst, dst, mid, bricks, *halos, flipped)
+
+
+def feature_edges(fill, unroll, dst, bricks, halos):
+    return pl.pallas_call(
+        functools.partial(edge_kernel, fill, unroll, len(halos)),
         in_specs=[SMEM_SPEC] + [VMEM_SPEC] * (1 + len(halos)),
-        out_specs=VMEM_SPEC,
-        out_shape=TAPS_SHAPE,
-        scratch_shapes=[ALL_BRICKS],
+        out_specs=[VMEM_SPEC] * 2,
+        out_shape=[EDGE_SHAPE, ALL_BRICKS],
+        input_output_aliases={1: 1},
         compiler_params=PARAMS,
         cost_estimate=COST,
-    )(dst, own_f, *halos)
-
-
-def product(kernel, taps, weights):
+    )(dst, bricks, *halos)[0]
+
+
+def product(kernel, mid, edge, weights):
     return pl.pallas_call(
         kernel,
-        in_specs=[VMEM_SPEC] * 2,
+        in_specs=[VMEM_SPEC] * 3,
         out_specs=VMEM_SPEC,
         out_shape=BRICK_SHAPE,
         compiler_params=PARAMS,
         cost_estimate=COST,
-    )(taps, weights)
-
-
-def convolve(fill, unroll, dst, own_f, own_c, halos, flipped, weights):
-    send, keep, taps_c = weight_sums(fill, unroll, dst, own_c, halos, flipped)
+    )(mid, edge, weights)
+
+
+def convolve(fill, unroll, dst, mids, halos, flipped, weights):
+    mid_f, mid_c, bricks_f, bricks_c = mids
+    send, keep, edge_c, _ = weight_sums(fill, unroll, dst, mid_c, bricks_c, halos, flipped)
     arrived = lax.ppermute(send, "c", [(0, 1), (1, 0)])
-    input_grad = product(grad_kernel, taps_c, weights)
-    taps_f = feature_taps(fill, unroll, dst, own_f, halos)
-    arrived, input_grad, taps_f = lax.optimization_barrier((arrived, input_grad, taps_f))
+    input_grad = product(grad_kernel, mid_c, edge_c, weights)
+    edge_f = feature_edges(fill, unroll, dst, bricks_f, halos)
+    arrived, input_grad, edge_f = lax.optimization_barrier((arrived, input_grad, edge_f))
     own = sum_everywhere(arrived, keep)
     other = lax.ppermute(own, "c", [(0, 1), (1, 0)])
-    outputs = product(output_kernel, taps_f, weights)
+    outputs = product(output_kernel, mid_f, edge_f, weights)
     return outputs, input_grad, own, other
 
 
@@ -408,13 +457,14 @@
     x_outer = lax.ppermute(relayed(to_outer, core), ("x", "c"), [(2 * x + 1, 2 * x + 2) for x in range(3)]
                            + [(2 * x + 2, 2 * x + 1) for x in range(3)])
     x_sibling = lax.ppermute(relayed(to_sibling, 1 - core), "c", [(0, 1), (1, 0)])
-    halos = (y_first, y_second, x_sibling, x_outer)
-    results = convolve(fill_layers, SLOTS, dst, own_f, own_c, halos, flipped, weights)
+    mids = mid_taps(fill_along_y, SLOTS, dst, own_f, own_c, (y_first, y_second))
+    results = convolve(fill_along_x, SLOTS, dst, mids, (x_sibling, x_outer), flipped, weights)
 
     def with_whole_bricks(results):
         packets = pack_bricks(recv_slot, features, cotangent)
         halos = [pass_to(packet, -heading[0], -heading[1]) for packet, heading in zip(packets, DIRECTIONS)]
-        return spread_out(*convolve(fill_bricks, 1, dst, own_f, own_c, halos, flipped, weights))
+        mids = mid_taps(fill_bricks, 1, dst, own_f, own_c, halos)
+        return spread_out(*convolve(fill_nothing, 1, dst, mids, (), flipped, weights))
 
     def as_they_are(results):
         return spread_out(*results)

time: 78.8 us -> 77.6 us (0.985)
  blocking collectives: 51.5 us -> 47.8 us
  starting transfers between devices: 12.3 us -> 13.8 us
  Pallas kernels: 8.36 us -> 9.37 us
    ppermute x1, starting transfers between devices: 0.09 us -> 3.47 us  [local(): lax.ppermute(relayed(to_sibling, 1 - core), 'c', [(0, 1), (1, 0)])]
    ppermute x1, starting transfers between devices: 4.75 us -> 1.92 us  [local(): lax.ppermute(relayed(to_outer, core), ('x', 'c'), [(2 * x + 1, 2 * x + 2)...]
    all_to_all x1, blocking collectives: 23.4 us -> 21.3 us  [sum_everywhere(): parts = lax.all_to_all(parts, ('x', 'y'), 0, 0)]
    all_to_all x1, blocking collectives: 13.3 us -> 11.6 us  [sum_everywhere(): lax.all_to_all(whole, ('x', 'y'), 0, 0).reshape(4, ROWS_M, 16, CHANNELS)]
    pallas_call x3 -> x4, Pallas kernels: 3.63 us -> 5.12 us  [the longest x2 2.18 us: product(): pl.pallas_call(kernel, in_specs=[VMEM_SPEC] * 3, out_specs=VMEM_SPEC, out...]
    ppermute x1, starting transfers between devices: 4.15 us -> 5.07 us  [convolve(): other = lax.ppermute(own, 'c', [(0, 1), (1, 0)])]
  transfers between devices with their start and end apart: 6 -> 6, of which waited for: 2 -> 2; matrix products, arithmetic and copies ran while one was open for 2% -> 2% of each run, Pallas kernels for 5% -> 7%
where the time goes in v9:
time: 77.6 us; the launch traced here: 77.3 us
  blocking collectives  47.8 us (62%)
  starting transfers between devices  13.8 us (18%)
  Pallas kernels  9.37 us (12%)
  waiting for transfers between devices  2.64 us (3%)
  between operations  1.7 us (2%)
  other arithmetic  1.06 us (1%)
    all_to_all x1, blocking collectives, sum_everywhere(): parts = lax.all_to_all(parts, ('x', 'y'), 0, 0)  21.3 us
    all_to_all x1, blocking collectives, sum_everywhere(): lax.all_to_all(jnp.broadcast_to(share[None], (8,) + share.shape), 'z', 0, 0)  14.9 us
    all_to_all x1, blocking collectives, sum_everywhere(): lax.all_to_all(whole, ('x', 'y'), 0, 0).reshape(4, ROWS_M, 16, CHANNELS)  11.6 us
    ppermute x1, starting transfers between devices, convolve(): other = lax.ppermute(own, 'c', [(0, 1), (1, 0)])  5.07 us
    ppermute x1, starting transfers between devices, local(): lax.ppermute(relayed(to_sibling, 1 - core), 'c', [(0, 1), (1, 0)])  3.47 us
    ppermute x1, starting transfers between devices, local(): lax.ppermute(to_first, ('y', 'z'), [(gy, gy ^ 1) for gy in range(32)])  2.55 us
    pallas_call x2, Pallas kernels, product(): pl.pallas_call(kernel, in_specs=[VMEM_SPEC] * 3, out_specs=VMEM_SPEC, out...  2.18 us
    ppermute x1, starting transfers between devices, local(): lax.ppermute(relayed(to_outer, core), ('x', 'c'), [(2 * x + 1, 2 * x + 2)...  1.92 us
  transfers between devices with their start and end apart: 6, of which 2 were waited for; matrix products, arithmetic and copies ran while one was open for 2% of the time, Pallas kernels for 7%

profile of v9, /device:TPU:1, one launch (start us, length us, event | category | flops | bytes accessed | tf_op | source)
XLA Modules:
  0.0 77.3 jit_solution(16694100584874395335)
XLA Ops:
  0.6 1.3 %shard_map.82 = (bf16[12,16,256]{2,1,0:T(8,128)(2,1)S(1)}, bf16[12,16,256]{2,1,0:T(8,128)(2,1)S(1)}, bf16[8,16,256]{2,1,0:T(8,128)(2,1)S(1)}, bf16[8,16,256]{2,1...) custom-call(s32[40]{0:T(128)} %recv_slot_ref.1, bf16[8,64,128]{2,1,0:T(8,128)(2,1)} %features_ref.1, ...), custom_call_target="tpu_custom_call" | custom-call | tf_op jit(solution)/shard_map/pallas_call | solution.py:105
  1.9 2.6 %collective-permute-start.10 = (bf16[12,16,256]{2,1,0:T(8,128)(2,1)S(1)}, bf16[12,16,256]{2,1,0:T(8,128)(2,1)S(1)}, u32[]{:S(2)}, u32[]{:S(2)}) collective-permute-start(bf16[12,16,256]{2,1,0:T(8,128)(2,1)S(1)} %get-tuple-element.77), channel_id=1, source_target_pairs={{0,1},{1,0},{2,3},{3,2},{4,5},{5,4},{6,7},{7,6},{8,9},{9,8},{10,11... | collective-permute-start | bytes 294920 | tf_op jit(solution)/shard_map/ppermute | solution.py:450
  4.5 0.7 collective-permute-start.11
  5.1 1.3 %collective-permute-done.10.rest_0_ = bf16[12,16,256]{2,1,0:T(8,128)(2,1)S(1)} collective-permute-done((bf16[12,16,256]{2,1,0:T(8,128)(2,1)S(1)}, bf16[12,16,256]{2,1,0:T(8,128)(2,1)S(1)}, u32[]{:S(2)}, u32[]{:S(2)}) %collective-permute-start.10) | collective-permute-done | bytes 98336 | tf_op jit(solution)/shard_map/ppermute | solution.py:450
  6.5 0.0 collective-permute-done.11.rest_1_
  6.5 3.5 %collective-permute-start.12 = (bf16[12,16,256]{2,1,0:T(8,128)(2,1)S(1)}, bf16[12,16,256]{2,1,0:T(8,128)(2,1)S(1)}, u32[]{:S(2)}, u32[]{:S(2)}) collective-permute-start(bf16[12,16,256]{2,1,0:T(8,128)(2,1)S(1)} %pad_maximum_fusion.1), channel_id=1, source_target_pairs={{0,32},{32,0},{1,33},{33,1},{2,34},{34,2},{3,35},{35,3},{4,36},{36... | collective-permute-start | bytes 294920 | tf_op jit(solution)/shard_map/ppermute | solution.py:459
  10.0 1.9 %collective-permute-start.13 = (bf16[12,16,256]{2,1,0:T(8,128)(2,1)S(1)}, bf16[12,16,256]{2,1,0:T(8,128)(2,1)S(1)}, u32[]{:S(2)}, u32[]{:S(2)}) collective-permute-start(bf16[12,16,256]{2,1,0:T(8,128)(2,1)S(1)} %pad_maximum_fusion.2), channel_id=1, source_target_pairs={{32,64},{96,128},{160,192},{64,32},{128,96},{192,160},{33,65},{97,... | collective-permute-start | bytes 294920 | tf_op jit(solution)/shard_map/ppermute | solution.py:457
  11.9 0.7 clamp_bitcast_fusion.dst_ref.table_ref
  12.6 0.1 copy.19
  12.8 1.9 %shard_map.83 = (bf16[8,4,16,1152]{3,2,1,0:T(8,128)(2,1)S(1)}, bf16[8,4,16,1152]{3,2,1,0:T(8,128)(2,1)S(1)}, bf16[49,64,128]{2,1,0:T(8,128)(2,1)S(1)}, bf16[49,64,128]{2,1,0:T(8,128)(2,1)S(1)}) custom-call(s32[8,27]{1,0:T(8,128)S(1)} %clamp_bitcast_fusion.dst_ref.table_ref, bf16[9,64,128]{2,1,0:T(8,128)(2,1)S(1)} %get-tuple-element.75.features_ref, ...), custom_call_target="tpu_custom_call" | custom-call | flops 905969664 | bytes 4000000 | tf_op jit(solution)/shard_map/pallas_call | solution.py:287
  14.6 0.0 collective-permute-done.12.rest_0_
  14.6 1.3 %collective-permute-done.13.rest_1_ = bf16[12,16,256]{2,1,0:T(8,128)(2,1)S(1)} collective-permute-done((bf16[12,16,256]{2,1,0:T(8,128)(2,1)S(1)}, bf16[12,16,256]{2,1,0:T(8,128)(2,1)S(1)}, u32[]{:S(2)}, u32[]{:S(2)}) %collective-permute-start.13) | collective-permute-done | bytes 98336 | tf_op jit(solution)/shard_map/ppermute | solution.py:457
  15.9 0.0 copy-start.3
  15.9 1.6 %shard_map.84 = (bf16[4,28,16,128]{3,2,1,0:T(8,128)(2,1)S(1)}, f32[4,28,16,128]{3,2,1,0:T(8,128)S(1)}, bf16[8,2,16,1152]{3,2,1,0:T(8,128)(2,1)S(1)}, bf16[49,64,128]{2,1,0:T(8,128)(2,1)S(1)}) custom-call(s32[8,27]{1,0:T(8,128)S(1)} %clamp_bitcast_fusion.dst_ref.table_ref, ...), custom_call_target="tpu_custom_call", output_to_operand_aliasing={{3}: (3, {})} | custom-call | flops 905969664 | bytes 4000000 | tf_op jit(solution)/shard_map/pallas_call | solution.py:298
  17.5 0.1 collective-permute-start.14
  17.6 0.0 copy-done.3
  17.6 1.1 %shard_map.85 = bf16[8,64,128]{2,1,0:T(8,128)(2,1)S(1)} custom-call(bf16[8,4,16,1152]{3,2,1,0:T(8,128)(2,1)S(1)} %get-tuple-element.79.mid, bf16[8,2,16,1152]{3,2,1,0:T(8,128)(2,1)S(1)} %get-tuple-element.85.edge, bf16[27,128,128]{2,1,0:T(8,128)(2,1)S(1)} %copy-done.3), custom_call_target="tpu_custom_call" | custom-call | flops 905969664 | bytes 4000000 | tf_op jit(solution)/shard_map/pallas_call | solution.py:327
  18.7 1.1 %shard_map.86 = (bf16[8,2,16,1152]{3,2,1,0:T(8,128)(2,1)S(1)}, bf16[49,64,128]{2,1,0:T(8,128)(2,1)S(1)}) custom-call(s32[8,27]{1,0:T(8,128)S(1)} %clamp_bitcast_fusion.dst_ref.table_ref, bf16[49,64,128]{2,1,0:T(8,128)(2,1)S(1)} %get-tuple-element.86._, bf16[12,16,256]{2,1,0:T(8,128)(2,1)S(1)} %collective-permute-done.12.rest_0_, ...), custom_call_target="tpu_custom_call", output_to_operand_aliasing={{1}: (1, {})} | custom-call | flops 905969664 | bytes 4000000 | tf_op jit(solution)/shard_map/pallas_call | solution.py:315
  19.8 0.0 collective-permute-done.14
  19.8 0.1 add_convert_fusion.1
  19.9 21.3 %all_to_all.30 = bf16[16,7,16,128]{3,2,1,0:T(8,128)(2,1)S(1)} all-to-all(bf16[16,7,16,128]{3,2,1,0:T(8,128)(2,1)S(1)} %bitcast.17), channel_id=1, replica_groups=mesh['x'=4,'c'=2,'y'=4,'z'=8] {'x','y'}, dimensions={0} | all-to-all | bytes 917504 | tf_op jit(solution)/shard_map/all_to_all | solution.py:394
  41.3 0.1 convert_reduce_fusion.1
  41.5 14.9 %all_to_all.31 = f16[8,8,16,128]{3,2,1,0:T(8,128)(2,1)S(1)} all-to-all(f16[8,8,16,128]{3,2,1,0:T(8,128)(2,1)S(1)} %broadcast_in_dim.13), channel_id=1, replica_groups=mesh['x'=4,'c'=2,'y'=4,'z'=8] {'z'}, dimensions={0} | all-to-all | bytes 524288 | tf_op jit(solution)/shard_map/all_to_all | solution.py:400
  56.5 0.1 broadcast_in_dim.14
  56.5 11.6 %all_to_all.32 = bf16[16,7,16,128]{3,2,1,0:T(8,128)(2,1)S(1)} all-to-all(bf16[16,7,16,128]{3,2,1,0:T(8,128)(2,1)S(1)} %broadcast_in_dim.14), channel_id=1, replica_groups=mesh['x'=4,'c'=2,'y'=4,'z'=8] {'x','y'}, dimensions={0} | all-to-all | bytes 917504 | tf_op jit(solution)/shard_map/all_to_all | solution.py:404
  68.2 5.1 %collective-permute-start.15 = (bf16[4,28,16,128]{3,2,1,0:T(8,128)(2,1)S(1)}, bf16[4,28,16,128]{3,2,1,0:T(8,128)(2,1)S(1)}, u32[]{:S(2)}, u32[]{:S(2)}) collective-permute-start(bf16[4,28,16,128]{3,2,1,0:T(8,128)(2,1)S(1)} %bitcast.19), channel_id=1, source_target_pairs={{0,32},{32,0},{1,33},{33,1},{2,34},{34,2},{3,35},{35,3},{4,36},{36... | collective-permute-start | bytes 1376264 | tf_op jit(solution)/shard_map/ppermute | solution.py:345
  73.2 0.0 copy-start
  73.2 0.0 copy-start.1
  73.2 0.0 copy-start.2
  73.2 1.1 %shard_map.87 = bf16[8,64,128]{2,1,0:T(8,128)(2,1)S(1)} custom-call(bf16[8,4,16,1152]{3,2,1,0:T(8,128)(2,1)S(1)} %get-tuple-element.89.mid, bf16[8,2,16,1152]{3,2,1,0:T(8,128)(2,1)S(1)} %get-tuple-element.90.edge, bf16[27,128,128]{2,1,0:T(8,128)(2,1)S(1)} %copy-done.3), custom_call_target="tpu_custom_call" | custom-call | flops 905969664 | bytes 4000000 | tf_op jit(solution)/shard_map/pallas_call | solution.py:327
  74.3 0.5 slice.26
  75.5 0.0 collective-permute-done.15
  75.5 0.0 copy-done
  75.5 0.0 copy-done.1
  75.5 0.0 copy-done.2
  75.5 1.6 %conditional.1 = ((bf16[8,64,128]{2,1,0:T(8,128)(2,1)}, bf16[8,64,128]{2,1,0:T(8,128)(2,1)}, f32[27,128,128]{2,1,0:T(8,128)})) conditional(s32[]{:T(128)} %bitcast.10, (bf16[4,28,16,128]{3,2,1,0:T(8,128)(2,1)S(1)}, bf16[4,28,16,128]{3,2,1,0:T(8,128)(2,1)S(1)}, bf16[8,64,128]{2,1,0:T(8,128)(2,1)S(1)}, bf16[8,64,128]{2,1,0:T(8,128)(2,1)S(1)}) %tuple.32, ...), branch_computations={%region_3.4_spmd, %region_4.8_spmd} | conditional | flops 4531463168 | bytes 36206744 | solution.py:473
  75.5 1.4 %branch_0_fun.1 = (bf16[8,64,128]{2,1,0:T(8,128)(2,1)}, bf16[8,64,128]{2,1,0:T(8,128)(2,1)}, f32[27,128,128]{2,1,0:T(8,128)}) custom-call(bf16[4,28,16,128]{3,2,1,0:T(8,128)(2,1)S(1)} %get-tuple-element.24.own_ref, bf16[4,28,16,128]{3,2,1,0:T(8,128)(2,1)S(1)} %get-tuple-element.25.other_ref, bf16[8,64,128]{2,1,0:T(8,128)(2,1)S(1)} %get-tuple-element.26.outputs_ref, ...), custom_call_target="tpu_custom_call" | custom-call | tf_op jit(solution)/shard_map/cond/branch_0_fun/pallas_call | solution.py:430
  (15 shorter events, 0.3 us)
Async XLA Ops:
  1.9 4.6 %collective-permute-start.10 = (bf16[12,16,256]{2,1,0:T(8,128)(2,1)S(1)}, bf16[12,16,256]{2,1,0:T(8,128)(2,1)S(1)}, u32[]{:S(2)}, u32[]{:S(2)}) collective-permute-start(bf16[12,16,256]{2,1,0:T(8,128)(2,1)S(1)} %get-tuple-element.77), channel_id=1, source_target_pairs={{0,1},{1,0},{2,3},{3,2},{4,5},{5,4},{6,7},{7,6},{8,9},{9,8},{10,11... | collective-permute-start | bytes 294920 | tf_op jit(solution)/shard_map/ppermute | solution.py:450
  4.5 2.0 %collective-permute-start.11 = (bf16[12,16,256]{2,1,0:T(8,128)(2,1)S(1)}, bf16[12,16,256]{2,1,0:T(8,128)(2,1)S(1)}, u32[]{:S(2)}, u32[]{:S(2)}) collective-permute-start(bf16[12,16,256]{2,1,0:T(8,128)(2,1)S(1)} %get-tuple-element.78), channel_id=1, source_target_pairs={{1,2},{2,1},{3,4},{4,3},{5,6},{6,5},{7,8},{8,7},{9,10},{10,9},{11,... | collective-permute-start | bytes 294920 | tf_op jit(solution)/shard_map/ppermute | solution.py:451
  6.5 8.1 %collective-permute-start.12 = (bf16[12,16,256]{2,1,0:T(8,128)(2,1)S(1)}, bf16[12,16,256]{2,1,0:T(8,128)(2,1)S(1)}, u32[]{:S(2)}, u32[]{:S(2)}) collective-permute-start(bf16[12,16,256]{2,1,0:T(8,128)(2,1)S(1)} %pad_maximum_fusion.1), channel_id=1, source_target_pairs={{0,32},{32,0},{1,33},{33,1},{2,34},{34,2},{3,35},{35,3},{4,36},{36... | collective-permute-start | bytes 294920 | tf_op jit(solution)/shard_map/ppermute | solution.py:459
  10.0 5.9 %collective-permute-start.13 = (bf16[12,16,256]{2,1,0:T(8,128)(2,1)S(1)}, bf16[12,16,256]{2,1,0:T(8,128)(2,1)S(1)}, u32[]{:S(2)}, u32[]{:S(2)}) collective-permute-start(bf16[12,16,256]{2,1,0:T(8,128)(2,1)S(1)} %pad_maximum_fusion.2), channel_id=1, source_target_pairs={{32,64},{96,128},{160,192},{64,32},{128,96},{192,160},{33,65},{97,... | collective-permute-start | bytes 294920 | tf_op jit(solution)/shard_map/ppermute | solution.py:457
  15.9 1.7 %copy-start.3 = (bf16[27,128,128]{2,1,0:T(8,128)(2,1)S(1)}, bf16[27,128,128]{2,1,0:T(8,128)(2,1)}, u32[]{:S(2)}) copy-start(bf16[27,128,128]{2,1,0:T(8,128)(2,1)} %weights_ref.3) | copy-start | bytes 2654212
  17.5 2.3 %collective-permute-start.14 = (bf16[4,28,16,128]{3,2,1,0:T(8,128)(2,1)S(1)}, bf16[4,28,16,128]{3,2,1,0:T(8,128)(2,1)S(1)}, u32[]{:S(2)}, u32[]{:S(2)}) collective-permute-start(bf16[4,28,16,128]{3,2,1,0:T(8,128)(2,1)S(1)} %get-tuple-element.84), channel_id=1, source_target_pairs={{0,32},{32,0},{1,33},{33,1},{2,34},{34,2},{3,35},{35,3},{4,36},{36... | collective-permute-start | bytes 1376264 | tf_op jit(solution)/shard_map/ppermute | solution.py:340
  68.2 7.3 %collective-permute-start.15 = (bf16[4,28,16,128]{3,2,1,0:T(8,128)(2,1)S(1)}, bf16[4,28,16,128]{3,2,1,0:T(8,128)(2,1)S(1)}, u32[]{:S(2)}, u32[]{:S(2)}) collective-permute-start(bf16[4,28,16,128]{3,2,1,0:T(8,128)(2,1)S(1)} %bitcast.19), channel_id=1, source_target_pairs={{0,32},{32,0},{1,33},{33,1},{2,34},{34,2},{3,35},{35,3},{4,36},{36... | collective-permute-start | bytes 1376264 | tf_op jit(solution)/shard_map/ppermute | solution.py:345
  73.2 2.3 %copy-start = (bf16[8,64,128]{2,1,0:T(8,128)(2,1)S(1)}, bf16[8,64,128]{2,1,0:T(8,128)(2,1)}, u32[]{:S(2)}) copy-start(bf16[8,64,128]{2,1,0:T(8,128)(2,1)} %features_ref.1) | copy-start | bytes 393220
  73.2 2.3 %copy-start.1 = (bf16[8,64,128]{2,1,0:T(8,128)(2,1)S(1)}, bf16[8,64,128]{2,1,0:T(8,128)(2,1)}, u32[]{:S(2)}) copy-start(bf16[8,64,128]{2,1,0:T(8,128)(2,1)} %cotangent_ref.1) | copy-start | bytes 393220
  73.2 2.3 %copy-start.2 = (s32[40]{0:T(128)S(1)}, s32[40]{0:T(128)}, u32[]{:S(2)}) copy-start(s32[40]{0:T(128)} %recv_slot_ref.1) | copy-start | bytes 484

commit v10 on v9

--- a/solution.py
+++ b/solution.py
@@ -42,15 +42,24 @@
 
 
 def layer_matrix():
-    row = lax.broadcasted_iota(jnp.int32, (2 * PLANE, VOXELS), 0)
-    column = lax.broadcasted_iota(jnp.int32, (2 * PLANE, VOXELS), 1)
-    return where_equal(column, ((row >> 2) & 3) * PLANE + (row >> 4) * 12 + (row & 3))
+    row = lax.broadcasted_iota(jnp.int32, (4 * PLANE, VOXELS), 0)
+    column = lax.broadcasted_iota(jnp.int32, (4 * PLANE, VOXELS), 1)
+    quarter = (row >> 2) & 3
+    vx = jnp.where(row < 2 * PLANE, quarter, (quarter >> 1) * 3)
+    return where_equal(column, vx * PLANE + ((row >> 4) & 1) * 12 + (row & 3))
 
 
 def expand_matrix(side):
     row = lax.broadcasted_iota(jnp.int32, (VOXELS, PLANE), 0)
     column = lax.broadcasted_iota(jnp.int32, (VOXELS, PLANE), 1)
     return where_equal(row, (column >> 2) * PLANE + side * 12 + (column & 3))
+
+
+def expand_corner_matrix(order, side):
+    row = lax.broadcasted_iota(jnp.int32, (2 * VOXELS, PLANE), 0)
+    column = lax.broadcasted_iota(jnp.int32, (2 * VOXELS, PLANE), 1)
+    vy = (row >> 2) & 3
+    return where_equal(column + vy * PLANE, order * 8 + (row >> 6) * 4 + (row & 3) + side * 3 * PLANE)
 
 
 def pack_layers_kernel(recv_slot_ref, features_ref, cotangent_ref, to_first, to_second, to_sibling, to_outer,
@@ -68,10 +77,12 @@
         copy.start()
     for own in bricks:
         own[SLOTS] = jnp.zeros((VOXELS, CHANNELS), jnp.bfloat16)
-    sides[:, SLOTS] = jnp.zeros((2, 2 * PLANE, CHANNELS), jnp.bfloat16)
+    sides[:, SLOTS] = jnp.zeros((2, 4 * PLANE, CHANNELS), jnp.bfloat16)
     core = lax.axis_index("c")
     odd = lax.axis_index("z") & 1
     layer = layer_matrix()
+    block = lax.broadcasted_iota(jnp.int32, (PLANE, CHANNELS), 0) >> 2
+    masks = [where_equal(block, number) for number in range(4)]
     for copy in copies:
         copy.wait()
     for kind in range(2):
@@ -88,11 +99,16 @@
 
     for packet, up in ((to_first, 1 - odd), (to_second, odd)):
         begin = pl.multiple_of(up * PLANE, PLANE)
-        position = 0
-        for number in (2, 4, 6):
-            for halo in range(LENGTHS[number]):
-                put(packet, position, STARTS[number] + up * LENGTHS[number] + halo, (sides.at[0], sides.at[1]), begin)
-                position += 1
+        for position in range(SLOTS):
+            put(packet, position, STARTS[2] + up * LENGTHS[2] + position, (sides.at[0], sides.at[1]), begin)
+        rows = pl.ds(pl.multiple_of((up + 2) * PLANE, PLANE), PLANE)
+        halos = [STARTS[number] + up * BZ + position for number in (4, 6) for position in range(BZ)]
+        slots = [jnp.clip(slot_ref[halo], 0, SLOTS) for halo in halos]
+        for kind in range(2):
+            tile = sides[kind, slots[0], rows] * masks[0]
+            for number in range(1, 4):
+                tile = tile + sides[kind, slots[number], rows] * masks[number]
+            packet[SLOTS, :, kind * CHANNELS : (kind + 1) * CHANNELS] = tile
     for packet, up in ((to_sibling, 1 - core), (to_outer, core)):
         begin = pl.multiple_of(up * (VOXELS - PLANE), PLANE)
         for position in range(LENGTHS[0]):
@@ -104,13 +120,13 @@
     hbm = pl.BlockSpec(memory_space=pltpu.HBM)
     return pl.pallas_call(
         pack_layers_kernel,
-        in_specs=[hbm, hbm, hbm],
+        in_specs=[hbm] * 3,
         out_specs=[vmem] * 6,
         out_shape=[
-            jax.ShapeDtypeStruct((length, PLANE, 2 * CHANNELS), jnp.bfloat16) for length in (12, 12, 8, 8)
+            jax.ShapeDtypeStruct((length, PLANE, 2 * CHANNELS), jnp.bfloat16) for length in (SLOTS + 1, SLOTS + 1, SLOTS, SLOTS)
         ] + [jax.ShapeDtypeStruct((SLOTS + 1, VOXELS, CHANNELS), jnp.bfloat16)] * 2,
         scratch_shapes=[
-            pltpu.VMEM((2, SLOTS + 1, 2 * PLANE, CHANNELS), jnp.bfloat16),
+            pltpu.VMEM((2, SLOTS + 1, 4 * PLANE, CHANNELS), jnp.bfloat16),
             pltpu.SMEM((HALO,), jnp.int32),
             pltpu.SemaphoreType.DMA((3,)),
         ],
@@ -125,20 +141,14 @@
         begin_at += halo.shape[0]
 
 
-def expand_tiles(side, tiles, targets, bricks):
-    whole = jnp.dot(
-        expand_matrix(side), jnp.concatenate(tiles, axis=1), preferred_element_type=jnp.float32
-    ).astype(jnp.bfloat16)
-    for position, target in enumerate(targets):
-        bricks[SLOTS + target] = whole[:, position * CHANNELS : (position + 1) * CHANNELS]
-
-
 def fill_along_y(halos, lanes, bricks):
     odd = lax.axis_index("z") & 1
     for faces, side in ((halos[0], odd), (halos[1], 1 - odd)):
-        tiles = [faces[position, :, lanes] for position in range(SLOTS)]
-        targets = [STARTS[2] + side * LENGTHS[2] + position for position in range(SLOTS)]
-        expand_tiles(side, tiles, targets, bricks)
+        tiles = jnp.concatenate([faces[position, :, lanes] for position in range(SLOTS)], axis=1)
+        whole = jnp.dot(expand_matrix(side), tiles, preferred_element_type=jnp.float32).astype(jnp.bfloat16)
+        for position in range(SLOTS):
+            target = SLOTS + STARTS[2] + side * LENGTHS[2] + position
+            bricks[target] = whole[:, position * CHANNELS : (position + 1) * CHANNELS]
 
 
 def fill_along_x(halos, lanes, bricks):
@@ -150,14 +160,17 @@
             target = SLOTS + below * LENGTHS[0] + position
             for begin in range(0, VOXELS, PLANE):
                 bricks[target, begin : begin + PLANE] = tile
+    tiles = jnp.concatenate([packet[SLOTS, :, lanes] for packet in halos], axis=1)
     for order, side in ((0, odd), (1, 1 - odd)):
-        tiles = []
-        targets = []
-        for packet, below in both:
+        whole = jnp.dot(
+            expand_corner_matrix(order, side), tiles, preferred_element_type=jnp.float32
+        ).astype(jnp.bfloat16)
+        for number, (_, below) in enumerate(both):
             for position in range(BZ):
-                tiles.append(packet[SLOTS + BZ * order + position, :, lanes])
-                targets.append(STARTS[4] + side * BZ + below * 2 * BZ + position)
-        expand_tiles(side, tiles, targets, bricks)
+                target = SLOTS + STARTS[4] + side * BZ + below * 2 * BZ + position
+                bricks[target] = whole[
+                    position * VOXELS : (position + 1) * VOXELS, number * CHANNELS : (number + 1) * CHANNELS
+                ]
 
 
 def fill_nothing(halos, lanes, bricks):
@@ -447,12 +460,13 @@
     to_first, to_second, to_sibling, to_outer, own_f, own_c = pack_layers(recv_slot, features, cotangent)
     flipped = jnp.transpose(own_f[:SLOTS].reshape(SLOTS * VOXELS, CHANNELS))
     flipped = flipped.reshape(2, CHANNELS // 2, SLOTS * VOXELS)
+    y_second = lax.ppermute(to_second, ("y", "z"), [(gy, ((gy + 1) ^ 1) - 1) for gy in range(1, 31)])
     y_first = lax.ppermute(to_first, ("y", "z"), [(gy, gy ^ 1) for gy in range(32)])
-    y_second = lax.ppermute(to_second, ("y", "z"), [(gy, ((gy + 1) ^ 1) - 1) for gy in range(1, 31)])
+    y_first, y_second, dst, flipped = lax.optimization_barrier((y_first, y_second, dst, flipped))
 
     def relayed(packet, up):
-        corners = [lax.dynamic_slice_in_dim(value, SLOTS + BZ * up, BZ, axis=0) for value in (y_first, y_second)]
-        return jnp.concatenate((packet, *corners), axis=0)
+        corners = [lax.dynamic_slice_in_dim(value[SLOTS:], 8 * up, 8, axis=1) for value in (y_first, y_second)]
+        return jnp.concatenate((packet, jnp.concatenate(corners, axis=1)), axis=0)
 
     x_outer = lax.ppermute(relayed(to_outer, core), ("x", "c"), [(2 * x + 1, 2 * x + 2) for x in range(3)]
                            + [(2 * x + 2, 2 * x + 1) for x in range(3)])

time: 77.6 us -> 77.2 us (level)
    ppermute x1, waiting for transfers between devices: 1.34 us -> 0.26 us  [local(): lax.ppermute(to_first, ('y', 'z'), [(gy, gy ^ 1) for gy in range(32)])]
where the time goes in v10:
time: 77.2 us; the launch traced here: 76.9 us
  blocking collectives  47.8 us (62%)
  starting transfers between devices  13.7 us (18%)
  Pallas kernels  9.48 us (12%)
  waiting for transfers between devices  2.13 us (3%)
  between operations  1.7 us (2%)
  other arithmetic  1.05 us (1%)
    all_to_all x1, blocking collectives, sum_everywhere(): parts = lax.all_to_all(parts, ('x', 'y'), 0, 0)  21.3 us
    all_to_all x1, blocking collectives, sum_everywhere(): lax.all_to_all(jnp.broadcast_to(share[None], (8,) + share.shape), 'z', 0, 0)  14.9 us
    all_to_all x1, blocking collectives, sum_everywhere(): lax.all_to_all(whole, ('x', 'y'), 0, 0).reshape(4, ROWS_M, 16, CHANNELS)  11.6 us
    ppermute x1, starting transfers between devices, convolve(): other = lax.ppermute(own, 'c', [(0, 1), (1, 0)])  5.05 us
    ppermute x1, starting transfers between devices, local(): lax.ppermute(relayed(to_sibling, 1 - core), 'c', [(0, 1), (1, 0)])  3.47 us
    ppermute x1, starting transfers between devices, local(): lax.ppermute(to_first, ('y', 'z'), [(gy, gy ^ 1) for gy in range(32)])  2.55 us
    pallas_call x2, Pallas kernels, product(): pl.pallas_call(kernel, in_specs=[VMEM_SPEC] * 3, out_specs=VMEM_SPEC, out...  2.18 us
    ppermute x1, starting transfers between devices, local(): lax.ppermute(relayed(to_outer, core), ('x', 'c'), [(2 * x + 1, 2 * x + 2)...  1.91 us
  transfers between devices with their start and end apart: 6, of which 2 were waited for; matrix products, arithmetic and copies ran while one was open for 2% of the time, Pallas kernels for 7%

profile of v10, /device:TPU:1, one launch (start us, length us, event | category | flops | bytes accessed | tf_op | source)
XLA Modules:
  0.0 76.9 jit_solution(821391212564073282)
XLA Ops:
  0.6 1.3 %shard_map.82 = (bf16[9,16,256]{2,1,0:T(8,128)(2,1)S(1)}, bf16[9,16,256]{2,1,0:T(8,128)(2,1)S(1)}, bf16[8,16,256]{2,1,0:T(8,128)(2,1)S(1)}, bf16[8,16,256]{2,1,0...) custom-call(s32[40]{0:T(128)} %recv_slot_ref.1, bf16[8,64,128]{2,1,0:T(8,128)(2,1)} %features_ref.1, ...), custom_call_target="tpu_custom_call" | custom-call | tf_op jit(solution)/shard_map/pallas_call | solution.py:121
  1.9 2.6 %collective-permute-start.10 = (bf16[9,16,256]{2,1,0:T(8,128)(2,1)S(1)}, bf16[9,16,256]{2,1,0:T(8,128)(2,1)S(1)}, u32[]{:S(2)}, u32[]{:S(2)}) collective-permute-start(bf16[9,16,256]{2,1,0:T(8,128)(2,1)S(1)} %get-tuple-element.79), channel_id=1, source_target_pairs={{0,1},{1,0},{2,3},{3,2},{4,5},{5,4},{6,7},{7,6},{8,9},{9,8},{10,11... | collective-permute-start | bytes 221192 | tf_op jit(solution)/shard_map/ppermute | solution.py:464
  4.5 0.7 collective-permute-start.11
  5.2 0.7 clamp_bitcast_fusion.dst_ref.table_ref
  5.9 0.1 copy.19
  6.0 0.3 collective-permute-done.10.rest_0_
  6.2 0.0 collective-permute-done.11.rest_1_
  6.3 3.5 %collective-permute-start.12 = (bf16[9,16,256]{2,1,0:T(8,128)(2,1)S(1)}, bf16[9,16,256]{2,1,0:T(8,128)(2,1)S(1)}, u32[]{:S(2)}, u32[]{:S(2)}) collective-permute-start(bf16[9,16,256]{2,1,0:T(8,128)(2,1)S(1)} %maximum_maximum_fusion), channel_id=1, source_target_pairs={{0,32},{32,0},{1,33},{33,1},{2,34},{34,2},{3,35},{35,3},{4,36},{36... | collective-permute-start | bytes 221192 | tf_op jit(solution)/shard_map/ppermute | solution.py:473
  9.8 1.9 %collective-permute-start.13 = (bf16[9,16,256]{2,1,0:T(8,128)(2,1)S(1)}, bf16[9,16,256]{2,1,0:T(8,128)(2,1)S(1)}, u32[]{:S(2)}, u32[]{:S(2)}) collective-permute-start(bf16[9,16,256]{2,1,0:T(8,128)(2,1)S(1)} %maximum_maximum_fusion.1), channel_id=1, source_target_pairs={{32,64},{96,128},{160,192},{64,32},{128,96},{192,160},{33,65},{97,... | collective-permute-start | bytes 221192 | tf_op jit(solution)/shard_map/ppermute | solution.py:471
  11.7 1.9 %shard_map.83 = (bf16[8,4,16,1152]{3,2,1,0:T(8,128)(2,1)S(1)}, bf16[8,4,16,1152]{3,2,1,0:T(8,128)(2,1)S(1)}, bf16[49,64,128]{2,1,0:T(8,128)(2,1)S(1)}, bf16[49,64,128]{2,1,0:T(8,128)(2,1)S(1)}) custom-call(s32[8,27]{1,0:T(8,128)S(1)} %clamp_bitcast_fusion.dst_ref.table_ref, bf16[9,64,128]{2,1,0:T(8,128)(2,1)S(1)} %get-tuple-element.81.features_ref, ...), custom_call_target="tpu_custom_call" | custom-call | flops 905969664 | bytes 4000000 | tf_op jit(solution)/shard_map/pallas_call | solution.py:300
  13.5 0.0 collective-permute-done.12.rest_0_
  13.6 1.9 %collective-permute-done.13.rest_1_ = bf16[9,16,256]{2,1,0:T(8,128)(2,1)S(1)} collective-permute-done((bf16[9,16,256]{2,1,0:T(8,128)(2,1)S(1)}, bf16[9,16,256]{2,1,0:T(8,128)(2,1)S(1)}, u32[]{:S(2)}, u32[]{:S(2)}) %collective-permute-start.13) | collective-permute-done | bytes 73760 | tf_op jit(solution)/shard_map/ppermute | solution.py:471
  15.4 0.0 copy-start.3
  15.4 1.6 %shard_map.84 = (bf16[4,28,16,128]{3,2,1,0:T(8,128)(2,1)S(1)}, f32[4,28,16,128]{3,2,1,0:T(8,128)S(1)}, bf16[8,2,16,1152]{3,2,1,0:T(8,128)(2,1)S(1)}, bf16[49,64,128]{2,1,0:T(8,128)(2,1)S(1)}) custom-call(s32[8,27]{1,0:T(8,128)S(1)} %clamp_bitcast_fusion.dst_ref.table_ref, ...), custom_call_target="tpu_custom_call", output_to_operand_aliasing={{3}: (3, {})} | custom-call | flops 905969664 | bytes 4000000 | tf_op jit(solution)/shard_map/pallas_call | solution.py:311
  17.1 0.1 collective-permute-start.14
  17.2 0.0 copy-done.3
  17.2 1.1 %shard_map.85 = bf16[8,64,128]{2,1,0:T(8,128)(2,1)S(1)} custom-call(bf16[8,4,16,1152]{3,2,1,0:T(8,128)(2,1)S(1)} %get-tuple-element.86.mid, bf16[8,2,16,1152]{3,2,1,0:T(8,128)(2,1)S(1)} %get-tuple-element.93.edge, bf16[27,128,128]{2,1,0:T(8,128)(2,1)S(1)} %copy-done.3), custom_call_target="tpu_custom_call" | custom-call | flops 905969664 | bytes 4000000 | tf_op jit(solution)/shard_map/pallas_call | solution.py:340
  18.3 1.1 %shard_map.86 = (bf16[8,2,16,1152]{3,2,1,0:T(8,128)(2,1)S(1)}, bf16[49,64,128]{2,1,0:T(8,128)(2,1)S(1)}) custom-call(s32[8,27]{1,0:T(8,128)S(1)} %clamp_bitcast_fusion.dst_ref.table_ref, bf16[49,64,128]{2,1,0:T(8,128)(2,1)S(1)} %get-tuple-element.94._, bf16[9,16,256]{2,1,0:T(8,128)(2,1)S(1)} %collective-permute-done.12.rest_0_, ...), custom_call_target="tpu_custom_call", output_to_operand_aliasing={{1}: (1, {})} | custom-call | flops 905969664 | bytes 4000000 | tf_op jit(solution)/shard_map/pallas_call | solution.py:328
  19.4 0.0 collective-permute-done.14
  19.4 0.1 add_convert_fusion.1
  19.5 21.3 %all_to_all.30 = bf16[16,7,16,128]{3,2,1,0:T(8,128)(2,1)S(1)} all-to-all(bf16[16,7,16,128]{3,2,1,0:T(8,128)(2,1)S(1)} %bitcast.17), channel_id=1, replica_groups=mesh['x'=4,'c'=2,'y'=4,'z'=8] {'x','y'}, dimensions={0} | all-to-all | bytes 917504 | tf_op jit(solution)/shard_map/all_to_all | solution.py:407
  40.9 0.1 convert_reduce_fusion.1
  41.1 14.9 %all_to_all.31 = f16[8,8,16,128]{3,2,1,0:T(8,128)(2,1)S(1)} all-to-all(f16[8,8,16,128]{3,2,1,0:T(8,128)(2,1)S(1)} %broadcast_in_dim.13), channel_id=1, replica_groups=mesh['x'=4,'c'=2,'y'=4,'z'=8] {'z'}, dimensions={0} | all-to-all | bytes 524288 | tf_op jit(solution)/shard_map/all_to_all | solution.py:413
  56.1 0.1 broadcast_in_dim.14
  56.1 11.6 %all_to_all.32 = bf16[16,7,16,128]{3,2,1,0:T(8,128)(2,1)S(1)} all-to-all(bf16[16,7,16,128]{3,2,1,0:T(8,128)(2,1)S(1)} %broadcast_in_dim.14), channel_id=1, replica_groups=mesh['x'=4,'c'=2,'y'=4,'z'=8] {'x','y'}, dimensions={0} | all-to-all | bytes 917504 | tf_op jit(solution)/shard_map/all_to_all | solution.py:417
  67.8 5.0 %collective-permute-start.15 = (bf16[4,28,16,128]{3,2,1,0:T(8,128)(2,1)S(1)}, bf16[4,28,16,128]{3,2,1,0:T(8,128)(2,1)S(1)}, u32[]{:S(2)}, u32[]{:S(2)}) collective-permute-start(bf16[4,28,16,128]{3,2,1,0:T(8,128)(2,1)S(1)} %bitcast.19), channel_id=1, source_target_pairs={{0,32},{32,0},{1,33},{33,1},{2,34},{34,2},{3,35},{35,3},{4,36},{36... | collective-permute-start | bytes 1376264 | tf_op jit(solution)/shard_map/ppermute | solution.py:358
  72.8 0.0 copy-start
  72.8 0.0 copy-start.1
  72.8 0.0 copy-start.2
  72.8 1.1 %shard_map.87 = bf16[8,64,128]{2,1,0:T(8,128)(2,1)S(1)} custom-call(bf16[8,4,16,1152]{3,2,1,0:T(8,128)(2,1)S(1)} %get-tuple-element.97.mid, bf16[8,2,16,1152]{3,2,1,0:T(8,128)(2,1)S(1)} %get-tuple-element.98.edge, bf16[27,128,128]{2,1,0:T(8,128)(2,1)S(1)} %copy-done.3), custom_call_target="tpu_custom_call" | custom-call | flops 905969664 | bytes 4000000 | tf_op jit(solution)/shard_map/pallas_call | solution.py:340
  73.9 0.5 slice.36
  75.1 0.0 collective-permute-done.15
  75.1 0.0 copy-done
  75.1 0.0 copy-done.1
  75.1 0.0 copy-done.2
  75.1 1.6 %conditional.1 = ((bf16[8,64,128]{2,1,0:T(8,128)(2,1)}, bf16[8,64,128]{2,1,0:T(8,128)(2,1)}, f32[27,128,128]{2,1,0:T(8,128)})) conditional(s32[]{:T(128)} %bitcast.10, (bf16[4,28,16,128]{3,2,1,0:T(8,128)(2,1)S(1)}, bf16[4,28,16,128]{3,2,1,0:T(8,128)(2,1)S(1)}, bf16[8,64,128]{2,1,0:T(8,128)(2,1)S(1)}, bf16[8,64,128]{2,1,0:T(8,128)(2,1)S(1)}) %tuple.36, ...), branch_computations={%region_3.4_spmd, %region_4.8_spmd} | conditional | flops 4531463168 | bytes 36206744 | solution.py:487
  75.1 1.4 %branch_0_fun.1 = (bf16[8,64,128]{2,1,0:T(8,128)(2,1)}, bf16[8,64,128]{2,1,0:T(8,128)(2,1)}, f32[27,128,128]{2,1,0:T(8,128)}) custom-call(bf16[4,28,16,128]{3,2,1,0:T(8,128)(2,1)S(1)} %get-tuple-element.24.own_ref, bf16[4,28,16,128]{3,2,1,0:T(8,128)(2,1)S(1)} %get-tuple-element.25.other_ref, bf16[8,64,128]{2,1,0:T(8,128)(2,1)S(1)} %get-tuple-element.26.outputs_ref, ...), custom_call_target="tpu_custom_call" | custom-call | tf_op jit(solution)/shard_map/cond/branch_0_fun/pallas_call | solution.py:443
  (16 shorter events, 0.3 us)
Async XLA Ops:
  1.9 4.3 %collective-permute-start.10 = (bf16[9,16,256]{2,1,0:T(8,128)(2,1)S(1)}, bf16[9,16,256]{2,1,0:T(8,128)(2,1)S(1)}, u32[]{:S(2)}, u32[]{:S(2)}) collective-permute-start(bf16[9,16,256]{2,1,0:T(8,128)(2,1)S(1)} %get-tuple-element.79), channel_id=1, source_target_pairs={{0,1},{1,0},{2,3},{3,2},{4,5},{5,4},{6,7},{7,6},{8,9},{9,8},{10,11... | collective-permute-start | bytes 221192 | tf_op jit(solution)/shard_map/ppermute | solution.py:464
  4.5 1.7 %collective-permute-start.11 = (bf16[9,16,256]{2,1,0:T(8,128)(2,1)S(1)}, bf16[9,16,256]{2,1,0:T(8,128)(2,1)S(1)}, u32[]{:S(2)}, u32[]{:S(2)}) collective-permute-start(bf16[9,16,256]{2,1,0:T(8,128)(2,1)S(1)} %get-tuple-element.80), channel_id=1, source_target_pairs={{1,2},{2,1},{3,4},{4,3},{5,6},{6,5},{7,8},{8,7},{9,10},{10,9},{11,... | collective-permute-start | bytes 221192 | tf_op jit(solution)/shard_map/ppermute | solution.py:463
  6.3 7.3 %collective-permute-start.12 = (bf16[9,16,256]{2,1,0:T(8,128)(2,1)S(1)}, bf16[9,16,256]{2,1,0:T(8,128)(2,1)S(1)}, u32[]{:S(2)}, u32[]{:S(2)}) collective-permute-start(bf16[9,16,256]{2,1,0:T(8,128)(2,1)S(1)} %maximum_maximum_fusion), channel_id=1, source_target_pairs={{0,32},{32,0},{1,33},{33,1},{2,34},{34,2},{3,35},{35,3},{4,36},{36... | collective-permute-start | bytes 221192 | tf_op jit(solution)/shard_map/ppermute | solution.py:473
  9.8 5.7 %collective-permute-start.13 = (bf16[9,16,256]{2,1,0:T(8,128)(2,1)S(1)}, bf16[9,16,256]{2,1,0:T(8,128)(2,1)S(1)}, u32[]{:S(2)}, u32[]{:S(2)}) collective-permute-start(bf16[9,16,256]{2,1,0:T(8,128)(2,1)S(1)} %maximum_maximum_fusion.1), channel_id=1, source_target_pairs={{32,64},{96,128},{160,192},{64,32},{128,96},{192,160},{33,65},{97,... | collective-permute-start | bytes 221192 | tf_op jit(solution)/shard_map/ppermute | solution.py:471
  15.4 1.7 %copy-start.3 = (bf16[27,128,128]{2,1,0:T(8,128)(2,1)S(1)}, bf16[27,128,128]{2,1,0:T(8,128)(2,1)}, u32[]{:S(2)}) copy-start(bf16[27,128,128]{2,1,0:T(8,128)(2,1)} %weights_ref.3) | copy-start | bytes 2654212
  17.1 2.3 %collective-permute-start.14 = (bf16[4,28,16,128]{3,2,1,0:T(8,128)(2,1)S(1)}, bf16[4,28,16,128]{3,2,1,0:T(8,128)(2,1)S(1)}, u32[]{:S(2)}, u32[]{:S(2)}) collective-permute-start(bf16[4,28,16,128]{3,2,1,0:T(8,128)(2,1)S(1)} %get-tuple-element.92), channel_id=1, source_target_pairs={{0,32},{32,0},{1,33},{33,1},{2,34},{34,2},{3,35},{35,3},{4,36},{36... | collective-permute-start | bytes 1376264 | tf_op jit(solution)/shard_map/ppermute | solution.py:353
  67.8 7.3 %collective-permute-start.15 = (bf16[4,28,16,128]{3,2,1,0:T(8,128)(2,1)S(1)}, bf16[4,28,16,128]{3,2,1,0:T(8,128)(2,1)S(1)}, u32[]{:S(2)}, u32[]{:S(2)}) collective-permute-start(bf16[4,28,16,128]{3,2,1,0:T(8,128)(2,1)S(1)} %bitcast.19), channel_id=1, source_target_pairs={{0,32},{32,0},{1,33},{33,1},{2,34},{34,2},{3,35},{35,3},{4,36},{36... | collective-permute-start | bytes 1376264 | tf_op jit(solution)/shard_map/ppermute | solution.py:358
  72.8 2.3 %copy-start = (bf16[8,64,128]{2,1,0:T(8,128)(2,1)S(1)}, bf16[8,64,128]{2,1,0:T(8,128)(2,1)}, u32[]{:S(2)}) copy-start(bf16[8,64,128]{2,1,0:T(8,128)(2,1)} %features_ref.1) | copy-start | bytes 393220
  72.8 2.3 %copy-start.1 = (bf16[8,64,128]{2,1,0:T(8,128)(2,1)S(1)}, bf16[8,64,128]{2,1,0:T(8,128)(2,1)}, u32[]{:S(2)}) copy-start(bf16[8,64,128]{2,1,0:T(8,128)(2,1)} %cotangent_ref.1) | copy-start | bytes 393220
  72.8 2.3 %copy-start.2 = (s32[40]{0:T(128)S(1)}, s32[40]{0:T(128)}, u32[]{:S(2)}) copy-start(s32[40]{0:T(128)} %recv_slot_ref.1) | copy-start | bytes 484

commit v11 on v10

--- a/solution.py
+++ b/solution.py
@@ -226,48 +226,57 @@
     return planes.reshape(SLOTS * VOXELS, WIDE)
 
 
-def mid_kernel(fill, unroll, count, dst_ref, features_ref, cotangent_ref, *rest):
+def store_products(flipped_ref, tap, first, send_ref, keep_ref):
+    core = lax.axis_index("c")
+    half = CHANNELS // 2
+    flipped = jnp.concatenate((flipped_ref[1 - core], flipped_ref[core]), axis=0)
+    part = jnp.dot(flipped, tap, preferred_element_type=jnp.float32)
+    for number in range(9):
+        block = part[:, number * CHANNELS : (number + 1) * CHANNELS]
+        for quarter in range(4):
+            rows = slice(quarter * 16, quarter * 16 + 16)
+            send_ref[quarter, first + number] = block[:half][rows].astype(jnp.bfloat16)
+            keep_ref[quarter, first + number] = block[half:][rows]
+
+
+def grad_part(tap, weights_ref, side):
+    matrix = jnp.concatenate([weights_ref[26 - side * 9 - number] for number in range(9)], axis=1)
+    return lax.dot_general(tap, matrix, (((1,), (1,)), ((), ())), preferred_element_type=jnp.float32)
+
+
+def mid_kernel(fill, unroll, count, dst_ref, features_ref, cotangent_ref, flipped_ref, weights_ref, *rest):
     halos = rest[:count]
-    mid_f, mid_c, bricks_f, bricks_c = rest[count:]
+    mid_f, mid_c, bricks_f, bricks_c, send_ref, keep_ref, grad_ref = rest[count:]
     for kind, (own, bricks, mid) in enumerate(((features_ref, bricks_f, mid_f), (cotangent_ref, bricks_c, mid_c))):
         bricks[:SLOTS] = own[:SLOTS]
         for begin, end in ((SLOTS, SLOTS + STARTS[2]), (SLOTS + STARTS[4], SLOTS + HALO + 1)):
             bricks[begin:end] = jnp.zeros((end - begin, VOXELS, CHANNELS), jnp.bfloat16)
         fill(halos, slice(kind * CHANNELS, (kind + 1) * CHANNELS), bricks)
         build_taps(unroll, dst_ref, bricks, (1, 2, 3, 4), mid)
+    tap = mid_c[...].reshape(SLOTS * VOXELS, WIDE)
+    store_products(flipped_ref, tap, 0, send_ref, keep_ref)
+    grad_ref[...] = grad_part(tap, weights_ref, 1)
 
 
 def weight_kernel(fill, unroll, count, dst_ref, table_ref, mid, _, *rest):
     halos = rest[:count]
-    flipped_ref, send_ref, keep_ref, edge, bricks = rest[count:]
+    flipped_ref, send_mid, keep_mid, send_ref, keep_ref, edge, bricks = rest[count:]
     fill(halos, slice(CHANNELS, 2 * CHANNELS), bricks)
     build_taps(unroll, dst_ref, bricks, (0, PLANES - 1), edge)
-    core = lax.axis_index("c")
-    flipped = jnp.concatenate((flipped_ref[1 - core], flipped_ref[core]), axis=0)
-    half = CHANNELS // 2
-    for side in (1, 0, 2):
-        part = jnp.dot(flipped, taps_of(mid, edge, side), preferred_element_type=jnp.float32)
-        for number in range(9):
-            block = part[:, number * CHANNELS : (number + 1) * CHANNELS]
-            m = side * 9 + number
-            for quarter in range(4):
-                rows = slice(quarter * 16, quarter * 16 + 16)
-                send_ref[quarter, m] = block[:half][rows].astype(jnp.bfloat16)
-                keep_ref[quarter, m] = block[half:][rows]
+    send_ref[:, 9:18] = send_mid[...]
+    keep_ref[:, 9:18] = keep_mid[...]
+    for side in (0, 2):
+        store_products(flipped_ref, taps_of(mid, edge, side), side * 9, send_ref, keep_ref)
     flag = jnp.broadcast_to(out_of_place(table_ref[...]), (16, CHANNELS))
     for quarter in range(4):
         send_ref[quarter, 27] = flag.astype(jnp.bfloat16)
         keep_ref[quarter, 27] = flag
 
 
-def grad_kernel(mid, edge, weights_ref, grad_ref):
-    grad = None
-    for side in range(3):
-        matrix = jnp.concatenate([weights_ref[26 - side * 9 - number] for number in range(9)], axis=1)
-        part = lax.dot_general(
-            taps_of(mid, edge, side), matrix, (((1,), (1,)), ((), ())), preferred_element_type=jnp.float32
-        )
-        grad = part if grad is None else grad + part
+def grad_kernel(mid, edge, weights_ref, grad_mid, grad_ref):
+    grad = grad_mid[...]
+    for side in (0, 2):
+        grad = grad + grad_part(taps_of(mid, edge, side), weights_ref, side)
     grad_ref[...] = grad.astype(jnp.bfloat16).reshape(SLOTS, VOXELS, CHANNELS)
 
 
@@ -296,21 +305,26 @@
 COST = pl.CostEstimate(flops=4 * SLOTS * VOXELS * 27 * CHANNELS * CHANNELS, bytes_accessed=4_000_000, transcendentals=0)
 
 
-def mid_taps(fill, unroll, dst, own_f, own_c, halos):
+def mid_taps(fill, unroll, dst, own_f, own_c, halos, flipped, weights):
     return pl.pallas_call(
         functools.partial(mid_kernel, fill, unroll, len(halos)),
-        in_specs=[SMEM_SPEC] + [VMEM_SPEC] * (2 + len(halos)),
-        out_specs=[VMEM_SPEC] * 4,
-        out_shape=[MID_SHAPE, MID_SHAPE, ALL_BRICKS, ALL_BRICKS],
+        in_specs=[SMEM_SPEC] + [VMEM_SPEC] * (4 + len(halos)),
+        out_specs=[VMEM_SPEC] * 7,
+        out_shape=[
+            MID_SHAPE, MID_SHAPE, ALL_BRICKS, ALL_BRICKS,
+            jax.ShapeDtypeStruct((4, 9, 16, CHANNELS), jnp.bfloat16),
+            jax.ShapeDtypeStruct((4, 9, 16, CHANNELS), jnp.float32),
+            jax.ShapeDtypeStruct((SLOTS * VOXELS, CHANNELS), jnp.float32),
+        ],
         compiler_params=PARAMS,
         cost_estimate=COST,
-    )(dst, own_f, own_c, *halos)
-
-
-def weight_sums(fill, unroll, dst, mid, bricks, halos, flipped):
+    )(dst, own_f, own_c, flipped, weights, *halos)
+
+
+def weight_sums(fill, unroll, dst, mid, bricks, halos, flipped, send, keep):
     return pl.pallas_call(
         functools.partial(weight_kernel, fill, unroll, len(halos)),
-        in_specs=[SMEM_SPEC] + [VMEM_SPEC] * (4 + len(halos)),
+        in_specs=[SMEM_SPEC] + [VMEM_SPEC] * (6 + len(halos)),
         out_specs=[VMEM_SPEC] * 4,
         out_shape=[
             jax.ShapeDtypeStruct((4, ROWS_M, 16, CHANNELS), jnp.bfloat16),
@@ -321,7 +335,7 @@
         input_output_aliases={3: 3},
         compiler_params=PARAMS,
         cost_estimate=COST,
-    )(dst, dst, mid, bricks, *halos, flipped)
+    )(dst, dst, mid, bricks, *halos, flipped, send, keep)
 
 
 def feature_edges(fill, unroll, dst, bricks, halos):
@@ -336,22 +350,22 @@
     )(dst, bricks, *halos)[0]
 
 
-def product(kernel, mid, edge, weights):
+def product(kernel, *operands):
     return pl.pallas_call(
         kernel,
-        in_specs=[VMEM_SPEC] * 3,
+        in_specs=[VMEM_SPEC] * len(operands),
         out_specs=VMEM_SPEC,
         out_shape=BRICK_SHAPE,
         compiler_params=PARAMS,
         cost_estimate=COST,
-    )(mid, edge, weights)
+    )(*operands)
 
 
 def convolve(fill, unroll, dst, mids, halos, flipped, weights):
-    mid_f, mid_c, bricks_f, bricks_c = mids
-    send, keep, edge_c, _ = weight_sums(fill, unroll, dst, mid_c, bricks_c, halos, flipped)
+    mid_f, mid_c, bricks_f, bricks_c, send, keep, grad_mid = mids
+    send, keep, edge_c, _ = weight_sums(fill, unroll, dst, mid_c, bricks_c, halos, flipped, send, keep)
     arrived = lax.ppermute(send, "c", [(0, 1), (1, 0)])
-    input_grad = product(grad_kernel, mid_c, edge_c, weights)
+    input_grad = product(grad_kernel, mid_c, edge_c, weights, grad_mid)
     edge_f = feature_edges(fill, unroll, dst, bricks_f, halos)
     arrived, input_grad, edge_f = lax.optimization_barrier((arrived, input_grad, edge_f))
     own = sum_everywhere(arrived, keep)
@@ -471,13 +485,13 @@
     x_outer = lax.ppermute(relayed(to_outer, core), ("x", "c"), [(2 * x + 1, 2 * x + 2) for x in range(3)]
                            + [(2 * x + 2, 2 * x + 1) for x in range(3)])
     x_sibling = lax.ppermute(relayed(to_sibling, 1 - core), "c", [(0, 1), (1, 0)])
-    mids = mid_taps(fill_along_y, SLOTS, dst, own_f, own_c, (y_first, y_second))
+    mids = mid_taps(fill_along_y, SLOTS, dst, own_f, own_c, (y_first, y_second), flipped, weights)
     results = convolve(fill_along_x, SLOTS, dst, mids, (x_sibling, x_outer), flipped, weights)
 
     def with_whole_bricks(results):
         packets = pack_bricks(recv_slot, features, cotangent)
         halos = [pass_to(packet, -heading[0], -heading[1]) for packet, heading in zip(packets, DIRECTIONS)]
-        mids = mid_taps(fill_bricks, 1, dst, own_f, own_c, halos)
+        mids = mid_taps(fill_bricks, 1, dst, own_f, own_c, halos, flipped, weights)
         return spread_out(*convolve(fill_nothing, 1, dst, mids, (), flipped, weights))
 
     def as_they_are(results):

time: 77.2 us -> 77 us (level)
  no operation moved by 1% of the time
where the time goes in v11:
time: 77 us; the launch traced here: 76.7 us
  blocking collectives  47.9 us (62%)
  starting transfers between devices  13.7 us (18%)
  Pallas kernels  9.83 us (13%)
  between operations  1.71 us (2%)
  waiting for transfers between devices  1.51 us (2%)
  other arithmetic  1.05 us (1%)
  local copies, waits for them, and re-layouts  0.77 us (1%)
    all_to_all x1, blocking collectives, sum_everywhere(): parts = lax.all_to_all(parts, ('x', 'y'), 0, 0)  21.3 us
    all_to_all x1, blocking collectives, sum_everywhere(): lax.all_to_all(jnp.broadcast_to(share[None], (8,) + share.shape), 'z', 0, 0)  14.9 us
    all_to_all x1, blocking collectives, sum_everywhere(): lax.all_to_all(whole, ('x', 'y'), 0, 0).reshape(4, ROWS_M, 16, CHANNELS)  11.6 us
    ppermute x1, starting transfers between devices, convolve(): other = lax.ppermute(own, 'c', [(0, 1), (1, 0)])  5.05 us
    ppermute x1, starting transfers between devices, local(): lax.ppermute(relayed(to_sibling, 1 - core), 'c', [(0, 1), (1, 0)])  3.46 us
    ppermute x1, starting transfers between devices, local(): lax.ppermute(to_first, ('y', 'z'), [(gy, gy ^ 1) for gy in range(32)])  2.56 us
    pallas_call x1, Pallas kernels, mid_taps(): pl.pallas_call(functools.partial(mid_kernel, fill, unroll, len(halos)), i...  2.47 us
    ppermute x1, starting transfers between devices, local(): lax.ppermute(relayed(to_outer, core), ('x', 'c'), [(2 * x + 1, 2 * x + 2)...  1.91 us
  transfers between devices with their start and end apart: 6, of which 2 were waited for; matrix products, arithmetic and copies ran while one was open for 2% of the time, Pallas kernels for 7%

profile of v11, /device:TPU:1, one launch (start us, length us, event | category | flops | bytes accessed | tf_op | source)
XLA Modules:
  0.0 76.7 jit_solution(354665576096653185)
XLA Ops:
  0.6 0.0 copy-start.3
  0.6 1.4 %shard_map.82 = (bf16[9,16,256]{2,1,0:T(8,128)(2,1)S(1)}, bf16[9,16,256]{2,1,0:T(8,128)(2,1)S(1)}, bf16[8,16,256]{2,1,0:T(8,128)(2,1)S(1)}, bf16[8,16,256]{2,1,0...) custom-call(s32[40]{0:T(128)} %recv_slot_ref.1, bf16[8,64,128]{2,1,0:T(8,128)(2,1)} %features_ref.1, ...), custom_call_target="tpu_custom_call" | custom-call | tf_op jit(solution)/shard_map/pallas_call | solution.py:121
  2.0 2.6 %collective-permute-start.10 = (bf16[9,16,256]{2,1,0:T(8,128)(2,1)S(1)}, bf16[9,16,256]{2,1,0:T(8,128)(2,1)S(1)}, u32[]{:S(2)}, u32[]{:S(2)}) collective-permute-start(bf16[9,16,256]{2,1,0:T(8,128)(2,1)S(1)} %get-tuple-element.85), channel_id=1, source_target_pairs={{0,1},{1,0},{2,3},{3,2},{4,5},{5,4},{6,7},{7,6},{8,9},{9,8},{10,11... | collective-permute-start | bytes 221192 | tf_op jit(solution)/shard_map/ppermute | solution.py:478
  4.6 0.7 collective-permute-start.11
  5.3 0.7 clamp_bitcast_fusion.dst_ref.table_ref
  6.0 0.1 copy.19
  6.1 0.3 collective-permute-done.10.rest_0_
  6.3 0.0 collective-permute-done.11.rest_1_
  6.4 3.5 %collective-permute-start.12 = (bf16[9,16,256]{2,1,0:T(8,128)(2,1)S(1)}, bf16[9,16,256]{2,1,0:T(8,128)(2,1)S(1)}, u32[]{:S(2)}, u32[]{:S(2)}) collective-permute-start(bf16[9,16,256]{2,1,0:T(8,128)(2,1)S(1)} %maximum_maximum_fusion), channel_id=1, source_target_pairs={{0,32},{32,0},{1,33},{33,1},{2,34},{34,2},{3,35},{35,3},{4,36},{36... | collective-permute-start | bytes 221192 | tf_op jit(solution)/shard_map/ppermute | solution.py:487
  9.8 1.9 %collective-permute-start.13 = (bf16[9,16,256]{2,1,0:T(8,128)(2,1)S(1)}, bf16[9,16,256]{2,1,0:T(8,128)(2,1)S(1)}, u32[]{:S(2)}, u32[]{:S(2)}) collective-permute-start(bf16[9,16,256]{2,1,0:T(8,128)(2,1)S(1)} %maximum_maximum_fusion.1), channel_id=1, source_target_pairs={{32,64},{96,128},{160,192},{64,32},{128,96},{192,160},{33,65},{97,... | collective-permute-start | bytes 221192 | tf_op jit(solution)/shard_map/ppermute | solution.py:485
  11.8 0.0 copy-done.3
  11.8 2.5 %shard_map.83 = (bf16[8,4,16,1152]{3,2,1,0:T(8,128)(2,1)S(1)}, bf16[8,4,16,1152]{3,2,1,0:T(8,128)(2,1)S(1)}, bf16[49,64,128]{2,1,0:T(8,128)(2,1)S(1)}, bf16[49,6...) custom-call(s32[8,27]{1,0:T(8,128)S(1)} %clamp_bitcast_fusion.dst_re, ...), custom_call_target="tpu_custom_call" | custom-call | flops 905969664 | bytes 4000000 | tf_op jit(solution)/shard_map/pallas_call | solution.py:309
  14.3 0.0 collective-permute-done.12.rest_0_
  14.3 1.2 %collective-permute-done.13.rest_1_ = bf16[9,16,256]{2,1,0:T(8,128)(2,1)S(1)} collective-permute-done((bf16[9,16,256]{2,1,0:T(8,128)(2,1)S(1)}, bf16[9,16,256]{2,1,0:T(8,128)(2,1)S(1)}, u32[]{:S(2)}, u32[]{:S(2)}) %collective-permute-start.13) | collective-permute-done | bytes 73760 | tf_op jit(solution)/shard_map/ppermute | solution.py:485
  15.5 1.6 %shard_map.84 = (bf16[4,28,16,128]{3,2,1,0:T(8,128)(2,1)S(1)}, f32[4,28,16,128]{3,2,1,0:T(8,128)S(1)}, bf16[8,2,16,1152]{3,2,1,0:T(8,128)(2,1)S(1)}, bf16[49,64,128]{2,1,0:T(8,128)(2,1)S(1)}) custom-call(s32[8,27]{1,0:T(8,128)S(1)} %clamp_bitcast_fusion.dst_ref.table_ref, ...), custom_call_target="tpu_custom_call", output_to_operand_aliasing={{3}: (3, {})} | custom-call | flops 905969664 | bytes 4000000 | tf_op jit(solution)/shard_map/pallas_call | solution.py:325
  17.1 0.1 collective-permute-start.14
  17.2 0.8 %shard_map.85 = bf16[8,64,128]{2,1,0:T(8,128)(2,1)S(1)} custom-call(bf16[8,4,16,1152]{3,2,1,0:T(8,128)(2,1)S(1)} %get-tuple-element.93.mid, bf16[8,2,16,1152]{3,2,1,0:T(8,128)(2,1)S(1)} %get-tuple-element.101.edge, bf16[27,128,128]{2,1,0:T(8,128)(2,1)S(1)} %copy-done.3, f32[512,128]{1,0:T(8,128)S(1)} %get-tuple-element.102.grad_mid), custom_call_target="tpu_custom_call" | custom-call | flops 905969664 | bytes 4000000 | tf_op jit(solution)/shard_map/pallas_call | solution.py:354
  18.0 1.1 %shard_map.86 = (bf16[8,2,16,1152]{3,2,1,0:T(8,128)(2,1)S(1)}, bf16[49,64,128]{2,1,0:T(8,128)(2,1)S(1)}) custom-call(s32[8,27]{1,0:T(8,128)S(1)} %clamp_bitcast_fusion.dst_ref.table_ref, bf16[49,64,128]{2,1,0:T(8,128)(2,1)S(1)} %get-tuple-element.103._, bf16[9,16,256]{2,1,0:T(8,128)(2,1)S(1)} %collective-permute-done.12.rest_0_, ...), custom_call_target="tpu_custom_call", output_to_operand_aliasing={{1}: (1, {})} | custom-call | flops 905969664 | bytes 4000000 | tf_op jit(solution)/shard_map/pallas_call | solution.py:342
  19.1 0.0 collective-permute-done.14
  19.2 0.1 add_convert_fusion.1
  19.3 21.3 %all_to_all.30 = bf16[16,7,16,128]{3,2,1,0:T(8,128)(2,1)S(1)} all-to-all(bf16[16,7,16,128]{3,2,1,0:T(8,128)(2,1)S(1)} %bitcast.17), channel_id=1, replica_groups=mesh['x'=4,'c'=2,'y'=4,'z'=8] {'x','y'}, dimensions={0} | all-to-all | bytes 917504 | tf_op jit(solution)/shard_map/all_to_all | solution.py:421
  40.6 0.1 convert_reduce_fusion.1
  40.8 14.9 %all_to_all.31 = f16[8,8,16,128]{3,2,1,0:T(8,128)(2,1)S(1)} all-to-all(f16[8,8,16,128]{3,2,1,0:T(8,128)(2,1)S(1)} %broadcast_in_dim.13), channel_id=1, replica_groups=mesh['x'=4,'c'=2,'y'=4,'z'=8] {'z'}, dimensions={0} | all-to-all | bytes 524288 | tf_op jit(solution)/shard_map/all_to_all | solution.py:427
  55.8 0.1 broadcast_in_dim.14
  55.9 11.6 %all_to_all.32 = bf16[16,7,16,128]{3,2,1,0:T(8,128)(2,1)S(1)} all-to-all(bf16[16,7,16,128]{3,2,1,0:T(8,128)(2,1)S(1)} %broadcast_in_dim.14), channel_id=1, replica_groups=mesh['x'=4,'c'=2,'y'=4,'z'=8] {'x','y'}, dimensions={0} | all-to-all | bytes 917504 | tf_op jit(solution)/shard_map/all_to_all | solution.py:431
  67.5 5.0 %collective-permute-start.15 = (bf16[4,28,16,128]{3,2,1,0:T(8,128)(2,1)S(1)}, bf16[4,28,16,128]{3,2,1,0:T(8,128)(2,1)S(1)}, u32[]{:S(2)}, u32[]{:S(2)}) collective-permute-start(bf16[4,28,16,128]{3,2,1,0:T(8,128)(2,1)S(1)} %bitcast.19), channel_id=1, source_target_pairs={{0,32},{32,0},{1,33},{33,1},{2,34},{34,2},{3,35},{35,3},{4,36},{36... | collective-permute-start | bytes 1376264 | tf_op jit(solution)/shard_map/ppermute | solution.py:372
  72.6 0.0 copy-start
  72.6 0.0 copy-start.1
  72.6 0.0 copy-start.2
  72.6 1.1 %shard_map.87 = bf16[8,64,128]{2,1,0:T(8,128)(2,1)S(1)} custom-call(bf16[8,4,16,1152]{3,2,1,0:T(8,128)(2,1)S(1)} %get-tuple-element.106.mid, bf16[8,2,16,1152]{3,2,1,0:T(8,128)(2,1)S(1)} %get-tuple-element.107.edge, bf16[27,128,128]{2,1,0:T(8,128)(2,1)S(1)} %copy-done.3), custom_call_target="tpu_custom_call" | custom-call | flops 905969664 | bytes 4000000 | tf_op jit(solution)/shard_map/pallas_call | solution.py:354
  73.7 0.5 slice.36
  74.8 0.0 collective-permute-done.15
  74.9 0.0 copy-done
  74.9 0.0 copy-done.1
  74.9 0.0 copy-done.2
  74.9 1.6 %conditional.1 = ((bf16[8,64,128]{2,1,0:T(8,128)(2,1)}, bf16[8,64,128]{2,1,0:T(8,128)(2,1)}, f32[27,128,128]{2,1,0:T(8,128)})) conditional(s32[]{:T(128)} %bitcast.10, (bf16[4,28,16,128]{3,2,1,0:T(8,128)(2,1)S(1)}, bf16[4,28,16,128]{3,2,1,0:T(8,128)(2,1)S(1)}, bf16[8,64,128]{2,1,0:T(8,128)(2,1)S(1)}, bf16[8,64,128]{2,1,0:T(8,128)(2,1)S(1)}) %tuple.36, ...), branch_computations={%region_3.4_spmd, %region_4.8_spmd} | conditional | flops 4531463168 | bytes 36206744 | solution.py:501
  74.9 1.4 %branch_0_fun.1 = (bf16[8,64,128]{2,1,0:T(8,128)(2,1)}, bf16[8,64,128]{2,1,0:T(8,128)(2,1)}, f32[27,128,128]{2,1,0:T(8,128)}) custom-call(bf16[4,28,16,128]{3,2,1,0:T(8,128)(2,1)S(1)} %get-tuple-element.24.own_ref, bf16[4,28,16,128]{3,2,1,0:T(8,128)(2,1)S(1)} %get-tuple-element.25.other_ref, bf16[8,64,128]{2,1,0:T(8,128)(2,1)S(1)} %get-tuple-element.26.outputs_ref, ...), custom_call_target="tpu_custom_call" | custom-call | tf_op jit(solution)/shard_map/cond/branch_0_fun/pallas_call | solution.py:457
  (16 shorter events, 0.3 us)
Async XLA Ops:
  0.6 11.1 %copy-start.3 = (bf16[27,128,128]{2,1,0:T(8,128)(2,1)S(1)}, bf16[27,128,128]{2,1,0:T(8,128)(2,1)}, u32[]{:S(2)}) copy-start(bf16[27,128,128]{2,1,0:T(8,128)(2,1)} %weights_ref.5) | copy-start | bytes 2654212
  2.0 4.3 %collective-permute-start.10 = (bf16[9,16,256]{2,1,0:T(8,128)(2,1)S(1)}, bf16[9,16,256]{2,1,0:T(8,128)(2,1)S(1)}, u32[]{:S(2)}, u32[]{:S(2)}) collective-permute-start(bf16[9,16,256]{2,1,0:T(8,128)(2,1)S(1)} %get-tuple-element.85), channel_id=1, source_target_pairs={{0,1},{1,0},{2,3},{3,2},{4,5},{5,4},{6,7},{7,6},{8,9},{9,8},{10,11... | collective-permute-start | bytes 221192 | tf_op jit(solution)/shard_map/ppermute | solution.py:478
  4.6 1.7 %collective-permute-start.11 = (bf16[9,16,256]{2,1,0:T(8,128)(2,1)S(1)}, bf16[9,16,256]{2,1,0:T(8,128)(2,1)S(1)}, u32[]{:S(2)}, u32[]{:S(2)}) collective-permute-start(bf16[9,16,256]{2,1,0:T(8,128)(2,1)S(1)} %get-tuple-element.86), channel_id=1, source_target_pairs={{1,2},{2,1},{3,4},{4,3},{5,6},{6,5},{7,8},{8,7},{9,10},{10,9},{11,... | collective-permute-start | bytes 221192 | tf_op jit(solution)/shard_map/ppermute | solution.py:477
  6.4 7.9 %collective-permute-start.12 = (bf16[9,16,256]{2,1,0:T(8,128)(2,1)S(1)}, bf16[9,16,256]{2,1,0:T(8,128)(2,1)S(1)}, u32[]{:S(2)}, u32[]{:S(2)}) collective-permute-start(bf16[9,16,256]{2,1,0:T(8,128)(2,1)S(1)} %maximum_maximum_fusion), channel_id=1, source_target_pairs={{0,32},{32,0},{1,33},{33,1},{2,34},{34,2},{3,35},{35,3},{4,36},{36... | collective-permute-start | bytes 221192 | tf_op jit(solution)/shard_map/ppermute | solution.py:487
  9.8 5.7 %collective-permute-start.13 = (bf16[9,16,256]{2,1,0:T(8,128)(2,1)S(1)}, bf16[9,16,256]{2,1,0:T(8,128)(2,1)S(1)}, u32[]{:S(2)}, u32[]{:S(2)}) collective-permute-start(bf16[9,16,256]{2,1,0:T(8,128)(2,1)S(1)} %maximum_maximum_fusion.1), channel_id=1, source_target_pairs={{32,64},{96,128},{160,192},{64,32},{128,96},{192,160},{33,65},{97,... | collective-permute-start | bytes 221192 | tf_op jit(solution)/shard_map/ppermute | solution.py:485
  17.1 2.0 %collective-permute-start.14 = (bf16[4,28,16,128]{3,2,1,0:T(8,128)(2,1)S(1)}, bf16[4,28,16,128]{3,2,1,0:T(8,128)(2,1)S(1)}, u32[]{:S(2)}, u32[]{:S(2)}) collective-permute-start(bf16[4,28,16,128]{3,2,1,0:T(8,128)(2,1)S(1)} %get-tuple-element.100), channel_id=1, source_target_pairs={{0,32},{32,0},{1,33},{33,1},{2,34},{34,2},{3,35},{35,3},{4,36},{36... | collective-permute-start | bytes 1376264 | tf_op jit(solution)/shard_map/ppermute | solution.py:367
  67.5 7.3 %collective-permute-start.15 = (bf16[4,28,16,128]{3,2,1,0:T(8,128)(2,1)S(1)}, bf16[4,28,16,128]{3,2,1,0:T(8,128)(2,1)S(1)}, u32[]{:S(2)}, u32[]{:S(2)}) collective-permute-start(bf16[4,28,16,128]{3,2,1,0:T(8,128)(2,1)S(1)} %bitcast.19), channel_id=1, source_target_pairs={{0,32},{32,0},{1,33},{33,1},{2,34},{34,2},{3,35},{35,3},{4,36},{36... | collective-permute-start | bytes 1376264 | tf_op jit(solution)/shard_map/ppermute | solution.py:372
  72.6 2.3 %copy-start = (bf16[8,64,128]{2,1,0:T(8,128)(2,1)S(1)}, bf16[8,64,128]{2,1,0:T(8,128)(2,1)}, u32[]{:S(2)}) copy-start(bf16[8,64,128]{2,1,0:T(8,128)(2,1)} %features_ref.1) | copy-start | bytes 393220
  72.6 2.3 %copy-start.1 = (bf16[8,64,128]{2,1,0:T(8,128)(2,1)S(1)}, bf16[8,64,128]{2,1,0:T(8,128)(2,1)}, u32[]{:S(2)}) copy-start(bf16[8,64,128]{2,1,0:T(8,128)(2,1)} %cotangent_ref.1) | copy-start | bytes 393220
  72.6 2.3 %copy-start.2 = (s32[40]{0:T(128)S(1)}, s32[40]{0:T(128)}, u32[]{:S(2)}) copy-start(s32[40]{0:T(128)} %recv_slot_ref.1) | copy-start | bytes 484

commit v12 on v11

--- a/solution.py
+++ b/solution.py
@@ -62,7 +62,7 @@
     return where_equal(column + vy * PLANE, order * 8 + (row >> 6) * 4 + (row & 3) + side * 3 * PLANE)
 
 
-def pack_layers_kernel(recv_slot_ref, features_ref, cotangent_ref, to_first, to_second, to_sibling, to_outer,
+def pack_layers_kernel(recv_slot_ref, features_ref, cotangent_ref, mine, theirs, to_outer,
                        own_f, own_c, sides, slot_ref, sems):
     bricks = (own_f, own_c)
     copies = [
@@ -97,7 +97,8 @@
         packet[position, :, :CHANNELS] = source[0][slot, rows]
         packet[position, :, CHANNELS:] = source[1][slot, rows]
 
-    for packet, up in ((to_first, 1 - odd), (to_second, odd)):
+    turn = odd ^ core
+    for packet, up in ((mine, 1 - turn), (theirs, turn)):
         begin = pl.multiple_of(up * PLANE, PLANE)
         for position in range(SLOTS):
             put(packet, position, STARTS[2] + up * LENGTHS[2] + position, (sides.at[0], sides.at[1]), begin)
@@ -109,10 +110,10 @@
             for number in range(1, 4):
                 tile = tile + sides[kind, slots[number], rows] * masks[number]
             packet[SLOTS, :, kind * CHANNELS : (kind + 1) * CHANNELS] = tile
-    for packet, up in ((to_sibling, 1 - core), (to_outer, core)):
+    for packet, first, up in ((theirs, SLOTS + 1, 1 - core), (to_outer, 0, core)):
         begin = pl.multiple_of(up * (VOXELS - PLANE), PLANE)
         for position in range(LENGTHS[0]):
-            put(packet, position, up * LENGTHS[0] + position, bricks, begin)
+            put(packet, first + position, up * LENGTHS[0] + position, bricks, begin)
 
 
 def pack_layers(recv_slot, features, cotangent):
@@ -121,9 +122,9 @@
     return pl.pallas_call(
         pack_layers_kernel,
         in_specs=[hbm] * 3,
-        out_specs=[vmem] * 6,
+        out_specs=[vmem] * 5,
         out_shape=[
-            jax.ShapeDtypeStruct((length, PLANE, 2 * CHANNELS), jnp.bfloat16) for length in (SLOTS + 1, SLOTS + 1, SLOTS, SLOTS)
+            jax.ShapeDtypeStruct((length, PLANE, 2 * CHANNELS), jnp.bfloat16) for length in (SLOTS + 1, 2 * SLOTS + 1, SLOTS)
         ] + [jax.ShapeDtypeStruct((SLOTS + 1, VOXELS, CHANNELS), jnp.bfloat16)] * 2,
         scratch_shapes=[
             pltpu.VMEM((2, SLOTS + 1, 4 * PLANE, CHANNELS), jnp.bfloat16),
@@ -142,8 +143,8 @@
 
 
 def fill_along_y(halos, lanes, bricks):
-    odd = lax.axis_index("z") & 1
-    for faces, side in ((halos[0], odd), (halos[1], 1 - odd)):
+    turn = lax.axis_index("z") & 1 ^ lax.axis_index("c")
+    for faces, side in ((halos[0], turn), (halos[1], 1 - turn)):
         tiles = jnp.concatenate([faces[position, :, lanes] for position in range(SLOTS)], axis=1)
         whole = jnp.dot(expand_matrix(side), tiles, preferred_element_type=jnp.float32).astype(jnp.bfloat16)
         for position in range(SLOTS):
@@ -152,7 +153,8 @@
 
 
 def fill_along_x(halos, lanes, bricks):
-    core, odd = lax.axis_index("c"), lax.axis_index("z") & 1
+    core = lax.axis_index("c")
+    turn = lax.axis_index("z") & 1 ^ core
     both = ((halos[0], core), (halos[1], 1 - core))
     for packet, below in both:
         for position in range(SLOTS):
@@ -161,7 +163,7 @@
             for begin in range(0, VOXELS, PLANE):
                 bricks[target, begin : begin + PLANE] = tile
     tiles = jnp.concatenate([packet[SLOTS, :, lanes] for packet in halos], axis=1)
-    for order, side in ((0, odd), (1, 1 - odd)):
+    for order, side in ((0, 1 - turn), (1, turn)):
         whole = jnp.dot(
             expand_corner_matrix(order, side), tiles, preferred_element_type=jnp.float32
         ).astype(jnp.bfloat16)
@@ -471,21 +473,30 @@
     core = lax.axis_index("c")
     dst = jnp.clip(dst_index.T, 0, SLOTS + HALO)
 
-    to_first, to_second, to_sibling, to_outer, own_f, own_c = pack_layers(recv_slot, features, cotangent)
+    mine, theirs, to_outer, own_f, own_c = pack_layers(recv_slot, features, cotangent)
     flipped = jnp.transpose(own_f[:SLOTS].reshape(SLOTS * VOXELS, CHANNELS))
     flipped = flipped.reshape(2, CHANNELS // 2, SLOTS * VOXELS)
-    y_second = lax.ppermute(to_second, ("y", "z"), [(gy, ((gy + 1) ^ 1) - 1) for gy in range(1, 31)])
-    y_first = lax.ppermute(to_first, ("y", "z"), [(gy, gy ^ 1) for gy in range(32)])
-    y_first, y_second, dst, flipped = lax.optimization_barrier((y_first, y_second, dst, flipped))
-
-    def relayed(packet, up):
-        corners = [lax.dynamic_slice_in_dim(value[SLOTS:], 8 * up, 8, axis=1) for value in (y_first, y_second)]
-        return jnp.concatenate((packet, jnp.concatenate(corners, axis=1)), axis=0)
-
-    x_outer = lax.ppermute(relayed(to_outer, core), ("x", "c"), [(2 * x + 1, 2 * x + 2) for x in range(3)]
-                           + [(2 * x + 2, 2 * x + 1) for x in range(3)])
-    x_sibling = lax.ppermute(relayed(to_sibling, 1 - core), "c", [(0, 1), (1, 0)])
-    mids = mid_taps(fill_along_y, SLOTS, dst, own_f, own_c, (y_first, y_second), flipped, weights)
+    count = SLOTS + 1
+    from_sibling = lax.ppermute(theirs, "c", [(0, 1), (1, 0)])
+    pairs = [(gy, gy ^ 1) for gy in range(32)]
+    pairs += [(32 + gy, 32 + ((gy + 1) ^ 1) - 1) for gy in range(1, 31)]
+    along_y = lax.ppermute(jnp.concatenate((mine, from_sibling[:count]), axis=0), ("c", "y", "z"), pairs)
+    along_y, dst, flipped = lax.optimization_barrier((along_y, dst, flipped))
+    handed_on = lax.ppermute(
+        jnp.concatenate((along_y[count:], along_y[SLOTS:count]), axis=0), "c", [(0, 1), (1, 0)]
+    )
+    y_mine, y_other = along_y[:count], handed_on[:count]
+
+    def with_corners(faces, *corners):
+        rows = [lax.dynamic_slice_in_dim(value, 8 * core, 8, axis=1) for value in corners]
+        return jnp.concatenate((faces, jnp.concatenate(rows, axis=1)), axis=0)
+
+    x_outer = lax.ppermute(
+        with_corners(to_outer, y_mine[SLOTS:], y_other[SLOTS:]), ("x", "c"),
+        [(2 * x + 1, 2 * x + 2) for x in range(3)] + [(2 * x + 2, 2 * x + 1) for x in range(3)],
+    )
+    x_sibling = with_corners(from_sibling[count:], handed_on[count:], along_y[count + SLOTS :])
+    mids = mid_taps(fill_along_y, SLOTS, dst, own_f, own_c, (y_mine, y_other), flipped, weights)
     results = convolve(fill_along_x, SLOTS, dst, mids, (x_sibling, x_outer), flipped, weights)
 
     def with_whole_bricks(results):

time: 77 us -> 78.5 us (1.019)
  starting transfers between devices: 13.7 us -> 17.1 us
  blocking collectives: 47.9 us -> 45 us
  waiting for transfers between devices: 1.51 us -> 3.02 us
    ppermute x4, starting transfers between devices: 8.58 us -> 12.7 us  [the longest x1 6.75 us: local(): lax.ppermute(jnp.concatenate((along_y[count:], along_y[SLOTS:count]), axi...]
    all_to_all x1, blocking collectives: 21.3 us -> 17.8 us  [sum_everywhere(): parts = lax.all_to_all(parts, ('x', 'y'), 0, 0)]
    ppermute x4, waiting for transfers between devices: 1.5 us -> 3.01 us  [the longest x1 1.22 us: local(): lax.ppermute(with_corners(to_outer, y_mine[SLOTS:], y_other[SLOTS:]), ('x...]
    all_to_all x1, blocking collectives: 11.6 us -> 12.6 us  [sum_everywhere(): lax.all_to_all(whole, ('x', 'y'), 0, 0).reshape(4, ROWS_M, 16, CHANNELS)]
  transfers between devices with their start and end apart: 6 -> 6, of which waited for: 2 -> 3; matrix products, arithmetic and copies ran while one was open for 2% -> 1% of each run, Pallas kernels for 7% -> 7%
where the time goes in v12:
time: 78.5 us; the launch traced here: 78.2 us
  blocking collectives  45 us (57%)
  starting transfers between devices  17.1 us (22%)
  Pallas kernels  9.84 us (13%)
  waiting for transfers between devices  3.02 us (4%)
  between operations  1.78 us (2%)
  local copies, waits for them, and re-layouts  0.82 us (1%)
    all_to_all x1, blocking collectives, sum_everywhere(): parts = lax.all_to_all(parts, ('x', 'y'), 0, 0)  17.8 us
    all_to_all x1, blocking collectives, sum_everywhere(): lax.all_to_all(jnp.broadcast_to(share[None], (8,) + share.shape), 'z', 0, 0)  14.7 us
    all_to_all x1, blocking collectives, sum_everywhere(): lax.all_to_all(whole, ('x', 'y'), 0, 0).reshape(4, ROWS_M, 16, CHANNELS)  12.6 us
    ppermute x1, starting transfers between devices, local(): lax.ppermute(jnp.concatenate((along_y[count:], along_y[SLOTS:count]), axi...  6.75 us
    ppermute x1, starting transfers between devices, convolve(): other = lax.ppermute(own, 'c', [(0, 1), (1, 0)])  4.36 us
    ppermute x1, starting transfers between devices, local(): from_sibling = lax.ppermute(theirs, 'c', [(0, 1), (1, 0)])  3.32 us
    pallas_call x1, Pallas kernels, mid_taps(): pl.pallas_call(functools.partial(mid_kernel, fill, unroll, len(halos)), i...  2.47 us
    ppermute x1, starting transfers between devices, local(): lax.ppermute(with_corners(to_outer, y_mine[SLOTS:], y_other[SLOTS:]), ('x...  1.92 us
  transfers between devices with their start and end apart: 6, of which 3 were waited for; matrix products, arithmetic and copies ran while one was open for 1% of the time, Pallas kernels for 7%

profile of v12, /device:TPU:1, one launch (start us, length us, event | category | flops | bytes accessed | tf_op | source)
XLA Modules:
  0.0 78.2 jit_solution(4129972472472145536)
XLA Ops:
  0.6 0.0 copy-start.2
  0.6 0.0 copy-start.4
  0.7 1.4 %shard_map.82 = (bf16[9,16,256]{2,1,0:T(8,128)(2,1)S(1)}, bf16[17,16,256]{2,1,0:T(8,128)(2,1)S(1)}, bf16[8,16,256]{2,1,0:T(8,128)(2,1)S(1)}, bf16[9,64,128]{2,1,0:T(8,128)(2,1)S(1)}, bf16[9,64,128]{2,1,0:T(8,128)(2,1)S(1)}) custom-call(s32[40]{0:T(128)} %recv_slot_ref.1, bf16[8,64,128]{2,1,0:T(8,128)(2,1)} %features_ref.1, bf16[8,64,128]{2,1,0:T(8,128)(2,1)} %cotangent_ref.1), custom_call_target="tpu_custom_call" | custom-call | tf_op jit(solution)/shard_map/pallas_call | solution.py:122
  2.1 3.3 %collective-permute-start.10 = (bf16[17,16,256]{2,1,0:T(8,128)(2,1)S(1)}, bf16[17,16,256]{2,1,0:T(8,128)(2,1)S(1)}, u32[]{:S(2)}, u32[]{:S(2)}) collective-permute-start(bf16[17,16,256]{2,1,0:T(8,128)(2,1)S(1)} %get-tuple-element.84), channel_id=1, source_target_pairs={{0,32},{32,0},{1,33},{33,1},{2,34},{34,2},{3,35},{35,3},{4,36},{36... | collective-permute-start | bytes 417800 | tf_op jit(solution)/shard_map/ppermute | solution.py:480
  5.4 0.1 copy.19
  5.5 0.9 %collective-permute-done.10 = bf16[17,16,256]{2,1,0:T(8,128)(2,1)S(1)} collective-permute-done((bf16[17,16,256]{2,1,0:T(8,128)(2,1)S(1)}, bf16[17,16,256]{2,1,0:T(8,128)(2,1)S(1)}, u32[]{:S(2)}, u32[]{:S(2)}) %collective-permute-start.10) | collective-permute-done | bytes 139296 | tf_op jit(solution)/shard_map/ppermute | solution.py:480
  6.4 0.7 collective-permute-start.11
  7.1 0.0 copy-done.2
  7.1 0.0 collective-permute-done.11
  7.2 6.7 %collective-permute-start.12 = (bf16[10,16,256]{2,1,0:T(8,128)(2,1)S(1)}, bf16[10,16,256]{2,1,0:T(8,128)(2,1)S(1)}, u32[]{:S(2)}, u32[]{:S(2)}) collective-permute-start(bf16[10,16,256]{2,1,0:T(8,128)(2,1)S(1)} %pad_maximum_fusion.2), channel_id=1, source_target_pairs={{0,32},{32,0},{1,33},{33,1},{2,34},{34,2},{3,35},{35,3},{4,36},{36... | collective-permute-start | bytes 245768 | tf_op jit(solution)/shard_map/ppermute | solution.py:485
  13.9 0.9 %collective-permute-done.12 = bf16[10,16,256]{2,1,0:T(8,128)(2,1)S(1)} collective-permute-done((bf16[10,16,256]{2,1,0:T(8,128)(2,1)S(1)}, bf16[10,16,256]{2,1,0:T(8,128)(2,1)S(1)}, u32[]{:S(2)}, u32[]{:S(2)}) %collective-permute-start.12) | collective-permute-done | bytes 81952 | tf_op jit(solution)/shard_map/ppermute | solution.py:485
  14.9 1.9 %collective-permute-start.13 = (bf16[9,16,256]{2,1,0:T(8,128)(2,1)S(1)}, bf16[9,16,256]{2,1,0:T(8,128)(2,1)S(1)}, u32[]{:S(2)}, u32[]{:S(2)}) collective-permute-start(bf16[9,16,256]{2,1,0:T(8,128)(2,1)S(1)} %maximum_maximum_fusion.1), channel_id=1, source_target_pairs={{32,64},{96,128},{160,192},{64,32},{128,96},{192,160},{33,65},{97,... | collective-permute-start | bytes 221192 | tf_op jit(solution)/shard_map/ppermute | solution.py:494
  16.8 0.0 copy-done.4
  16.8 2.5 %shard_map.83 = (bf16[8,4,16,1152]{3,2,1,0:T(8,128)(2,1)S(1)}, bf16[8,4,16,1152]{3,2,1,0:T(8,128)(2,1)S(1)}, bf16[49,64,128]{2,1,0:T(8,128)(2,1)S(1)}, bf16[49,6...) custom-call(s32[8,27]{1,0:T(8,128)S(1)} %clamp_bitcast_fusion.dst_re, ...), custom_call_target="tpu_custom_call" | custom-call | flops 905969664 | bytes 4000000 | tf_op jit(solution)/shard_map/pallas_call | solution.py:311
  19.3 1.2 %collective-permute-done.13.rest_1_ = bf16[9,16,256]{2,1,0:T(8,128)(2,1)S(1)} collective-permute-done((bf16[9,16,256]{2,1,0:T(8,128)(2,1)S(1)}, bf16[9,16,256]{2,1,0:T(8,128)(2,1)S(1)}, u32[]{:S(2)}, u32[]{:S(2)}) %collective-permute-start.13) | collective-permute-done | bytes 73760 | tf_op jit(solution)/shard_map/ppermute | solution.py:494
  20.5 1.6 %shard_map.84 = (bf16[4,28,16,128]{3,2,1,0:T(8,128)(2,1)S(1)}, f32[4,28,16,128]{3,2,1,0:T(8,128)S(1)}, bf16[8,2,16,1152]{3,2,1,0:T(8,128)(2,1)S(1)}, bf16[49,64,128]{2,1,0:T(8,128)(2,1)S(1)}) custom-call(s32[8,27]{1,0:T(8,128)S(1)} %clamp_bitcast_fusion.dst_ref.table_ref, ...), custom_call_target="tpu_custom_call", output_to_operand_aliasing={{3}: (3, {})} | custom-call | flops 905969664 | bytes 4000000 | tf_op jit(solution)/shard_map/pallas_call | solution.py:327
  22.2 0.1 collective-permute-start.14
  22.3 0.8 shard_map.85
  23.0 1.1 %shard_map.86 = (bf16[8,2,16,1152]{3,2,1,0:T(8,128)(2,1)S(1)}, bf16[49,64,128]{2,1,0:T(8,128)(2,1)S(1)}) custom-call(s32[8,27]{1,0:T(8,128)S(1)} %clamp_bitcast_fusion.dst_ref.table_ref, bf16[49,64,128]{2,1,0:T(8,128)(2,1)S(1)} %get-tuple-element.99._, bf16[9,16,256]{2,1,0:T(8,128)(2,1)S(1)} %maximum_maximum_fusion.rest_0_, ...), custom_call_target="tpu_custom_call", output_to_operand_aliasing={{1}: (1, {})} | custom-call | flops 905969664 | bytes 4000000 | tf_op jit(solution)/shard_map/pallas_call | solution.py:344
  24.2 0.0 collective-permute-done.14
  24.2 0.1 add_convert_fusion.1
  24.3 17.8 %all_to_all.30 = bf16[16,7,16,128]{3,2,1,0:T(8,128)(2,1)S(1)} all-to-all(bf16[16,7,16,128]{3,2,1,0:T(8,128)(2,1)S(1)} %bitcast.17), channel_id=1, replica_groups=mesh['x'=4,'c'=2,'y'=4,'z'=8] {'x','y'}, dimensions={0} | all-to-all | bytes 917504 | tf_op jit(solution)/shard_map/all_to_all | solution.py:423
  42.1 0.1 convert_reduce_fusion.1
  42.3 14.7 %all_to_all.31 = f16[8,8,16,128]{3,2,1,0:T(8,128)(2,1)S(1)} all-to-all(f16[8,8,16,128]{3,2,1,0:T(8,128)(2,1)S(1)} %broadcast_in_dim.13), channel_id=1, replica_groups=mesh['x'=4,'c'=2,'y'=4,'z'=8] {'z'}, dimensions={0} | all-to-all | bytes 524288 | tf_op jit(solution)/shard_map/all_to_all | solution.py:429
  57.1 0.1 broadcast_in_dim.14
  57.2 12.6 %all_to_all.32 = bf16[16,7,16,128]{3,2,1,0:T(8,128)(2,1)S(1)} all-to-all(bf16[16,7,16,128]{3,2,1,0:T(8,128)(2,1)S(1)} %broadcast_in_dim.14), channel_id=1, replica_groups=mesh['x'=4,'c'=2,'y'=4,'z'=8] {'x','y'}, dimensions={0} | all-to-all | bytes 917504 | tf_op jit(solution)/shard_map/all_to_all | solution.py:433
  69.8 4.4 %collective-permute-start.15 = (bf16[4,28,16,128]{3,2,1,0:T(8,128)(2,1)S(1)}, bf16[4,28,16,128]{3,2,1,0:T(8,128)(2,1)S(1)}, u32[]{:S(2)}, u32[]{:S(2)}) collective-permute-start(bf16[4,28,16,128]{3,2,1,0:T(8,128)(2,1)S(1)} %bitcast.19), channel_id=1, source_target_pairs={{0,32},{32,0},{1,33},{33,1},{2,34},{34,2},{3,35},{35,3},{4,36},{36... | collective-permute-start | bytes 1376264 | tf_op jit(solution)/shard_map/ppermute | solution.py:374
  74.1 0.0 copy-start
  74.1 0.0 copy-start.1
  74.1 0.0 copy-start.3
  74.1 1.1 %shard_map.87 = bf16[8,64,128]{2,1,0:T(8,128)(2,1)S(1)} custom-call(bf16[8,4,16,1152]{3,2,1,0:T(8,128)(2,1)S(1)} %get-tuple-element.102.mid, bf16[8,2,16,1152]{3,2,1,0:T(8,128)(2,1)S(1)} %get-tuple-element.103.edge, bf16[27,128,128]{2,1,0:T(8,128)(2,1)S(1)} %copy-done.4), custom_call_target="tpu_custom_call" | custom-call | flops 905969664 | bytes 4000000 | tf_op jit(solution)/shard_map/pallas_call | solution.py:356
  75.2 0.5 slice.70
  76.4 0.0 collective-permute-done.15
  76.4 0.0 copy-done
  76.4 0.0 copy-done.1
  76.4 0.0 copy-done.3
  76.4 1.6 %conditional.1 = ((bf16[8,64,128]{2,1,0:T(8,128)(2,1)}, bf16[8,64,128]{2,1,0:T(8,128)(2,1)}, f32[27,128,128]{2,1,0:T(8,128)})) conditional(s32[]{:T(128)} %bitcast.10, (bf16[4,28,16,128]{3,2,1,0:T(8,128)(2,1)S(1)}, bf16[4,28,16,128]{3,2,1,0:T(8,128)(2,1)S(1)}, bf16[8,64,128]{2,1,0:T(8,128)(2,1)S(1)}, bf16[8,64,128]{2,1,0:T(8,128)(2,1)S(1)}) %tuple.35, ...), branch_computations={%region_3.4_spmd, %region_4.8_spmd} | conditional | flops 4531463168 | bytes 36206744 | solution.py:512
  76.4 1.4 %branch_0_fun.1 = (bf16[8,64,128]{2,1,0:T(8,128)(2,1)}, bf16[8,64,128]{2,1,0:T(8,128)(2,1)}, f32[27,128,128]{2,1,0:T(8,128)}) custom-call(bf16[4,28,16,128]{3,2,1,0:T(8,128)(2,1)S(1)} %get-tuple-element.24.own_ref, bf16[4,28,16,128]{3,2,1,0:T(8,128)(2,1)S(1)} %get-tuple-element.25.other_ref, bf16[8,64,128]{2,1,0:T(8,128)(2,1)S(1)} %get-tuple-element.26.outputs_ref, ...), custom_call_target="tpu_custom_call" | custom-call | tf_op jit(solution)/shard_map/cond/branch_0_fun/pallas_call | solution.py:459
  (26 shorter events, 0.3 us)
Async XLA Ops:
  0.6 6.4 %copy-start.2 = (s32[27,8]{0,1:T(8,128)S(1)}, s32[27,8]{0,1:T(8,128)}, u32[]{:S(2)}) copy-start(s32[27,8]{0,1:T(8,128)} %param.10) | copy-start | bytes 2596
  0.6 16.2 %copy-start.4 = (bf16[27,128,128]{2,1,0:T(8,128)(2,1)S(1)}, bf16[27,128,128]{2,1,0:T(8,128)(2,1)}, u32[]{:S(2)}) copy-start(bf16[27,128,128]{2,1,0:T(8,128)(2,1)} %weights_ref.5) | copy-start | bytes 2654212
  2.1 4.3 %collective-permute-start.10 = (bf16[17,16,256]{2,1,0:T(8,128)(2,1)S(1)}, bf16[17,16,256]{2,1,0:T(8,128)(2,1)S(1)}, u32[]{:S(2)}, u32[]{:S(2)}) collective-permute-start(bf16[17,16,256]{2,1,0:T(8,128)(2,1)S(1)} %get-tuple-element.84), channel_id=1, source_target_pairs={{0,32},{32,0},{1,33},{33,1},{2,34},{34,2},{3,35},{35,3},{4,36},{36... | collective-permute-start | bytes 417800 | tf_op jit(solution)/shard_map/ppermute | solution.py:480
  6.4 0.7 collective-permute-start.11
  7.2 7.7 %collective-permute-start.12 = (bf16[10,16,256]{2,1,0:T(8,128)(2,1)S(1)}, bf16[10,16,256]{2,1,0:T(8,128)(2,1)S(1)}, u32[]{:S(2)}, u32[]{:S(2)}) collective-permute-start(bf16[10,16,256]{2,1,0:T(8,128)(2,1)S(1)} %pad_maximum_fusion.2), channel_id=1, source_target_pairs={{0,32},{32,0},{1,33},{33,1},{2,34},{34,2},{3,35},{35,3},{4,36},{36... | collective-permute-start | bytes 245768 | tf_op jit(solution)/shard_map/ppermute | solution.py:485
  14.9 5.7 %collective-permute-start.13 = (bf16[9,16,256]{2,1,0:T(8,128)(2,1)S(1)}, bf16[9,16,256]{2,1,0:T(8,128)(2,1)S(1)}, u32[]{:S(2)}, u32[]{:S(2)}) collective-permute-start(bf16[9,16,256]{2,1,0:T(8,128)(2,1)S(1)} %maximum_maximum_fusion.1), channel_id=1, source_target_pairs={{32,64},{96,128},{160,192},{64,32},{128,96},{192,160},{33,65},{97,... | collective-permute-start | bytes 221192 | tf_op jit(solution)/shard_map/ppermute | solution.py:494
  22.2 2.0 %collective-permute-start.14 = (bf16[4,28,16,128]{3,2,1,0:T(8,128)(2,1)S(1)}, bf16[4,28,16,128]{3,2,1,0:T(8,128)(2,1)S(1)}, u32[]{:S(2)}, u32[]{:S(2)}) collective-permute-start(bf16[4,28,16,128]{3,2,1,0:T(8,128)(2,1)S(1)} %get-tuple-element.96), channel_id=1, source_target_pairs={{0,32},{32,0},{1,33},{33,1},{2,34},{34,2},{3,35},{35,3},{4,36},{36... | collective-permute-start | bytes 1376264 | tf_op jit(solution)/shard_map/ppermute | solution.py:369
  69.8 6.6 %collective-permute-start.15 = (bf16[4,28,16,128]{3,2,1,0:T(8,128)(2,1)S(1)}, bf16[4,28,16,128]{3,2,1,0:T(8,128)(2,1)S(1)}, u32[]{:S(2)}, u32[]{:S(2)}) collective-permute-start(bf16[4,28,16,128]{3,2,1,0:T(8,128)(2,1)S(1)} %bitcast.19), channel_id=1, source_target_pairs={{0,32},{32,0},{1,33},{33,1},{2,34},{34,2},{3,35},{35,3},{4,36},{36... | collective-permute-start | bytes 1376264 | tf_op jit(solution)/shard_map/ppermute | solution.py:374
  74.1 2.3 %copy-start = (bf16[8,64,128]{2,1,0:T(8,128)(2,1)S(1)}, bf16[8,64,128]{2,1,0:T(8,128)(2,1)}, u32[]{:S(2)}) copy-start(bf16[8,64,128]{2,1,0:T(8,128)(2,1)} %features_ref.1) | copy-start | bytes 393220
  74.1 2.3 %copy-start.1 = (bf16[8,64,128]{2,1,0:T(8,128)(2,1)S(1)}, bf16[8,64,128]{2,1,0:T(8,128)(2,1)}, u32[]{:S(2)}) copy-start(bf16[8,64,128]{2,1,0:T(8,128)(2,1)} %cotangent_ref.1) | copy-start | bytes 393220
  74.1 2.3 %copy-start.3 = (s32[40]{0:T(128)S(1)}, s32[40]{0:T(128)}, u32[]{:S(2)}) copy-start(s32[40]{0:T(128)} %recv_slot_ref.1) | copy-start | bytes 484

commit v13 on v11

--- a/solution.py
+++ b/solution.py
@@ -476,15 +476,15 @@
     flipped = flipped.reshape(2, CHANNELS // 2, SLOTS * VOXELS)
     y_second = lax.ppermute(to_second, ("y", "z"), [(gy, ((gy + 1) ^ 1) - 1) for gy in range(1, 31)])
     y_first = lax.ppermute(to_first, ("y", "z"), [(gy, gy ^ 1) for gy in range(32)])
-    y_first, y_second, dst, flipped = lax.optimization_barrier((y_first, y_second, dst, flipped))
+    y_second, y_first, dst, flipped = lax.optimization_barrier((y_second, y_first, dst, flipped))
 
     def relayed(packet, up):
         corners = [lax.dynamic_slice_in_dim(value[SLOTS:], 8 * up, 8, axis=1) for value in (y_first, y_second)]
         return jnp.concatenate((packet, jnp.concatenate(corners, axis=1)), axis=0)
 
+    x_sibling = lax.ppermute(relayed(to_sibling, 1 - core), "c", [(0, 1), (1, 0)])
     x_outer = lax.ppermute(relayed(to_outer, core), ("x", "c"), [(2 * x + 1, 2 * x + 2) for x in range(3)]
                            + [(2 * x + 2, 2 * x + 1) for x in range(3)])
-    x_sibling = lax.ppermute(relayed(to_sibling, 1 - core), "c", [(0, 1), (1, 0)])
     mids = mid_taps(fill_along_y, SLOTS, dst, own_f, own_c, (y_first, y_second), flipped, weights)
     results = convolve(fill_along_x, SLOTS, dst, mids, (x_sibling, x_outer), flipped, weights)
 

time: 77 us -> 75.9 us (0.986)
  blocking collectives: 47.9 us -> 44.8 us
  starting transfers between devices: 13.7 us -> 16.2 us
    ppermute x1, starting transfers between devices: 2.56 us -> 5.44 us  [local(): lax.ppermute(to_first, ('y', 'z'), [(gy, gy ^ 1) for gy in range(32)])]
    all_to_all x1, blocking collectives: 14.9 us -> 12.8 us  [sum_everywhere(): lax.all_to_all(jnp.broadcast_to(share[None], (8,) + share.shape), 'z', 0, 0)]
    ppermute x1, starting transfers between devices: 3.46 us -> 1.9 us  [local(): lax.ppermute(relayed(to_sibling, 1 - core), 'c', [(0, 1), (1, 0)])]
    ppermute x1, waiting for transfers between devices: 1.24 us -> 0.13 us  [local(): lax.ppermute(relayed(to_outer, core), ('x', 'c'), [(2 * x + 1, 2 * x + 2)...]
    ppermute x1, starting transfers between devices: 1.91 us -> 3.03 us  [local(): lax.ppermute(relayed(to_outer, core), ('x', 'c'), [(2 * x + 1, 2 * x + 2)...]
    all_to_all x1, blocking collectives: 21.3 us -> 20.4 us  [sum_everywhere(): parts = lax.all_to_all(parts, ('x', 'y'), 0, 0)]
where the time goes in v13:
time: 75.9 us; the launch traced here: 75.6 us
  blocking collectives  44.8 us (59%)
  starting transfers between devices  16.2 us (21%)
  Pallas kernels  9.83 us (13%)
  between operations  1.71 us (2%)
  other arithmetic  1.04 us (1%)
  waiting for transfers between devices  1.04 us (1%)
  local copies, waits for them, and re-layouts  0.77 us (1%)
    all_to_all x1, blocking collectives, sum_everywhere(): parts = lax.all_to_all(parts, ('x', 'y'), 0, 0)  20.4 us
    all_to_all x1, blocking collectives, sum_everywhere(): lax.all_to_all(jnp.broadcast_to(share[None], (8,) + share.shape), 'z', 0, 0)  12.8 us
    all_to_all x1, blocking collectives, sum_everywhere(): lax.all_to_all(whole, ('x', 'y'), 0, 0).reshape(4, ROWS_M, 16, CHANNELS)  11.6 us
    ppermute x1, starting transfers between devices, local(): lax.ppermute(to_first, ('y', 'z'), [(gy, gy ^ 1) for gy in range(32)])  5.44 us
    ppermute x1, starting transfers between devices, convolve(): other = lax.ppermute(own, 'c', [(0, 1), (1, 0)])  5.04 us
    ppermute x1, starting transfers between devices, local(): lax.ppermute(relayed(to_outer, core), ('x', 'c'), [(2 * x + 1, 2 * x + 2)...  3.03 us
    pallas_call x1, Pallas kernels, mid_taps(): pl.pallas_call(functools.partial(mid_kernel, fill, unroll, len(halos)), i...  2.47 us
    ppermute x1, starting transfers between devices, local(): lax.ppermute(relayed(to_sibling, 1 - core), 'c', [(0, 1), (1, 0)])  1.9 us
  transfers between devices with their start and end apart: 6, of which 2 were waited for; matrix products, arithmetic and copies ran while one was open for 2% of the time, Pallas kernels for 7%

profile of v13, /device:TPU:1, one launch (start us, length us, event | category | flops | bytes accessed | tf_op | source)
XLA Modules:
  0.0 75.6 jit_solution(17871917836035167321)
XLA Ops:
  0.6 0.0 copy-start.3
  0.6 1.4 %shard_map.82 = (bf16[9,16,256]{2,1,0:T(8,128)(2,1)S(1)}, bf16[9,16,256]{2,1,0:T(8,128)(2,1)S(1)}, bf16[8,16,256]{2,1,0:T(8,128)(2,1)S(1)}, bf16[8,16,256]{2,1,0...) custom-call(s32[40]{0:T(128)} %recv_slot_ref.1, bf16[8,64,128]{2,1,0:T(8,128)(2,1)} %features_ref.1, ...), custom_call_target="tpu_custom_call" | custom-call | tf_op jit(solution)/shard_map/pallas_call | solution.py:121
  2.0 0.7 collective-permute-start.10
  2.7 5.4 %collective-permute-start.11 = (bf16[9,16,256]{2,1,0:T(8,128)(2,1)S(1)}, bf16[9,16,256]{2,1,0:T(8,128)(2,1)S(1)}, u32[]{:S(2)}, u32[]{:S(2)}) collective-permute-start(bf16[9,16,256]{2,1,0:T(8,128)(2,1)S(1)} %get-tuple-element.86), channel_id=1, source_target_pairs={{0,1},{1,0},{2,3},{3,2},{4,5},{5,4},{6,7},{7,6},{8,9},{9,8},{10,11... | collective-permute-start | bytes 221192 | tf_op jit(solution)/shard_map/ppermute | solution.py:478
  8.1 0.7 clamp_bitcast_fusion.dst_ref.table_ref
  8.9 0.1 copy.19
  9.0 0.0 collective-permute-done.10.rest_1_
  9.0 0.9 %collective-permute-done.11.rest_0_ = bf16[9,16,256]{2,1,0:T(8,128)(2,1)S(1)} collective-permute-done((bf16[9,16,256]{2,1,0:T(8,128)(2,1)S(1)}, bf16[9,16,256]{2,1,0:T(8,128)(2,1)S(1)}, u32[]{:S(2)}, u32[]{:S(2)}) %collective-permute-start.11) | collective-permute-done | bytes 73760 | tf_op jit(solution)/shard_map/ppermute | solution.py:478
  9.9 1.9 %collective-permute-start.12 = (bf16[9,16,256]{2,1,0:T(8,128)(2,1)S(1)}, bf16[9,16,256]{2,1,0:T(8,128)(2,1)S(1)}, u32[]{:S(2)}, u32[]{:S(2)}) collective-permute-start(bf16[9,16,256]{2,1,0:T(8,128)(2,1)S(1)} %maximum_maximum_fusion), channel_id=1, source_target_pairs={{0,32},{32,0},{1,33},{33,1},{2,34},{34,2},{3,35},{35,3},{4,36},{36... | collective-permute-start | bytes 221192 | tf_op jit(solution)/shard_map/ppermute | solution.py:485
  11.8 3.0 %collective-permute-start.13 = (bf16[9,16,256]{2,1,0:T(8,128)(2,1)S(1)}, bf16[9,16,256]{2,1,0:T(8,128)(2,1)S(1)}, u32[]{:S(2)}, u32[]{:S(2)}) collective-permute-start(bf16[9,16,256]{2,1,0:T(8,128)(2,1)S(1)} %maximum_maximum_fusion.1), channel_id=1, source_target_pairs={{32,64},{96,128},{160,192},{64,32},{128,96},{192,160},{33,65},{97,... | collective-permute-start | bytes 221192 | tf_op jit(solution)/shard_map/ppermute | solution.py:486
  14.9 0.0 copy-done.3
  14.9 2.5 %shard_map.83 = (bf16[8,4,16,1152]{3,2,1,0:T(8,128)(2,1)S(1)}, bf16[8,4,16,1152]{3,2,1,0:T(8,128)(2,1)S(1)}, bf16[49,64,128]{2,1,0:T(8,128)(2,1)S(1)}, bf16[49,6...) custom-call(s32[8,27]{1,0:T(8,128)S(1)} %clamp_bitcast_fusion.dst_re, ...), custom_call_target="tpu_custom_call" | custom-call | flops 905969664 | bytes 4000000 | tf_op jit(solution)/shard_map/pallas_call | solution.py:309
  17.4 0.0 collective-permute-done.12.rest_0_
  17.4 0.1 collective-permute-done.13.rest_1_
  17.5 1.6 %shard_map.84 = (bf16[4,28,16,128]{3,2,1,0:T(8,128)(2,1)S(1)}, f32[4,28,16,128]{3,2,1,0:T(8,128)S(1)}, bf16[8,2,16,1152]{3,2,1,0:T(8,128)(2,1)S(1)}, bf16[49,64,128]{2,1,0:T(8,128)(2,1)S(1)}) custom-call(s32[8,27]{1,0:T(8,128)S(1)} %clamp_bitcast_fusion.dst_ref.table_ref, ...), custom_call_target="tpu_custom_call", output_to_operand_aliasing={{3}: (3, {})} | custom-call | flops 905969664 | bytes 4000000 | tf_op jit(solution)/shard_map/pallas_call | solution.py:325
  19.1 0.1 collective-permute-start.14
  19.2 0.8 %shard_map.85 = bf16[8,64,128]{2,1,0:T(8,128)(2,1)S(1)} custom-call(bf16[8,4,16,1152]{3,2,1,0:T(8,128)(2,1)S(1)} %get-tuple-element.93.mid, bf16[8,2,16,1152]{3,2,1,0:T(8,128)(2,1)S(1)} %get-tuple-element.101.edge, bf16[27,128,128]{2,1,0:T(8,128)(2,1)S(1)} %copy-done.3, f32[512,128]{1,0:T(8,128)S(1)} %get-tuple-element.102.grad_mid), custom_call_target="tpu_custom_call" | custom-call | flops 905969664 | bytes 4000000 | tf_op jit(solution)/shard_map/pallas_call | solution.py:354
  20.0 1.1 %shard_map.86 = (bf16[8,2,16,1152]{3,2,1,0:T(8,128)(2,1)S(1)}, bf16[49,64,128]{2,1,0:T(8,128)(2,1)S(1)}) custom-call(s32[8,27]{1,0:T(8,128)S(1)} %clamp_bitcast_fusion.dst_ref.table_ref, bf16[49,64,128]{2,1,0:T(8,128)(2,1)S(1)} %get-tuple-element.103._, bf16[9,16,256]{2,1,0:T(8,128)(2,1)S(1)} %collective-permute-done.12.rest_0_, ...), custom_call_target="tpu_custom_call", output_to_operand_aliasing={{1}: (1, {})} | custom-call | flops 905969664 | bytes 4000000 | tf_op jit(solution)/shard_map/pallas_call | solution.py:342
  21.1 0.0 collective-permute-done.14
  21.1 0.1 add_convert_fusion.1
  21.2 20.4 %all_to_all.30 = bf16[16,7,16,128]{3,2,1,0:T(8,128)(2,1)S(1)} all-to-all(bf16[16,7,16,128]{3,2,1,0:T(8,128)(2,1)S(1)} %bitcast.17), channel_id=1, replica_groups=mesh['x'=4,'c'=2,'y'=4,'z'=8] {'x','y'}, dimensions={0} | all-to-all | bytes 917504 | tf_op jit(solution)/shard_map/all_to_all | solution.py:421
  41.6 0.1 convert_reduce_fusion.1
  41.9 12.8 %all_to_all.31 = f16[8,8,16,128]{3,2,1,0:T(8,128)(2,1)S(1)} all-to-all(f16[8,8,16,128]{3,2,1,0:T(8,128)(2,1)S(1)} %broadcast_in_dim.13), channel_id=1, replica_groups=mesh['x'=4,'c'=2,'y'=4,'z'=8] {'z'}, dimensions={0} | all-to-all | bytes 524288 | tf_op jit(solution)/shard_map/all_to_all | solution.py:427
  54.7 0.1 broadcast_in_dim.14
  54.8 11.6 %all_to_all.32 = bf16[16,7,16,128]{3,2,1,0:T(8,128)(2,1)S(1)} all-to-all(bf16[16,7,16,128]{3,2,1,0:T(8,128)(2,1)S(1)} %broadcast_in_dim.14), channel_id=1, replica_groups=mesh['x'=4,'c'=2,'y'=4,'z'=8] {'x','y'}, dimensions={0} | all-to-all | bytes 917504 | tf_op jit(solution)/shard_map/all_to_all | solution.py:431
  66.5 5.0 %collective-permute-start.15 = (bf16[4,28,16,128]{3,2,1,0:T(8,128)(2,1)S(1)}, bf16[4,28,16,128]{3,2,1,0:T(8,128)(2,1)S(1)}, u32[]{:S(2)}, u32[]{:S(2)}) collective-permute-start(bf16[4,28,16,128]{3,2,1,0:T(8,128)(2,1)S(1)} %bitcast.19), channel_id=1, source_target_pairs={{0,32},{32,0},{1,33},{33,1},{2,34},{34,2},{3,35},{35,3},{4,36},{36... | collective-permute-start | bytes 1376264 | tf_op jit(solution)/shard_map/ppermute | solution.py:372
  71.5 0.0 copy-start
  71.5 0.0 copy-start.1
  71.5 0.0 copy-start.2
  71.5 1.1 %shard_map.87 = bf16[8,64,128]{2,1,0:T(8,128)(2,1)S(1)} custom-call(bf16[8,4,16,1152]{3,2,1,0:T(8,128)(2,1)S(1)} %get-tuple-element.106.mid, bf16[8,2,16,1152]{3,2,1,0:T(8,128)(2,1)S(1)} %get-tuple-element.107.edge, bf16[27,128,128]{2,1,0:T(8,128)(2,1)S(1)} %copy-done.3), custom_call_target="tpu_custom_call" | custom-call | flops 905969664 | bytes 4000000 | tf_op jit(solution)/shard_map/pallas_call | solution.py:354
  72.6 0.5 slice.36
  73.8 0.0 collective-permute-done.15
  73.8 0.0 copy-done
  73.8 0.0 copy-done.1
  73.8 0.0 copy-done.2
  73.8 1.6 %conditional.1 = ((bf16[8,64,128]{2,1,0:T(8,128)(2,1)}, bf16[8,64,128]{2,1,0:T(8,128)(2,1)}, f32[27,128,128]{2,1,0:T(8,128)})) conditional(s32[]{:T(128)} %bitcast.10, (bf16[4,28,16,128]{3,2,1,0:T(8,128)(2,1)S(1)}, bf16[4,28,16,128]{3,2,1,0:T(8,128)(2,1)S(1)}, bf16[8,64,128]{2,1,0:T(8,128)(2,1)S(1)}, bf16[8,64,128]{2,1,0:T(8,128)(2,1)S(1)}) %tuple.36, ...), branch_computations={%region_3.4_spmd, %region_4.8_spmd} | conditional | flops 4531463168 | bytes 36206744 | solution.py:501
  73.8 1.4 %branch_0_fun.1 = (bf16[8,64,128]{2,1,0:T(8,128)(2,1)}, bf16[8,64,128]{2,1,0:T(8,128)(2,1)}, f32[27,128,128]{2,1,0:T(8,128)}) custom-call(bf16[4,28,16,128]{3,2,1,0:T(8,128)(2,1)S(1)} %get-tuple-element.24.own_ref, bf16[4,28,16,128]{3,2,1,0:T(8,128)(2,1)S(1)} %get-tuple-element.25.other_ref, bf16[8,64,128]{2,1,0:T(8,128)(2,1)S(1)} %get-tuple-element.26.outputs_ref, ...), custom_call_target="tpu_custom_call" | custom-call | tf_op jit(solution)/shard_map/cond/branch_0_fun/pallas_call | solution.py:457
  (16 shorter events, 0.3 us)
Async XLA Ops:
  0.6 14.2 %copy-start.3 = (bf16[27,128,128]{2,1,0:T(8,128)(2,1)S(1)}, bf16[27,128,128]{2,1,0:T(8,128)(2,1)}, u32[]{:S(2)}) copy-start(bf16[27,128,128]{2,1,0:T(8,128)(2,1)} %weights_ref.5) | copy-start | bytes 2654212
  2.0 6.9 %collective-permute-start.10 = (bf16[9,16,256]{2,1,0:T(8,128)(2,1)S(1)}, bf16[9,16,256]{2,1,0:T(8,128)(2,1)S(1)}, u32[]{:S(2)}, u32[]{:S(2)}) collective-permute-start(bf16[9,16,256]{2,1,0:T(8,128)(2,1)S(1)} %get-tuple-element.85), channel_id=1, source_target_pairs={{1,2},{2,1},{3,4},{4,3},{5,6},{6,5},{7,8},{8,7},{9,10},{10,9},{11,... | collective-permute-start | bytes 221192 | tf_op jit(solution)/shard_map/ppermute | solution.py:477
  2.7 7.2 %collective-permute-start.11 = (bf16[9,16,256]{2,1,0:T(8,128)(2,1)S(1)}, bf16[9,16,256]{2,1,0:T(8,128)(2,1)S(1)}, u32[]{:S(2)}, u32[]{:S(2)}) collective-permute-start(bf16[9,16,256]{2,1,0:T(8,128)(2,1)S(1)} %get-tuple-element.86), channel_id=1, source_target_pairs={{0,1},{1,0},{2,3},{3,2},{4,5},{5,4},{6,7},{7,6},{8,9},{9,8},{10,11... | collective-permute-start | bytes 221192 | tf_op jit(solution)/shard_map/ppermute | solution.py:478
  9.9 7.4 %collective-permute-start.12 = (bf16[9,16,256]{2,1,0:T(8,128)(2,1)S(1)}, bf16[9,16,256]{2,1,0:T(8,128)(2,1)S(1)}, u32[]{:S(2)}, u32[]{:S(2)}) collective-permute-start(bf16[9,16,256]{2,1,0:T(8,128)(2,1)S(1)} %maximum_maximum_fusion), channel_id=1, source_target_pairs={{0,32},{32,0},{1,33},{33,1},{2,34},{34,2},{3,35},{35,3},{4,36},{36... | collective-permute-start | bytes 221192 | tf_op jit(solution)/shard_map/ppermute | solution.py:485
  11.8 5.7 %collective-permute-start.13 = (bf16[9,16,256]{2,1,0:T(8,128)(2,1)S(1)}, bf16[9,16,256]{2,1,0:T(8,128)(2,1)S(1)}, u32[]{:S(2)}, u32[]{:S(2)}) collective-permute-start(bf16[9,16,256]{2,1,0:T(8,128)(2,1)S(1)} %maximum_maximum_fusion.1), channel_id=1, source_target_pairs={{32,64},{96,128},{160,192},{64,32},{128,96},{192,160},{33,65},{97,... | collective-permute-start | bytes 221192 | tf_op jit(solution)/shard_map/ppermute | solution.py:486
  19.1 2.0 %collective-permute-start.14 = (bf16[4,28,16,128]{3,2,1,0:T(8,128)(2,1)S(1)}, bf16[4,28,16,128]{3,2,1,0:T(8,128)(2,1)S(1)}, u32[]{:S(2)}, u32[]{:S(2)}) collective-permute-start(bf16[4,28,16,128]{3,2,1,0:T(8,128)(2,1)S(1)} %get-tuple-element.100), channel_id=1, source_target_pairs={{0,32},{32,0},{1,33},{33,1},{2,34},{34,2},{3,35},{35,3},{4,36},{36... | collective-permute-start | bytes 1376264 | tf_op jit(solution)/shard_map/ppermute | solution.py:367
  66.5 7.3 %collective-permute-start.15 = (bf16[4,28,16,128]{3,2,1,0:T(8,128)(2,1)S(1)}, bf16[4,28,16,128]{3,2,1,0:T(8,128)(2,1)S(1)}, u32[]{:S(2)}, u32[]{:S(2)}) collective-permute-start(bf16[4,28,16,128]{3,2,1,0:T(8,128)(2,1)S(1)} %bitcast.19), channel_id=1, source_target_pairs={{0,32},{32,0},{1,33},{33,1},{2,34},{34,2},{3,35},{35,3},{4,36},{36... | collective-permute-start | bytes 1376264 | tf_op jit(solution)/shard_map/ppermute | solution.py:372
  71.5 2.3 %copy-start = (bf16[8,64,128]{2,1,0:T(8,128)(2,1)S(1)}, bf16[8,64,128]{2,1,0:T(8,128)(2,1)}, u32[]{:S(2)}) copy-start(bf16[8,64,128]{2,1,0:T(8,128)(2,1)} %features_ref.1) | copy-start | bytes 393220
  71.5 2.3 %copy-start.1 = (bf16[8,64,128]{2,1,0:T(8,128)(2,1)S(1)}, bf16[8,64,128]{2,1,0:T(8,128)(2,1)}, u32[]{:S(2)}) copy-start(bf16[8,64,128]{2,1,0:T(8,128)(2,1)} %cotangent_ref.1) | copy-start | bytes 393220
  71.5 2.3 %copy-start.2 = (s32[40]{0:T(128)S(1)}, s32[40]{0:T(128)}, u32[]{:S(2)}) copy-start(s32[40]{0:T(128)} %recv_slot_ref.1) | copy-start | bytes 484

commit v14 on v13

--- a/solution.py
+++ b/solution.py
@@ -158,8 +158,8 @@
         for position in range(SLOTS):
             tile = packet[position, :, lanes]
             target = SLOTS + below * LENGTHS[0] + position
-            for begin in range(0, VOXELS, PLANE):
-                bricks[target, begin : begin + PLANE] = tile
+            bricks[target, :PLANE] = tile
+            bricks[target, VOXELS - PLANE :] = tile
     tiles = jnp.concatenate([packet[SLOTS, :, lanes] for packet in halos], axis=1)
     for order, side in ((0, odd), (1, 1 - odd)):
         whole = jnp.dot(
@@ -239,14 +239,16 @@
             keep_ref[quarter, first + number] = block[half:][rows]
 
 
-def grad_part(tap, weights_ref, side):
-    matrix = jnp.concatenate([weights_ref[26 - side * 9 - number] for number in range(9)], axis=1)
+def grad_part(tap, matrices):
+    matrix = jnp.concatenate(matrices, axis=1)
     return lax.dot_general(tap, matrix, (((1,), (1,)), ((), ())), preferred_element_type=jnp.float32)
 
 
 def mid_kernel(fill, unroll, count, dst_ref, features_ref, cotangent_ref, flipped_ref, weights_ref, *rest):
     halos = rest[:count]
-    mid_f, mid_c, bricks_f, bricks_c, send_ref, keep_ref, grad_ref = rest[count:]
+    mid_f, mid_c, bricks_f, bricks_c, send_ref, keep_ref, grad_ref, middle, sem = rest[count:]
+    copy = pltpu.make_async_copy(weights_ref.at[pl.ds(9, 9)], middle, sem)
+    copy.start()
     for kind, (own, bricks, mid) in enumerate(((features_ref, bricks_f, mid_f), (cotangent_ref, bricks_c, mid_c))):
         bricks[:SLOTS] = own[:SLOTS]
         for begin, end in ((SLOTS, SLOTS + STARTS[2]), (SLOTS + STARTS[4], SLOTS + HALO + 1)):
@@ -255,7 +257,8 @@
         build_taps(unroll, dst_ref, bricks, (1, 2, 3, 4), mid)
     tap = mid_c[...].reshape(SLOTS * VOXELS, WIDE)
     store_products(flipped_ref, tap, 0, send_ref, keep_ref)
-    grad_ref[...] = grad_part(tap, weights_ref, 1)
+    copy.wait()
+    grad_ref[...] = grad_part(tap, [middle[8 - number] for number in range(9)])
 
 
 def weight_kernel(fill, unroll, count, dst_ref, table_ref, mid, _, *rest):
@@ -276,7 +279,8 @@
 def grad_kernel(mid, edge, weights_ref, grad_mid, grad_ref):
     grad = grad_mid[...]
     for side in (0, 2):
-        grad = grad + grad_part(taps_of(mid, edge, side), weights_ref, side)
+        matrices = [weights_ref[26 - side * 9 - number] for number in range(9)]
+        grad = grad + grad_part(taps_of(mid, edge, side), matrices)
     grad_ref[...] = grad.astype(jnp.bfloat16).reshape(SLOTS, VOXELS, CHANNELS)
 
 
@@ -286,20 +290,46 @@
     build_taps(unroll, dst_ref, bricks, (0, PLANES - 1), edge)
 
 
-def output_kernel(mid, edge, weights_ref, outputs_ref):
+def spread_half(half_ref, whole, out_ref, core, sem):
+    for m in range(27):
+        for quarter in range(4):
+            whole[26 - m, quarter * 16 : quarter * 16 + 16] = half_ref[quarter, m].astype(jnp.float32)
+    half = CHANNELS // 2
+    copy = pltpu.make_async_copy(whole, out_ref.at[:, pl.ds(pl.multiple_of(core * half, half), half)], sem)
+    copy.start()
+    return copy
+
+
+def output_kernel(mid, edge, weights_ref, own_ref, outputs_ref, out_ref, whole, sem):
+    copy = spread_half(own_ref, whole, out_ref, lax.axis_index("c"), sem)
     outputs = None
     for side in range(3):
         matrix = weights_ref[side * 9 : side * 9 + 9].reshape(WIDE, CHANNELS)
         part = jnp.dot(taps_of(mid, edge, side), matrix, preferred_element_type=jnp.float32)
         outputs = part if outputs is None else outputs + part
     outputs_ref[...] = outputs.astype(jnp.bfloat16).reshape(SLOTS, VOXELS, CHANNELS)
+    copy.wait()
+
+
+def last_kernel(other_ref, outputs_ref, grad_ref, _, outputs_out, grad_out, out_ref, whole, sem, sems):
+    copies = [
+        pltpu.make_async_copy(outputs_ref, outputs_out, sems.at[0]),
+        pltpu.make_async_copy(grad_ref, grad_out, sems.at[1]),
+    ]
+    for copy in copies:
+        copy.start()
+    copies.append(spread_half(other_ref, whole, out_ref, 1 - lax.axis_index("c"), sem))
+    for copy in copies:
+        copy.wait()
 
 
 VMEM_SPEC = pl.BlockSpec(memory_space=pltpu.VMEM)
+HBM_SPEC = pl.BlockSpec(memory_space=pltpu.HBM)
 SMEM_SPEC = pl.BlockSpec(memory_space=pltpu.SMEM)
 BRICK_SHAPE = jax.ShapeDtypeStruct((SLOTS, VOXELS, CHANNELS), jnp.bfloat16)
 MID_SHAPE = jax.ShapeDtypeStruct((SLOTS, BRICK, PLANE, WIDE), jnp.bfloat16)
 EDGE_SHAPE = jax.ShapeDtypeStruct((SLOTS, 2, PLANE, WIDE), jnp.bfloat16)
+WHOLE_SHAPE = jax.ShapeDtypeStruct((27, CHANNELS, CHANNELS), jnp.float32)
 ALL_BRICKS = jax.ShapeDtypeStruct((SLOTS + HALO + 1, VOXELS, CHANNELS), jnp.bfloat16)
 PARAMS = pltpu.CompilerParams(vmem_limit_bytes=VMEM_LIMIT)
 COST = pl.CostEstimate(flops=4 * SLOTS * VOXELS * 27 * CHANNELS * CHANNELS, bytes_accessed=4_000_000, transcendentals=0)
@@ -308,7 +338,7 @@
 def mid_taps(fill, unroll, dst, own_f, own_c, halos, flipped, weights):
     return pl.pallas_call(
         functools.partial(mid_kernel, fill, unroll, len(halos)),
-        in_specs=[SMEM_SPEC] + [VMEM_SPEC] * (4 + len(halos)),
+        in_specs=[SMEM_SPEC] + [VMEM_SPEC] * 3 + [HBM_SPEC] + [VMEM_SPEC] * len(halos),
         out_specs=[VMEM_SPEC] * 7,
         out_shape=[
             MID_SHAPE, MID_SHAPE, ALL_BRICKS, ALL_BRICKS,
@@ -316,6 +346,7 @@
             jax.ShapeDtypeStruct((4, 9, 16, CHANNELS), jnp.float32),
             jax.ShapeDtypeStruct((SLOTS * VOXELS, CHANNELS), jnp.float32),
         ],
+        scratch_shapes=[pltpu.VMEM((9, CHANNELS, CHANNELS), jnp.bfloat16), pltpu.SemaphoreType.DMA(())],
         compiler_params=PARAMS,
         cost_estimate=COST,
     )(dst, own_f, own_c, flipped, weights, *halos)
@@ -350,28 +381,56 @@
     )(dst, bricks, *halos)[0]
 
 
-def product(kernel, *operands):
-    return pl.pallas_call(
-        kernel,
-        in_specs=[VMEM_SPEC] * len(operands),
+def input_gradient(mid, edge, weights, grad_mid):
+    return pl.pallas_call(
+        grad_kernel,
+        in_specs=[VMEM_SPEC] * 4,
         out_specs=VMEM_SPEC,
         out_shape=BRICK_SHAPE,
         compiler_params=PARAMS,
         cost_estimate=COST,
-    )(*operands)
+    )(mid, edge, weights, grad_mid)
+
+
+def outputs_and_half(mid, edge, weights, own):
+    return pl.pallas_call(
+        output_kernel,
+        in_specs=[VMEM_SPEC] * 4,
+        out_specs=[VMEM_SPEC, HBM_SPEC],
+        out_shape=[BRICK_SHAPE, WHOLE_SHAPE],
+        scratch_shapes=[pltpu.VMEM((27, CHANNELS // 2, CHANNELS), jnp.float32), pltpu.SemaphoreType.DMA(())],
+        compiler_params=PARAMS,
+        cost_estimate=COST,
+    )(mid, edge, weights, own)
+
+
+def write_rest(other, outputs, grad, whole):
+    return pl.pallas_call(
+        last_kernel,
+        in_specs=[VMEM_SPEC] * 3 + [HBM_SPEC],
+        out_specs=[HBM_SPEC] * 3,
+        out_shape=[BRICK_SHAPE, BRICK_SHAPE, WHOLE_SHAPE],
+        scratch_shapes=[
+            pltpu.VMEM((27, CHANNELS // 2, CHANNELS), jnp.float32),
+            pltpu.SemaphoreType.DMA(()),
+            pltpu.SemaphoreType.DMA((2,)),
+        ],
+        input_output_aliases={3: 2},
+        compiler_params=PARAMS,
+    )(other, outputs, grad, whole)
 
 
 def convolve(fill, unroll, dst, mids, halos, flipped, weights):
     mid_f, mid_c, bricks_f, bricks_c, send, keep, grad_mid = mids
     send, keep, edge_c, _ = weight_sums(fill, unroll, dst, mid_c, bricks_c, halos, flipped, send, keep)
     arrived = lax.ppermute(send, "c", [(0, 1), (1, 0)])
-    input_grad = product(grad_kernel, mid_c, edge_c, weights, grad_mid)
+    input_grad = input_gradient(mid_c, edge_c, weights, grad_mid)
     edge_f = feature_edges(fill, unroll, dst, bricks_f, halos)
     arrived, input_grad, edge_f = lax.optimization_barrier((arrived, input_grad, edge_f))
     own = sum_everywhere(arrived, keep)
     other = lax.ppermute(own, "c", [(0, 1), (1, 0)])
-    outputs = product(output_kernel, mid_f, edge_f, weights)
-    return outputs, input_grad, own, other
+    outputs, whole = outputs_and_half(mid_f, edge_f, weights, own)
+    return write_rest(other, outputs, input_grad, whole), own
 
 
 def pack_bricks_kernel(slot_ref, features_ref, cotangent_ref, *packets):
@@ -422,49 +481,14 @@
     total = jnp.sum(parts.astype(jnp.float32), axis=0)
     largest = jnp.max(jnp.abs(total), axis=(0, 1))
     power = jnp.clip(jnp.ceil(jnp.log2(jnp.maximum(largest, 1e-37))), -100.0, 100.0)
-    power = jnp.broadcast_to(power, (1, 16, CHANNELS))
-    share = jnp.concatenate((total * jnp.exp2(14.0 - power), power), axis=0).astype(jnp.float16)
+    power = jnp.broadcast_to(power, (8, CHANNELS))
+    scaled = (total * jnp.exp2(14.0 - power[0])).reshape(7 * 16, CHANNELS)
+    share = jnp.concatenate((scaled, power), axis=0).astype(jnp.float16)
     column = lax.all_to_all(jnp.broadcast_to(share[None], (8,) + share.shape), "z", 0, 0).astype(jnp.float32)
-    total = jnp.sum(column[:, :7] * jnp.exp2(column[:, 7:] - 14.0), axis=0)
-    share = (total * (1.0 / (VOXELS * SLOTS))).astype(jnp.bfloat16)
+    total = jnp.sum(column[:, : 7 * 16] * jnp.exp2(column[:, 7 * 16 : 7 * 16 + 1] - 14.0), axis=0)
+    share = (total * (1.0 / (VOXELS * SLOTS))).astype(jnp.bfloat16).reshape(7, 16, CHANNELS)
     whole = jnp.broadcast_to(share[None], (16,) + share.shape)
     return lax.all_to_all(whole, ("x", "y"), 0, 0).reshape(4, ROWS_M, 16, CHANNELS)
-
-
-def spread_kernel(own_ref, other_ref, outputs_ref, grad_ref, outputs_out, grad_out, out_ref, whole, sems):
-    half = CHANNELS // 2
-    core = lax.axis_index("c")
-    copies = [
-        pltpu.make_async_copy(outputs_ref, outputs_out, sems.at[9]),
-        pltpu.make_async_copy(grad_ref, grad_out, sems.at[10]),
-    ]
-    for copy in copies:
-        copy.start()
-    for chunk in range(9):
-        for m in range(3 * chunk, 3 * chunk + 3):
-            for quarter in range(4):
-                for ref, side in ((own_ref, core), (other_ref, 1 - core)):
-                    begin = pl.multiple_of(side * half + quarter * 16, 16)
-                    whole[26 - m, pl.ds(begin, 16)] = ref[quarter, m].astype(jnp.float32)
-        rows = pl.ds(24 - 3 * chunk, 3)
-        copies.append(pltpu.make_async_copy(whole.at[rows], out_ref.at[rows], sems.at[chunk]))
-        copies[-1].start()
-    for copy in copies:
-        copy.wait()
-
-
-def spread_out(outputs, input_grad, own, other):
-    return pl.pallas_call(
-        spread_kernel,
-        in_specs=[VMEM_SPEC] * 4,
-        out_specs=[pl.BlockSpec(memory_space=pltpu.HBM)] * 3,
-        out_shape=[BRICK_SHAPE, BRICK_SHAPE, jax.ShapeDtypeStruct((27, CHANNELS, CHANNELS), jnp.float32)],
-        scratch_shapes=[
-            pltpu.VMEM((27, CHANNELS, CHANNELS), jnp.float32),
-            pltpu.SemaphoreType.DMA((11,)),
-        ],
-        compiler_params=PARAMS,
-    )(own, other, outputs, input_grad)
 
 
 def local(features, weights, cotangent, dst_index, recv_slot):
@@ -486,19 +510,15 @@
     x_outer = lax.ppermute(relayed(to_outer, core), ("x", "c"), [(2 * x + 1, 2 * x + 2) for x in range(3)]
                            + [(2 * x + 2, 2 * x + 1) for x in range(3)])
     mids = mid_taps(fill_along_y, SLOTS, dst, own_f, own_c, (y_first, y_second), flipped, weights)
-    results = convolve(fill_along_x, SLOTS, dst, mids, (x_sibling, x_outer), flipped, weights)
+    results, own = convolve(fill_along_x, SLOTS, dst, mids, (x_sibling, x_outer), flipped, weights)
 
     def with_whole_bricks(results):
         packets = pack_bricks(recv_slot, features, cotangent)
         halos = [pass_to(packet, -heading[0], -heading[1]) for packet, heading in zip(packets, DIRECTIONS)]
         mids = mid_taps(fill_bricks, 1, dst, own_f, own_c, halos, flipped, weights)
-        return spread_out(*convolve(fill_nothing, 1, dst, mids, (), flipped, weights))
-
-    def as_they_are(results):
-        return spread_out(*results)
-
-    own = results[2]
-    return tuple(lax.cond(own[0, 27, 0, 0] != 0, with_whole_bricks, as_they_are, results))
+        return convolve(fill_nothing, 1, dst, mids, (), flipped, weights)[0]
+
+    return tuple(lax.cond(own[0, 27, 0, 0] != 0, with_whole_bricks, lambda results: results, results))
 
 
 def solution(mesh):

time: 75.9 us -> 76.4 us (level)
  Pallas kernels: 9.83 us -> 11 us
  transfers between devices with their start and end apart: 6 -> 6, of which waited for: 2 -> 1; matrix products, arithmetic and copies ran while one was open for 2% -> 2% of each run, Pallas kernels for 7% -> 9%
where the time goes in v14:
time: 76.4 us; the launch traced here: 76 us
  blocking collectives  44.3 us (58%)
  starting transfers between devices  16.1 us (21%)
  Pallas kernels  11 us (14%)
  between operations  1.73 us (2%)
  other arithmetic  1.03 us (1%)
  waiting for transfers between devices  0.92 us (1%)
  local copies, waits for them, and re-layouts  0.8 us (1%)
    all_to_all x1, blocking collectives, sum_everywhere(): parts = lax.all_to_all(parts, ('x', 'y'), 0, 0)  20.1 us
    all_to_all x1, blocking collectives, sum_everywhere(): lax.all_to_all(jnp.broadcast_to(share[None], (8,) + share.shape), 'z', 0, 0)  12.5 us
    all_to_all x1, blocking collectives, sum_everywhere(): lax.all_to_all(whole, ('x', 'y'), 0, 0).reshape(4, ROWS_M, 16, CHANNELS)  11.7 us
    ppermute x1, starting transfers between devices, local(): lax.ppermute(to_first, ('y', 'z'), [(gy, gy ^ 1) for gy in range(32)])  5.43 us
    ppermute x1, starting transfers between devices, convolve(): other = lax.ppermute(own, 'c', [(0, 1), (1, 0)])  4.93 us
    pallas_call x1, Pallas kernels, mid_taps(): pl.pallas_call(functools.partial(mid_kernel, fill, unroll, len(halos)), i...  3.1 us
    ppermute x1, starting transfers between devices, local(): lax.ppermute(relayed(to_outer, core), ('x', 'c'), [(2 * x + 1, 2 * x + 2)...  3.03 us
    pallas_call x1, Pallas kernels, outputs_and_half(): pl.pallas_call(output_kernel, in_specs=[VMEM_SPEC] * 4, out_specs=[VMEM_S...  1.99 us
  transfers between devices with their start and end apart: 6, of which 1 were waited for; matrix products, arithmetic and copies ran while one was open for 2% of the time, Pallas kernels for 9%

profile of v14, /device:TPU:1, one launch (start us, length us, event | category | flops | bytes accessed | tf_op | source)
XLA Modules:
  0.0 76.0 jit_solution(15734485601310126219)
XLA Ops:
  0.6 1.3 %shard_map.82 = (bf16[9,16,256]{2,1,0:T(8,128)(2,1)S(1)}, bf16[9,16,256]{2,1,0:T(8,128)(2,1)S(1)}, bf16[8,16,256]{2,1,0:T(8,128)(2,1)S(1)}, bf16[8,16,256]{2,1,0...) custom-call(s32[40]{0:T(128)} %recv_slot_ref.1, bf16[8,64,128]{2,1,0:T(8,128)(2,1)} %features_ref.1, ...), custom_call_target="tpu_custom_call" | custom-call | tf_op jit(solution)/shard_map/pallas_call | solution.py:121
  1.9 0.7 collective-permute-start.10
  2.6 5.4 %collective-permute-start.11 = (bf16[9,16,256]{2,1,0:T(8,128)(2,1)S(1)}, bf16[9,16,256]{2,1,0:T(8,128)(2,1)S(1)}, u32[]{:S(2)}, u32[]{:S(2)}) collective-permute-start(bf16[9,16,256]{2,1,0:T(8,128)(2,1)S(1)} %get-tuple-element.84), channel_id=1, source_target_pairs={{0,1},{1,0},{2,3},{3,2},{4,5},{5,4},{6,7},{7,6},{8,9},{9,8},{10,11... | collective-permute-start | bytes 221192 | tf_op jit(solution)/shard_map/ppermute | solution.py:502
  8.0 0.7 clamp_bitcast_fusion.dst_ref.table_ref
  8.8 0.1 copy.21
  8.9 0.0 collective-permute-done.10.rest_1_
  8.9 0.9 %collective-permute-done.11.rest_0_ = bf16[9,16,256]{2,1,0:T(8,128)(2,1)S(1)} collective-permute-done((bf16[9,16,256]{2,1,0:T(8,128)(2,1)S(1)}, bf16[9,16,256]{2,1,0:T(8,128)(2,1)S(1)}, u32[]{:S(2)}, u32[]{:S(2)}) %collective-permute-start.11) | collective-permute-done | bytes 73760 | tf_op jit(solution)/shard_map/ppermute | solution.py:502
  9.8 1.9 %collective-permute-start.12 = (bf16[9,16,256]{2,1,0:T(8,128)(2,1)S(1)}, bf16[9,16,256]{2,1,0:T(8,128)(2,1)S(1)}, u32[]{:S(2)}, u32[]{:S(2)}) collective-permute-start(bf16[9,16,256]{2,1,0:T(8,128)(2,1)S(1)} %maximum_maximum_fusion), channel_id=1, source_target_pairs={{0,32},{32,0},{1,33},{33,1},{2,34},{34,2},{3,35},{35,3},{4,36},{36... | collective-permute-start | bytes 221192 | tf_op jit(solution)/shard_map/ppermute | solution.py:509
  11.7 3.0 %collective-permute-start.13 = (bf16[9,16,256]{2,1,0:T(8,128)(2,1)S(1)}, bf16[9,16,256]{2,1,0:T(8,128)(2,1)S(1)}, u32[]{:S(2)}, u32[]{:S(2)}) collective-permute-start(bf16[9,16,256]{2,1,0:T(8,128)(2,1)S(1)} %maximum_maximum_fusion.1), channel_id=1, source_target_pairs={{32,64},{96,128},{160,192},{64,32},{128,96},{192,160},{33,65},{97,... | collective-permute-start | bytes 221192 | tf_op jit(solution)/shard_map/ppermute | solution.py:510
  14.8 3.1 %shard_map.83 = (bf16[8,4,16,1152]{3,2,1,0:T(8,128)(2,1)S(1)}, bf16[8,4,16,1152]{3,2,1,0:T(8,128)(2,1)S(1)}, bf16[49,64,128]{2,1,0:T(8,128)(2,1)S(1)}, bf16[49,6...) custom-call(s32[8,27]{1,0:T(8,128)S(1)} %clamp_bitcast_fusion.dst_re, ...), custom_call_target="tpu_custom_call" | custom-call | flops 905969664 | bytes 4000000 | tf_op jit(solution)/shard_map/pallas_call | solution.py:339
  17.9 0.0 copy-start.3
  17.9 0.0 collective-permute-done.12.rest_0_
  17.9 0.0 collective-permute-done.13.rest_1_
  17.9 1.6 %shard_map.84 = (bf16[4,28,16,128]{3,2,1,0:T(8,128)(2,1)S(1)}, f32[4,28,16,128]{3,2,1,0:T(8,128)S(1)}, bf16[8,2,16,1152]{3,2,1,0:T(8,128)(2,1)S(1)}, bf16[49,64,128]{2,1,0:T(8,128)(2,1)S(1)}) custom-call(s32[8,27]{1,0:T(8,128)S(1)} %clamp_bitcast_fusion.dst_ref.table_ref, ...), custom_call_target="tpu_custom_call", output_to_operand_aliasing={{3}: (3, {})} | custom-call | flops 905969664 | bytes 4000000 | tf_op jit(solution)/shard_map/pallas_call | solution.py:356
  19.5 0.1 collective-permute-start.14
  19.6 0.0 copy-done.3
  19.6 0.8 %shard_map.85.grad_ref = bf16[8,64,128]{2,1,0:T(8,128)(2,1)S(1)} custom-call(bf16[8,4,16,1152]{3,2,1,0:T(8,128)(2,1)S(1)} %get-tuple-element.91.mid, bf16[8,2,16,1152]{3,2,1,0:T(8,128)(2,1)S(1)} %get-tuple-element.99.edge, bf16[27,128,128]{2,1,0:T(8,128)(2,1)S(1)} %copy-done.3, f32[512,128]{1,0:T(8,128)S(1)} %get-tuple-element.100.grad_mid), custom_call_target="tpu_custom_call" | custom-call | flops 905969664 | bytes 4000000 | tf_op jit(solution)/shard_map/pallas_call | solution.py:385
  20.4 1.1 %shard_map.86 = (bf16[8,2,16,1152]{3,2,1,0:T(8,128)(2,1)S(1)}, bf16[49,64,128]{2,1,0:T(8,128)(2,1)S(1)}) custom-call(s32[8,27]{1,0:T(8,128)S(1)} %clamp_bitcast_fusion.dst_ref.table_ref, bf16[49,64,128]{2,1,0:T(8,128)(2,1)S(1)} %get-tuple-element.101._, bf16[9,16,256]{2,1,0:T(8,128)(2,1)S(1)} %collective-permute-done.12.rest_0_, ...), custom_call_target="tpu_custom_call", output_to_operand_aliasing={{1}: (1, {})} | custom-call | flops 905969664 | bytes 4000000 | tf_op jit(solution)/shard_map/pallas_call | solution.py:373
  21.6 0.0 collective-permute-done.14
  21.6 0.1 add_convert_fusion.1
  21.7 20.1 %all_to_all.30 = bf16[16,7,16,128]{3,2,1,0:T(8,128)(2,1)S(1)} all-to-all(bf16[16,7,16,128]{3,2,1,0:T(8,128)(2,1)S(1)} %bitcast.28), channel_id=1, replica_groups=mesh['x'=4,'c'=2,'y'=4,'z'=8] {'x','y'}, dimensions={0} | all-to-all | bytes 917504 | tf_op jit(solution)/shard_map/all_to_all | solution.py:480
  41.8 0.1 convert_reduce_fusion.1
  42.0 12.5 %all_to_all.31 = f16[8,120,128]{2,1,0:T(8,128)(2,1)S(1)} all-to-all(f16[8,120,128]{2,1,0:T(8,128)(2,1)S(1)} %broadcast_in_dim.13), channel_id=1, replica_groups=mesh['x'=4,'c'=2,'y'=4,'z'=8] {'z'}, dimensions={0} | all-to-all | bytes 491520 | tf_op jit(solution)/shard_map/all_to_all | solution.py:487
  54.6 0.1 broadcast_in_dim.14
  54.7 11.7 %all_to_all.32 = bf16[16,7,16,128]{3,2,1,0:T(8,128)(2,1)S(1)} all-to-all(bf16[16,7,16,128]{3,2,1,0:T(8,128)(2,1)S(1)} %broadcast_in_dim.14), channel_id=1, replica_groups=mesh['x'=4,'c'=2,'y'=4,'z'=8] {'x','y'}, dimensions={0} | all-to-all | bytes 917504 | tf_op jit(solution)/shard_map/all_to_all | solution.py:491
  66.4 4.9 %collective-permute-start.15 = (bf16[4,28,16,128]{3,2,1,0:T(8,128)(2,1)S(1)}, bf16[4,28,16,128]{3,2,1,0:T(8,128)(2,1)S(1)}, u32[]{:S(2)}, u32[]{:S(2)}) collective-permute-start(bf16[4,28,16,128]{3,2,1,0:T(8,128)(2,1)S(1)} %bitcast.23), channel_id=1, source_target_pairs={{0,32},{32,0},{1,33},{33,1},{2,34},{34,2},{3,35},{35,3},{4,36},{36... | collective-permute-start | bytes 1376264 | tf_op jit(solution)/shard_map/ppermute | solution.py:431
  71.3 0.5 slice.38
  72.5 2.0 %shard_map.87 = (bf16[8,64,128]{2,1,0:T(8,128)(2,1)S(1)}, f32[27,128,128]{2,1,0:T(8,128)}) custom-call(bf16[8,4,16,1152]{3,2,1,0:T(8,128)(2,1)S(1)} %get-tuple-element.104.mid, bf16[8,2,16,1152]{3,2,1,0:T(8,128)(2,1)S(1)} %get-tuple-element.105.edge, bf16[27,128,128]{2,1,0:T(8,128)(2,1)S(1)} %copy-done.3, bf16[4,28,16,128]{3,2,1,0:T(8,128)(2,1)S(1)} %bitcast.25), custom_call_target="tpu_custom_call" | custom-call | flops 905969664 | bytes 4000000 | tf_op jit(solution)/shard_map/pallas_call | solution.py:396
  74.5 0.0 copy-start
  74.5 0.0 copy-start.1
  74.5 0.0 copy-start.2
  74.5 0.0 collective-permute-done.15.other_ref
  74.5 1.0 %shard_map.88 = (bf16[8,64,128]{2,1,0:T(8,128)(2,1)}, bf16[8,64,128]{2,1,0:T(8,128)(2,1)}, f32[27,128,128]{2,1,0:T(8,128)}) custom-call(bf16[4,28,16,128]{3,2,1,0:T(8,128)(2,1)S(1)} %collective-permute-done.15.other_ref, bf16[8,64,128]{2,1,0:T(8,128)(2,1)S(1)} %get-tuple-element.106.outputs_ref, ...), custom_call_target="tpu_custom_call", output_to_operand_aliasing={{2}: (3, {})} | custom-call | tf_op jit(solution)/shard_map/pallas_call | solution.py:408
  75.6 0.0 copy-done
  75.6 0.0 copy-done.1
  75.6 0.0 copy-done.2
  75.6 0.2 conditional.1
  (16 shorter events, 0.2 us)
Async XLA Ops:
  1.9 6.9 %collective-permute-start.10 = (bf16[9,16,256]{2,1,0:T(8,128)(2,1)S(1)}, bf16[9,16,256]{2,1,0:T(8,128)(2,1)S(1)}, u32[]{:S(2)}, u32[]{:S(2)}) collective-permute-start(bf16[9,16,256]{2,1,0:T(8,128)(2,1)S(1)} %get-tuple-element.83), channel_id=1, source_target_pairs={{1,2},{2,1},{3,4},{4,3},{5,6},{6,5},{7,8},{8,7},{9,10},{10,9},{11,... | collective-permute-start | bytes 221192 | tf_op jit(solution)/shard_map/ppermute | solution.py:501
  2.6 7.2 %collective-permute-start.11 = (bf16[9,16,256]{2,1,0:T(8,128)(2,1)S(1)}, bf16[9,16,256]{2,1,0:T(8,128)(2,1)S(1)}, u32[]{:S(2)}, u32[]{:S(2)}) collective-permute-start(bf16[9,16,256]{2,1,0:T(8,128)(2,1)S(1)} %get-tuple-element.84), channel_id=1, source_target_pairs={{0,1},{1,0},{2,3},{3,2},{4,5},{5,4},{6,7},{7,6},{8,9},{9,8},{10,11... | collective-permute-start | bytes 221192 | tf_op jit(solution)/shard_map/ppermute | solution.py:502
  9.8 8.1 %collective-permute-start.12 = (bf16[9,16,256]{2,1,0:T(8,128)(2,1)S(1)}, bf16[9,16,256]{2,1,0:T(8,128)(2,1)S(1)}, u32[]{:S(2)}, u32[]{:S(2)}) collective-permute-start(bf16[9,16,256]{2,1,0:T(8,128)(2,1)S(1)} %maximum_maximum_fusion), channel_id=1, source_target_pairs={{0,32},{32,0},{1,33},{33,1},{2,34},{34,2},{3,35},{35,3},{4,36},{36... | collective-permute-start | bytes 221192 | tf_op jit(solution)/shard_map/ppermute | solution.py:509
  11.7 6.2 %collective-permute-start.13 = (bf16[9,16,256]{2,1,0:T(8,128)(2,1)S(1)}, bf16[9,16,256]{2,1,0:T(8,128)(2,1)S(1)}, u32[]{:S(2)}, u32[]{:S(2)}) collective-permute-start(bf16[9,16,256]{2,1,0:T(8,128)(2,1)S(1)} %maximum_maximum_fusion.1), channel_id=1, source_target_pairs={{32,64},{96,128},{160,192},{64,32},{128,96},{192,160},{33,65},{97,... | collective-permute-start | bytes 221192 | tf_op jit(solution)/shard_map/ppermute | solution.py:510
  17.9 1.8 %copy-start.3 = (bf16[27,128,128]{2,1,0:T(8,128)(2,1)S(1)}, bf16[27,128,128]{2,1,0:T(8,128)(2,1)}, u32[]{:S(2)}) copy-start(bf16[27,128,128]{2,1,0:T(8,128)(2,1)} %weights_ref.5) | copy-start | bytes 2654212
  19.5 2.0 %collective-permute-start.14 = (bf16[4,28,16,128]{3,2,1,0:T(8,128)(2,1)S(1)}, bf16[4,28,16,128]{3,2,1,0:T(8,128)(2,1)S(1)}, u32[]{:S(2)}, u32[]{:S(2)}) collective-permute-start(bf16[4,28,16,128]{3,2,1,0:T(8,128)(2,1)S(1)} %get-tuple-element.98), channel_id=1, source_target_pairs={{0,32},{32,0},{1,33},{33,1},{2,34},{34,2},{3,35},{35,3},{4,36},{36... | collective-permute-start | bytes 1376264 | tf_op jit(solution)/shard_map/ppermute | solution.py:426
  66.4 8.1 %collective-permute-start.15 = (bf16[4,28,16,128]{3,2,1,0:T(8,128)(2,1)S(1)}, bf16[4,28,16,128]{3,2,1,0:T(8,128)(2,1)S(1)}, u32[]{:S(2)}, u32[]{:S(2)}) collective-permute-start(bf16[4,28,16,128]{3,2,1,0:T(8,128)(2,1)S(1)} %bitcast.23), channel_id=1, source_target_pairs={{0,32},{32,0},{1,33},{33,1},{2,34},{34,2},{3,35},{35,3},{4,36},{36... | collective-permute-start | bytes 1376264 | tf_op jit(solution)/shard_map/ppermute | solution.py:431
  74.5 1.1 %copy-start = (bf16[8,64,128]{2,1,0:T(8,128)(2,1)S(1)}, bf16[8,64,128]{2,1,0:T(8,128)(2,1)}, u32[]{:S(2)}) copy-start(bf16[8,64,128]{2,1,0:T(8,128)(2,1)} %features_ref.1) | copy-start | bytes 393220
  74.5 1.1 %copy-start.1 = (bf16[8,64,128]{2,1,0:T(8,128)(2,1)S(1)}, bf16[8,64,128]{2,1,0:T(8,128)(2,1)}, u32[]{:S(2)}) copy-start(bf16[8,64,128]{2,1,0:T(8,128)(2,1)} %cotangent_ref.1) | copy-start | bytes 393220
  74.5 1.1 %copy-start.2 = (s32[40]{0:T(128)S(1)}, s32[40]{0:T(128)}, u32[]{:S(2)}) copy-start(s32[40]{0:T(128)} %recv_slot_ref.1) | copy-start | bytes 484

commit v15 on v13

--- a/solution.py
+++ b/solution.py
@@ -158,8 +158,8 @@
         for position in range(SLOTS):
             tile = packet[position, :, lanes]
             target = SLOTS + below * LENGTHS[0] + position
-            for begin in range(0, VOXELS, PLANE):
-                bricks[target, begin : begin + PLANE] = tile
+            bricks[target, :PLANE] = tile
+            bricks[target, VOXELS - PLANE :] = tile
     tiles = jnp.concatenate([packet[SLOTS, :, lanes] for packet in halos], axis=1)
     for order, side in ((0, odd), (1, 1 - odd)):
         whole = jnp.dot(
@@ -422,11 +422,12 @@
     total = jnp.sum(parts.astype(jnp.float32), axis=0)
     largest = jnp.max(jnp.abs(total), axis=(0, 1))
     power = jnp.clip(jnp.ceil(jnp.log2(jnp.maximum(largest, 1e-37))), -100.0, 100.0)
-    power = jnp.broadcast_to(power, (1, 16, CHANNELS))
-    share = jnp.concatenate((total * jnp.exp2(14.0 - power), power), axis=0).astype(jnp.float16)
+    power = jnp.broadcast_to(power, (8, CHANNELS))
+    scaled = (total * jnp.exp2(14.0 - power[0])).reshape(7 * 16, CHANNELS)
+    share = jnp.concatenate((scaled, power), axis=0).astype(jnp.float16)
     column = lax.all_to_all(jnp.broadcast_to(share[None], (8,) + share.shape), "z", 0, 0).astype(jnp.float32)
-    total = jnp.sum(column[:, :7] * jnp.exp2(column[:, 7:] - 14.0), axis=0)
-    share = (total * (1.0 / (VOXELS * SLOTS))).astype(jnp.bfloat16)
+    total = jnp.sum(column[:, : 7 * 16] * jnp.exp2(column[:, 7 * 16 : 7 * 16 + 1] - 14.0), axis=0)
+    share = (total * (1.0 / (VOXELS * SLOTS))).astype(jnp.bfloat16).reshape(7, 16, CHANNELS)
     whole = jnp.broadcast_to(share[None], (16,) + share.shape)
     return lax.all_to_all(whole, ("x", "y"), 0, 0).reshape(4, ROWS_M, 16, CHANNELS)
 

time: 75.9 us -> 75.6 us (level)
  no operation moved by 1% of the time
where the time goes in v15:
time: 75.6 us; the launch traced here: 75.3 us
  blocking collectives  44.7 us (59%)
  starting transfers between devices  16 us (21%)
  Pallas kernels  9.83 us (13%)
  between operations  1.71 us (2%)
  waiting for transfers between devices  1.04 us (1%)
  other arithmetic  1.03 us (1%)
  local copies, waits for them, and re-layouts  0.77 us (1%)
    all_to_all x1, blocking collectives, sum_everywhere(): parts = lax.all_to_all(parts, ('x', 'y'), 0, 0)  20.4 us
    all_to_all x1, blocking collectives, sum_everywhere(): lax.all_to_all(jnp.broadcast_to(share[None], (8,) + share.shape), 'z', 0, 0)  12.5 us
    all_to_all x1, blocking collectives, sum_everywhere(): lax.all_to_all(whole, ('x', 'y'), 0, 0).reshape(4, ROWS_M, 16, CHANNELS)  11.7 us
    ppermute x1, starting transfers between devices, local(): lax.ppermute(to_first, ('y', 'z'), [(gy, gy ^ 1) for gy in range(32)])  5.44 us
    ppermute x1, starting transfers between devices, convolve(): other = lax.ppermute(own, 'c', [(0, 1), (1, 0)])  4.91 us
    ppermute x1, starting transfers between devices, local(): lax.ppermute(relayed(to_outer, core), ('x', 'c'), [(2 * x + 1, 2 * x + 2)...  3.03 us
    pallas_call x1, Pallas kernels, mid_taps(): pl.pallas_call(functools.partial(mid_kernel, fill, unroll, len(halos)), i...  2.47 us
    ppermute x1, starting transfers between devices, local(): lax.ppermute(relayed(to_sibling, 1 - core), 'c', [(0, 1), (1, 0)])  1.9 us
  transfers between devices with their start and end apart: 6, of which 2 were waited for; matrix products, arithmetic and copies ran while one was open for 2% of the time, Pallas kernels for 7%

profile of v15, /device:TPU:1, one launch (start us, length us, event | category | flops | bytes accessed | tf_op | source)
XLA Modules:
  0.0 75.3 jit_solution(138493258970464450)
XLA Ops:
  0.6 0.0 copy-start.3
  0.6 1.4 %shard_map.82 = (bf16[9,16,256]{2,1,0:T(8,128)(2,1)S(1)}, bf16[9,16,256]{2,1,0:T(8,128)(2,1)S(1)}, bf16[8,16,256]{2,1,0:T(8,128)(2,1)S(1)}, bf16[8,16,256]{2,1,0...) custom-call(s32[40]{0:T(128)} %recv_slot_ref.1, bf16[8,64,128]{2,1,0:T(8,128)(2,1)} %features_ref.1, ...), custom_call_target="tpu_custom_call" | custom-call | tf_op jit(solution)/shard_map/pallas_call | solution.py:121
  2.0 0.7 collective-permute-start.10
  2.7 5.4 %collective-permute-start.11 = (bf16[9,16,256]{2,1,0:T(8,128)(2,1)S(1)}, bf16[9,16,256]{2,1,0:T(8,128)(2,1)S(1)}, u32[]{:S(2)}, u32[]{:S(2)}) collective-permute-start(bf16[9,16,256]{2,1,0:T(8,128)(2,1)S(1)} %get-tuple-element.86), channel_id=1, source_target_pairs={{0,1},{1,0},{2,3},{3,2},{4,5},{5,4},{6,7},{7,6},{8,9},{9,8},{10,11... | collective-permute-start | bytes 221192 | tf_op jit(solution)/shard_map/ppermute | solution.py:479
  8.1 0.7 clamp_bitcast_fusion.dst_ref.table_ref
  8.9 0.1 copy.19
  9.0 0.0 collective-permute-done.10.rest_1_
  9.0 0.9 %collective-permute-done.11.rest_0_ = bf16[9,16,256]{2,1,0:T(8,128)(2,1)S(1)} collective-permute-done((bf16[9,16,256]{2,1,0:T(8,128)(2,1)S(1)}, bf16[9,16,256]{2,1,0:T(8,128)(2,1)S(1)}, u32[]{:S(2)}, u32[]{:S(2)}) %collective-permute-start.11) | collective-permute-done | bytes 73760 | tf_op jit(solution)/shard_map/ppermute | solution.py:479
  9.9 1.9 %collective-permute-start.12 = (bf16[9,16,256]{2,1,0:T(8,128)(2,1)S(1)}, bf16[9,16,256]{2,1,0:T(8,128)(2,1)S(1)}, u32[]{:S(2)}, u32[]{:S(2)}) collective-permute-start(bf16[9,16,256]{2,1,0:T(8,128)(2,1)S(1)} %maximum_maximum_fusion), channel_id=1, source_target_pairs={{0,32},{32,0},{1,33},{33,1},{2,34},{34,2},{3,35},{35,3},{4,36},{36... | collective-permute-start | bytes 221192 | tf_op jit(solution)/shard_map/ppermute | solution.py:486
  11.8 3.0 %collective-permute-start.13 = (bf16[9,16,256]{2,1,0:T(8,128)(2,1)S(1)}, bf16[9,16,256]{2,1,0:T(8,128)(2,1)S(1)}, u32[]{:S(2)}, u32[]{:S(2)}) collective-permute-start(bf16[9,16,256]{2,1,0:T(8,128)(2,1)S(1)} %maximum_maximum_fusion.1), channel_id=1, source_target_pairs={{32,64},{96,128},{160,192},{64,32},{128,96},{192,160},{33,65},{97,... | collective-permute-start | bytes 221192 | tf_op jit(solution)/shard_map/ppermute | solution.py:487
  14.9 0.0 copy-done.3
  14.9 2.5 %shard_map.83 = (bf16[8,4,16,1152]{3,2,1,0:T(8,128)(2,1)S(1)}, bf16[8,4,16,1152]{3,2,1,0:T(8,128)(2,1)S(1)}, bf16[49,64,128]{2,1,0:T(8,128)(2,1)S(1)}, bf16[49,6...) custom-call(s32[8,27]{1,0:T(8,128)S(1)} %clamp_bitcast_fusion.dst_re, ...), custom_call_target="tpu_custom_call" | custom-call | flops 905969664 | bytes 4000000 | tf_op jit(solution)/shard_map/pallas_call | solution.py:309
  17.4 0.0 collective-permute-done.12.rest_0_
  17.4 0.1 collective-permute-done.13.rest_1_
  17.5 1.6 %shard_map.84 = (bf16[4,28,16,128]{3,2,1,0:T(8,128)(2,1)S(1)}, f32[4,28,16,128]{3,2,1,0:T(8,128)S(1)}, bf16[8,2,16,1152]{3,2,1,0:T(8,128)(2,1)S(1)}, bf16[49,64,128]{2,1,0:T(8,128)(2,1)S(1)}) custom-call(s32[8,27]{1,0:T(8,128)S(1)} %clamp_bitcast_fusion.dst_ref.table_ref, ...), custom_call_target="tpu_custom_call", output_to_operand_aliasing={{3}: (3, {})} | custom-call | flops 905969664 | bytes 4000000 | tf_op jit(solution)/shard_map/pallas_call | solution.py:325
  19.1 0.1 collective-permute-start.14
  19.2 0.8 %shard_map.85 = bf16[8,64,128]{2,1,0:T(8,128)(2,1)S(1)} custom-call(bf16[8,4,16,1152]{3,2,1,0:T(8,128)(2,1)S(1)} %get-tuple-element.93.mid, bf16[8,2,16,1152]{3,2,1,0:T(8,128)(2,1)S(1)} %get-tuple-element.101.edge, bf16[27,128,128]{2,1,0:T(8,128)(2,1)S(1)} %copy-done.3, f32[512,128]{1,0:T(8,128)S(1)} %get-tuple-element.102.grad_mid), custom_call_target="tpu_custom_call" | custom-call | flops 905969664 | bytes 4000000 | tf_op jit(solution)/shard_map/pallas_call | solution.py:354
  20.0 1.1 %shard_map.86 = (bf16[8,2,16,1152]{3,2,1,0:T(8,128)(2,1)S(1)}, bf16[49,64,128]{2,1,0:T(8,128)(2,1)S(1)}) custom-call(s32[8,27]{1,0:T(8,128)S(1)} %clamp_bitcast_fusion.dst_ref.table_ref, bf16[49,64,128]{2,1,0:T(8,128)(2,1)S(1)} %get-tuple-element.103._, bf16[9,16,256]{2,1,0:T(8,128)(2,1)S(1)} %collective-permute-done.12.rest_0_, ...), custom_call_target="tpu_custom_call", output_to_operand_aliasing={{1}: (1, {})} | custom-call | flops 905969664 | bytes 4000000 | tf_op jit(solution)/shard_map/pallas_call | solution.py:342
  21.1 0.0 collective-permute-done.14
  21.1 0.1 add_convert_fusion.1
  21.2 20.4 %all_to_all.30 = bf16[16,7,16,128]{3,2,1,0:T(8,128)(2,1)S(1)} all-to-all(bf16[16,7,16,128]{3,2,1,0:T(8,128)(2,1)S(1)} %bitcast.25), channel_id=1, replica_groups=mesh['x'=4,'c'=2,'y'=4,'z'=8] {'x','y'}, dimensions={0} | all-to-all | bytes 917504 | tf_op jit(solution)/shard_map/all_to_all | solution.py:421
  41.6 0.1 convert_reduce_fusion.1
  41.9 12.5 %all_to_all.31 = f16[8,120,128]{2,1,0:T(8,128)(2,1)S(1)} all-to-all(f16[8,120,128]{2,1,0:T(8,128)(2,1)S(1)} %broadcast_in_dim.13), channel_id=1, replica_groups=mesh['x'=4,'c'=2,'y'=4,'z'=8] {'z'}, dimensions={0} | all-to-all | bytes 491520 | tf_op jit(solution)/shard_map/all_to_all | solution.py:428
  54.5 0.1 broadcast_in_dim.14
  54.6 11.7 %all_to_all.32 = bf16[16,7,16,128]{3,2,1,0:T(8,128)(2,1)S(1)} all-to-all(bf16[16,7,16,128]{3,2,1,0:T(8,128)(2,1)S(1)} %broadcast_in_dim.14), channel_id=1, replica_groups=mesh['x'=4,'c'=2,'y'=4,'z'=8] {'x','y'}, dimensions={0} | all-to-all | bytes 917504 | tf_op jit(solution)/shard_map/all_to_all | solution.py:432
  66.3 4.9 %collective-permute-start.15 = (bf16[4,28,16,128]{3,2,1,0:T(8,128)(2,1)S(1)}, bf16[4,28,16,128]{3,2,1,0:T(8,128)(2,1)S(1)}, u32[]{:S(2)}, u32[]{:S(2)}) collective-permute-start(bf16[4,28,16,128]{3,2,1,0:T(8,128)(2,1)S(1)} %bitcast.27), channel_id=1, source_target_pairs={{0,32},{32,0},{1,33},{33,1},{2,34},{34,2},{3,35},{35,3},{4,36},{36... | collective-permute-start | bytes 1376264 | tf_op jit(solution)/shard_map/ppermute | solution.py:372
  71.2 0.0 copy-start
  71.2 0.0 copy-start.1
  71.2 0.0 copy-start.2
  71.2 1.1 %shard_map.87 = bf16[8,64,128]{2,1,0:T(8,128)(2,1)S(1)} custom-call(bf16[8,4,16,1152]{3,2,1,0:T(8,128)(2,1)S(1)} %get-tuple-element.106.mid, bf16[8,2,16,1152]{3,2,1,0:T(8,128)(2,1)S(1)} %get-tuple-element.107.edge, bf16[27,128,128]{2,1,0:T(8,128)(2,1)S(1)} %copy-done.3), custom_call_target="tpu_custom_call" | custom-call | flops 905969664 | bytes 4000000 | tf_op jit(solution)/shard_map/pallas_call | solution.py:354
  72.3 0.5 slice.38
  73.5 0.0 collective-permute-done.15
  73.5 0.0 copy-done
  73.5 0.0 copy-done.1
  73.5 0.0 copy-done.2
  73.5 1.6 %conditional.1 = ((bf16[8,64,128]{2,1,0:T(8,128)(2,1)}, bf16[8,64,128]{2,1,0:T(8,128)(2,1)}, f32[27,128,128]{2,1,0:T(8,128)})) conditional(s32[]{:T(128)} %bitcast.14, (bf16[4,28,16,128]{3,2,1,0:T(8,128)(2,1)S(1)}, bf16[4,28,16,128]{3,2,1,0:T(8,128)(2,1)S(1)}, bf16[8,64,128]{2,1,0:T(8,128)(2,1)S(1)}, bf16[8,64,128]{2,1,0:T(8,128)(2,1)S(1)}) %tuple.36, ...), branch_computations={%region_3.4_spmd, %region_4.8_spmd} | conditional | flops 4531423232 | bytes 35915928 | solution.py:502
  73.5 1.4 %branch_0_fun.1 = (bf16[8,64,128]{2,1,0:T(8,128)(2,1)}, bf16[8,64,128]{2,1,0:T(8,128)(2,1)}, f32[27,128,128]{2,1,0:T(8,128)}) custom-call(bf16[4,28,16,128]{3,2,1,0:T(8,128)(2,1)S(1)} %get-tuple-element.24.own_ref, bf16[4,28,16,128]{3,2,1,0:T(8,128)(2,1)S(1)} %get-tuple-element.25.other_ref, bf16[8,64,128]{2,1,0:T(8,128)(2,1)S(1)} %get-tuple-element.26.outputs_ref, ...), custom_call_target="tpu_custom_call" | custom-call | tf_op jit(solution)/shard_map/cond/branch_0_fun/pallas_call | solution.py:458
  (16 shorter events, 0.2 us)
Async XLA Ops:
  0.6 14.2 %copy-start.3 = (bf16[27,128,128]{2,1,0:T(8,128)(2,1)S(1)}, bf16[27,128,128]{2,1,0:T(8,128)(2,1)}, u32[]{:S(2)}) copy-start(bf16[27,128,128]{2,1,0:T(8,128)(2,1)} %weights_ref.5) | copy-start | bytes 2654212
  2.0 6.9 %collective-permute-start.10 = (bf16[9,16,256]{2,1,0:T(8,128)(2,1)S(1)}, bf16[9,16,256]{2,1,0:T(8,128)(2,1)S(1)}, u32[]{:S(2)}, u32[]{:S(2)}) collective-permute-start(bf16[9,16,256]{2,1,0:T(8,128)(2,1)S(1)} %get-tuple-element.85), channel_id=1, source_target_pairs={{1,2},{2,1},{3,4},{4,3},{5,6},{6,5},{7,8},{8,7},{9,10},{10,9},{11,... | collective-permute-start | bytes 221192 | tf_op jit(solution)/shard_map/ppermute | solution.py:478
  2.7 7.2 %collective-permute-start.11 = (bf16[9,16,256]{2,1,0:T(8,128)(2,1)S(1)}, bf16[9,16,256]{2,1,0:T(8,128)(2,1)S(1)}, u32[]{:S(2)}, u32[]{:S(2)}) collective-permute-start(bf16[9,16,256]{2,1,0:T(8,128)(2,1)S(1)} %get-tuple-element.86), channel_id=1, source_target_pairs={{0,1},{1,0},{2,3},{3,2},{4,5},{5,4},{6,7},{7,6},{8,9},{9,8},{10,11... | collective-permute-start | bytes 221192 | tf_op jit(solution)/shard_map/ppermute | solution.py:479
  9.9 7.4 %collective-permute-start.12 = (bf16[9,16,256]{2,1,0:T(8,128)(2,1)S(1)}, bf16[9,16,256]{2,1,0:T(8,128)(2,1)S(1)}, u32[]{:S(2)}, u32[]{:S(2)}) collective-permute-start(bf16[9,16,256]{2,1,0:T(8,128)(2,1)S(1)} %maximum_maximum_fusion), channel_id=1, source_target_pairs={{0,32},{32,0},{1,33},{33,1},{2,34},{34,2},{3,35},{35,3},{4,36},{36... | collective-permute-start | bytes 221192 | tf_op jit(solution)/shard_map/ppermute | solution.py:486
  11.8 5.7 %collective-permute-start.13 = (bf16[9,16,256]{2,1,0:T(8,128)(2,1)S(1)}, bf16[9,16,256]{2,1,0:T(8,128)(2,1)S(1)}, u32[]{:S(2)}, u32[]{:S(2)}) collective-permute-start(bf16[9,16,256]{2,1,0:T(8,128)(2,1)S(1)} %maximum_maximum_fusion.1), channel_id=1, source_target_pairs={{32,64},{96,128},{160,192},{64,32},{128,96},{192,160},{33,65},{97,... | collective-permute-start | bytes 221192 | tf_op jit(solution)/shard_map/ppermute | solution.py:487
  19.1 2.0 %collective-permute-start.14 = (bf16[4,28,16,128]{3,2,1,0:T(8,128)(2,1)S(1)}, bf16[4,28,16,128]{3,2,1,0:T(8,128)(2,1)S(1)}, u32[]{:S(2)}, u32[]{:S(2)}) collective-permute-start(bf16[4,28,16,128]{3,2,1,0:T(8,128)(2,1)S(1)} %get-tuple-element.100), channel_id=1, source_target_pairs={{0,32},{32,0},{1,33},{33,1},{2,34},{34,2},{3,35},{35,3},{4,36},{36... | collective-permute-start | bytes 1376264 | tf_op jit(solution)/shard_map/ppermute | solution.py:367
  66.3 7.2 %collective-permute-start.15 = (bf16[4,28,16,128]{3,2,1,0:T(8,128)(2,1)S(1)}, bf16[4,28,16,128]{3,2,1,0:T(8,128)(2,1)S(1)}, u32[]{:S(2)}, u32[]{:S(2)}) collective-permute-start(bf16[4,28,16,128]{3,2,1,0:T(8,128)(2,1)S(1)} %bitcast.27), channel_id=1, source_target_pairs={{0,32},{32,0},{1,33},{33,1},{2,34},{34,2},{3,35},{35,3},{4,36},{36... | collective-permute-start | bytes 1376264 | tf_op jit(solution)/shard_map/ppermute | solution.py:372
  71.2 2.3 %copy-start = (bf16[8,64,128]{2,1,0:T(8,128)(2,1)S(1)}, bf16[8,64,128]{2,1,0:T(8,128)(2,1)}, u32[]{:S(2)}) copy-start(bf16[8,64,128]{2,1,0:T(8,128)(2,1)} %features_ref.1) | copy-start | bytes 393220
  71.2 2.3 %copy-start.1 = (bf16[8,64,128]{2,1,0:T(8,128)(2,1)S(1)}, bf16[8,64,128]{2,1,0:T(8,128)(2,1)}, u32[]{:S(2)}) copy-start(bf16[8,64,128]{2,1,0:T(8,128)(2,1)} %cotangent_ref.1) | copy-start | bytes 393220
  71.2 2.3 %copy-start.2 = (s32[40]{0:T(128)S(1)}, s32[40]{0:T(128)}, u32[]{:S(2)}) copy-start(s32[40]{0:T(128)} %recv_slot_ref.1) | copy-start | bytes 484

commit v16 on v15

--- a/solution.py
+++ b/solution.py
@@ -226,10 +226,28 @@
     return planes.reshape(SLOTS * VOXELS, WIDE)
 
 
+def own_half():
+    return lax.axis_index("c") ^ (lax.axis_index("x") >> 1) ^ (lax.axis_index("z") >> 2)
+
+
+def exchange_groups(fixed, spread):
+    sizes = {"x": 4, "y": 4, "z": 8}
+    groups = []
+    for half in range(2):
+        for kept in np.ndindex(*[sizes[axis] for axis in fixed]):
+            group = []
+            for free in np.ndindex(*[sizes[axis] for axis in spread]):
+                at = dict(zip(fixed + spread, kept + free))
+                core = half ^ (at["x"] >> 1) ^ (at["z"] >> 2)
+                group.append(((at["x"] * 2 + core) * 4 + at["y"]) * 8 + at["z"])
+            groups.append([int(device) for device in group])
+    return groups
+
+
 def store_products(flipped_ref, tap, first, send_ref, keep_ref):
-    core = lax.axis_index("c")
+    mine = own_half()
     half = CHANNELS // 2
-    flipped = jnp.concatenate((flipped_ref[1 - core], flipped_ref[core]), axis=0)
+    flipped = jnp.concatenate((flipped_ref[1 - mine], flipped_ref[mine]), axis=0)
     part = jnp.dot(flipped, tap, preferred_element_type=jnp.float32)
     for number in range(9):
         block = part[:, number * CHANNELS : (number + 1) * CHANNELS]
@@ -418,23 +436,24 @@
 def sum_everywhere(arrived, keep):
     chip_sum = (keep + arrived.astype(jnp.float32)).astype(jnp.bfloat16)
     parts = chip_sum.reshape(16, 7, 16, CHANNELS)
-    parts = lax.all_to_all(parts, ("x", "y"), 0, 0)
+    parts = lax.all_to_all(parts, AXES, 0, 0, axis_index_groups=exchange_groups(("z",), ("x", "y")))
     total = jnp.sum(parts.astype(jnp.float32), axis=0)
     largest = jnp.max(jnp.abs(total), axis=(0, 1))
     power = jnp.clip(jnp.ceil(jnp.log2(jnp.maximum(largest, 1e-37))), -100.0, 100.0)
     power = jnp.broadcast_to(power, (8, CHANNELS))
     scaled = (total * jnp.exp2(14.0 - power[0])).reshape(7 * 16, CHANNELS)
     share = jnp.concatenate((scaled, power), axis=0).astype(jnp.float16)
-    column = lax.all_to_all(jnp.broadcast_to(share[None], (8,) + share.shape), "z", 0, 0).astype(jnp.float32)
+    column = lax.all_to_all(jnp.broadcast_to(share[None], (8,) + share.shape), AXES, 0, 0,
+                            axis_index_groups=exchange_groups(("x", "y"), ("z",))).astype(jnp.float32)
     total = jnp.sum(column[:, : 7 * 16] * jnp.exp2(column[:, 7 * 16 : 7 * 16 + 1] - 14.0), axis=0)
     share = (total * (1.0 / (VOXELS * SLOTS))).astype(jnp.bfloat16).reshape(7, 16, CHANNELS)
     whole = jnp.broadcast_to(share[None], (16,) + share.shape)
-    return lax.all_to_all(whole, ("x", "y"), 0, 0).reshape(4, ROWS_M, 16, CHANNELS)
+    return lax.all_to_all(whole, AXES, 0, 0, axis_index_groups=exchange_groups(("z",), ("x", "y"))).reshape(4, ROWS_M, 16, CHANNELS)
 
 
 def spread_kernel(own_ref, other_ref, outputs_ref, grad_ref, outputs_out, grad_out, out_ref, whole, sems):
     half = CHANNELS // 2
-    core = lax.axis_index("c")
+    core = own_half()
     copies = [
         pltpu.make_async_copy(outputs_ref, outputs_out, sems.at[9]),
         pltpu.make_async_copy(grad_ref, grad_out, sems.at[10]),

time: 75.6 us -> 77.1 us (1.020)
  blocking collectives: 44.7 us -> 51.1 us
  starting transfers between devices: 16 us -> 11.1 us
    all_to_all x3, blocking collectives: 44.7 us -> 51.1 us  [the longest x1 21.9 us: sum_everywhere(): lax.all_to_all(parts, AXES, 0, 0, axis_index_groups=exchange_groups(('z',...]
    ppermute x1, starting transfers between devices: 4.91 us -> 0.01 us  [convolve(): other = lax.ppermute(own, 'c', [(0, 1), (1, 0)])]
where the time goes in v16:
time: 77.1 us; the launch traced here: 76.9 us
  blocking collectives  51.1 us (66%)
  starting transfers between devices  11.1 us (14%)
  Pallas kernels  9.83 us (13%)
  between operations  1.71 us (2%)
  waiting for transfers between devices  1.05 us (1%)
  other arithmetic  1.03 us (1%)
    all_to_all x1, blocking collectives, sum_everywhere(): lax.all_to_all(parts, AXES, 0, 0, axis_index_groups=exchange_groups(('z',...  21.9 us
    all_to_all x1, blocking collectives, sum_everywhere(): lax.all_to_all(jnp.broadcast_to(share[None], (8,) + share.shape), AXES, 0...  14.6 us
    all_to_all x1, blocking collectives, sum_everywhere(): lax.all_to_all(whole, AXES, 0, 0, axis_index_groups=exchange_groups(('z',...  14.5 us
    ppermute x1, starting transfers between devices, local(): lax.ppermute(to_first, ('y', 'z'), [(gy, gy ^ 1) for gy in range(32)])  5.44 us
    ppermute x1, starting transfers between devices, local(): lax.ppermute(relayed(to_outer, core), ('x', 'c'), [(2 * x + 1, 2 * x + 2)...  3.03 us
    pallas_call x1, Pallas kernels, mid_taps(): pl.pallas_call(functools.partial(mid_kernel, fill, unroll, len(halos)), i...  2.47 us
    ppermute x1, starting transfers between devices, local(): lax.ppermute(relayed(to_sibling, 1 - core), 'c', [(0, 1), (1, 0)])  1.9 us
    pallas_call x2, Pallas kernels, product(): pl.pallas_call(kernel, in_specs=[VMEM_SPEC] * len(operands), out_specs=VM...  1.87 us
  transfers between devices with their start and end apart: 6, of which 2 were waited for; matrix products, arithmetic and copies ran while one was open for 2% of the time, Pallas kernels for 7%

profile of v16, /device:TPU:1, one launch (start us, length us, event | category | flops | bytes accessed | tf_op | source)
XLA Modules:
  0.0 76.9 jit_solution(15952982759626971190)
XLA Ops:
  0.6 0.0 copy-start.3
  0.6 1.4 %shard_map.82 = (bf16[9,16,256]{2,1,0:T(8,128)(2,1)S(1)}, bf16[9,16,256]{2,1,0:T(8,128)(2,1)S(1)}, bf16[8,16,256]{2,1,0:T(8,128)(2,1)S(1)}, bf16[8,16,256]{2,1,0...) custom-call(s32[40]{0:T(128)} %recv_slot_ref.1, bf16[8,64,128]{2,1,0:T(8,128)(2,1)} %features_ref.1, ...), custom_call_target="tpu_custom_call" | custom-call | tf_op jit(solution)/shard_map/pallas_call | solution.py:121
  2.0 0.7 collective-permute-start.10
  2.7 5.4 %collective-permute-start.11 = (bf16[9,16,256]{2,1,0:T(8,128)(2,1)S(1)}, bf16[9,16,256]{2,1,0:T(8,128)(2,1)S(1)}, u32[]{:S(2)}, u32[]{:S(2)}) collective-permute-start(bf16[9,16,256]{2,1,0:T(8,128)(2,1)S(1)} %get-tuple-element.86), channel_id=1, source_target_pairs={{0,1},{1,0},{2,3},{3,2},{4,5},{5,4},{6,7},{7,6},{8,9},{9,8},{10,11... | collective-permute-start | bytes 221192 | tf_op jit(solution)/shard_map/ppermute | solution.py:498
  8.1 0.7 clamp_bitcast_fusion.dst_ref.table_ref
  8.9 0.1 copy.19
  9.0 0.0 collective-permute-done.10.rest_1_
  9.0 0.9 %collective-permute-done.11.rest_0_ = bf16[9,16,256]{2,1,0:T(8,128)(2,1)S(1)} collective-permute-done((bf16[9,16,256]{2,1,0:T(8,128)(2,1)S(1)}, bf16[9,16,256]{2,1,0:T(8,128)(2,1)S(1)}, u32[]{:S(2)}, u32[]{:S(2)}) %collective-permute-start.11) | collective-permute-done | bytes 73760 | tf_op jit(solution)/shard_map/ppermute | solution.py:498
  9.9 1.9 %collective-permute-start.12 = (bf16[9,16,256]{2,1,0:T(8,128)(2,1)S(1)}, bf16[9,16,256]{2,1,0:T(8,128)(2,1)S(1)}, u32[]{:S(2)}, u32[]{:S(2)}) collective-permute-start(bf16[9,16,256]{2,1,0:T(8,128)(2,1)S(1)} %maximum_maximum_fusion), channel_id=1, source_target_pairs={{0,32},{32,0},{1,33},{33,1},{2,34},{34,2},{3,35},{35,3},{4,36},{36... | collective-permute-start | bytes 221192 | tf_op jit(solution)/shard_map/ppermute | solution.py:505
  11.8 3.0 %collective-permute-start.13 = (bf16[9,16,256]{2,1,0:T(8,128)(2,1)S(1)}, bf16[9,16,256]{2,1,0:T(8,128)(2,1)S(1)}, u32[]{:S(2)}, u32[]{:S(2)}) collective-permute-start(bf16[9,16,256]{2,1,0:T(8,128)(2,1)S(1)} %maximum_maximum_fusion.1), channel_id=1, source_target_pairs={{32,64},{96,128},{160,192},{64,32},{128,96},{192,160},{33,65},{97,... | collective-permute-start | bytes 221192 | tf_op jit(solution)/shard_map/ppermute | solution.py:506
  14.9 0.0 copy-done.3
  14.9 2.5 %shard_map.83 = (bf16[8,4,16,1152]{3,2,1,0:T(8,128)(2,1)S(1)}, bf16[8,4,16,1152]{3,2,1,0:T(8,128)(2,1)S(1)}, bf16[49,64,128]{2,1,0:T(8,128)(2,1)S(1)}, bf16[49,6...) custom-call(s32[8,27]{1,0:T(8,128)S(1)} %clamp_bitcast_fusion.dst_re, ...), custom_call_target="tpu_custom_call" | custom-call | flops 905969664 | bytes 4000000 | tf_op jit(solution)/shard_map/pallas_call | solution.py:327
  17.3 0.0 collective-permute-done.12.rest_0_
  17.4 0.1 collective-permute-done.13.rest_1_
  17.5 1.6 %shard_map.84 = (bf16[4,28,16,128]{3,2,1,0:T(8,128)(2,1)S(1)}, f32[4,28,16,128]{3,2,1,0:T(8,128)S(1)}, bf16[8,2,16,1152]{3,2,1,0:T(8,128)(2,1)S(1)}, bf16[49,64,128]{2,1,0:T(8,128)(2,1)S(1)}) custom-call(s32[8,27]{1,0:T(8,128)S(1)} %clamp_bitcast_fusion.dst_ref.table_ref, ...), custom_call_target="tpu_custom_call", output_to_operand_aliasing={{3}: (3, {})} | custom-call | flops 905969664 | bytes 4000000 | tf_op jit(solution)/shard_map/pallas_call | solution.py:343
  19.1 0.1 collective-permute-start.14
  19.2 0.8 %shard_map.85 = bf16[8,64,128]{2,1,0:T(8,128)(2,1)S(1)} custom-call(bf16[8,4,16,1152]{3,2,1,0:T(8,128)(2,1)S(1)} %get-tuple-element.93.mid, bf16[8,2,16,1152]{3,2,1,0:T(8,128)(2,1)S(1)} %get-tuple-element.101.edge, bf16[27,128,128]{2,1,0:T(8,128)(2,1)S(1)} %copy-done.3, f32[512,128]{1,0:T(8,128)S(1)} %get-tuple-element.102.grad_mid), custom_call_target="tpu_custom_call" | custom-call | flops 905969664 | bytes 4000000 | tf_op jit(solution)/shard_map/pallas_call | solution.py:372
  20.0 1.1 %shard_map.86 = (bf16[8,2,16,1152]{3,2,1,0:T(8,128)(2,1)S(1)}, bf16[49,64,128]{2,1,0:T(8,128)(2,1)S(1)}) custom-call(s32[8,27]{1,0:T(8,128)S(1)} %clamp_bitcast_fusion.dst_ref.table_ref, bf16[49,64,128]{2,1,0:T(8,128)(2,1)S(1)} %get-tuple-element.103._, bf16[9,16,256]{2,1,0:T(8,128)(2,1)S(1)} %collective-permute-done.12.rest_0_, ...), custom_call_target="tpu_custom_call", output_to_operand_aliasing={{1}: (1, {})} | custom-call | flops 905969664 | bytes 4000000 | tf_op jit(solution)/shard_map/pallas_call | solution.py:360
  21.1 0.0 collective-permute-done.14
  21.1 0.1 add_convert_fusion.1
  21.2 21.9 %all_to_all.30 = bf16[16,7,16,128]{3,2,1,0:T(8,128)(2,1)S(1)} all-to-all(bf16[16,7,16,128]{3,2,1,0:T(8,128)(2,1)S(1)} %bitcast.25), channel_id=1, replica_groups={{0,8,16,24,64,72,80,88,160,168,176,184,224,232,240,248},{1,9,17,25,65,7..., dimensions={0} | all-to-all | bytes 917504 | tf_op jit(solution)/shard_map/all_to_all | solution.py:439
  43.2 0.1 convert_reduce_fusion.1
  43.4 14.6 %all_to_all.31 = f16[8,120,128]{2,1,0:T(8,128)(2,1)S(1)} all-to-all(f16[8,120,128]{2,1,0:T(8,128)(2,1)S(1)} %broadcast_in_dim.13), channel_id=1, replica_groups={{0,1,2,3,36,37,38,39},{8,9,10,11,44,45,46,47},{16,17,18,19,52,53,54,55}..., dimensions={0} | all-to-all | bytes 491520 | tf_op jit(solution)/shard_map/all_to_all | solution.py:446
  58.1 0.1 broadcast_in_dim.14
  58.2 14.5 %all_to_all.32 = bf16[16,7,16,128]{3,2,1,0:T(8,128)(2,1)S(1)} all-to-all(bf16[16,7,16,128]{3,2,1,0:T(8,128)(2,1)S(1)} %broadcast_in_dim.14), channel_id=1, replica_groups={{0,8,16,24,64,72,80,88,160,168,176,184,224,232,240,248},{1,9,17,25,65,7..., dimensions={0} | all-to-all | bytes 917504 | tf_op jit(solution)/shard_map/all_to_all | solution.py:451
  72.7 0.0 collective-permute-start.15
  72.7 0.0 copy-start
  72.7 0.0 copy-start.1
  72.7 0.0 copy-start.2
  72.7 1.1 %shard_map.87 = bf16[8,64,128]{2,1,0:T(8,128)(2,1)S(1)} custom-call(bf16[8,4,16,1152]{3,2,1,0:T(8,128)(2,1)S(1)} %get-tuple-element.106.mid, bf16[8,2,16,1152]{3,2,1,0:T(8,128)(2,1)S(1)} %get-tuple-element.107.edge, bf16[27,128,128]{2,1,0:T(8,128)(2,1)S(1)} %copy-done.3), custom_call_target="tpu_custom_call" | custom-call | flops 905969664 | bytes 4000000 | tf_op jit(solution)/shard_map/pallas_call | solution.py:372
  73.8 0.5 slice.38
  75.0 0.0 collective-permute-done.15
  75.0 0.0 copy-done
  75.0 0.0 copy-done.1
  75.0 0.0 copy-done.2
  75.1 1.6 %conditional.1 = ((bf16[8,64,128]{2,1,0:T(8,128)(2,1)}, bf16[8,64,128]{2,1,0:T(8,128)(2,1)}, f32[27,128,128]{2,1,0:T(8,128)})) conditional(s32[]{:T(128)} %bitcast.14, (bf16[4,28,16,128]{3,2,1,0:T(8,128)(2,1)S(1)}, bf16[4,28,16,128]{3,2,1,0:T(8,128)(2,1)S(1)}, bf16[8,64,128]{2,1,0:T(8,128)(2,1)S(1)}, bf16[8,64,128]{2,1,0:T(8,128)(2,1)S(1)}) %tuple.36, ...), branch_computations={%region_3.4_spmd, %region_4.8_spmd} | conditional | flops 4531423232 | bytes 35915928 | solution.py:521
  75.1 1.4 %branch_0_fun.1 = (bf16[8,64,128]{2,1,0:T(8,128)(2,1)}, bf16[8,64,128]{2,1,0:T(8,128)(2,1)}, f32[27,128,128]{2,1,0:T(8,128)}) custom-call(bf16[4,28,16,128]{3,2,1,0:T(8,128)(2,1)S(1)} %get-tuple-element.24.own_ref, bf16[4,28,16,128]{3,2,1,0:T(8,128)(2,1)S(1)} %get-tuple-element.25.other_ref, bf16[8,64,128]{2,1,0:T(8,128)(2,1)S(1)} %get-tuple-element.26.outputs_ref, ...), custom_call_target="tpu_custom_call" | custom-call | tf_op jit(solution)/shard_map/cond/branch_0_fun/pallas_call | solution.py:477
  (16 shorter events, 0.2 us)
Async XLA Ops:
  0.6 14.2 %copy-start.3 = (bf16[27,128,128]{2,1,0:T(8,128)(2,1)S(1)}, bf16[27,128,128]{2,1,0:T(8,128)(2,1)}, u32[]{:S(2)}) copy-start(bf16[27,128,128]{2,1,0:T(8,128)(2,1)} %weights_ref.5) | copy-start | bytes 2654212
  2.0 6.9 %collective-permute-start.10 = (bf16[9,16,256]{2,1,0:T(8,128)(2,1)S(1)}, bf16[9,16,256]{2,1,0:T(8,128)(2,1)S(1)}, u32[]{:S(2)}, u32[]{:S(2)}) collective-permute-start(bf16[9,16,256]{2,1,0:T(8,128)(2,1)S(1)} %get-tuple-element.85), channel_id=1, source_target_pairs={{1,2},{2,1},{3,4},{4,3},{5,6},{6,5},{7,8},{8,7},{9,10},{10,9},{11,... | collective-permute-start | bytes 221192 | tf_op jit(solution)/shard_map/ppermute | solution.py:497
  2.7 7.2 %collective-permute-start.11 = (bf16[9,16,256]{2,1,0:T(8,128)(2,1)S(1)}, bf16[9,16,256]{2,1,0:T(8,128)(2,1)S(1)}, u32[]{:S(2)}, u32[]{:S(2)}) collective-permute-start(bf16[9,16,256]{2,1,0:T(8,128)(2,1)S(1)} %get-tuple-element.86), channel_id=1, source_target_pairs={{0,1},{1,0},{2,3},{3,2},{4,5},{5,4},{6,7},{7,6},{8,9},{9,8},{10,11... | collective-permute-start | bytes 221192 | tf_op jit(solution)/shard_map/ppermute | solution.py:498
  9.9 7.4 %collective-permute-start.12 = (bf16[9,16,256]{2,1,0:T(8,128)(2,1)S(1)}, bf16[9,16,256]{2,1,0:T(8,128)(2,1)S(1)}, u32[]{:S(2)}, u32[]{:S(2)}) collective-permute-start(bf16[9,16,256]{2,1,0:T(8,128)(2,1)S(1)} %maximum_maximum_fusion), channel_id=1, source_target_pairs={{0,32},{32,0},{1,33},{33,1},{2,34},{34,2},{3,35},{35,3},{4,36},{36... | collective-permute-start | bytes 221192 | tf_op jit(solution)/shard_map/ppermute | solution.py:505
  11.8 5.7 %collective-permute-start.13 = (bf16[9,16,256]{2,1,0:T(8,128)(2,1)S(1)}, bf16[9,16,256]{2,1,0:T(8,128)(2,1)S(1)}, u32[]{:S(2)}, u32[]{:S(2)}) collective-permute-start(bf16[9,16,256]{2,1,0:T(8,128)(2,1)S(1)} %maximum_maximum_fusion.1), channel_id=1, source_target_pairs={{32,64},{96,128},{160,192},{64,32},{128,96},{192,160},{33,65},{97,... | collective-permute-start | bytes 221192 | tf_op jit(solution)/shard_map/ppermute | solution.py:506
  19.1 2.0 %collective-permute-start.14 = (bf16[4,28,16,128]{3,2,1,0:T(8,128)(2,1)S(1)}, bf16[4,28,16,128]{3,2,1,0:T(8,128)(2,1)S(1)}, u32[]{:S(2)}, u32[]{:S(2)}) collective-permute-start(bf16[4,28,16,128]{3,2,1,0:T(8,128)(2,1)S(1)} %get-tuple-element.100), channel_id=1, source_target_pairs={{0,32},{32,0},{1,33},{33,1},{2,34},{34,2},{3,35},{35,3},{4,36},{36... | collective-permute-start | bytes 1376264 | tf_op jit(solution)/shard_map/ppermute | solution.py:385
  72.7 2.3 %collective-permute-start.15 = (bf16[4,28,16,128]{3,2,1,0:T(8,128)(2,1)S(1)}, bf16[4,28,16,128]{3,2,1,0:T(8,128)(2,1)S(1)}, u32[]{:S(2)}, u32[]{:S(2)}) collective-permute-start(bf16[4,28,16,128]{3,2,1,0:T(8,128)(2,1)S(1)} %bitcast.27), channel_id=1, source_target_pairs={{0,32},{32,0},{1,33},{33,1},{2,34},{34,2},{3,35},{35,3},{4,36},{36... | collective-permute-start | bytes 1376264 | tf_op jit(solution)/shard_map/ppermute | solution.py:390
  72.7 2.3 %copy-start = (bf16[8,64,128]{2,1,0:T(8,128)(2,1)S(1)}, bf16[8,64,128]{2,1,0:T(8,128)(2,1)}, u32[]{:S(2)}) copy-start(bf16[8,64,128]{2,1,0:T(8,128)(2,1)} %features_ref.1) | copy-start | bytes 393220
  72.7 2.3 %copy-start.1 = (bf16[8,64,128]{2,1,0:T(8,128)(2,1)S(1)}, bf16[8,64,128]{2,1,0:T(8,128)(2,1)}, u32[]{:S(2)}) copy-start(bf16[8,64,128]{2,1,0:T(8,128)(2,1)} %cotangent_ref.1) | copy-start | bytes 393220
  72.7 2.3 %copy-start.2 = (s32[40]{0:T(128)S(1)}, s32[40]{0:T(128)}, u32[]{:S(2)}) copy-start(s32[40]{0:T(128)} %recv_slot_ref.1) | copy-start | bytes 484

commit v17 on v15

--- a/solution.py
+++ b/solution.py
@@ -477,7 +477,7 @@
     flipped = flipped.reshape(2, CHANNELS // 2, SLOTS * VOXELS)
     y_second = lax.ppermute(to_second, ("y", "z"), [(gy, ((gy + 1) ^ 1) - 1) for gy in range(1, 31)])
     y_first = lax.ppermute(to_first, ("y", "z"), [(gy, gy ^ 1) for gy in range(32)])
-    y_second, y_first, dst, flipped = lax.optimization_barrier((y_second, y_first, dst, flipped))
+    y_first, y_second, dst, flipped = lax.optimization_barrier((y_first, y_second, dst, flipped))
 
     def relayed(packet, up):
         corners = [lax.dynamic_slice_in_dim(value[SLOTS:], 8 * up, 8, axis=1) for value in (y_first, y_second)]

time: 75.6 us -> 76.7 us (1.015)
  blocking collectives: 44.7 us -> 47.7 us
  starting transfers between devices: 16 us -> 13.6 us
    ppermute x1, starting transfers between devices: 5.44 us -> 2.56 us  [local(): lax.ppermute(to_first, ('y', 'z'), [(gy, gy ^ 1) for gy in range(32)])]
    all_to_all x1, blocking collectives: 12.5 us -> 14.6 us  [sum_everywhere(): lax.all_to_all(jnp.broadcast_to(share[None], (8,) + share.shape), 'z', 0, 0)]
    ppermute x1, starting transfers between devices: 1.9 us -> 3.46 us  [local(): lax.ppermute(relayed(to_sibling, 1 - core), 'c', [(0, 1), (1, 0)])]
    ppermute x1, waiting for transfers between devices: 0.13 us -> 1.24 us  [local(): lax.ppermute(relayed(to_outer, core), ('x', 'c'), [(2 * x + 1, 2 * x + 2)...]
    ppermute x1, starting transfers between devices: 3.03 us -> 1.91 us  [local(): lax.ppermute(relayed(to_outer, core), ('x', 'c'), [(2 * x + 1, 2 * x + 2)...]
    all_to_all x1, blocking collectives: 20.4 us -> 21.3 us  [sum_everywhere(): parts = lax.all_to_all(parts, ('x', 'y'), 0, 0)]
where the time goes in v17:
time: 76.7 us; the launch traced here: 76.4 us
  blocking collectives  47.7 us (62%)
  starting transfers between devices  13.6 us (18%)
  Pallas kernels  9.84 us (13%)
  between operations  1.71 us (2%)
  waiting for transfers between devices  1.51 us (2%)
  other arithmetic  1.03 us (1%)
  local copies, waits for them, and re-layouts  0.77 us (1%)
    all_to_all x1, blocking collectives, sum_everywhere(): parts = lax.all_to_all(parts, ('x', 'y'), 0, 0)  21.3 us
    all_to_all x1, blocking collectives, sum_everywhere(): lax.all_to_all(jnp.broadcast_to(share[None], (8,) + share.shape), 'z', 0, 0)  14.6 us
    all_to_all x1, blocking collectives, sum_everywhere(): lax.all_to_all(whole, ('x', 'y'), 0, 0).reshape(4, ROWS_M, 16, CHANNELS)  11.7 us
    ppermute x1, starting transfers between devices, convolve(): other = lax.ppermute(own, 'c', [(0, 1), (1, 0)])  4.92 us
    ppermute x1, starting transfers between devices, local(): lax.ppermute(relayed(to_sibling, 1 - core), 'c', [(0, 1), (1, 0)])  3.46 us
    ppermute x1, starting transfers between devices, local(): lax.ppermute(to_first, ('y', 'z'), [(gy, gy ^ 1) for gy in range(32)])  2.56 us
    pallas_call x1, Pallas kernels, mid_taps(): pl.pallas_call(functools.partial(mid_kernel, fill, unroll, len(halos)), i...  2.47 us
    ppermute x1, starting transfers between devices, local(): lax.ppermute(relayed(to_outer, core), ('x', 'c'), [(2 * x + 1, 2 * x + 2)...  1.91 us
  transfers between devices with their start and end apart: 6, of which 2 were waited for; matrix products, arithmetic and copies ran while one was open for 2% of the time, Pallas kernels for 7%

profile of v17, /device:TPU:1, one launch (start us, length us, event | category | flops | bytes accessed | tf_op | source)
XLA Modules:
  0.0 76.4 jit_solution(16865911963636881749)
XLA Ops:
  0.6 0.0 copy-start.3
  0.6 1.4 %shard_map.82 = (bf16[9,16,256]{2,1,0:T(8,128)(2,1)S(1)}, bf16[9,16,256]{2,1,0:T(8,128)(2,1)S(1)}, bf16[8,16,256]{2,1,0:T(8,128)(2,1)S(1)}, bf16[8,16,256]{2,1,0...) custom-call(s32[40]{0:T(128)} %recv_slot_ref.1, bf16[8,64,128]{2,1,0:T(8,128)(2,1)} %features_ref.1, ...), custom_call_target="tpu_custom_call" | custom-call | tf_op jit(solution)/shard_map/pallas_call | solution.py:121
  2.0 2.6 %collective-permute-start.10 = (bf16[9,16,256]{2,1,0:T(8,128)(2,1)S(1)}, bf16[9,16,256]{2,1,0:T(8,128)(2,1)S(1)}, u32[]{:S(2)}, u32[]{:S(2)}) collective-permute-start(bf16[9,16,256]{2,1,0:T(8,128)(2,1)S(1)} %get-tuple-element.85), channel_id=1, source_target_pairs={{0,1},{1,0},{2,3},{3,2},{4,5},{5,4},{6,7},{7,6},{8,9},{9,8},{10,11... | collective-permute-start | bytes 221192 | tf_op jit(solution)/shard_map/ppermute | solution.py:479
  4.6 0.7 collective-permute-start.11
  5.3 0.7 clamp_bitcast_fusion.dst_ref.table_ref
  6.0 0.1 copy.19
  6.1 0.3 collective-permute-done.10.rest_0_
  6.3 0.0 collective-permute-done.11.rest_1_
  6.4 3.5 %collective-permute-start.12 = (bf16[9,16,256]{2,1,0:T(8,128)(2,1)S(1)}, bf16[9,16,256]{2,1,0:T(8,128)(2,1)S(1)}, u32[]{:S(2)}, u32[]{:S(2)}) collective-permute-start(bf16[9,16,256]{2,1,0:T(8,128)(2,1)S(1)} %maximum_maximum_fusion), channel_id=1, source_target_pairs={{0,32},{32,0},{1,33},{33,1},{2,34},{34,2},{3,35},{35,3},{4,36},{36... | collective-permute-start | bytes 221192 | tf_op jit(solution)/shard_map/ppermute | solution.py:486
  9.8 1.9 %collective-permute-start.13 = (bf16[9,16,256]{2,1,0:T(8,128)(2,1)S(1)}, bf16[9,16,256]{2,1,0:T(8,128)(2,1)S(1)}, u32[]{:S(2)}, u32[]{:S(2)}) collective-permute-start(bf16[9,16,256]{2,1,0:T(8,128)(2,1)S(1)} %maximum_maximum_fusion.1), channel_id=1, source_target_pairs={{32,64},{96,128},{160,192},{64,32},{128,96},{192,160},{33,65},{97,... | collective-permute-start | bytes 221192 | tf_op jit(solution)/shard_map/ppermute | solution.py:487
  11.8 0.0 copy-done.3
  11.8 2.5 %shard_map.83 = (bf16[8,4,16,1152]{3,2,1,0:T(8,128)(2,1)S(1)}, bf16[8,4,16,1152]{3,2,1,0:T(8,128)(2,1)S(1)}, bf16[49,64,128]{2,1,0:T(8,128)(2,1)S(1)}, bf16[49,6...) custom-call(s32[8,27]{1,0:T(8,128)S(1)} %clamp_bitcast_fusion.dst_re, ...), custom_call_target="tpu_custom_call" | custom-call | flops 905969664 | bytes 4000000 | tf_op jit(solution)/shard_map/pallas_call | solution.py:309
  14.3 0.0 collective-permute-done.12.rest_0_
  14.3 1.2 %collective-permute-done.13.rest_1_ = bf16[9,16,256]{2,1,0:T(8,128)(2,1)S(1)} collective-permute-done((bf16[9,16,256]{2,1,0:T(8,128)(2,1)S(1)}, bf16[9,16,256]{2,1,0:T(8,128)(2,1)S(1)}, u32[]{:S(2)}, u32[]{:S(2)}) %collective-permute-start.13) | collective-permute-done | bytes 73760 | tf_op jit(solution)/shard_map/ppermute | solution.py:487
  15.5 1.6 %shard_map.84 = (bf16[4,28,16,128]{3,2,1,0:T(8,128)(2,1)S(1)}, f32[4,28,16,128]{3,2,1,0:T(8,128)S(1)}, bf16[8,2,16,1152]{3,2,1,0:T(8,128)(2,1)S(1)}, bf16[49,64,128]{2,1,0:T(8,128)(2,1)S(1)}) custom-call(s32[8,27]{1,0:T(8,128)S(1)} %clamp_bitcast_fusion.dst_ref.table_ref, ...), custom_call_target="tpu_custom_call", output_to_operand_aliasing={{3}: (3, {})} | custom-call | flops 905969664 | bytes 4000000 | tf_op jit(solution)/shard_map/pallas_call | solution.py:325
  17.1 0.1 collective-permute-start.14
  17.2 0.8 %shard_map.85 = bf16[8,64,128]{2,1,0:T(8,128)(2,1)S(1)} custom-call(bf16[8,4,16,1152]{3,2,1,0:T(8,128)(2,1)S(1)} %get-tuple-element.93.mid, bf16[8,2,16,1152]{3,2,1,0:T(8,128)(2,1)S(1)} %get-tuple-element.101.edge, bf16[27,128,128]{2,1,0:T(8,128)(2,1)S(1)} %copy-done.3, f32[512,128]{1,0:T(8,128)S(1)} %get-tuple-element.102.grad_mid), custom_call_target="tpu_custom_call" | custom-call | flops 905969664 | bytes 4000000 | tf_op jit(solution)/shard_map/pallas_call | solution.py:354
  18.0 1.1 %shard_map.86 = (bf16[8,2,16,1152]{3,2,1,0:T(8,128)(2,1)S(1)}, bf16[49,64,128]{2,1,0:T(8,128)(2,1)S(1)}) custom-call(s32[8,27]{1,0:T(8,128)S(1)} %clamp_bitcast_fusion.dst_ref.table_ref, bf16[49,64,128]{2,1,0:T(8,128)(2,1)S(1)} %get-tuple-element.103._, bf16[9,16,256]{2,1,0:T(8,128)(2,1)S(1)} %collective-permute-done.12.rest_0_, ...), custom_call_target="tpu_custom_call", output_to_operand_aliasing={{1}: (1, {})} | custom-call | flops 905969664 | bytes 4000000 | tf_op jit(solution)/shard_map/pallas_call | solution.py:342
  19.1 0.0 collective-permute-done.14
  19.2 0.1 add_convert_fusion.1
  19.3 21.3 %all_to_all.30 = bf16[16,7,16,128]{3,2,1,0:T(8,128)(2,1)S(1)} all-to-all(bf16[16,7,16,128]{3,2,1,0:T(8,128)(2,1)S(1)} %bitcast.25), channel_id=1, replica_groups=mesh['x'=4,'c'=2,'y'=4,'z'=8] {'x','y'}, dimensions={0} | all-to-all | bytes 917504 | tf_op jit(solution)/shard_map/all_to_all | solution.py:421
  40.6 0.1 convert_reduce_fusion.1
  40.8 14.6 %all_to_all.31 = f16[8,120,128]{2,1,0:T(8,128)(2,1)S(1)} all-to-all(f16[8,120,128]{2,1,0:T(8,128)(2,1)S(1)} %broadcast_in_dim.13), channel_id=1, replica_groups=mesh['x'=4,'c'=2,'y'=4,'z'=8] {'z'}, dimensions={0} | all-to-all | bytes 491520 | tf_op jit(solution)/shard_map/all_to_all | solution.py:428
  55.6 0.1 broadcast_in_dim.14
  55.6 11.7 %all_to_all.32 = bf16[16,7,16,128]{3,2,1,0:T(8,128)(2,1)S(1)} all-to-all(bf16[16,7,16,128]{3,2,1,0:T(8,128)(2,1)S(1)} %broadcast_in_dim.14), channel_id=1, replica_groups=mesh['x'=4,'c'=2,'y'=4,'z'=8] {'x','y'}, dimensions={0} | all-to-all | bytes 917504 | tf_op jit(solution)/shard_map/all_to_all | solution.py:432
  67.4 4.9 %collective-permute-start.15 = (bf16[4,28,16,128]{3,2,1,0:T(8,128)(2,1)S(1)}, bf16[4,28,16,128]{3,2,1,0:T(8,128)(2,1)S(1)}, u32[]{:S(2)}, u32[]{:S(2)}) collective-permute-start(bf16[4,28,16,128]{3,2,1,0:T(8,128)(2,1)S(1)} %bitcast.27), channel_id=1, source_target_pairs={{0,32},{32,0},{1,33},{33,1},{2,34},{34,2},{3,35},{35,3},{4,36},{36... | collective-permute-start | bytes 1376264 | tf_op jit(solution)/shard_map/ppermute | solution.py:372
  72.3 0.0 copy-start
  72.3 0.0 copy-start.1
  72.3 0.0 copy-start.2
  72.3 1.1 %shard_map.87 = bf16[8,64,128]{2,1,0:T(8,128)(2,1)S(1)} custom-call(bf16[8,4,16,1152]{3,2,1,0:T(8,128)(2,1)S(1)} %get-tuple-element.106.mid, bf16[8,2,16,1152]{3,2,1,0:T(8,128)(2,1)S(1)} %get-tuple-element.107.edge, bf16[27,128,128]{2,1,0:T(8,128)(2,1)S(1)} %copy-done.3), custom_call_target="tpu_custom_call" | custom-call | flops 905969664 | bytes 4000000 | tf_op jit(solution)/shard_map/pallas_call | solution.py:354
  73.4 0.5 slice.38
  74.6 0.0 collective-permute-done.15
  74.6 0.0 copy-done
  74.6 0.0 copy-done.1
  74.6 0.0 copy-done.2
  74.6 1.6 %conditional.1 = ((bf16[8,64,128]{2,1,0:T(8,128)(2,1)}, bf16[8,64,128]{2,1,0:T(8,128)(2,1)}, f32[27,128,128]{2,1,0:T(8,128)})) conditional(s32[]{:T(128)} %bitcast.14, (bf16[4,28,16,128]{3,2,1,0:T(8,128)(2,1)S(1)}, bf16[4,28,16,128]{3,2,1,0:T(8,128)(2,1)S(1)}, bf16[8,64,128]{2,1,0:T(8,128)(2,1)S(1)}, bf16[8,64,128]{2,1,0:T(8,128)(2,1)S(1)}) %tuple.36, ...), branch_computations={%region_3.4_spmd, %region_4.8_spmd} | conditional | flops 4531423232 | bytes 35915928 | solution.py:502
  74.6 1.4 %branch_0_fun.1 = (bf16[8,64,128]{2,1,0:T(8,128)(2,1)}, bf16[8,64,128]{2,1,0:T(8,128)(2,1)}, f32[27,128,128]{2,1,0:T(8,128)}) custom-call(bf16[4,28,16,128]{3,2,1,0:T(8,128)(2,1)S(1)} %get-tuple-element.24.own_ref, bf16[4,28,16,128]{3,2,1,0:T(8,128)(2,1)S(1)} %get-tuple-element.25.other_ref, bf16[8,64,128]{2,1,0:T(8,128)(2,1)S(1)} %get-tuple-element.26.outputs_ref, ...), custom_call_target="tpu_custom_call" | custom-call | tf_op jit(solution)/shard_map/cond/branch_0_fun/pallas_call | solution.py:458
  (16 shorter events, 0.2 us)
Async XLA Ops:
  0.6 11.1 %copy-start.3 = (bf16[27,128,128]{2,1,0:T(8,128)(2,1)S(1)}, bf16[27,128,128]{2,1,0:T(8,128)(2,1)}, u32[]{:S(2)}) copy-start(bf16[27,128,128]{2,1,0:T(8,128)(2,1)} %weights_ref.5) | copy-start | bytes 2654212
  2.0 4.3 %collective-permute-start.10 = (bf16[9,16,256]{2,1,0:T(8,128)(2,1)S(1)}, bf16[9,16,256]{2,1,0:T(8,128)(2,1)S(1)}, u32[]{:S(2)}, u32[]{:S(2)}) collective-permute-start(bf16[9,16,256]{2,1,0:T(8,128)(2,1)S(1)} %get-tuple-element.85), channel_id=1, source_target_pairs={{0,1},{1,0},{2,3},{3,2},{4,5},{5,4},{6,7},{7,6},{8,9},{9,8},{10,11... | collective-permute-start | bytes 221192 | tf_op jit(solution)/shard_map/ppermute | solution.py:479
  4.6 1.7 %collective-permute-start.11 = (bf16[9,16,256]{2,1,0:T(8,128)(2,1)S(1)}, bf16[9,16,256]{2,1,0:T(8,128)(2,1)S(1)}, u32[]{:S(2)}, u32[]{:S(2)}) collective-permute-start(bf16[9,16,256]{2,1,0:T(8,128)(2,1)S(1)} %get-tuple-element.86), channel_id=1, source_target_pairs={{1,2},{2,1},{3,4},{4,3},{5,6},{6,5},{7,8},{8,7},{9,10},{10,9},{11,... | collective-permute-start | bytes 221192 | tf_op jit(solution)/shard_map/ppermute | solution.py:478
  6.4 7.9 %collective-permute-start.12 = (bf16[9,16,256]{2,1,0:T(8,128)(2,1)S(1)}, bf16[9,16,256]{2,1,0:T(8,128)(2,1)S(1)}, u32[]{:S(2)}, u32[]{:S(2)}) collective-permute-start(bf16[9,16,256]{2,1,0:T(8,128)(2,1)S(1)} %maximum_maximum_fusion), channel_id=1, source_target_pairs={{0,32},{32,0},{1,33},{33,1},{2,34},{34,2},{3,35},{35,3},{4,36},{36... | collective-permute-start | bytes 221192 | tf_op jit(solution)/shard_map/ppermute | solution.py:486
  9.8 5.7 %collective-permute-start.13 = (bf16[9,16,256]{2,1,0:T(8,128)(2,1)S(1)}, bf16[9,16,256]{2,1,0:T(8,128)(2,1)S(1)}, u32[]{:S(2)}, u32[]{:S(2)}) collective-permute-start(bf16[9,16,256]{2,1,0:T(8,128)(2,1)S(1)} %maximum_maximum_fusion.1), channel_id=1, source_target_pairs={{32,64},{96,128},{160,192},{64,32},{128,96},{192,160},{33,65},{97,... | collective-permute-start | bytes 221192 | tf_op jit(solution)/shard_map/ppermute | solution.py:487
  17.1 2.0 %collective-permute-start.14 = (bf16[4,28,16,128]{3,2,1,0:T(8,128)(2,1)S(1)}, bf16[4,28,16,128]{3,2,1,0:T(8,128)(2,1)S(1)}, u32[]{:S(2)}, u32[]{:S(2)}) collective-permute-start(bf16[4,28,16,128]{3,2,1,0:T(8,128)(2,1)S(1)} %get-tuple-element.100), channel_id=1, source_target_pairs={{0,32},{32,0},{1,33},{33,1},{2,34},{34,2},{3,35},{35,3},{4,36},{36... | collective-permute-start | bytes 1376264 | tf_op jit(solution)/shard_map/ppermute | solution.py:367
  67.4 7.2 %collective-permute-start.15 = (bf16[4,28,16,128]{3,2,1,0:T(8,128)(2,1)S(1)}, bf16[4,28,16,128]{3,2,1,0:T(8,128)(2,1)S(1)}, u32[]{:S(2)}, u32[]{:S(2)}) collective-permute-start(bf16[4,28,16,128]{3,2,1,0:T(8,128)(2,1)S(1)} %bitcast.27), channel_id=1, source_target_pairs={{0,32},{32,0},{1,33},{33,1},{2,34},{34,2},{3,35},{35,3},{4,36},{36... | collective-permute-start | bytes 1376264 | tf_op jit(solution)/shard_map/ppermute | solution.py:372
  72.3 2.3 %copy-start = (bf16[8,64,128]{2,1,0:T(8,128)(2,1)S(1)}, bf16[8,64,128]{2,1,0:T(8,128)(2,1)}, u32[]{:S(2)}) copy-start(bf16[8,64,128]{2,1,0:T(8,128)(2,1)} %features_ref.1) | copy-start | bytes 393220
  72.3 2.3 %copy-start.1 = (bf16[8,64,128]{2,1,0:T(8,128)(2,1)S(1)}, bf16[8,64,128]{2,1,0:T(8,128)(2,1)}, u32[]{:S(2)}) copy-start(bf16[8,64,128]{2,1,0:T(8,128)(2,1)} %cotangent_ref.1) | copy-start | bytes 393220
  72.3 2.3 %copy-start.2 = (s32[40]{0:T(128)S(1)}, s32[40]{0:T(128)}, u32[]{:S(2)}) copy-start(s32[40]{0:T(128)} %recv_slot_ref.1) | copy-start | bytes 484

commit v18 on v15

--- a/solution.py
+++ b/solution.py
@@ -483,9 +483,9 @@
         corners = [lax.dynamic_slice_in_dim(value[SLOTS:], 8 * up, 8, axis=1) for value in (y_first, y_second)]
         return jnp.concatenate((packet, jnp.concatenate(corners, axis=1)), axis=0)
 
-    x_sibling = lax.ppermute(relayed(to_sibling, 1 - core), "c", [(0, 1), (1, 0)])
     x_outer = lax.ppermute(relayed(to_outer, core), ("x", "c"), [(2 * x + 1, 2 * x + 2) for x in range(3)]
                            + [(2 * x + 2, 2 * x + 1) for x in range(3)])
+    x_sibling = lax.ppermute(relayed(to_sibling, 1 - core), "c", [(0, 1), (1, 0)])
     mids = mid_taps(fill_along_y, SLOTS, dst, own_f, own_c, (y_first, y_second), flipped, weights)
     results = convolve(fill_along_x, SLOTS, dst, mids, (x_sibling, x_outer), flipped, weights)
 

time: 75.6 us -> 75.6 us (level)
  no operation moved by 1% of the time
where the time goes in v18:
time: 75.6 us; the launch traced here: 75.3 us
  blocking collectives  44.7 us (59%)
  starting transfers between devices  16 us (21%)
  Pallas kernels  9.83 us (13%)
  between operations  1.71 us (2%)
  waiting for transfers between devices  1.04 us (1%)
  other arithmetic  1.03 us (1%)
  local copies, waits for them, and re-layouts  0.77 us (1%)
    all_to_all x1, blocking collectives, sum_everywhere(): parts = lax.all_to_all(parts, ('x', 'y'), 0, 0)  20.4 us
    all_to_all x1, blocking collectives, sum_everywhere(): lax.all_to_all(jnp.broadcast_to(share[None], (8,) + share.shape), 'z', 0, 0)  12.5 us
    all_to_all x1, blocking collectives, sum_everywhere(): lax.all_to_all(whole, ('x', 'y'), 0, 0).reshape(4, ROWS_M, 16, CHANNELS)  11.7 us
    ppermute x1, starting transfers between devices, local(): lax.ppermute(to_first, ('y', 'z'), [(gy, gy ^ 1) for gy in range(32)])  5.44 us
    ppermute x1, starting transfers between devices, convolve(): other = lax.ppermute(own, 'c', [(0, 1), (1, 0)])  4.91 us
    ppermute x1, starting transfers between devices, local(): lax.ppermute(relayed(to_outer, core), ('x', 'c'), [(2 * x + 1, 2 * x + 2)...  3.03 us
    pallas_call x1, Pallas kernels, mid_taps(): pl.pallas_call(functools.partial(mid_kernel, fill, unroll, len(halos)), i...  2.47 us
    ppermute x1, starting transfers between devices, local(): lax.ppermute(relayed(to_sibling, 1 - core), 'c', [(0, 1), (1, 0)])  1.9 us
  transfers between devices with their start and end apart: 6, of which 2 were waited for; matrix products, arithmetic and copies ran while one was open for 2% of the time, Pallas kernels for 7%

profile of v18, /device:TPU:1, one launch (start us, length us, event | category | flops | bytes accessed | tf_op | source)
XLA Modules:
  0.0 75.3 jit_solution(138493258970464450)
XLA Ops:
  0.6 0.0 copy-start.3
  0.6 1.4 %shard_map.82 = (bf16[9,16,256]{2,1,0:T(8,128)(2,1)S(1)}, bf16[9,16,256]{2,1,0:T(8,128)(2,1)S(1)}, bf16[8,16,256]{2,1,0:T(8,128)(2,1)S(1)}, bf16[8,16,256]{2,1,0...) custom-call(s32[40]{0:T(128)} %recv_slot_ref.1, bf16[8,64,128]{2,1,0:T(8,128)(2,1)} %features_ref.1, ...), custom_call_target="tpu_custom_call" | custom-call | tf_op jit(solution)/shard_map/pallas_call | solution.py:121
  2.0 0.7 collective-permute-start.10
  2.7 5.4 %collective-permute-start.11 = (bf16[9,16,256]{2,1,0:T(8,128)(2,1)S(1)}, bf16[9,16,256]{2,1,0:T(8,128)(2,1)S(1)}, u32[]{:S(2)}, u32[]{:S(2)}) collective-permute-start(bf16[9,16,256]{2,1,0:T(8,128)(2,1)S(1)} %get-tuple-element.86), channel_id=1, source_target_pairs={{0,1},{1,0},{2,3},{3,2},{4,5},{5,4},{6,7},{7,6},{8,9},{9,8},{10,11... | collective-permute-start | bytes 221192 | tf_op jit(solution)/shard_map/ppermute | solution.py:479
  8.1 0.7 clamp_bitcast_fusion.dst_ref.table_ref
  8.9 0.1 copy.19
  9.0 0.0 collective-permute-done.10.rest_1_
  9.0 0.9 %collective-permute-done.11.rest_0_ = bf16[9,16,256]{2,1,0:T(8,128)(2,1)S(1)} collective-permute-done((bf16[9,16,256]{2,1,0:T(8,128)(2,1)S(1)}, bf16[9,16,256]{2,1,0:T(8,128)(2,1)S(1)}, u32[]{:S(2)}, u32[]{:S(2)}) %collective-permute-start.11) | collective-permute-done | bytes 73760 | tf_op jit(solution)/shard_map/ppermute | solution.py:479
  9.9 1.9 %collective-permute-start.12 = (bf16[9,16,256]{2,1,0:T(8,128)(2,1)S(1)}, bf16[9,16,256]{2,1,0:T(8,128)(2,1)S(1)}, u32[]{:S(2)}, u32[]{:S(2)}) collective-permute-start(bf16[9,16,256]{2,1,0:T(8,128)(2,1)S(1)} %maximum_maximum_fusion), channel_id=1, source_target_pairs={{0,32},{32,0},{1,33},{33,1},{2,34},{34,2},{3,35},{35,3},{4,36},{36... | collective-permute-start | bytes 221192 | tf_op jit(solution)/shard_map/ppermute | solution.py:488
  11.8 3.0 %collective-permute-start.13 = (bf16[9,16,256]{2,1,0:T(8,128)(2,1)S(1)}, bf16[9,16,256]{2,1,0:T(8,128)(2,1)S(1)}, u32[]{:S(2)}, u32[]{:S(2)}) collective-permute-start(bf16[9,16,256]{2,1,0:T(8,128)(2,1)S(1)} %maximum_maximum_fusion.1), channel_id=1, source_target_pairs={{32,64},{96,128},{160,192},{64,32},{128,96},{192,160},{33,65},{97,... | collective-permute-start | bytes 221192 | tf_op jit(solution)/shard_map/ppermute | solution.py:486
  14.9 0.0 copy-done.3
  14.9 2.5 %shard_map.83 = (bf16[8,4,16,1152]{3,2,1,0:T(8,128)(2,1)S(1)}, bf16[8,4,16,1152]{3,2,1,0:T(8,128)(2,1)S(1)}, bf16[49,64,128]{2,1,0:T(8,128)(2,1)S(1)}, bf16[49,6...) custom-call(s32[8,27]{1,0:T(8,128)S(1)} %clamp_bitcast_fusion.dst_re, ...), custom_call_target="tpu_custom_call" | custom-call | flops 905969664 | bytes 4000000 | tf_op jit(solution)/shard_map/pallas_call | solution.py:309
  17.4 0.0 collective-permute-done.12.rest_0_
  17.4 0.1 collective-permute-done.13.rest_1_
  17.5 1.6 %shard_map.84 = (bf16[4,28,16,128]{3,2,1,0:T(8,128)(2,1)S(1)}, f32[4,28,16,128]{3,2,1,0:T(8,128)S(1)}, bf16[8,2,16,1152]{3,2,1,0:T(8,128)(2,1)S(1)}, bf16[49,64,128]{2,1,0:T(8,128)(2,1)S(1)}) custom-call(s32[8,27]{1,0:T(8,128)S(1)} %clamp_bitcast_fusion.dst_ref.table_ref, ...), custom_call_target="tpu_custom_call", output_to_operand_aliasing={{3}: (3, {})} | custom-call | flops 905969664 | bytes 4000000 | tf_op jit(solution)/shard_map/pallas_call | solution.py:325
  19.1 0.1 collective-permute-start.14
  19.2 0.8 %shard_map.85 = bf16[8,64,128]{2,1,0:T(8,128)(2,1)S(1)} custom-call(bf16[8,4,16,1152]{3,2,1,0:T(8,128)(2,1)S(1)} %get-tuple-element.93.mid, bf16[8,2,16,1152]{3,2,1,0:T(8,128)(2,1)S(1)} %get-tuple-element.101.edge, bf16[27,128,128]{2,1,0:T(8,128)(2,1)S(1)} %copy-done.3, f32[512,128]{1,0:T(8,128)S(1)} %get-tuple-element.102.grad_mid), custom_call_target="tpu_custom_call" | custom-call | flops 905969664 | bytes 4000000 | tf_op jit(solution)/shard_map/pallas_call | solution.py:354
  20.0 1.1 %shard_map.86 = (bf16[8,2,16,1152]{3,2,1,0:T(8,128)(2,1)S(1)}, bf16[49,64,128]{2,1,0:T(8,128)(2,1)S(1)}) custom-call(s32[8,27]{1,0:T(8,128)S(1)} %clamp_bitcast_fusion.dst_ref.table_ref, bf16[49,64,128]{2,1,0:T(8,128)(2,1)S(1)} %get-tuple-element.103._, bf16[9,16,256]{2,1,0:T(8,128)(2,1)S(1)} %collective-permute-done.12.rest_0_, ...), custom_call_target="tpu_custom_call", output_to_operand_aliasing={{1}: (1, {})} | custom-call | flops 905969664 | bytes 4000000 | tf_op jit(solution)/shard_map/pallas_call | solution.py:342
  21.1 0.0 collective-permute-done.14
  21.1 0.1 add_convert_fusion.1
  21.2 20.4 %all_to_all.30 = bf16[16,7,16,128]{3,2,1,0:T(8,128)(2,1)S(1)} all-to-all(bf16[16,7,16,128]{3,2,1,0:T(8,128)(2,1)S(1)} %bitcast.25), channel_id=1, replica_groups=mesh['x'=4,'c'=2,'y'=4,'z'=8] {'x','y'}, dimensions={0} | all-to-all | bytes 917504 | tf_op jit(solution)/shard_map/all_to_all | solution.py:421
  41.7 0.1 convert_reduce_fusion.1
  41.9 12.5 %all_to_all.31 = f16[8,120,128]{2,1,0:T(8,128)(2,1)S(1)} all-to-all(f16[8,120,128]{2,1,0:T(8,128)(2,1)S(1)} %broadcast_in_dim.13), channel_id=1, replica_groups=mesh['x'=4,'c'=2,'y'=4,'z'=8] {'z'}, dimensions={0} | all-to-all | bytes 491520 | tf_op jit(solution)/shard_map/all_to_all | solution.py:428
  54.5 0.1 broadcast_in_dim.14
  54.6 11.7 %all_to_all.32 = bf16[16,7,16,128]{3,2,1,0:T(8,128)(2,1)S(1)} all-to-all(bf16[16,7,16,128]{3,2,1,0:T(8,128)(2,1)S(1)} %broadcast_in_dim.14), channel_id=1, replica_groups=mesh['x'=4,'c'=2,'y'=4,'z'=8] {'x','y'}, dimensions={0} | all-to-all | bytes 917504 | tf_op jit(solution)/shard_map/all_to_all | solution.py:432
  66.3 4.9 %collective-permute-start.15 = (bf16[4,28,16,128]{3,2,1,0:T(8,128)(2,1)S(1)}, bf16[4,28,16,128]{3,2,1,0:T(8,128)(2,1)S(1)}, u32[]{:S(2)}, u32[]{:S(2)}) collective-permute-start(bf16[4,28,16,128]{3,2,1,0:T(8,128)(2,1)S(1)} %bitcast.27), channel_id=1, source_target_pairs={{0,32},{32,0},{1,33},{33,1},{2,34},{34,2},{3,35},{35,3},{4,36},{36... | collective-permute-start | bytes 1376264 | tf_op jit(solution)/shard_map/ppermute | solution.py:372
  71.2 0.0 copy-start
  71.2 0.0 copy-start.1
  71.2 0.0 copy-start.2
  71.2 1.1 %shard_map.87 = bf16[8,64,128]{2,1,0:T(8,128)(2,1)S(1)} custom-call(bf16[8,4,16,1152]{3,2,1,0:T(8,128)(2,1)S(1)} %get-tuple-element.106.mid, bf16[8,2,16,1152]{3,2,1,0:T(8,128)(2,1)S(1)} %get-tuple-element.107.edge, bf16[27,128,128]{2,1,0:T(8,128)(2,1)S(1)} %copy-done.3), custom_call_target="tpu_custom_call" | custom-call | flops 905969664 | bytes 4000000 | tf_op jit(solution)/shard_map/pallas_call | solution.py:354
  72.3 0.5 slice.38
  73.5 0.0 collective-permute-done.15
  73.5 0.0 copy-done
  73.5 0.0 copy-done.1
  73.5 0.0 copy-done.2
  73.5 1.6 %conditional.1 = ((bf16[8,64,128]{2,1,0:T(8,128)(2,1)}, bf16[8,64,128]{2,1,0:T(8,128)(2,1)}, f32[27,128,128]{2,1,0:T(8,128)})) conditional(s32[]{:T(128)} %bitcast.14, (bf16[4,28,16,128]{3,2,1,0:T(8,128)(2,1)S(1)}, bf16[4,28,16,128]{3,2,1,0:T(8,128)(2,1)S(1)}, bf16[8,64,128]{2,1,0:T(8,128)(2,1)S(1)}, bf16[8,64,128]{2,1,0:T(8,128)(2,1)S(1)}) %tuple.36, ...), branch_computations={%region_3.4_spmd, %region_4.8_spmd} | conditional | flops 4531423232 | bytes 35915928 | solution.py:502
  73.5 1.4 %branch_0_fun.1 = (bf16[8,64,128]{2,1,0:T(8,128)(2,1)}, bf16[8,64,128]{2,1,0:T(8,128)(2,1)}, f32[27,128,128]{2,1,0:T(8,128)}) custom-call(bf16[4,28,16,128]{3,2,1,0:T(8,128)(2,1)S(1)} %get-tuple-element.24.own_ref, bf16[4,28,16,128]{3,2,1,0:T(8,128)(2,1)S(1)} %get-tuple-element.25.other_ref, bf16[8,64,128]{2,1,0:T(8,128)(2,1)S(1)} %get-tuple-element.26.outputs_ref, ...), custom_call_target="tpu_custom_call" | custom-call | tf_op jit(solution)/shard_map/cond/branch_0_fun/pallas_call | solution.py:458
  (16 shorter events, 0.2 us)
Async XLA Ops:
  0.6 14.2 %copy-start.3 = (bf16[27,128,128]{2,1,0:T(8,128)(2,1)S(1)}, bf16[27,128,128]{2,1,0:T(8,128)(2,1)}, u32[]{:S(2)}) copy-start(bf16[27,128,128]{2,1,0:T(8,128)(2,1)} %weights_ref.5) | copy-start | bytes 2654212
  2.0 6.9 %collective-permute-start.10 = (bf16[9,16,256]{2,1,0:T(8,128)(2,1)S(1)}, bf16[9,16,256]{2,1,0:T(8,128)(2,1)S(1)}, u32[]{:S(2)}, u32[]{:S(2)}) collective-permute-start(bf16[9,16,256]{2,1,0:T(8,128)(2,1)S(1)} %get-tuple-element.85), channel_id=1, source_target_pairs={{1,2},{2,1},{3,4},{4,3},{5,6},{6,5},{7,8},{8,7},{9,10},{10,9},{11,... | collective-permute-start | bytes 221192 | tf_op jit(solution)/shard_map/ppermute | solution.py:478
  2.7 7.2 %collective-permute-start.11 = (bf16[9,16,256]{2,1,0:T(8,128)(2,1)S(1)}, bf16[9,16,256]{2,1,0:T(8,128)(2,1)S(1)}, u32[]{:S(2)}, u32[]{:S(2)}) collective-permute-start(bf16[9,16,256]{2,1,0:T(8,128)(2,1)S(1)} %get-tuple-element.86), channel_id=1, source_target_pairs={{0,1},{1,0},{2,3},{3,2},{4,5},{5,4},{6,7},{7,6},{8,9},{9,8},{10,11... | collective-permute-start | bytes 221192 | tf_op jit(solution)/shard_map/ppermute | solution.py:479
  9.9 7.4 %collective-permute-start.12 = (bf16[9,16,256]{2,1,0:T(8,128)(2,1)S(1)}, bf16[9,16,256]{2,1,0:T(8,128)(2,1)S(1)}, u32[]{:S(2)}, u32[]{:S(2)}) collective-permute-start(bf16[9,16,256]{2,1,0:T(8,128)(2,1)S(1)} %maximum_maximum_fusion), channel_id=1, source_target_pairs={{0,32},{32,0},{1,33},{33,1},{2,34},{34,2},{3,35},{35,3},{4,36},{36... | collective-permute-start | bytes 221192 | tf_op jit(solution)/shard_map/ppermute | solution.py:488
  11.8 5.7 %collective-permute-start.13 = (bf16[9,16,256]{2,1,0:T(8,128)(2,1)S(1)}, bf16[9,16,256]{2,1,0:T(8,128)(2,1)S(1)}, u32[]{:S(2)}, u32[]{:S(2)}) collective-permute-start(bf16[9,16,256]{2,1,0:T(8,128)(2,1)S(1)} %maximum_maximum_fusion.1), channel_id=1, source_target_pairs={{32,64},{96,128},{160,192},{64,32},{128,96},{192,160},{33,65},{97,... | collective-permute-start | bytes 221192 | tf_op jit(solution)/shard_map/ppermute | solution.py:486
  19.1 2.0 %collective-permute-start.14 = (bf16[4,28,16,128]{3,2,1,0:T(8,128)(2,1)S(1)}, bf16[4,28,16,128]{3,2,1,0:T(8,128)(2,1)S(1)}, u32[]{:S(2)}, u32[]{:S(2)}) collective-permute-start(bf16[4,28,16,128]{3,2,1,0:T(8,128)(2,1)S(1)} %get-tuple-element.100), channel_id=1, source_target_pairs={{0,32},{32,0},{1,33},{33,1},{2,34},{34,2},{3,35},{35,3},{4,36},{36... | collective-permute-start | bytes 1376264 | tf_op jit(solution)/shard_map/ppermute | solution.py:367
  66.3 7.2 %collective-permute-start.15 = (bf16[4,28,16,128]{3,2,1,0:T(8,128)(2,1)S(1)}, bf16[4,28,16,128]{3,2,1,0:T(8,128)(2,1)S(1)}, u32[]{:S(2)}, u32[]{:S(2)}) collective-permute-start(bf16[4,28,16,128]{3,2,1,0:T(8,128)(2,1)S(1)} %bitcast.27), channel_id=1, source_target_pairs={{0,32},{32,0},{1,33},{33,1},{2,34},{34,2},{3,35},{35,3},{4,36},{36... | collective-permute-start | bytes 1376264 | tf_op jit(solution)/shard_map/ppermute | solution.py:372
  71.2 2.3 %copy-start = (bf16[8,64,128]{2,1,0:T(8,128)(2,1)S(1)}, bf16[8,64,128]{2,1,0:T(8,128)(2,1)}, u32[]{:S(2)}) copy-start(bf16[8,64,128]{2,1,0:T(8,128)(2,1)} %features_ref.1) | copy-start | bytes 393220
  71.2 2.3 %copy-start.1 = (bf16[8,64,128]{2,1,0:T(8,128)(2,1)S(1)}, bf16[8,64,128]{2,1,0:T(8,128)(2,1)}, u32[]{:S(2)}) copy-start(bf16[8,64,128]{2,1,0:T(8,128)(2,1)} %cotangent_ref.1) | copy-start | bytes 393220
  71.2 2.3 %copy-start.2 = (s32[40]{0:T(128)S(1)}, s32[40]{0:T(128)}, u32[]{:S(2)}) copy-start(s32[40]{0:T(128)} %recv_slot_ref.1) | copy-start | bytes 484

commit v19 on v15

--- a/solution.py
+++ b/solution.py
@@ -244,9 +244,14 @@
     return lax.dot_general(tap, matrix, (((1,), (1,)), ((), ())), preferred_element_type=jnp.float32)
 
 
+def output_part(tap, weights_ref, side):
+    matrix = weights_ref[side * 9 : side * 9 + 9].reshape(WIDE, CHANNELS)
+    return jnp.dot(tap, matrix, preferred_element_type=jnp.float32)
+
+
 def mid_kernel(fill, unroll, count, dst_ref, features_ref, cotangent_ref, flipped_ref, weights_ref, *rest):
     halos = rest[:count]
-    mid_f, mid_c, bricks_f, bricks_c, send_ref, keep_ref, grad_ref = rest[count:]
+    mid_f, mid_c, bricks_f, bricks_c, send_ref, keep_ref, grad_ref, outputs_ref = rest[count:]
     for kind, (own, bricks, mid) in enumerate(((features_ref, bricks_f, mid_f), (cotangent_ref, bricks_c, mid_c))):
         bricks[:SLOTS] = own[:SLOTS]
         for begin, end in ((SLOTS, SLOTS + STARTS[2]), (SLOTS + STARTS[4], SLOTS + HALO + 1)):
@@ -256,6 +261,7 @@
     tap = mid_c[...].reshape(SLOTS * VOXELS, WIDE)
     store_products(flipped_ref, tap, 0, send_ref, keep_ref)
     grad_ref[...] = grad_part(tap, weights_ref, 1)
+    outputs_ref[...] = output_part(mid_f[...].reshape(SLOTS * VOXELS, WIDE), weights_ref, 1)
 
 
 def weight_kernel(fill, unroll, count, dst_ref, table_ref, mid, _, *rest):
@@ -286,12 +292,10 @@
     build_taps(unroll, dst_ref, bricks, (0, PLANES - 1), edge)
 
 
-def output_kernel(mid, edge, weights_ref, outputs_ref):
-    outputs = None
-    for side in range(3):
-        matrix = weights_ref[side * 9 : side * 9 + 9].reshape(WIDE, CHANNELS)
-        part = jnp.dot(taps_of(mid, edge, side), matrix, preferred_element_type=jnp.float32)
-        outputs = part if outputs is None else outputs + part
+def output_kernel(mid, edge, weights_ref, outputs_mid, outputs_ref):
+    outputs = outputs_mid[...]
+    for side in (0, 2):
+        outputs = outputs + output_part(taps_of(mid, edge, side), weights_ref, side)
     outputs_ref[...] = outputs.astype(jnp.bfloat16).reshape(SLOTS, VOXELS, CHANNELS)
 
 
@@ -309,11 +313,12 @@
     return pl.pallas_call(
         functools.partial(mid_kernel, fill, unroll, len(halos)),
         in_specs=[SMEM_SPEC] + [VMEM_SPEC] * (4 + len(halos)),
-        out_specs=[VMEM_SPEC] * 7,
+        out_specs=[VMEM_SPEC] * 8,
         out_shape=[
             MID_SHAPE, MID_SHAPE, ALL_BRICKS, ALL_BRICKS,
             jax.ShapeDtypeStruct((4, 9, 16, CHANNELS), jnp.bfloat16),
             jax.ShapeDtypeStruct((4, 9, 16, CHANNELS), jnp.float32),
+            jax.ShapeDtypeStruct((SLOTS * VOXELS, CHANNELS), jnp.float32),
             jax.ShapeDtypeStruct((SLOTS * VOXELS, CHANNELS), jnp.float32),
         ],
         compiler_params=PARAMS,
@@ -362,7 +367,7 @@
 
 
 def convolve(fill, unroll, dst, mids, halos, flipped, weights):
-    mid_f, mid_c, bricks_f, bricks_c, send, keep, grad_mid = mids
+    mid_f, mid_c, bricks_f, bricks_c, send, keep, grad_mid, outputs_mid = mids
     send, keep, edge_c, _ = weight_sums(fill, unroll, dst, mid_c, bricks_c, halos, flipped, send, keep)
     arrived = lax.ppermute(send, "c", [(0, 1), (1, 0)])
     input_grad = product(grad_kernel, mid_c, edge_c, weights, grad_mid)
@@ -370,7 +375,7 @@
     arrived, input_grad, edge_f = lax.optimization_barrier((arrived, input_grad, edge_f))
     own = sum_everywhere(arrived, keep)
     other = lax.ppermute(own, "c", [(0, 1), (1, 0)])
-    outputs = product(output_kernel, mid_f, edge_f, weights)
+    outputs = product(output_kernel, mid_f, edge_f, weights, outputs_mid)
     return outputs, input_grad, own, other
 
 

time: 75.6 us -> 75.3 us (level)
  transfers between devices with their start and end apart: 6 -> 6, of which waited for: 2 -> 1; matrix products, arithmetic and copies ran while one was open for 2% -> 2% of each run, Pallas kernels for 7% -> 7%
where the time goes in v19:
time: 75.3 us; the launch traced here: 75 us
  blocking collectives  44.5 us (59%)
  starting transfers between devices  16 us (21%)
  Pallas kernels  9.81 us (13%)
  between operations  1.71 us (2%)
  other arithmetic  1.03 us (1%)
  waiting for transfers between devices  0.92 us (1%)
  local copies, waits for them, and re-layouts  0.77 us (1%)
    all_to_all x1, blocking collectives, sum_everywhere(): parts = lax.all_to_all(parts, ('x', 'y'), 0, 0)  20.2 us
    all_to_all x1, blocking collectives, sum_everywhere(): lax.all_to_all(jnp.broadcast_to(share[None], (8,) + share.shape), 'z', 0, 0)  12.5 us
    all_to_all x1, blocking collectives, sum_everywhere(): lax.all_to_all(whole, ('x', 'y'), 0, 0).reshape(4, ROWS_M, 16, CHANNELS)  11.7 us
    ppermute x1, starting transfers between devices, local(): lax.ppermute(to_first, ('y', 'z'), [(gy, gy ^ 1) for gy in range(32)])  5.44 us
    ppermute x1, starting transfers between devices, convolve(): other = lax.ppermute(own, 'c', [(0, 1), (1, 0)])  4.91 us
    ppermute x1, starting transfers between devices, local(): lax.ppermute(relayed(to_outer, core), ('x', 'c'), [(2 * x + 1, 2 * x + 2)...  3.03 us
    pallas_call x1, Pallas kernels, mid_taps(): pl.pallas_call(functools.partial(mid_kernel, fill, unroll, len(halos)), i...  2.76 us
    ppermute x1, starting transfers between devices, local(): lax.ppermute(relayed(to_sibling, 1 - core), 'c', [(0, 1), (1, 0)])  1.9 us
  transfers between devices with their start and end apart: 6, of which 1 were waited for; matrix products, arithmetic and copies ran while one was open for 2% of the time, Pallas kernels for 7%

profile of v19, /device:TPU:1, one launch (start us, length us, event | category | flops | bytes accessed | tf_op | source)
XLA Modules:
  0.0 75.0 jit_solution(11216753980843206351)
XLA Ops:
  0.6 0.0 copy-start.3
  0.6 1.4 %shard_map.82 = (bf16[9,16,256]{2,1,0:T(8,128)(2,1)S(1)}, bf16[9,16,256]{2,1,0:T(8,128)(2,1)S(1)}, bf16[8,16,256]{2,1,0:T(8,128)(2,1)S(1)}, bf16[8,16,256]{2,1,0...) custom-call(s32[40]{0:T(128)} %recv_slot_ref.1, bf16[8,64,128]{2,1,0:T(8,128)(2,1)} %features_ref.1, ...), custom_call_target="tpu_custom_call" | custom-call | tf_op jit(solution)/shard_map/pallas_call | solution.py:121
  2.0 0.7 collective-permute-start.10
  2.7 5.4 %collective-permute-start.11 = (bf16[9,16,256]{2,1,0:T(8,128)(2,1)S(1)}, bf16[9,16,256]{2,1,0:T(8,128)(2,1)S(1)}, u32[]{:S(2)}, u32[]{:S(2)}) collective-permute-start(bf16[9,16,256]{2,1,0:T(8,128)(2,1)S(1)} %get-tuple-element.88), channel_id=1, source_target_pairs={{0,1},{1,0},{2,3},{3,2},{4,5},{5,4},{6,7},{7,6},{8,9},{9,8},{10,11... | collective-permute-start | bytes 221192 | tf_op jit(solution)/shard_map/ppermute | solution.py:484
  8.1 0.7 clamp_bitcast_fusion.dst_ref.table_ref
  8.9 0.1 copy.19
  9.0 0.0 collective-permute-done.10.rest_1_
  9.0 0.9 %collective-permute-done.11.rest_0_ = bf16[9,16,256]{2,1,0:T(8,128)(2,1)S(1)} collective-permute-done((bf16[9,16,256]{2,1,0:T(8,128)(2,1)S(1)}, bf16[9,16,256]{2,1,0:T(8,128)(2,1)S(1)}, u32[]{:S(2)}, u32[]{:S(2)}) %collective-permute-start.11) | collective-permute-done | bytes 73760 | tf_op jit(solution)/shard_map/ppermute | solution.py:484
  9.9 1.9 %collective-permute-start.12 = (bf16[9,16,256]{2,1,0:T(8,128)(2,1)S(1)}, bf16[9,16,256]{2,1,0:T(8,128)(2,1)S(1)}, u32[]{:S(2)}, u32[]{:S(2)}) collective-permute-start(bf16[9,16,256]{2,1,0:T(8,128)(2,1)S(1)} %maximum_maximum_fusion), channel_id=1, source_target_pairs={{0,32},{32,0},{1,33},{33,1},{2,34},{34,2},{3,35},{35,3},{4,36},{36... | collective-permute-start | bytes 221192 | tf_op jit(solution)/shard_map/ppermute | solution.py:491
  11.8 3.0 %collective-permute-start.13 = (bf16[9,16,256]{2,1,0:T(8,128)(2,1)S(1)}, bf16[9,16,256]{2,1,0:T(8,128)(2,1)S(1)}, u32[]{:S(2)}, u32[]{:S(2)}) collective-permute-start(bf16[9,16,256]{2,1,0:T(8,128)(2,1)S(1)} %maximum_maximum_fusion.1), channel_id=1, source_target_pairs={{32,64},{96,128},{160,192},{64,32},{128,96},{192,160},{33,65},{97,... | collective-permute-start | bytes 221192 | tf_op jit(solution)/shard_map/ppermute | solution.py:492
  14.9 0.0 copy-done.3
  14.9 2.8 %shard_map.83 = (bf16[8,4,16,1152]{3,2,1,0:T(8,128)(2,1)S(1)}, bf16[8,4,16,1152]{3,2,1,0:T(8,128)(2,1)S(1)}, bf16[49,64,128]{2,1,0:T(8,128)(2,1)S(1)}, bf16[49,6...) custom-call(s32[8,27]{1,0:T(8,128)S(1)} %clamp_bitcast_fusion.dst_re, ...), custom_call_target="tpu_custom_call" | custom-call | flops 905969664 | bytes 4000000 | tf_op jit(solution)/shard_map/pallas_call | solution.py:313
  17.6 0.0 collective-permute-done.12.rest_0_
  17.6 0.0 collective-permute-done.13.rest_1_
  17.7 1.6 %shard_map.84 = (bf16[4,28,16,128]{3,2,1,0:T(8,128)(2,1)S(1)}, f32[4,28,16,128]{3,2,1,0:T(8,128)S(1)}, bf16[8,2,16,1152]{3,2,1,0:T(8,128)(2,1)S(1)}, bf16[49,64,128]{2,1,0:T(8,128)(2,1)S(1)}) custom-call(s32[8,27]{1,0:T(8,128)S(1)} %clamp_bitcast_fusion.dst_ref.table_ref, ...), custom_call_target="tpu_custom_call", output_to_operand_aliasing={{3}: (3, {})} | custom-call | flops 905969664 | bytes 4000000 | tf_op jit(solution)/shard_map/pallas_call | solution.py:330
  19.3 0.1 collective-permute-start.14
  19.4 0.8 %shard_map.85 = bf16[8,64,128]{2,1,0:T(8,128)(2,1)S(1)} custom-call(bf16[8,4,16,1152]{3,2,1,0:T(8,128)(2,1)S(1)} %get-tuple-element.95.mid, bf16[8,2,16,1152]{3,2,1,0:T(8,128)(2,1)S(1)} %get-tuple-element.103.edge, bf16[27,128,128]{2,1,0:T(8,128)(2,1)S(1)} %copy-done.3, f32[512,128]{1,0:T(8,128)S(1)} %get-tuple-element.104.grad_mid), custom_call_target="tpu_custom_call" | custom-call | flops 905969664 | bytes 4000000 | tf_op jit(solution)/shard_map/pallas_call | solution.py:359
  20.2 1.1 %shard_map.86 = (bf16[8,2,16,1152]{3,2,1,0:T(8,128)(2,1)S(1)}, bf16[49,64,128]{2,1,0:T(8,128)(2,1)S(1)}) custom-call(s32[8,27]{1,0:T(8,128)S(1)} %clamp_bitcast_fusion.dst_ref.table_ref, bf16[49,64,128]{2,1,0:T(8,128)(2,1)S(1)} %get-tuple-element.105._, bf16[9,16,256]{2,1,0:T(8,128)(2,1)S(1)} %collective-permute-done.12.rest_0_, ...), custom_call_target="tpu_custom_call", output_to_operand_aliasing={{1}: (1, {})} | custom-call | flops 905969664 | bytes 4000000 | tf_op jit(solution)/shard_map/pallas_call | solution.py:347
  21.3 0.0 collective-permute-done.14
  21.3 0.1 add_convert_fusion.1
  21.4 20.2 %all_to_all.30 = bf16[16,7,16,128]{3,2,1,0:T(8,128)(2,1)S(1)} all-to-all(bf16[16,7,16,128]{3,2,1,0:T(8,128)(2,1)S(1)} %bitcast.25), channel_id=1, replica_groups=mesh['x'=4,'c'=2,'y'=4,'z'=8] {'x','y'}, dimensions={0} | all-to-all | bytes 917504 | tf_op jit(solution)/shard_map/all_to_all | solution.py:426
  41.6 0.1 convert_reduce_fusion.1
  41.9 12.5 %all_to_all.31 = f16[8,120,128]{2,1,0:T(8,128)(2,1)S(1)} all-to-all(f16[8,120,128]{2,1,0:T(8,128)(2,1)S(1)} %broadcast_in_dim.13), channel_id=1, replica_groups=mesh['x'=4,'c'=2,'y'=4,'z'=8] {'z'}, dimensions={0} | all-to-all | bytes 491520 | tf_op jit(solution)/shard_map/all_to_all | solution.py:433
  54.5 0.1 broadcast_in_dim.14
  54.6 11.7 %all_to_all.32 = bf16[16,7,16,128]{3,2,1,0:T(8,128)(2,1)S(1)} all-to-all(bf16[16,7,16,128]{3,2,1,0:T(8,128)(2,1)S(1)} %broadcast_in_dim.14), channel_id=1, replica_groups=mesh['x'=4,'c'=2,'y'=4,'z'=8] {'x','y'}, dimensions={0} | all-to-all | bytes 917504 | tf_op jit(solution)/shard_map/all_to_all | solution.py:437
  66.3 4.9 %collective-permute-start.15 = (bf16[4,28,16,128]{3,2,1,0:T(8,128)(2,1)S(1)}, bf16[4,28,16,128]{3,2,1,0:T(8,128)(2,1)S(1)}, u32[]{:S(2)}, u32[]{:S(2)}) collective-permute-start(bf16[4,28,16,128]{3,2,1,0:T(8,128)(2,1)S(1)} %bitcast.27), channel_id=1, source_target_pairs={{0,32},{32,0},{1,33},{33,1},{2,34},{34,2},{3,35},{35,3},{4,36},{36... | collective-permute-start | bytes 1376264 | tf_op jit(solution)/shard_map/ppermute | solution.py:377
  71.2 0.0 copy-start
  71.2 0.0 copy-start.1
  71.2 0.0 copy-start.2
  71.2 0.8 %shard_map.87 = bf16[8,64,128]{2,1,0:T(8,128)(2,1)S(1)} custom-call(bf16[8,4,16,1152]{3,2,1,0:T(8,128)(2,1)S(1)} %get-tuple-element.108.mid, bf16[8,2,16,1152]{3,2,1,0:T(8,128)(2,1)S(1)} %get-tuple-element.109.edge, bf16[27,128,128]{2,1,0:T(8,128)(2,1)S(1)} %copy-done.3, f32[512,128]{1,0:T(8,128)S(1)} %get-tuple-element.110.outputs_mid), custom_call_target="tpu_custom_call" | custom-call | flops 905969664 | bytes 4000000 | tf_op jit(solution)/shard_map/pallas_call | solution.py:359
  72.0 0.5 slice.38
  73.2 0.0 collective-permute-done.15
  73.2 0.0 copy-done
  73.2 0.0 copy-done.1
  73.2 0.0 copy-done.2
  73.2 1.6 %conditional.1 = ((bf16[8,64,128]{2,1,0:T(8,128)(2,1)}, bf16[8,64,128]{2,1,0:T(8,128)(2,1)}, f32[27,128,128]{2,1,0:T(8,128)})) conditional(s32[]{:T(128)} %bitcast.14, (bf16[4,28,16,128]{3,2,1,0:T(8,128)(2,1)S(1)}, bf16[4,28,16,128]{3,2,1,0:T(8,128)(2,1)S(1)}, bf16[8,64,128]{2,1,0:T(8,128)(2,1)S(1)}, bf16[8,64,128]{2,1,0:T(8,128)(2,1)S(1)}) %tuple.36, ...), branch_computations={%region_3.4_spmd, %region_4.8_spmd} | conditional | flops 4531423232 | bytes 35915928 | solution.py:507
  73.2 1.4 %branch_0_fun.1 = (bf16[8,64,128]{2,1,0:T(8,128)(2,1)}, bf16[8,64,128]{2,1,0:T(8,128)(2,1)}, f32[27,128,128]{2,1,0:T(8,128)}) custom-call(bf16[4,28,16,128]{3,2,1,0:T(8,128)(2,1)S(1)} %get-tuple-element.24.own_ref, bf16[4,28,16,128]{3,2,1,0:T(8,128)(2,1)S(1)} %get-tuple-element.25.other_ref, bf16[8,64,128]{2,1,0:T(8,128)(2,1)S(1)} %get-tuple-element.26.outputs_ref, ...), custom_call_target="tpu_custom_call" | custom-call | tf_op jit(solution)/shard_map/cond/branch_0_fun/pallas_call | solution.py:463
  (16 shorter events, 0.2 us)
Async XLA Ops:
  0.6 14.2 %copy-start.3 = (bf16[27,128,128]{2,1,0:T(8,128)(2,1)S(1)}, bf16[27,128,128]{2,1,0:T(8,128)(2,1)}, u32[]{:S(2)}) copy-start(bf16[27,128,128]{2,1,0:T(8,128)(2,1)} %weights_ref.5) | copy-start | bytes 2654212
  2.0 6.9 %collective-permute-start.10 = (bf16[9,16,256]{2,1,0:T(8,128)(2,1)S(1)}, bf16[9,16,256]{2,1,0:T(8,128)(2,1)S(1)}, u32[]{:S(2)}, u32[]{:S(2)}) collective-permute-start(bf16[9,16,256]{2,1,0:T(8,128)(2,1)S(1)} %get-tuple-element.87), channel_id=1, source_target_pairs={{1,2},{2,1},{3,4},{4,3},{5,6},{6,5},{7,8},{8,7},{9,10},{10,9},{11,... | collective-permute-start | bytes 221192 | tf_op jit(solution)/shard_map/ppermute | solution.py:483
  2.7 7.2 %collective-permute-start.11 = (bf16[9,16,256]{2,1,0:T(8,128)(2,1)S(1)}, bf16[9,16,256]{2,1,0:T(8,128)(2,1)S(1)}, u32[]{:S(2)}, u32[]{:S(2)}) collective-permute-start(bf16[9,16,256]{2,1,0:T(8,128)(2,1)S(1)} %get-tuple-element.88), channel_id=1, source_target_pairs={{0,1},{1,0},{2,3},{3,2},{4,5},{5,4},{6,7},{7,6},{8,9},{9,8},{10,11... | collective-permute-start | bytes 221192 | tf_op jit(solution)/shard_map/ppermute | solution.py:484
  9.9 7.7 %collective-permute-start.12 = (bf16[9,16,256]{2,1,0:T(8,128)(2,1)S(1)}, bf16[9,16,256]{2,1,0:T(8,128)(2,1)S(1)}, u32[]{:S(2)}, u32[]{:S(2)}) collective-permute-start(bf16[9,16,256]{2,1,0:T(8,128)(2,1)S(1)} %maximum_maximum_fusion), channel_id=1, source_target_pairs={{0,32},{32,0},{1,33},{33,1},{2,34},{34,2},{3,35},{35,3},{4,36},{36... | collective-permute-start | bytes 221192 | tf_op jit(solution)/shard_map/ppermute | solution.py:491
  11.8 5.8 %collective-permute-start.13 = (bf16[9,16,256]{2,1,0:T(8,128)(2,1)S(1)}, bf16[9,16,256]{2,1,0:T(8,128)(2,1)S(1)}, u32[]{:S(2)}, u32[]{:S(2)}) collective-permute-start(bf16[9,16,256]{2,1,0:T(8,128)(2,1)S(1)} %maximum_maximum_fusion.1), channel_id=1, source_target_pairs={{32,64},{96,128},{160,192},{64,32},{128,96},{192,160},{33,65},{97,... | collective-permute-start | bytes 221192 | tf_op jit(solution)/shard_map/ppermute | solution.py:492
  19.3 2.0 %collective-permute-start.14 = (bf16[4,28,16,128]{3,2,1,0:T(8,128)(2,1)S(1)}, bf16[4,28,16,128]{3,2,1,0:T(8,128)(2,1)S(1)}, u32[]{:S(2)}, u32[]{:S(2)}) collective-permute-start(bf16[4,28,16,128]{3,2,1,0:T(8,128)(2,1)S(1)} %get-tuple-element.102), channel_id=1, source_target_pairs={{0,32},{32,0},{1,33},{33,1},{2,34},{34,2},{3,35},{35,3},{4,36},{36... | collective-permute-start | bytes 1376264 | tf_op jit(solution)/shard_map/ppermute | solution.py:372
  66.3 6.9 %collective-permute-start.15 = (bf16[4,28,16,128]{3,2,1,0:T(8,128)(2,1)S(1)}, bf16[4,28,16,128]{3,2,1,0:T(8,128)(2,1)S(1)}, u32[]{:S(2)}, u32[]{:S(2)}) collective-permute-start(bf16[4,28,16,128]{3,2,1,0:T(8,128)(2,1)S(1)} %bitcast.27), channel_id=1, source_target_pairs={{0,32},{32,0},{1,33},{33,1},{2,34},{34,2},{3,35},{35,3},{4,36},{36... | collective-permute-start | bytes 1376264 | tf_op jit(solution)/shard_map/ppermute | solution.py:377
  71.2 2.0 %copy-start = (bf16[8,64,128]{2,1,0:T(8,128)(2,1)S(1)}, bf16[8,64,128]{2,1,0:T(8,128)(2,1)}, u32[]{:S(2)}) copy-start(bf16[8,64,128]{2,1,0:T(8,128)(2,1)} %features_ref.1) | copy-start | bytes 393220
  71.2 2.0 %copy-start.1 = (bf16[8,64,128]{2,1,0:T(8,128)(2,1)S(1)}, bf16[8,64,128]{2,1,0:T(8,128)(2,1)}, u32[]{:S(2)}) copy-start(bf16[8,64,128]{2,1,0:T(8,128)(2,1)} %cotangent_ref.1) | copy-start | bytes 393220
  71.2 2.0 %copy-start.2 = (s32[40]{0:T(128)S(1)}, s32[40]{0:T(128)}, u32[]{:S(2)}) copy-start(s32[40]{0:T(128)} %recv_slot_ref.1) | copy-start | bytes 484
